TPU v7x, 32 devices: a whole 2x2x4 slice. The times are simulated.
32 devices in a mesh: rep: 2 (over y), tp: 4 (over z), ad: 4 (over x, core).
Axes of the slice: x: 2, y: 2, z: 4, core: 2. Of those that a mesh axis runs over, the one named last changes fastest.
Arguments:
- activations: bfloat16 [4096, 8192], P(('rep', 'ad'), 'tp'), parts along dimension 0, may hold values from -6 to 6
- adapter_of_row: int32 [4096], P(('rep', 'ad')), parts along dimension 0, may hold values from 0 to 4095, as said below
- adapter_resident_slot: int32 [8192], P('rep'), parts along dimension 0, may hold values from -1 to 31, as said below
- key_value_weight: bfloat16 [8192, 2048], P('tp'), may hold values from -0.09375 to 0.09375
- resident_down_factors: bfloat16 [16384, 2048], P(('rep', 'tp'), 'ad'), parts along dimension 0, may hold values from -0.0625 to 0.0625
- resident_up_factors: bfloat16 [4096, 2048], P(('rep', 'ad'), 'tp'), parts along dimension 0, may hold values from -0.75 to 0.75
Outputs:
- kv_out: bfloat16 [4096, 2048], P(('rep', 'ad'), 'tp'), parts along dimension 0
There are 2 independent parts, one for each index of `rep`. A program takes and returns all parts, laid end to end along the dimension named above; an argument that names none is the same for every part. Nothing has to cross between parts.
Inputs may be any that keep to these rules, and one draw needn't show every extreme that they name: `adapter_of_row`: every row names a resident adapter. Of the rows owned by one index of ad, at most 128 have their slot on any one index of ad; in every draw there is one index of ad (which one is drawn) that receives exactly 128 rows from every index of ad. `adapter_resident_slot`: exactly 32 adapters are resident, each slot 0 to 31 holding one; all others are -1.
All inputs are finite; a program needn't handle non-finite values.
Results may differ from a plain program's by a relative error of at most 0.014.
Values may be sent and summed in bfloat16 or wider, within the bound.
No kernel may reach another device: no remote copies, remote signals or barrier semaphores. Data moves between devices by JAX's collectives and lax.ppermute only.
A program may use at most 64 MiB of HBM per device.

v0:
```python
import jax
import jax.numpy as jnp
from jax import lax
from jax.sharding import PartitionSpec as P

ADAPTER_RANK = 64


def bucket_positions(holder, holders):
    onehot = (holder[:, None] == jnp.arange(holders, dtype=jnp.int32)[None, :]).astype(jnp.int32)
    before = jnp.cumsum(onehot, axis=0) - onehot
    return jnp.sum(before * onehot, axis=1)


def adapter_updates(received_rows, slot_numbers, resident_down_factors, resident_up_factors):
    resident_slot_count = resident_up_factors.shape[0] // ADAPTER_RANK
    row_count = received_rows.shape[0]
    selector = slot_numbers[:, None] == jnp.arange(resident_slot_count, dtype=jnp.int32)[None, :]
    partial_result = jnp.dot(
        received_rows, resident_down_factors, preferred_element_type=jnp.float32
    ).reshape(row_count, resident_slot_count, ADAPTER_RANK)
    partial_result = jnp.sum(partial_result * selector[:, :, None].astype(jnp.float32), axis=1)
    shrink = lax.psum(partial_result.astype(jnp.bfloat16), "tp")
    spread_rows = (shrink[:, None, :] * selector[:, :, None].astype(jnp.bfloat16)).reshape(
        row_count, resident_slot_count * ADAPTER_RANK
    )
    return jnp.dot(spread_rows, resident_up_factors, preferred_element_type=jnp.float32).astype(
        jnp.bfloat16
    )


def shards(
    activations,
    adapter_of_row,
    adapter_resident_slot,
    key_value_weight,
    resident_down_factors,
    resident_up_factors,
):
    holders = lax.axis_size("ad")
    rows_dev, input_features = activations.shape
    capacity = rows_dev // 4
    resident_slot_count = resident_up_factors.shape[0] // ADAPTER_RANK
    key_value_shard = resident_up_factors.shape[1]
    base_sum = lax.psum_scatter(
        lax.dot_general(
            key_value_weight,
            activations,
            (((0,), (1,)), ((), ())),
            preferred_element_type=jnp.float32,
        ).astype(jnp.bfloat16),
        "tp",
        scatter_dimension=0,
        tiled=True,
    ).astype(jnp.float32)
    holder_index = lax.axis_index("ad")
    gathered, all_ids = (
        lax.all_gather(activations, "ad", axis=0, tiled=True),
        lax.all_gather(adapter_of_row, "ad", axis=0, tiled=True),
    )
    slot_all = adapter_resident_slot[all_ids]
    holder_all = (slot_all // resident_slot_count).reshape(holders, rows_dev)
    local_all = (slot_all % resident_slot_count).reshape(holders, rows_dev)

    def row_positions(holder_line):
        return bucket_positions(holder_line, holders)

    position = jax.vmap(row_positions)(holder_all)
    owners = jnp.broadcast_to(jnp.arange(holders, dtype=jnp.int32)[:, None], (holders, rows_dev))
    column = jnp.where(holder_all == holder_index, position, capacity)
    row_number = jnp.arange(holders * rows_dev, dtype=jnp.int32).reshape(holders, rows_dev)
    source = (
        jnp.full((holders, capacity), holders * rows_dev, jnp.int32)
        .at[owners, column]
        .set(row_number, mode="drop")
    )
    slot_numbers = (
        jnp.full((holders, capacity), -1, jnp.int32).at[owners, column].set(local_all, mode="drop")
    )
    received_rows = jnp.take(gathered, source.reshape(-1), axis=0, mode="clip")
    row_updates = adapter_updates(
        received_rows, slot_numbers.reshape(-1), resident_down_factors, resident_up_factors
    )
    row_updates = lax.optimization_barrier(row_updates).astype(jnp.float32)
    placed = (
        jnp.zeros((holders * rows_dev, key_value_shard), jnp.float32)
        .at[source.reshape(-1)]
        .set(row_updates, mode="drop")
    )
    own_deltas = lax.psum_scatter(
        placed.astype(jnp.bfloat16), "ad", scatter_dimension=0, tiled=True
    ).astype(jnp.float32)
    return (base_sum.T + own_deltas).astype(jnp.bfloat16)


def solution(mesh):
    in_specs = (
        P(("rep", "ad"), "tp"),
        P(("rep", "ad")),
        P("rep"),
        P("tp", None),
        P(("rep", "tp"), "ad"),
        P(("rep", "ad"), "tp"),
    )
    out_specs = P(("rep", "ad"), "tp")
    return jax.shard_map(shards, mesh=mesh, in_specs=in_specs, out_specs=out_specs, check_vma=False)
```

profile of v0, /device:TPU:0, one launch (start us, length us, event | category | flops | bytes accessed | tf_op | source)
XLA Modules:
  0.0 205.4 jit_solution(10422485656415721772)
XLA Ops:
  6.5 0.7 all-gather.3.cloned.1.call-update
  7.4 6.1 %all-gather = s32[4,1,512]{2,1,0:T(1,128)S(1)} all-gather(s32[1,1,512]{2,1,0:T(1,128)S(1)} %bitcast.50), channel_id=1, replica_groups=mesh['rep'=2,'tp'=4,'ad'=4] {'ad'}, dimensions={0}, use_global_device_ids=true | all-gather | bytes 10240 | tf_op jit(solution)/shard_map/all_gather | solution.py:59
  13.5 11.8 %gather_fusion = s32[2048]{0:T(1024)S(1)} fusion(s32[4096]{0:T(1024)S(1)} %copy-done.1, s32[2048]{0:T(1024)S(1)} %fusion.13), kind=kCustom, calls=%fused_computation | custom fusion | bytes 24576 | tf_op jit(solution)/shard_map/gather | solution.py:61
  25.4 4.8 %reduce-window.6 = s32[4,4,4,128]{3,2,1,0:T(4,128)S(1)} reduce-window(s32[4,4,4,128]{3,2,1,0:T(4,128)S(1)} %fusion.6, s32[]{:T(128)} %constant.46.clone.1), window={size=1x1x1x128 pad=0_0x0_0x0_0x127_0}, to_apply=%region_1.2 | reduce-window | flops 1040384 | bytes 65540 | tf_op jit(solution)/shard_map/reduce-window
  30.2 0.4 slice_reduce_fusion
  30.7 0.7 reduce-window.9
  31.7 0.1 and_reduce_fusion
  31.8 8.0 %scatter_custom_fusion.1 = s32[512]{0:T(512)S(1)} fusion(s32[2048]{0:T(1024)S(1)} %bitcast.48, s32[2048]{0:T(1024)S(1)} %bitcast.46, s32[]{:T(128)} %constant.45.clone.1), kind=kCustom, calls=%fused_computation.62 | custom fusion | bytes 2052 | tf_op jit(solution)/shard_map/reshape | solution.py:87
  39.8 8.0 %scatter_custom_fusion.2 = s32[512]{0:T(512)S(1)} fusion(s32[2048]{0:T(1024)S(1)} %bitcast.49, s32[2048]{0:T(1024)S(1)} %bitcast.47, s32[]{:T(128)} %constant.51.clone.1), kind=kCustom, calls=%fused_computation.60 | custom fusion | bytes 2052
  47.9 22.0 %all-gather.3.cloned.1.call-done = bf16[2048,2048]{1,0:T(8,128)(2,1)} async-done(((bf16[512,2048]{1,0:T(8,128)(2,1)}), bf16[2048,2048]{1,0:T(8,128)(2,1)}) %all-gather.3.cloned.1.call-update) | async-done | bytes 8388624 | tf_op jit(solution)/shard_map/all_gather | solution.py:58
  69.9 9.7 %gather_fusion.1 = bf16[512,2048]{1,0:T(8,128)(2,1)} fusion(bf16[2048,2048]{1,0:T(8,128)(2,1)} %all-gather.3.cloned.1.call-done, s32[1024]{0:T(1024)S(1)} %pad_clamp_fusion), kind=kCustom, calls=%fused_computation.1 | custom fusion | bytes 4196352 | tf_op jit(solution)/shard_map/jit(_take)/gather | solution.py:80
  79.6 2.9 %fusion.21 = f32[512,512]{0,1:T(8,128)S(1)} fusion(bf16[512,2048]{1,0:T(8,128)(2,1)} %gather_fusion.1, bf16[2048,512]{1,0:T(8,128)(2,1)S(1)} %copy-done), kind=kOutput, calls=%fused_computation.64 | convolution fusion | flops 1073741824 | bytes 5242880 | tf_op jit(solution)/shard_map/dot_general | solution.py:19
  82.5 0.8 multiply_reduce_fusion
  83.3 0.2 reduce-scatter.3.cloned.1.call-start
  83.5 9.9 %convolution_convert_fusion = bf16[2048,512]{1,0:T(8,128)(2,1)} fusion(bf16[2048,2048]{1,0:T(8,128)(2,1)} %param.9, bf16[512,2048]{1,0:T(8,128)(2,1)} %param.6), kind=kOutput, calls=%fused_computation.5 | convolution fusion | flops 4296015872 | bytes 12582912 | tf_op jit(solution)/shard_map/dot_general | solution.py:46
  93.5 23.9 %all-reduce.2.cloned.1.call-done = bf16[512,64]{0,1:T(8,128)(2,1)} async-done(((bf16[512,64]{0,1:T(8,128)(2,1)}), bf16[512,64]{0,1:T(8,128)(2,1)}) %all-reduce.2.cloned.1.call-update) | async-done | bytes 65552 | tf_op jit(solution)/shard_map/psum | solution.py:23
  117.4 0.9 broadcast_multiply_fusion
  118.3 0.5 convolution_convert_fusion.1
  118.8 4.5 %scatter_custom_fusion = f32[2048,512]{1,0:T(8,128)} fusion(s32[512]{0:T(512)S(1)} %bitcast.51, f32[]{:T(128)} %constant.44.clone.1, bf16[512,512]{1,0:T(8,128)(2,1)S(1)} %convolution_convert_fusion.1), kind=kCustom, calls=%fused_computation.6 | custom fusion | flops 262144 | bytes 4718596 | tf_op jit(solution)/shard_map/scatter | solution.py:88
  123.2 4.7 %copy.12 = bf16[2048,512]{0,1:T(8,128)(2,1)} copy(f32[2048,512]{1,0:T(8,128)} %scatter_custom_fusion) | data formatting | bytes 6291456 | tf_op jit(solution)/shard_map/scatter | solution.py:88
  128.0 35.4 %reduce-scatter.3.cloned.1.call-done = bf16[512,512]{1,0:T(8,128)(2,1)} async-done(((bf16[2048,512]{1,0:T(8,128)(2,1)}), bf16[512,512]{1,0:T(8,128)(2,1)}) %reduce-scatter.3.cloned.1.call-update) | async-done | bytes 524304 | tf_op jit(solution)/shard_map/reduce_scatter | solution.py:45
  163.4 33.1 %reduce-scatter.5.cloned.1.call-done = bf16[512,512]{0,1:T(8,128)(2,1)} async-done(((bf16[2048,512]{0,1:T(8,128)(2,1)}), bf16[512,512]{0,1:T(8,128)(2,1)}) %reduce-scatter.5.cloned.1.call-update) | async-done | bytes 524304 | tf_op jit(solution)/shard_map/reduce_scatter | solution.py:90
  196.6 1.3 fusion.2
  197.9 1.0 copy.13
  (38 shorter events, 0.6 us)
Async XLA Ops:
  6.5 73.1 %copy-start = (bf16[2048,512]{1,0:T(8,128)(2,1)S(1)}, bf16[2048,512]{1,0:T(8,128)(2,1)}, u32[]{:S(2)}) copy-start(bf16[2048,512]{1,0:T(8,128)(2,1)} %param.10) | copy-start | bytes 6291460
  6.5 0.8 copy-start.2
  6.5 6.9 %copy-start.1 = (s32[4096]{0:T(1024)S(1)}, s32[4096]{0:T(1024)}, u32[]{:S(2)}) copy-start(s32[4096]{0:T(1024)} %param.8) | copy-start | bytes 49156
  6.5 63.4 %all-gather.3.cloned.1.call-start = ((), (), s32[]{:S(2)}) async-start(), calls=%async_computation.3 | async-start | bytes 10485760 | tf_op jit(solution)/shard_map/all_gather | solution.py:58
  7.3 110.2 %all-reduce.2.cloned.1.call-start = ((), (), s32[]{:S(2)}) async-start(), calls=%async_computation.4 | async-start | bytes 131072 | tf_op jit(solution)/shard_map/psum | solution.py:23
  13.5 18.1 %copy-start.4 = (s32[2]{0:T(128)S(1)}, s32[2]{0:T(128)}, u32[]{:S(2)}) copy-start(s32[2]{0:T(128)} %constant.56) | copy-start | bytes 28
  13.5 18.2 %copy-start.3 = (s32[2]{0:T(128)S(1)}, s32[2]{0:T(128)}, u32[]{:S(2)}) copy-start(s32[2]{0:T(128)} %constant.59) | copy-start | bytes 28
  83.3 80.1 %reduce-scatter.3.cloned.1.call-start = ((), (), s32[]{:S(2)}) async-start(), calls=%async_computation.2 | async-start | bytes 2621440 | tf_op jit(solution)/shard_map/reduce_scatter | solution.py:45
  93.4 24.9 %copy-start.5 = (bf16[512,512]{1,0:T(8,128)(2,1)S(1)}, bf16[512,512]{1,0:T(8,128)(2,1)}, u32[]{:S(2)}) copy-start(bf16[512,512]{1,0:T(8,128)(2,1)} %param.11) | copy-start | bytes 1572868
  93.5 103.1 %reduce-scatter.5.cloned.1.call-start = ((), (), s32[]{:S(2)}) async-start(), calls=%async_computation.5 | async-start | bytes 2621440 | tf_op jit(solution)/shard_map/reduce_scatter | solution.py:90
Sparse Core Ops, SparseCore 0:
  8.9 60.9 all-gather.2
  83.4 33.9 all-reduce.1
  119.8 43.5 reduce-scatter.2
  165.8 30.7 reduce-scatter.4
where the time goes:
time: 206 us; the launch traced here: 205 us
  waiting for transfers between devices  115 us (56%)
  local copies, waits for them, and re-layouts  43.8 us (21%)
  other arithmetic  13.4 us (7%)
  between operations  13.3 us (6%)
  matrix products  13.2 us (6%)
  blocking collectives  6.1 us (3%)
    reduce_scatter x1, waiting for transfers between devices, shards(): lax.psum_scatter(lax.dot_general(key_value_weight, activations, (((0,), (...  35.4 us
    reduce_scatter x1, waiting for transfers between devices, shards(): lax.psum_scatter(placed.astype(jnp.bfloat16), 'ad', scatter_dimension=0,...  33.1 us
    psum x1, waiting for transfers between devices, adapter_updates(): shrink = lax.psum(partial_result.astype(jnp.bfloat16), 'tp')  23.9 us
    all_gather x1, waiting for transfers between devices, shards(): lax.all_gather(activations, 'ad', axis=0, tiled=True)  22 us
    gather x3, local copies, waits for them, and re-layouts, shards(): slot_all = adapter_resident_slot[all_ids]  11.8 us
    dot_general x1, matrix products, shards(): lax.dot_general(key_value_weight, activations, (((0,), (1,)), ((), ())),...  9.9 us
    gather x1, local copies, waits for them, and re-layouts, shards(): received_rows = jnp.take(gathered, source.reshape(-1), axis=0, mode='clip')  9.69 us
    unnamed x16, local copies, waits for them, and re-layouts  8.13 us
  transfers between devices with their start and end apart: 4, of which 4 were waited for; matrix products, arithmetic and copies ran while one was open for 27% of the time, Pallas kernels for 0%

commit v1 on v0

v1 whole, which is shorter than its diff:
```python
import functools

import jax
import jax.numpy as jnp
from jax import lax
from jax.experimental import pallas as pl
from jax.experimental.pallas import tpu as pltpu
from jax.sharding import PartitionSpec as P

ADAPTER_RANK = 64
LANES = 128
VMEM_BYTES = 32 * 1024 * 1024

bf16 = jnp.bfloat16
f32 = jnp.float32
i32 = jnp.int32


def params():
    return pltpu.CompilerParams(vmem_limit_bytes=VMEM_BYTES)


def cost(flops, nbytes):
    return pl.CostEstimate(flops=flops, bytes_accessed=nbytes, transcendentals=0)


def dot(a, b, contract=((1,), (0,))):
    return lax.dot_general(a, b, (contract, ((), ())), preferred_element_type=f32)


def iota(shape, dim):
    return lax.broadcasted_iota(i32, shape, dim)


def sort_body(slots, capacity, me_ref, ids_ref, table_ref, x_ref, place_ref, *outs):
    rows, features = x_ref.shape
    holders = len(outs)
    ids = ids_ref[...]
    table = table_ref[...].astype(f32).astype(bf16)
    low = (iota((LANES, rows), 0) == (ids & (LANES - 1))).astype(f32).astype(bf16)
    high = iota((table.shape[0], rows), 0) == lax.shift_right_logical(ids, 7)
    slot = jnp.sum(jnp.where(high, dot(table, low), 0.0), axis=0, keepdims=True).astype(i32)
    holder = lax.div(slot, slots)
    tag = (slot - holder * slots + 1).astype(f32)
    partner = holder ^ me_ref[0]
    mine = iota((max(8, holders), rows), 0) == partner
    earlier = (iota((rows, rows), 0) < iota((rows, rows), 1)).astype(f32).astype(bf16)
    before = dot(mine.astype(f32).astype(bf16), earlier)
    rank = jnp.sum(jnp.where(mine, before, 0.0), axis=0, keepdims=True).astype(i32)
    place = partner * capacity + rank
    place_ref[...] = jnp.broadcast_to(place, place_ref.shape)
    tags = jnp.broadcast_to(tag, (LANES, rows)).astype(bf16)
    x = x_ref[...]
    for j, out in enumerate(outs):
        pick = (iota((capacity, rows), 0) + j * capacity == place).astype(f32).astype(bf16)
        out[:, :features] = dot(pick, x).astype(bf16)
        out[:, features:] = dot(pick, tags, ((1,), (1,))).astype(bf16)


def sort_rows(me, ids, table, x, holders, slots, capacity):
    rows, features = x.shape
    out = jax.ShapeDtypeStruct((capacity, features + LANES), bf16)
    return pl.pallas_call(
        functools.partial(sort_body, slots, capacity),
        out_shape=[jax.ShapeDtypeStruct((8, rows), i32)] + [out] * holders,
        in_specs=[pl.BlockSpec(memory_space=pltpu.SMEM)] + [pl.BlockSpec(memory_space=pltpu.VMEM)] * 3,
        out_specs=[pl.BlockSpec(memory_space=pltpu.VMEM)] * (holders + 1),
        compiler_params=params(),
        cost_estimate=cost(2 * holders * capacity * rows * features, 4 * rows * features),
        name="sort_rows",
    )(me.reshape(1), ids.reshape(1, rows), table.reshape(-1, LANES), x)


def base_body(order_ref, x_ref, w_ref, out_ref):
    out_ref[...] = dot(x_ref[...], w_ref[...]).astype(bf16)


def base_blocks(order, x, weight, width, tile):
    rows, features = x.shape
    count = order.shape[0]
    tiles = width // tile
    return pl.pallas_call(
        base_body,
        out_shape=jax.ShapeDtypeStruct((count, rows, width), bf16),
        grid_spec=pltpu.PrefetchScalarGridSpec(
            num_scalar_prefetch=1,
            grid=(count, tiles),
            in_specs=[
                pl.BlockSpec((rows, features), lambda b, t, order: (0, 0)),
                pl.BlockSpec((features, tile), lambda b, t, order: (0, order[b] * tiles + t)),
            ],
            out_specs=pl.BlockSpec((None, rows, tile), lambda b, t, order: (b, 0, t)),
        ),
        compiler_params=params(),
        cost_estimate=cost(2 * count * rows * features * width, 2 * (rows + count * width) * features),
        name="base_blocks",
    )(order, x, weight)


def slot_mask(tag, group):
    lane = iota(tag.shape, 1)
    return tag == jnp.where(lane < ADAPTER_RANK, 2 * group + 1, 2 * group + 2).astype(f32)


def shrink_body(down_ref, *refs):
    parts, out = refs[:-1], refs[-1]
    features, width = down_ref.shape
    down = down_ref[...]
    capacity = parts[0].shape[0]
    half = len(parts) // 2
    sums = []
    for part in parts:
        full = dot(part[:, :features], down)
        tag = part[:, features:].astype(f32)
        total = jnp.zeros((capacity, LANES), f32)
        for group in range(width // LANES):
            total += jnp.where(slot_mask(tag, group), full[:, group * LANES:(group + 1) * LANES], 0.0)
        sums.append(total + pltpu.roll(total, ADAPTER_RANK, 1))
    first = iota((capacity, LANES), 1) < ADAPTER_RANK
    for k in range(half):
        out[k * capacity:(k + 1) * capacity, :] = jnp.where(first, sums[k], sums[k + half]).astype(bf16)


def shrink_partial(parts, down):
    features, width = down.shape
    capacity = parts[0].shape[0]
    total = len(parts) * capacity
    return pl.pallas_call(
        shrink_body,
        out_shape=jax.ShapeDtypeStruct((total // 2, LANES), bf16),
        compiler_params=params(),
        cost_estimate=cost(2 * total * features * width, 2 * features * (total + width)),
        name="shrink_partial",
    )(down, *parts)


def expand_body(count, one_ref, two_ref, up_ref, *refs):
    tags, outs = refs[:count], refs[count:]
    capacity = outs[0].shape[0]
    half = count // 2
    shrink = (one_ref[...].astype(f32) + two_ref[...].astype(f32)).astype(bf16).astype(f32)
    up = up_ref[...]
    first = iota((capacity, LANES), 1) < ADAPTER_RANK
    for k in range(count):
        rows = shrink[(k % half) * capacity:(k % half + 1) * capacity]
        turned = pltpu.roll(rows, ADAPTER_RANK, 1)
        rows = jnp.where(first, rows, turned) if k < half else jnp.where(first, turned, rows)
        tag = tags[k][...].astype(f32)
        spread = [
            jnp.where(slot_mask(tag, group), rows, 0.0).astype(bf16) for group in range(up.shape[0] // LANES)
        ]
        outs[k][...] = dot(jnp.concatenate(spread, axis=1), up).astype(bf16)


def expand(one, two, up, parts):
    capacity, width = parts[0].shape
    count = len(parts)
    tag_block = pl.BlockSpec((capacity, LANES), lambda i: (0, width // LANES - 1))
    whole = lambda a: pl.BlockSpec(a.shape, lambda i: (0, 0))
    columns = up.shape[1]
    return pl.pallas_call(
        functools.partial(expand_body, count),
        grid=(1,),
        out_shape=[jax.ShapeDtypeStruct((capacity, columns), bf16)] * count,
        in_specs=[whole(one), whole(two), whole(up)] + [tag_block] * count,
        out_specs=[pl.BlockSpec((capacity, columns), lambda i: (0, 0))] * count,
        compiler_params=params(),
        cost_estimate=cost(2 * count * capacity * up.size, 2 * (up.size + count * capacity * columns)),
        name="expand",
    )(one, two, up, *parts)


def finish_body(count, place_ref, *refs):
    deltas, sums, out = refs[:count], refs[count:-1], refs[-1]
    rows = out.shape[0]
    place = place_ref[0:1, :]
    capacity = deltas[0].shape[0]
    total = sums[0][...].astype(f32)
    for term in sums[1:]:
        total += term[...].astype(f32)
    own = jnp.zeros(out.shape, f32)
    for j, delta in enumerate(deltas):
        pick = (iota((capacity, rows), 0) + j * capacity == place).astype(f32).astype(bf16)
        own += dot(pick, delta[...], ((0,), (0,)))
    out[...] = (total + own).astype(bf16)


def finish(place, deltas, sums, own):
    rows, columns = own.shape[1:]
    count = len(deltas)
    return pl.pallas_call(
        functools.partial(finish_body, count),
        grid=(1,),
        out_shape=jax.ShapeDtypeStruct((rows, columns), bf16),
        in_specs=[pl.BlockSpec(place.shape, lambda i: (0, 0))]
        + [pl.BlockSpec(d.shape, lambda i: (0, 0)) for d in deltas]
        + [pl.BlockSpec((None, rows, columns), lambda i: (own.shape[0] - 1, 0, 0))]
        + [pl.BlockSpec((rows, columns), lambda i: (0, 0)) for s in sums],
        out_specs=pl.BlockSpec((rows, columns), lambda i: (0, 0)),
        compiler_params=params(),
        cost_estimate=cost(2 * rows * rows * columns, 12 * rows * columns),
        name="finish",
    )(place, *deltas, own, *sums)


def both(a, b):
    return (a.astype(f32) + b.astype(f32)).astype(bf16)


def swap(value, axis, bit):
    return lax.ppermute(value, axis, [(i, i ^ bit) for i in range(lax.axis_size(axis))])


ORDER = ((3, 2, 1, 0), (3, 2, 0, 1), (0, 1, 3, 2), (0, 1, 2, 3))
EDGE = [(0, 1), (3, 2)]
MIDDLE = [(1, 2), (2, 1)]


def base_terms(x, weight, width):
    if lax.axis_size("tp") != len(ORDER):
        full = dot(x, weight).astype(bf16)
        return [], lax.psum_scatter(full, "tp", scatter_dimension=1, tiled=True)[None]
    order = jnp.array(ORDER, i32)[lax.axis_index("tp")]
    tile = min(width, 256)
    first = base_blocks(order[:1], x, weight, width, tile)[0]
    rest = base_blocks(order[1:], x, weight, width, tile)
    edge0 = lax.ppermute(first, "tp", EDGE)
    edge1 = lax.ppermute(rest[0], "tp", EDGE)
    middle0 = lax.ppermute(both(first, edge0), "tp", MIDDLE)
    middle1 = lax.ppermute(both(rest[0], edge1), "tp", MIDDLE)
    last = swap(both(rest[1], middle0), "tp", 1)
    return [middle1, last], rest


def shards(x, ids, table, weight, down, up):
    holders = lax.axis_size("ad")
    rows = x.shape[0]
    capacity = rows // 4
    slots = up.shape[0] // ADAPTER_RANK
    place, *send = sort_rows(lax.axis_index("ad"), ids, table, x, holders, slots, capacity)
    parts = [send[0]] + [swap(send[j], "ad", j) for j in range(1, holders)]
    sums, own = base_terms(x, weight, up.shape[1])
    mine = shrink_partial(parts, down)
    bit = 1
    while bit < lax.axis_size("tp"):
        other = swap(mine, "tp", bit)
        bit *= 2
        if bit < lax.axis_size("tp"):
            mine = both(mine, other)
    deltas = expand(mine, other, up, parts)
    back = [deltas[0]] + [swap(deltas[j], "ad", j) for j in range(1, holders)]
    return finish(place, back, sums, own)


def solution(mesh):
    in_specs = (
        P(("rep", "ad"), "tp"),
        P(("rep", "ad")),
        P("rep"),
        P("tp", None),
        P(("rep", "tp"), "ad"),
        P(("rep", "ad"), "tp"),
    )
    out_specs = P(("rep", "ad"), "tp")
    return jax.shard_map(shards, mesh=mesh, in_specs=in_specs, out_specs=out_specs, check_vma=False)
```

time: 206 us -> 81.3 us (0.39)
  waiting for transfers between devices: 115 us -> 31.3 us
  local copies, waits for them, and re-layouts: 43.8 us -> 7.38 us
  starting transfers between devices: 0.3 us -> 27.8 us
  matrix products: 13.2 us -> 0 us
  between operations: 13.3 us -> 0.14 us
  Pallas kernels: 0 us -> 12.8 us
  other arithmetic: 13.4 us -> 1.49 us
  blocking collectives: 6.1 us -> 0 us
    reduce_scatter x2 -> x0, waiting for transfers between devices: 68.6 us -> none  [the longest x1 35.4 us: shards(): lax.psum_scatter(lax.dot_general(key_value_weight, activations, (((0,), (...]
    ppermute x0 -> x13, waiting for transfers between devices: none -> 31.3 us  [the longest x9 23.2 us: swap(): lax.ppermute(value, axis, [(i, i ^ bit) for i in range(lax.axis_size(axis...]
    ppermute x0 -> x13, starting transfers between devices: none -> 27.8 us  [the longest x9 19.2 us: swap(): lax.ppermute(value, axis, [(i, i ^ bit) for i in range(lax.axis_size(axis...]
    psum x1 -> x0, waiting for transfers between devices: 23.9 us -> none  [adapter_updates(): shrink = lax.psum(partial_result.astype(jnp.bfloat16), 'tp')]
    all_gather x1 -> x0, waiting for transfers between devices: 22 us -> none  [shards(): lax.all_gather(activations, 'ad', axis=0, tiled=True)]
    gather x4 -> x0, local copies, waits for them, and re-layouts: 21.5 us -> none  [the longest x3 11.8 us: shards(): slot_all = adapter_resident_slot[all_ids]]
    dot_general x3 -> x0, matrix products: 13.2 us -> none  [the longest x1 9.9 us: shards(): lax.dot_general(key_value_weight, activations, (((0,), (1,)), ((), ())),...]
    pallas_call x0 -> x6, Pallas kernels: none -> 12.8 us  [the longest x2 7.78 us: base_blocks(): pl.pallas_call(base_body, out_shape=jax.ShapeDtypeStruct((count, rows, wi...]
  transfers between devices with their start and end apart: 4 -> 13, of which waited for: 4 -> 7; matrix products, arithmetic and copies ran while one was open for 27% -> 2% of each run, Pallas kernels for 0% -> 12%
where the time goes in v1:
time: 81.3 us; the launch traced here: 80.9 us
  waiting for transfers between devices  31.3 us (38%)
  starting transfers between devices  27.8 us (34%)
  Pallas kernels  12.8 us (16%)
  local copies, waits for them, and re-layouts  7.38 us (9%)
  other arithmetic  1.49 us (2%)
    ppermute x9, waiting for transfers between devices, swap(): lax.ppermute(value, axis, [(i, i ^ bit) for i in range(lax.axis_size(axis...  23.2 us
    ppermute x9, starting transfers between devices, swap(): lax.ppermute(value, axis, [(i, i ^ bit) for i in range(lax.axis_size(axis...  19.2 us
    pallas_call x2, Pallas kernels, base_blocks(): pl.pallas_call(base_body, out_shape=jax.ShapeDtypeStruct((count, rows, wi...  7.78 us
    unnamed x16, local copies, waits for them, and re-layouts  6.59 us
    ppermute x1, starting transfers between devices, base_terms(): edge0 = lax.ppermute(first, 'tp', EDGE)  5.09 us
    ppermute x1, waiting for transfers between devices, base_terms(): edge0 = lax.ppermute(first, 'tp', EDGE)  4.86 us
    ppermute x1, waiting for transfers between devices, base_terms(): edge1 = lax.ppermute(rest[0], 'tp', EDGE)  3.21 us
    pallas_call x1, Pallas kernels, sort_rows(): pl.pallas_call(functools.partial(sort_body, slots, capacity), out_shape=[...  1.71 us
  transfers between devices with their start and end apart: 13, of which 7 were waited for; matrix products, arithmetic and copies ran while one was open for 2% of the time, Pallas kernels for 12%

profile of v1, /device:TPU:0, one launch (start us, length us, event | category | flops | bytes accessed | tf_op | source)
XLA Modules:
  0.0 80.9 jit_solution(16816461129298323543)
XLA Ops:
  0.7 3.4 %copy-done = bf16[2048,2048]{1,0:T(8,128)(2,1)S(1)} copy-done((bf16[2048,2048]{1,0:T(8,128)(2,1)S(1)}, bf16[2048,2048]{1,0:T(8,128)(2,1)}, u32[]{:S(2)}) %copy-start) | copy-done | bytes 8388632
  4.1 1.6 %copy-done.2 = bf16[512,2048]{1,0:T(8,128)(2,1)S(1)} copy-done((bf16[512,2048]{1,0:T(8,128)(2,1)S(1)}, bf16[512,2048]{1,0:T(8,128)(2,1)}, u32[]{:S(2)}) %copy-start.2) | copy-done | bytes 2097176
  5.7 1.8 %base_blocks.3 = bf16[1,512,512]{2,1,0:T(8,128)(2,1)S(1)} custom-call(s32[1]{0:T(128)S(1)} %bitcast.19, bf16[512,2048]{1,0:T(8,128)(2,1)S(1)} %copy-done.2, bf16[2048,2048]{1,0:T(8,128)(2,1)S(1)} %copy-done), custom_call_target="tpu_custom_call" | custom-call | flops 1073741824 | bytes 4194304 | tf_op jit(solution)/shard_map/base_blocks/pallas_call | solution.py:82
  7.5 5.1 %collective-permute-start.10 = (bf16[512,512]{1,0:T(8,128)(2,1)S(1)}, bf16[512,512]{1,0:T(8,128)(2,1)S(1)}, u32[]{:S(2)}, u32[]{:S(2)}) collective-permute-start(bf16[512,512]{1,0:T(8,128)(2,1)S(1)} %bitcast.18), channel_id=1, source_target_pairs={{0,4},{12,8},{1,5},{13,9},{2,6},{14,10},{3,7},{15,11},{16,20},{28,... | collective-permute-start | bytes 1572872 | tf_op jit(solution)/shard_map/ppermute | solution.py:227
  12.7 5.9 %base_blocks.2.refs_4_ = bf16[3,512,512]{2,1,0:T(8,128)(2,1)S(1)} custom-call(s32[3]{0:T(128)S(1)} %slice_bitcast_fusion.2.order_ref, bf16[512,2048]{1,0:T(8,128)(2,1)S(1)} %copy-done.2, bf16[2048,2048]{1,0:T(8,128)(2,1)S(1)} %copy-done.1), custom_call_target="tpu_custom_call" | custom-call | flops 3221225472 | bytes 8388608 | tf_op jit(solution)/shard_map/base_blocks/pallas_call | solution.py:82
  18.7 1.3 %collective-permute-start.8 = (bf16[512,512]{1,0:T(8,128)(2,1)S(1)}, bf16[512,512]{1,0:T(8,128)(2,1)S(1)}, u32[]{:S(2)}, u32[]{:S(2)}) collective-permute-start(bf16[512,512]{1,0:T(8,128)(2,1)S(1)} %slice_bitcast_fusion.1), channel_id=1, source_target_pairs={{0,4},{12,8},{1,5},{13,9},{2,6},{14,10},{3,7},{15,11},{16,20},{28,... | collective-permute-start | bytes 1572872 | tf_op jit(solution)/shard_map/ppermute | solution.py:228
  20.0 4.9 %collective-permute-done.10 = bf16[512,512]{1,0:T(8,128)(2,1)S(1)} collective-permute-done((bf16[512,512]{1,0:T(8,128)(2,1)S(1)}, bf16[512,512]{1,0:T(8,128)(2,1)S(1)}, u32[]{:S(2)}, u32[]{:S(2)}) %collective-permute-start.10) | collective-permute-done | bytes 524320 | tf_op jit(solution)/shard_map/ppermute | solution.py:227
  25.0 1.5 %collective-permute-start.11 = (bf16[512,512]{1,0:T(8,128)(2,1)S(1)}, bf16[512,512]{1,0:T(8,128)(2,1)}, u32[]{:S(2)}, u32[]{:S(2)}) collective-permute-start(bf16[512,512]{1,0:T(8,128)(2,1)S(1)} %add_convert_fusion), channel_id=1, source_target_pairs={{4,8},{8,4},{5,9},{9,5},{6,10},{10,6},{7,11},{11,7},{20,24},{24,20... | collective-permute-start | bytes 1572872 | tf_op jit(solution)/shard_map/ppermute | solution.py:229
  26.5 1.6 %copy-done.3 = bf16[512,2048]{1,0:T(8,128)(2,1)S(1)} copy-done((bf16[512,2048]{1,0:T(8,128)(2,1)S(1)}, bf16[512,2048]{1,0:T(8,128)(2,1)}, u32[]{:S(2)}) %copy-start.3) | copy-done | bytes 2097176
  28.1 1.7 %sort_rows.1 = (s32[8,512]{1,0:T(8,128)S(1)}, bf16[128,2176]{1,0:T(8,128)(2,1)S(1)}, bf16[128,2176]{1,0:T(8,128)(2,1)S(1)}, bf16[128,2176]{1,0:T(8,128)(2,1)S(1)}, bf16[128,2176]{1,0:T(8,128)(2,1)S(1)}) custom-call(s32[1]{0:T(128)} %bitcast.me_ref, s32[1,512]{1,0:T(1,128)S(1)} %bitcast.21, s32[32,128]{1,0:T(8,128)S(1)} %bitcast.20, ...), custom_call_target="tpu_custom_call" | custom-call | flops 1073741824 | bytes 4194304 | tf_op jit(solution)/shard_map/sort_rows/pallas_call | solution.py:63
  29.9 1.6 %collective-permute-start.1 = (bf16[128,2176]{1,0:T(8,128)(2,1)S(1)}, bf16[128,2176]{1,0:T(8,128)(2,1)S(1)}, u32[]{:S(2)}, u32[]{:S(2)}) collective-permute-start(bf16[128,2176]{1,0:T(8,128)(2,1)S(1)} %get-tuple-element.17), channel_id=1, source_target_pairs={{0,2},{1,3},{2,0},{3,1},{4,6},{5,7},{6,4},{7,5},{8,10},{9,11},{10,... | collective-permute-start | bytes 1671176 | tf_op jit(solution)/shard_map/ppermute | solution.py:211
  31.8 3.2 %collective-permute-done.8 = bf16[512,512]{1,0:T(8,128)(2,1)S(1)} collective-permute-done((bf16[512,512]{1,0:T(8,128)(2,1)S(1)}, bf16[512,512]{1,0:T(8,128)(2,1)S(1)}, u32[]{:S(2)}, u32[]{:S(2)}) %collective-permute-start.8) | collective-permute-done | bytes 524320 | tf_op jit(solution)/shard_map/ppermute | solution.py:228
  35.0 1.3 %fusion = (bf16[512,512]{1,0:T(8,128)(2,1)S(1)}, bf16[512,512]{1,0:T(8,128)(2,1)S(1)}) fusion(bf16[512,512]{1,0:T(8,128)(2,1)} %collective-permute-done.11, bf16[3,512,512]{2,1,0:T(8,128)(2,1)S(1)} %base_blocks.2.refs_4_, bf16[512,512]{1,0:T(8,128)(2,1)S(1)} %collective-permute-done.8), kind=kLoop, calls=%fused_computation.1 | loop fusion | flops 2097152 | bytes 3145728 | tf_op jit(solution)/shard_map/convert_element_type | solution.py:207
  37.0 9.0 %collective-permute-start.12 = (bf16[512,512]{1,0:T(8,128)(2,1)S(1)}, bf16[512,512]{1,0:T(8,128)(2,1)S(1)}, u32[]{:S(2)}, u32[]{:S(2)}) collective-permute-start(bf16[512,512]{1,0:T(8,128)(2,1)S(1)} %get-tuple-element.23), channel_id=1, source_target_pairs={{0,4},{4,0},{8,12},{12,8},{1,5},{5,1},{9,13},{13,9},{2,6},{6,2},{1... | collective-permute-start | bytes 1572872 | tf_op jit(solution)/shard_map/ppermute | solution.py:211
  46.1 10.4 %collective-permute-done.2.refs_3_ = bf16[128,2176]{1,0:T(8,128)(2,1)S(1)} collective-permute-done((bf16[128,2176]{1,0:T(8,128)(2,1)S(1)}, bf16[128,2176]{1,0:T(8,128)(2,1)S(1)}, u32[]{:S(2)}, u32[]{:S(2)}) %collective-permute-start.2) | collective-permute-done | bytes 557088 | tf_op jit(solution)/shard_map/ppermute | solution.py:211
  56.4 1.3 %shrink_partial.1 = bf16[256,128]{1,0:T(8,128)(2,1)S(1)} custom-call(bf16[2048,512]{1,0:T(8,128)(2,1)S(1)} %copy-done.4, bf16[128,2176]{1,0:T(8,128)(2,1)S(1)} %get-tuple-element.15.refs_0_, bf16[128,2176]{1,0:T(8,128)(2,1)S(1)} %collective-permute-done.refs_1_, bf16[128,2176]{1,0:T(8,128)(2,1)S(1)} %collective-permute-done.1.refs_2_, ...), custom_call_target="tpu_custom_call" | custom-call | flops 1073741824 | bytes 4194304 | tf_op jit(solution)/shard_map/shrink_partial/pallas_call | solution.py:128
  57.8 4.6 %collective-permute-start.3 = (bf16[256,128]{1,0:T(8,128)(2,1)S(1)}, bf16[256,128]{1,0:T(8,128)(2,1)S(1)}, u32[]{:S(2)}, u32[]{:S(2)}) collective-permute-start(bf16[256,128]{1,0:T(8,128)(2,1)S(1)} %shrink_partial.1), channel_id=1, source_target_pairs={{0,4},{4,0},{8,12},{12,8},{1,5},{5,1},{9,13},{13,9},{2,6},{6,2},{1... | collective-permute-start | bytes 196616 | tf_op jit(solution)/shard_map/ppermute | solution.py:211
  62.4 2.5 %collective-permute-done.3 = bf16[256,128]{1,0:T(8,128)(2,1)S(1)} collective-permute-done((bf16[256,128]{1,0:T(8,128)(2,1)S(1)}, bf16[256,128]{1,0:T(8,128)(2,1)S(1)}, u32[]{:S(2)}, u32[]{:S(2)}) %collective-permute-start.3) | collective-permute-done | bytes 65568 | tf_op jit(solution)/shard_map/ppermute | solution.py:211
  64.9 1.7 %collective-permute-start.4 = (bf16[256,128]{1,0:T(8,128)(2,1)S(1)}, bf16[256,128]{1,0:T(8,128)(2,1)S(1)}, u32[]{:S(2)}, u32[]{:S(2)}) collective-permute-start(bf16[256,128]{1,0:T(8,128)(2,1)S(1)} %add_convert_fusion.2.one_ref), channel_id=1, source_target_pairs={{0,8},{4,12},{8,0},{12,4},{1,9},{5,13},{9,1},{13,5},{2,10},{6,14},... | collective-permute-start | bytes 196616 | tf_op jit(solution)/shard_map/ppermute | solution.py:211
  66.6 3.9 %collective-permute-done.4.two_ref = bf16[256,128]{1,0:T(8,128)(2,1)S(1)} collective-permute-done((bf16[256,128]{1,0:T(8,128)(2,1)S(1)}, bf16[256,128]{1,0:T(8,128)(2,1)S(1)}, u32[]{:S(2)}, u32[]{:S(2)}) %collective-permute-start.4) | collective-permute-done | bytes 65568 | tf_op jit(solution)/shard_map/ppermute | solution.py:211
  71.1 1.4 %collective-permute-start.6 = (bf16[128,512]{1,0:T(8,128)(2,1)S(1)}, bf16[128,512]{1,0:T(8,128)(2,1)S(1)}, u32[]{:S(2)}, u32[]{:S(2)}) collective-permute-start(bf16[128,512]{1,0:T(8,128)(2,1)S(1)} %get-tuple-element.21), channel_id=1, source_target_pairs={{0,2},{1,3},{2,0},{3,1},{4,6},{5,7},{6,4},{7,5},{8,10},{9,11},{10,... | collective-permute-start | bytes 393224 | tf_op jit(solution)/shard_map/ppermute | solution.py:211
  73.0 4.5 %collective-permute-done.6.refs_2_ = bf16[128,512]{1,0:T(8,128)(2,1)S(1)} collective-permute-done((bf16[128,512]{1,0:T(8,128)(2,1)S(1)}, bf16[128,512]{1,0:T(8,128)(2,1)S(1)}, u32[]{:S(2)}, u32[]{:S(2)}) %collective-permute-start.6) | collective-permute-done | bytes 131104 | tf_op jit(solution)/shard_map/ppermute | solution.py:211
  77.5 1.9 %collective-permute-done.7.refs_3_ = bf16[128,512]{1,0:T(8,128)(2,1)S(1)} collective-permute-done((bf16[128,512]{1,0:T(8,128)(2,1)S(1)}, bf16[128,512]{1,0:T(8,128)(2,1)S(1)}, u32[]{:S(2)}, u32[]{:S(2)}) %collective-permute-start.7) | collective-permute-done | bytes 131104 | tf_op jit(solution)/shard_map/ppermute | solution.py:211
  79.4 1.5 %finish.1 = bf16[512,512]{1,0:T(8,128)(2,1)} custom-call(s32[8,512]{1,0:T(8,128)S(1)} %get-tuple-element.14.place_ref, bf16[128,512]{1,0:T(8,128)(2,1)S(1)} %get-tuple-element.19.refs_0_, bf16[128,512]{1,0:T(8,128)(2,1)S(1)} %collective-permute-done.5.refs_1_, bf16[128,512]{1,0:T(8,128)(2,1)S(1)} %collective-permute-done.6.refs_2_, ...), custom_call_target="tpu_custom_call" | custom-call | flops 268435456 | bytes 3145728 | tf_op jit(solution)/shard_map/finish/pallas_call | solution.py:191
  (30 shorter events, 3.1 us)
Async XLA Ops:
  0.7 3.4 %copy-start = (bf16[2048,2048]{1,0:T(8,128)(2,1)S(1)}, bf16[2048,2048]{1,0:T(8,128)(2,1)}, u32[]{:S(2)}) copy-start(bf16[2048,2048]{1,0:T(8,128)(2,1)} %w_ref.3) | copy-start | bytes 25165828
  4.1 1.6 %copy-start.2 = (bf16[512,2048]{1,0:T(8,128)(2,1)S(1)}, bf16[512,2048]{1,0:T(8,128)(2,1)}, u32[]{:S(2)}) copy-start(bf16[512,2048]{1,0:T(8,128)(2,1)} %x_ref.5) | copy-start | bytes 6291460
  5.7 7.0 %copy-start.1 = (bf16[2048,2048]{1,0:T(8,128)(2,1)S(1)}, bf16[2048,2048]{1,0:T(8,128)(2,1)}, u32[]{:S(2)}) copy-start(bf16[2048,2048]{1,0:T(8,128)(2,1)} %w_ref.3) | copy-start | bytes 25165828
  7.5 17.4 %collective-permute-start.10 = (bf16[512,512]{1,0:T(8,128)(2,1)S(1)}, bf16[512,512]{1,0:T(8,128)(2,1)S(1)}, u32[]{:S(2)}, u32[]{:S(2)}) collective-permute-start(bf16[512,512]{1,0:T(8,128)(2,1)S(1)} %bitcast.18), channel_id=1, source_target_pairs={{0,4},{12,8},{1,5},{13,9},{2,6},{14,10},{3,7},{15,11},{16,20},{28,... | collective-permute-start | bytes 1572872 | tf_op jit(solution)/shard_map/ppermute | solution.py:227
  18.6 7.9 %copy-start.6 = (s32[4096]{0:T(1024)S(1)}, s32[4096]{0:T(1024)}, u32[]{:S(2)}) copy-start(s32[4096]{0:T(1024)} %param.9) | copy-start | bytes 49156
  18.6 7.9 %copy-start.7 = (s32[512]{0:T(512)S(1)}, s32[512]{0:T(512)}, u32[]{:S(2)}) copy-start(s32[512]{0:T(512)} %param.8) | copy-start | bytes 6148
  18.7 16.3 %collective-permute-start.8 = (bf16[512,512]{1,0:T(8,128)(2,1)S(1)}, bf16[512,512]{1,0:T(8,128)(2,1)S(1)}, u32[]{:S(2)}, u32[]{:S(2)}) collective-permute-start(bf16[512,512]{1,0:T(8,128)(2,1)S(1)} %slice_bitcast_fusion.1), channel_id=1, source_target_pairs={{0,4},{12,8},{1,5},{13,9},{2,6},{14,10},{3,7},{15,11},{16,20},{28,... | collective-permute-start | bytes 1572872 | tf_op jit(solution)/shard_map/ppermute | solution.py:228
  25.0 10.0 %collective-permute-start.11 = (bf16[512,512]{1,0:T(8,128)(2,1)S(1)}, bf16[512,512]{1,0:T(8,128)(2,1)}, u32[]{:S(2)}, u32[]{:S(2)}) collective-permute-start(bf16[512,512]{1,0:T(8,128)(2,1)S(1)} %add_convert_fusion), channel_id=1, source_target_pairs={{4,8},{8,4},{5,9},{9,5},{6,10},{10,6},{7,11},{11,7},{20,24},{24,20... | collective-permute-start | bytes 1572872 | tf_op jit(solution)/shard_map/ppermute | solution.py:229
  26.5 1.6 %copy-start.3 = (bf16[512,2048]{1,0:T(8,128)(2,1)S(1)}, bf16[512,2048]{1,0:T(8,128)(2,1)}, u32[]{:S(2)}) copy-start(bf16[512,2048]{1,0:T(8,128)(2,1)} %x_ref.5) | copy-start | bytes 6291460
  29.8 26.6 %copy-start.4 = (bf16[2048,512]{1,0:T(8,128)(2,1)S(1)}, bf16[2048,512]{1,0:T(8,128)(2,1)}, u32[]{:S(2)}) copy-start(bf16[2048,512]{1,0:T(8,128)(2,1)} %down_ref.1) | copy-start | bytes 6291460
  29.8 16.2 %collective-permute-start = (bf16[128,2176]{1,0:T(8,128)(2,1)S(1)}, bf16[128,2176]{1,0:T(8,128)(2,1)S(1)}, u32[]{:S(2)}, u32[]{:S(2)}) collective-permute-start(bf16[128,2176]{1,0:T(8,128)(2,1)S(1)} %get-tuple-element.16), channel_id=1, source_target_pairs={{0,1},{1,0},{2,3},{3,2},{4,5},{5,4},{6,7},{7,6},{8,9},{9,8},{10,11... | collective-permute-start | bytes 1671176 | tf_op jit(solution)/shard_map/ppermute | solution.py:211
  29.9 16.2 %collective-permute-start.1 = (bf16[128,2176]{1,0:T(8,128)(2,1)S(1)}, bf16[128,2176]{1,0:T(8,128)(2,1)S(1)}, u32[]{:S(2)}, u32[]{:S(2)}) collective-permute-start(bf16[128,2176]{1,0:T(8,128)(2,1)S(1)} %get-tuple-element.17), channel_id=1, source_target_pairs={{0,2},{1,3},{2,0},{3,1},{4,6},{5,7},{6,4},{7,5},{8,10},{9,11},{10,... | collective-permute-start | bytes 1671176 | tf_op jit(solution)/shard_map/ppermute | solution.py:211
  31.5 25.0 %collective-permute-start.2 = (bf16[128,2176]{1,0:T(8,128)(2,1)S(1)}, bf16[128,2176]{1,0:T(8,128)(2,1)S(1)}, u32[]{:S(2)}, u32[]{:S(2)}) collective-permute-start(bf16[128,2176]{1,0:T(8,128)(2,1)S(1)} %get-tuple-element.18), channel_id=1, source_target_pairs={{0,3},{1,2},{2,1},{3,0},{4,7},{5,6},{6,5},{7,4},{8,11},{9,10},{10,... | collective-permute-start | bytes 1671176 | tf_op jit(solution)/shard_map/ppermute | solution.py:211
  36.3 43.0 %collective-permute-start.9 = (bf16[512,512]{1,0:T(8,128)(2,1)S(1)}, bf16[512,512]{1,0:T(8,128)(2,1)S(1)}, u32[]{:S(2)}, u32[]{:S(2)}) collective-permute-start(bf16[512,512]{1,0:T(8,128)(2,1)S(1)} %get-tuple-element.24), channel_id=1, source_target_pairs={{4,8},{8,4},{5,9},{9,5},{6,10},{10,6},{7,11},{11,7},{20,24},{24,20... | collective-permute-start | bytes 1572872 | tf_op jit(solution)/shard_map/ppermute | solution.py:230
  37.0 42.3 %collective-permute-start.12 = (bf16[512,512]{1,0:T(8,128)(2,1)S(1)}, bf16[512,512]{1,0:T(8,128)(2,1)S(1)}, u32[]{:S(2)}, u32[]{:S(2)}) collective-permute-start(bf16[512,512]{1,0:T(8,128)(2,1)S(1)} %get-tuple-element.23), channel_id=1, source_target_pairs={{0,4},{4,0},{8,12},{12,8},{1,5},{5,1},{9,13},{13,9},{2,6},{6,2},{1... | collective-permute-start | bytes 1572872 | tf_op jit(solution)/shard_map/ppermute | solution.py:211
  56.4 14.1 %copy-start.5 = (bf16[512,512]{1,0:T(8,128)(2,1)S(1)}, bf16[512,512]{1,0:T(8,128)(2,1)}, u32[]{:S(2)}) copy-start(bf16[512,512]{1,0:T(8,128)(2,1)} %up_ref.1) | copy-start | bytes 1572868
  57.8 7.1 %collective-permute-start.3 = (bf16[256,128]{1,0:T(8,128)(2,1)S(1)}, bf16[256,128]{1,0:T(8,128)(2,1)S(1)}, u32[]{:S(2)}, u32[]{:S(2)}) collective-permute-start(bf16[256,128]{1,0:T(8,128)(2,1)S(1)} %shrink_partial.1), channel_id=1, source_target_pairs={{0,4},{4,0},{8,12},{12,8},{1,5},{5,1},{9,13},{13,9},{2,6},{6,2},{1... | collective-permute-start | bytes 196616 | tf_op jit(solution)/shard_map/ppermute | solution.py:211
  64.9 5.6 %collective-permute-start.4 = (bf16[256,128]{1,0:T(8,128)(2,1)S(1)}, bf16[256,128]{1,0:T(8,128)(2,1)S(1)}, u32[]{:S(2)}, u32[]{:S(2)}) collective-permute-start(bf16[256,128]{1,0:T(8,128)(2,1)S(1)} %add_convert_fusion.2.one_ref), channel_id=1, source_target_pairs={{0,8},{4,12},{8,0},{12,4},{1,9},{5,13},{9,1},{13,5},{2,10},{6,14},... | collective-permute-start | bytes 196616 | tf_op jit(solution)/shard_map/ppermute | solution.py:211
  71.0 1.9 %collective-permute-start.5 = (bf16[128,512]{1,0:T(8,128)(2,1)S(1)}, bf16[128,512]{1,0:T(8,128)(2,1)S(1)}, u32[]{:S(2)}, u32[]{:S(2)}) collective-permute-start(bf16[128,512]{1,0:T(8,128)(2,1)S(1)} %get-tuple-element.20), channel_id=1, source_target_pairs={{0,1},{1,0},{2,3},{3,2},{4,5},{5,4},{6,7},{7,6},{8,9},{9,8},{10,11... | collective-permute-start | bytes 393224 | tf_op jit(solution)/shard_map/ppermute | solution.py:211
  71.1 6.4 %collective-permute-start.6 = (bf16[128,512]{1,0:T(8,128)(2,1)S(1)}, bf16[128,512]{1,0:T(8,128)(2,1)S(1)}, u32[]{:S(2)}, u32[]{:S(2)}) collective-permute-start(bf16[128,512]{1,0:T(8,128)(2,1)S(1)} %get-tuple-element.21), channel_id=1, source_target_pairs={{0,2},{1,3},{2,0},{3,1},{4,6},{5,7},{6,4},{7,5},{8,10},{9,11},{10,... | collective-permute-start | bytes 393224 | tf_op jit(solution)/shard_map/ppermute | solution.py:211
  72.5 6.9 %collective-permute-start.7 = (bf16[128,512]{1,0:T(8,128)(2,1)S(1)}, bf16[128,512]{1,0:T(8,128)(2,1)S(1)}, u32[]{:S(2)}, u32[]{:S(2)}) collective-permute-start(bf16[128,512]{1,0:T(8,128)(2,1)S(1)} %get-tuple-element.22), channel_id=1, source_target_pairs={{0,3},{1,2},{2,1},{3,0},{4,7},{5,6},{6,5},{7,4},{8,11},{9,10},{10,... | collective-permute-start | bytes 393224 | tf_op jit(solution)/shard_map/ppermute | solution.py:211

commit v2 on v1

v2 whole, which is shorter than its diff:
```python
import functools

import jax
import jax.numpy as jnp
from jax import lax
from jax.experimental import pallas as pl
from jax.experimental.pallas import tpu as pltpu
from jax.sharding import PartitionSpec as P

ADAPTER_RANK = 64
LANES = 128
VMEM_BYTES = 32 * 1024 * 1024

bf16 = jnp.bfloat16
f32 = jnp.float32
i32 = jnp.int32


def params():
    return pltpu.CompilerParams(vmem_limit_bytes=VMEM_BYTES)


def cost(flops, nbytes):
    return pl.CostEstimate(flops=flops, bytes_accessed=nbytes, transcendentals=0)


def dot(a, b, contract=((1,), (0,))):
    return lax.dot_general(a, b, (contract, ((), ())), preferred_element_type=f32)


def in_hbm(a):
    return pltpu.with_memory_space_constraint(a, pltpu.HBM)


def iota(shape, dim):
    return lax.broadcasted_iota(i32, shape, dim)


def places(slots, capacity, holders, me, ids, table):
    rows = ids.shape[1]
    low = (iota((LANES, rows), 0) == (ids & (LANES - 1))).astype(f32).astype(bf16)
    high = iota((table.shape[0], rows), 0) == lax.shift_right_logical(ids, 7)
    found = dot(table.astype(f32).astype(bf16), low)
    slot = jnp.sum(jnp.where(high, found, 0.0), axis=0, keepdims=True).astype(i32)
    holder = lax.div(slot, slots)
    tag = (slot - holder * slots + 1).astype(f32)
    partner = holder ^ me
    mine = iota((max(8, holders), rows), 0) == partner
    earlier = (iota((rows, rows), 0) < iota((rows, rows), 1)).astype(f32).astype(bf16)
    before = dot(mine.astype(f32).astype(bf16), earlier)
    rank = jnp.sum(jnp.where(mine, before, 0.0), axis=0, keepdims=True).astype(i32)
    return partner * capacity + rank, tag


def head_body(slots, capacity, holders, block, me_ref, z_ref, ids_hbm, table_hbm, x_hbm, w_hbm, place_ref, *refs):
    outs = refs[:holders]
    if block:
        first_ref, x_buf, ids_buf, table_buf, x_sem, i_sem, w_buf, w_sem = refs[holders:]
    else:
        x_buf, ids_buf, table_buf, x_sem, i_sem = refs[holders:]
    rows, features = x_buf.shape
    chunks = x_sem.shape[0]
    step = features // chunks

    def x_copy(c):
        part = pl.ds(c * step, step)
        return pltpu.make_async_copy(x_hbm.at[:, part], x_buf.at[:, part], x_sem.at[c])

    small = [
        pltpu.make_async_copy(ids_hbm, ids_buf, i_sem.at[0]),
        pltpu.make_async_copy(table_hbm, table_buf, i_sem.at[1]),
    ]
    for copy in small:
        copy.start()
    for c in range(chunks):
        x_copy(c).start()
    if block:
        column = pl.multiple_of(jnp.where(z_ref[0] < 2, 3, 0) * block, block)
        w_copy = pltpu.make_async_copy(w_hbm.at[:, pl.ds(column, block)], w_buf, w_sem)
        w_copy.start()
    for copy in small:
        copy.wait()
    place, tag = places(slots, capacity, holders, me_ref[0], ids_buf[...], table_buf[...])
    place_ref[...] = jnp.broadcast_to(place, place_ref.shape)
    pick = (iota((holders * capacity, rows), 0) == place).astype(f32).astype(bf16)
    tags = dot(pick, jnp.broadcast_to(tag, (LANES, rows)).astype(bf16), ((1,), (1,))).astype(bf16)
    for j, out in enumerate(outs):
        out[:, features:] = tags[j * capacity:(j + 1) * capacity]
    for c in range(chunks):
        x_copy(c).wait()
        moved = dot(pick, x_buf[:, c * step:(c + 1) * step]).astype(bf16)
        for j, out in enumerate(outs):
            out[:, c * step:(c + 1) * step] = moved[j * capacity:(j + 1) * capacity]
    if block:
        w_copy.wait()
        first_ref[...] = dot(x_buf[...], w_buf[...]).astype(bf16)


def head(me, z, ids, table, x, weight, holders, slots, capacity, block):
    rows, features = x.shape
    chunks = max(1, features // 512)
    smem, vmem, hbm = (pl.BlockSpec(memory_space=m) for m in (pltpu.SMEM, pltpu.VMEM, pltpu.HBM))
    shapes = [jax.ShapeDtypeStruct((8, rows), i32)]
    shapes += [jax.ShapeDtypeStruct((capacity, features + LANES), bf16)] * holders
    ids = ids.reshape(1, rows)
    table = table.reshape(-1, LANES)
    scratch = [pltpu.VMEM((rows, features), bf16), pltpu.VMEM(ids.shape, i32), pltpu.VMEM(table.shape, i32)]
    scratch += [pltpu.SemaphoreType.DMA((chunks,)), pltpu.SemaphoreType.DMA((2,))]
    if block:
        shapes.append(jax.ShapeDtypeStruct((rows, block), bf16))
        scratch += [pltpu.VMEM((features, block), bf16), pltpu.SemaphoreType.DMA(())]
    return pl.pallas_call(
        functools.partial(head_body, slots, capacity, holders, block),
        out_shape=shapes,
        in_specs=[smem, smem, hbm, hbm, hbm, hbm],
        out_specs=[vmem] * len(shapes),
        scratch_shapes=scratch,
        compiler_params=params(),
        cost_estimate=cost(2 * (holders * capacity + block) * rows * features, 4 * rows * features),
        name="head",
    )(me.reshape(1), z.reshape(1), in_hbm(ids), in_hbm(table), in_hbm(x), in_hbm(weight))


def rest_body(z_ref, place_ref, x_ref, w_ref, second, third, own, unsort):
    z = z_ref[0]
    width = own.shape[1]
    x = x_ref[...]
    for block, out in ((jnp.where(z < 2, 2, 1), second), (z ^ 1, third), (z, own)):
        column = pl.multiple_of(block * width, width)
        out[...] = dot(x, w_ref[:, pl.ds(column, width)]).astype(bf16)
    unsort_matrix(place_ref, unsort)


def unsort_matrix(place_ref, unsort):
    rows, total = unsort.shape
    place = jnp.broadcast_to(place_ref[0:1, :].astype(f32), (LANES, rows)).T
    lane = iota((rows, LANES), 1).astype(f32)
    for k in range(total // LANES):
        unsort[:, k * LANES:(k + 1) * LANES] = (place == lane + float(k * LANES)).astype(f32).astype(bf16)


def rest(z, place, x, weight, width, total):
    rows, features = x.shape
    smem, vmem = (pl.BlockSpec(memory_space=m) for m in (pltpu.SMEM, pltpu.VMEM))
    return pl.pallas_call(
        rest_body,
        out_shape=[jax.ShapeDtypeStruct((rows, width), bf16)] * 3 + [jax.ShapeDtypeStruct((rows, total), bf16)],
        in_specs=[smem, vmem, vmem, vmem],
        out_specs=[vmem] * 4,
        compiler_params=params(),
        cost_estimate=cost(6 * rows * features * width, 2 * features * (rows + 4 * width)),
        name="rest",
    )(z.reshape(1), place, x, weight)


def unsort_only(place, total):
    return pl.pallas_call(
        unsort_matrix,
        out_shape=jax.ShapeDtypeStruct((place.shape[1], total), bf16),
        compiler_params=params(),
        name="unsort",
    )(place)


def slot_mask(tag, group):
    lane = iota(tag.shape, 1)
    return tag == jnp.where(lane < ADAPTER_RANK, 2 * group + 1, 2 * group + 2).astype(f32)


def shrink_body(down_ref, *refs):
    parts, out = refs[:-1], refs[-1]
    features, width = down_ref.shape
    capacity = parts[0].shape[0]
    half = capacity // 2
    first = iota((half, LANES), 1) < ADAPTER_RANK
    for k, part in enumerate(parts):
        full = dot(part[:, :features], down_ref[...])
        tag = part[:, features:].astype(f32)
        total = jnp.zeros((capacity, LANES), f32)
        for group in range(width // LANES):
            total += jnp.where(slot_mask(tag, group), full[:, group * LANES:(group + 1) * LANES], 0.0)
        total += pltpu.roll(total, ADAPTER_RANK, 1)
        out[k * half:(k + 1) * half, :] = jnp.where(first, total[:half], total[half:]).astype(bf16)


def shrink_partial(parts, down):
    features, width = down.shape
    capacity = parts[0].shape[0]
    total = len(parts) * capacity
    return pl.pallas_call(
        shrink_body,
        out_shape=jax.ShapeDtypeStruct((total // 2, LANES), bf16),
        compiler_params=params(),
        cost_estimate=cost(2 * total * features * width, 2 * features * (total + width)),
        name="shrink_partial",
    )(down, *parts)


def expand_body(count, one_ref, two_ref, up_ref, *refs):
    tags, outs = refs[:count], refs[count:]
    capacity = outs[0].shape[0]
    half = capacity // 2
    up = up_ref[...]
    first = iota((half, LANES), 1) < ADAPTER_RANK
    for k in range(count):
        part = pl.ds(k * half, half)
        shrink = (one_ref[part, :].astype(f32) + two_ref[part, :].astype(f32)).astype(bf16).astype(f32)
        turned = pltpu.roll(shrink, ADAPTER_RANK, 1)
        rows = jnp.concatenate([jnp.where(first, shrink, turned), jnp.where(first, turned, shrink)], axis=0)
        tag = tags[k][...].astype(f32)
        spread = [
            jnp.where(slot_mask(tag, group), rows, 0.0).astype(bf16) for group in range(up.shape[0] // LANES)
        ]
        outs[k][...] = dot(jnp.concatenate(spread, axis=1), up).astype(bf16)


def expand(one, two, up, parts):
    capacity, width = parts[0].shape
    count = len(parts)
    tag_block = pl.BlockSpec((capacity, LANES), lambda i: (0, width // LANES - 1))
    whole = lambda a: pl.BlockSpec(a.shape, lambda i: (0, 0))
    columns = up.shape[1]
    return pl.pallas_call(
        functools.partial(expand_body, count),
        grid=(1,),
        out_shape=[jax.ShapeDtypeStruct((capacity, columns), bf16)] * count,
        in_specs=[whole(one), whole(two), whole(up)] + [tag_block] * count,
        out_specs=[pl.BlockSpec((capacity, columns), lambda i: (0, 0))] * count,
        compiler_params=params(),
        cost_estimate=cost(2 * count * capacity * up.size, 2 * (up.size + count * capacity * columns)),
        name="expand",
    )(one, two, up, *parts)


def finish_body(count, unsort_ref, *refs):
    deltas, sums, out = refs[:count], refs[count:-1], refs[-1]
    capacity = deltas[0].shape[0]
    total = sums[0][...].astype(f32)
    for term in sums[1:]:
        total += term[...].astype(f32)
    own = dot(unsort_ref[...], jnp.concatenate([d[...] for d in deltas], axis=0))
    out[...] = (total + own).astype(bf16)


def finish(unsort, deltas, sums):
    rows, columns = sums[0].shape
    return pl.pallas_call(
        functools.partial(finish_body, len(deltas)),
        out_shape=jax.ShapeDtypeStruct((rows, columns), bf16),
        compiler_params=params(),
        cost_estimate=cost(2 * rows * unsort.shape[1] * columns, 12 * rows * columns),
        name="finish",
    )(unsort, *deltas, *sums)


def both(a, b):
    return (a.astype(f32) + b.astype(f32)).astype(bf16)


def after(value, *others):
    return lax.optimization_barrier((value,) + others)[0]


def swap(value, axis, bit):
    return lax.ppermute(value, axis, [(i, i ^ bit) for i in range(lax.axis_size(axis))])


EDGE = [(0, 1), (3, 2)]
MIDDLE = [(1, 2), (2, 1)]
OUTER = [(1, 0), (2, 3)]


def tp_sums(mine):
    bit = 1
    while True:
        other = swap(mine, "tp", bit)
        bit *= 2
        if bit >= lax.axis_size("tp"):
            return mine, other
        mine = both(mine, other)


def shards(x, ids, table, weight, down, up):
    holders = lax.axis_size("ad")
    rows = x.shape[0]
    capacity = rows // 4
    slots = up.shape[0] // ADAPTER_RANK
    width = up.shape[1]
    me, z = lax.axis_index("ad"), lax.axis_index("tp")
    line = lax.axis_size("tp") == 4
    place, *send = head(me, z, ids, table, x, weight, holders, slots, capacity, width if line else 0)
    total = holders * capacity
    if line:
        first = send.pop()
        edge0 = lax.ppermute(first, "tp", EDGE)
        parts = [send[0]] + [swap(send[j], "ad", j) for j in range(1, holders)]
        second, third, own, unsort = rest(z, place, x, weight, width, total)
        edge1 = lax.ppermute(second, "tp", EDGE)
        inner = both(first, edge0)
        middle0 = lax.ppermute(inner, "tp", MIDDLE)
        parts[2] = after(parts[2], inner)
    else:
        parts = [send[0]] + [swap(send[j], "ad", j) for j in range(1, holders)]
        unsort = unsort_only(place, total)
        full = dot(x, weight).astype(bf16)
        sums = [lax.psum_scatter(full, "tp", scatter_dimension=1, tiled=True)]
    early, late = parts[:-1], parts[-1:]
    one, two = tp_sums(shrink_partial(early, down))
    deltas = expand(one, two, up, early)
    back = [deltas[0]] + [swap(deltas[j], "ad", j) for j in range(1, holders - 1)]
    if line:
        edge2 = lax.ppermute(after(third, two), "tp", EDGE)
        middle1 = lax.ppermute(both(second, edge1), "tp", MIDDLE)
        outer = lax.ppermute(both(after(third, parts[-1]), middle0), "tp", OUTER)
        sums = [own, middle1, edge2, outer]
    late = [after(late[0], *deltas)]
    one, two = tp_sums(shrink_partial(late, down))
    back.append(swap(expand(one, two, up, late)[0], "ad", holders - 1))
    return finish(unsort, back, sums)


def solution(mesh):
    in_specs = (
        P(("rep", "ad"), "tp"),
        P(("rep", "ad")),
        P("rep"),
        P("tp", None),
        P(("rep", "tp"), "ad"),
        P(("rep", "ad"), "tp"),
    )
    out_specs = P(("rep", "ad"), "tp")
    return jax.shard_map(shards, mesh=mesh, in_specs=in_specs, out_specs=out_specs, check_vma=False)
```

time: 81.3 us -> 74.8 us (0.920)
  waiting for transfers between devices: 31.3 us -> 40.8 us
  local copies, waits for them, and re-layouts: 7.38 us -> 0.02 us
  starting transfers between devices: 27.8 us -> 20.9 us
  other arithmetic: 1.49 us -> 0.43 us
    ppermute x9 -> x10, waiting for transfers between devices: 23.2 us -> 35.3 us  [swap(): lax.ppermute(value, axis, [(i, i ^ bit) for i in range(lax.axis_size(axis...]
    ppermute x9 -> x10, starting transfers between devices: 19.2 us -> 10.2 us  [swap(): lax.ppermute(value, axis, [(i, i ^ bit) for i in range(lax.axis_size(axis...]
    unnamed x16 -> x8, local copies, waits for them, and re-layouts: 6.59 us -> 0.02 us
    ppermute x4 -> x6, waiting for transfers between devices: 8.08 us -> 5.55 us  [the longest x1 5.54 us: shards(): edge0 = lax.ppermute(first, 'tp', EDGE)]
    ppermute x4 -> x6, starting transfers between devices: 8.58 us -> 10.7 us  [the longest x1 4.96 us: shards(): edge0 = lax.ppermute(first, 'tp', EDGE)]
    convert_element_type x3 -> x5, other arithmetic: 1.49 us -> 0.43 us  [both(): return (a.astype(f32) + b.astype(f32)).astype(bf16)]
    pallas_call x4 -> x3, Pallas kernels: 11 us -> 10 us  [the longest x1 5.24 us: head(): pl.pallas_call(functools.partial(head_body, slots, capacity, holders, blo...]
  transfers between devices with their start and end apart: 13 -> 16, of which waited for: 7 -> 8; matrix products, arithmetic and copies ran while one was open for 2% -> 1% of each run, Pallas kernels for 12% -> 8%
where the time goes in v2:
time: 74.8 us; the launch traced here: 74.6 us
  waiting for transfers between devices  40.8 us (55%)
  starting transfers between devices  20.9 us (28%)
  Pallas kernels  12.3 us (16%)
    ppermute x10, waiting for transfers between devices, swap(): lax.ppermute(value, axis, [(i, i ^ bit) for i in range(lax.axis_size(axis...  35.3 us
    ppermute x10, starting transfers between devices, swap(): lax.ppermute(value, axis, [(i, i ^ bit) for i in range(lax.axis_size(axis...  10.2 us
    ppermute x1, waiting for transfers between devices, shards(): edge0 = lax.ppermute(first, 'tp', EDGE)  5.54 us
    pallas_call x1, Pallas kernels, head(): pl.pallas_call(functools.partial(head_body, slots, capacity, holders, blo...  5.24 us
    ppermute x1, starting transfers between devices, shards(): edge0 = lax.ppermute(first, 'tp', EDGE)  4.96 us
    pallas_call x1, Pallas kernels, rest(): pl.pallas_call(rest_body, out_shape=[jax.ShapeDtypeStruct((rows, width),...  3.46 us
    ppermute x1, starting transfers between devices, shards(): edge2 = lax.ppermute(after(third, two), 'tp', EDGE)  1.58 us
    pallas_call x2, Pallas kernels, shrink_partial(): pl.pallas_call(shrink_body, out_shape=jax.ShapeDtypeStruct((total // 2, L...  1.57 us
  transfers between devices with their start and end apart: 16, of which 8 were waited for; matrix products, arithmetic and copies ran while one was open for 1% of the time, Pallas kernels for 8%

profile of v2, /device:TPU:0, one launch (start us, length us, event | category | flops | bytes accessed | tf_op | source)
XLA Modules:
  0.0 74.6 jit_solution(17360960283135191231)
XLA Ops:
  0.0 5.2 %head.1 = (s32[8,512]{1,0:T(8,128)S(1)}, bf16[128,2176]{1,0:T(8,128)(2,1)S(1)}, bf16[128,2176]{1,0:T(8,128)(2,1)S(1)}, bf16[128,2176]{1,0:T(8,128)(2,1)S(1)}, bf...) custom-call(s32[1]{0:T(128)} %bitcast.1.me_ref, s32[1]{0:T(128)} %bitcast.z_ref, s32[1,512]{1,0:T(1,128)} %bitcast.5, ...), custom_call_target="tpu_custom_call" | custom-call | flops 2147483648 | bytes 4194304 | tf_op jit(solution)/shard_map/head/pallas_call | solution.py:112
  5.3 5.0 %collective-permute-start.2 = (bf16[512,512]{1,0:T(8,128)(2,1)S(1)}, bf16[512,512]{1,0:T(8,128)(2,1)S(1)}, u32[]{:S(2)}, u32[]{:S(2)}) collective-permute-start(bf16[512,512]{1,0:T(8,128)(2,1)S(1)} %get-tuple-element.27), channel_id=1, source_target_pairs={{0,4},{12,8},{1,5},{13,9},{2,6},{14,10},{3,7},{15,11},{16,20},{28,... | collective-permute-start | bytes 1572872 | tf_op jit(solution)/shard_map/ppermute | solution.py:295
  10.3 1.6 %collective-permute-start.1 = (bf16[128,2176]{1,0:T(8,128)(2,1)S(1)}, bf16[128,2176]{1,0:T(8,128)(2,1)S(1)}, u32[]{:S(2)}, u32[]{:S(2)}) collective-permute-start(bf16[128,2176]{1,0:T(8,128)(2,1)S(1)} %get-tuple-element.26), channel_id=1, source_target_pairs={{0,2},{1,3},{2,0},{3,1},{4,6},{5,7},{6,4},{7,5},{8,10},{9,11},{10,... | collective-permute-start | bytes 1671176 | tf_op jit(solution)/shard_map/ppermute | solution.py:265
  12.2 3.5 %rest.1 = (bf16[512,512]{1,0:T(8,128)(2,1)S(1)}, bf16[512,512]{1,0:T(8,128)(2,1)S(1)}, bf16[512,512]{1,0:T(8,128)(2,1)S(1)}, bf16[512,512]{1,0:T(8,128)(2,1)S(1)}) custom-call(s32[1]{0:T(128)} %bitcast.z_ref, s32[8,512]{1,0:T(8,128)S(1)} %get-tuple-element.22.place_ref, bf16[512,2048]{1,0:T(8,128)(2,1)S(1)} %copy-done.3, bf16[2048,2048]{1,0:T(8,128)(2,1)S(1)} %copy-done), custom_call_target="tpu_custom_call" | custom-call | flops 3221225472 | bytes 10485760 | tf_op jit(solution)/shard_map/rest/pallas_call | solution.py:145
  15.6 1.3 %collective-permute-start.11 = (bf16[512,512]{1,0:T(8,128)(2,1)S(1)}, bf16[512,512]{1,0:T(8,128)(2,1)S(1)}, u32[]{:S(2)}, u32[]{:S(2)}) collective-permute-start(bf16[512,512]{1,0:T(8,128)(2,1)S(1)} %get-tuple-element.35), channel_id=1, source_target_pairs={{0,4},{12,8},{1,5},{13,9},{2,6},{14,10},{3,7},{15,11},{16,20},{28,... | collective-permute-start | bytes 1572872 | tf_op jit(solution)/shard_map/ppermute | solution.py:298
  17.0 5.5 %collective-permute-done.2 = bf16[512,512]{1,0:T(8,128)(2,1)S(1)} collective-permute-done((bf16[512,512]{1,0:T(8,128)(2,1)S(1)}, bf16[512,512]{1,0:T(8,128)(2,1)S(1)}, u32[]{:S(2)}, u32[]{:S(2)}) %collective-permute-start.2) | collective-permute-done | bytes 524320 | tf_op jit(solution)/shard_map/ppermute | solution.py:295
  22.6 3.2 %collective-permute-done.1.refs_2_ = bf16[128,2176]{1,0:T(8,128)(2,1)S(1)} collective-permute-done((bf16[128,2176]{1,0:T(8,128)(2,1)S(1)}, bf16[128,2176]{1,0:T(8,128)(2,1)S(1)}, u32[]{:S(2)}, u32[]{:S(2)}) %collective-permute-start.1) | collective-permute-done | bytes 557088 | tf_op jit(solution)/shard_map/ppermute | solution.py:265
  25.8 1.1 %shrink_partial.2 = bf16[192,128]{1,0:T(8,128)(2,1)S(1)} custom-call(bf16[2048,512]{1,0:T(8,128)(2,1)S(1)} %copy-done.1, bf16[128,2176]{1,0:T(8,128)(2,1)S(1)} %get-tuple-element.24.refs_0_, bf16[128,2176]{1,0:T(8,128)(2,1)S(1)} %collective-permute-done.refs_1_, bf16[128,2176]{1,0:T(8,128)(2,1)S(1)} %collective-permute-done.1.refs_2_), custom_call_target="tpu_custom_call" | custom-call | flops 805306368 | bytes 3670016 | tf_op jit(solution)/shard_map/shrink_partial/pallas_call | solution.py:190
  26.9 0.8 %collective-permute-start.14 = (bf16[512,512]{1,0:T(8,128)(2,1)S(1)}, bf16[512,512]{1,0:T(8,128)(2,1)S(1)}, u32[]{:S(2)}, u32[]{:S(2)}) collective-permute-start(bf16[512,512]{1,0:T(8,128)(2,1)S(1)} %add_convert_fusion.2), channel_id=1, source_target_pairs={{4,8},{8,4},{5,9},{9,5},{6,10},{10,6},{7,11},{11,7},{20,24},{24,20... | collective-permute-start | bytes 1572872 | tf_op jit(solution)/shard_map/ppermute | solution.py:300
  27.8 5.9 %collective-permute-done.3 = bf16[192,128]{1,0:T(8,128)(2,1)S(1)} collective-permute-done((bf16[192,128]{1,0:T(8,128)(2,1)S(1)}, bf16[192,128]{1,0:T(8,128)(2,1)S(1)}, u32[]{:S(2)}, u32[]{:S(2)}) %collective-permute-start.3) | collective-permute-done | bytes 49184 | tf_op jit(solution)/shard_map/ppermute | solution.py:265
  33.7 3.6 %collective-permute-start.4 = (bf16[192,128]{1,0:T(8,128)(2,1)S(1)}, bf16[192,128]{1,0:T(8,128)(2,1)S(1)}, u32[]{:S(2)}, u32[]{:S(2)}) collective-permute-start(bf16[192,128]{1,0:T(8,128)(2,1)S(1)} %add_convert_fusion.3.one_ref), channel_id=1, source_target_pairs={{0,8},{4,12},{8,0},{12,4},{1,9},{5,13},{9,1},{13,5},{2,10},{6,14},... | collective-permute-start | bytes 147464 | tf_op jit(solution)/shard_map/ppermute | solution.py:265
  37.4 0.7 collective-permute-start.12
  38.1 9.2 %collective-permute-done.4.two_ref = bf16[192,128]{1,0:T(8,128)(2,1)S(1)} collective-permute-done((bf16[192,128]{1,0:T(8,128)(2,1)S(1)}, bf16[192,128]{1,0:T(8,128)(2,1)S(1)}, u32[]{:S(2)}, u32[]{:S(2)}) %collective-permute-start.4) | collective-permute-done | bytes 49184 | tf_op jit(solution)/shard_map/ppermute | solution.py:265
  47.3 1.6 %collective-permute-start.13 = (bf16[512,512]{1,0:T(8,128)(2,1)S(1)}, bf16[512,512]{1,0:T(8,128)(2,1)S(1)}, u32[]{:S(2)}, u32[]{:S(2)}) collective-permute-start(bf16[512,512]{1,0:T(8,128)(2,1)S(1)} %get-tuple-element.38), channel_id=1, source_target_pairs={{0,4},{12,8},{1,5},{13,9},{2,6},{14,10},{3,7},{15,11},{16,20},{28,... | collective-permute-start | bytes 1572872 | tf_op jit(solution)/shard_map/ppermute | solution.py:312
  49.0 1.3 %collective-permute-start.15 = (bf16[512,512]{1,0:T(8,128)(2,1)S(1)}, bf16[512,512]{1,0:T(8,128)(2,1)S(1)}, u32[]{:S(2)}, u32[]{:S(2)}) collective-permute-start(bf16[512,512]{1,0:T(8,128)(2,1)S(1)} %add_convert_fusion), channel_id=1, source_target_pairs={{4,0},{8,12},{5,1},{9,13},{6,2},{10,14},{7,3},{11,15},{20,16},{24,... | collective-permute-start | bytes 1572872 | tf_op jit(solution)/shard_map/ppermute | solution.py:314
  50.3 0.4 expand.2
  50.7 0.5 shrink_partial.3
  51.3 2.7 %collective-permute-start.8 = (bf16[64,128]{1,0:T(8,128)(2,1)S(1)}, bf16[64,128]{1,0:T(8,128)(2,1)S(1)}, u32[]{:S(2)}, u32[]{:S(2)}) collective-permute-start(bf16[64,128]{1,0:T(8,128)(2,1)S(1)} %shrink_partial.3), channel_id=1, source_target_pairs={{0,4},{4,0},{8,12},{12,8},{1,5},{5,1},{9,13},{13,9},{2,6},{6,2},{1... | collective-permute-start | bytes 49160 | tf_op jit(solution)/shard_map/ppermute | solution.py:265
  54.0 6.9 %collective-permute-done.8 = bf16[64,128]{1,0:T(8,128)(2,1)S(1)} collective-permute-done((bf16[64,128]{1,0:T(8,128)(2,1)S(1)}, bf16[64,128]{1,0:T(8,128)(2,1)S(1)}, u32[]{:S(2)}, u32[]{:S(2)}) %collective-permute-start.8) | collective-permute-done | bytes 16416 | tf_op jit(solution)/shard_map/ppermute | solution.py:265
  61.2 4.4 %collective-permute-done.9.two_ref = bf16[64,128]{1,0:T(8,128)(2,1)S(1)} collective-permute-done((bf16[64,128]{1,0:T(8,128)(2,1)S(1)}, bf16[64,128]{1,0:T(8,128)(2,1)S(1)}, u32[]{:S(2)}, u32[]{:S(2)}) %collective-permute-start.9) | collective-permute-done | bytes 16416 | tf_op jit(solution)/shard_map/ppermute | solution.py:265
  65.6 1.5 %collective-permute-start.6 = (bf16[128,512]{1,0:T(8,128)(2,1)S(1)}, bf16[128,512]{1,0:T(8,128)(2,1)S(1)}, u32[]{:S(2)}, u32[]{:S(2)}) collective-permute-start(bf16[128,512]{1,0:T(8,128)(2,1)S(1)} %get-tuple-element.31), channel_id=1, source_target_pairs={{0,2},{1,3},{2,0},{3,1},{4,6},{5,7},{6,4},{7,5},{8,10},{9,11},{10,... | collective-permute-start | bytes 393224 | tf_op jit(solution)/shard_map/ppermute | solution.py:265
  67.4 3.2 %collective-permute-done.6.refs_2_ = bf16[128,512]{1,0:T(8,128)(2,1)S(1)} collective-permute-done((bf16[128,512]{1,0:T(8,128)(2,1)S(1)}, bf16[128,512]{1,0:T(8,128)(2,1)S(1)}, u32[]{:S(2)}, u32[]{:S(2)}) %collective-permute-start.6) | collective-permute-done | bytes 131104 | tf_op jit(solution)/shard_map/ppermute | solution.py:265
  70.7 2.6 %collective-permute-done.10.refs_3_ = bf16[128,512]{1,0:T(8,128)(2,1)S(1)} collective-permute-done((bf16[128,512]{1,0:T(8,128)(2,1)S(1)}, bf16[128,512]{1,0:T(8,128)(2,1)S(1)}, u32[]{:S(2)}, u32[]{:S(2)}) %collective-permute-start.10) | collective-permute-done | bytes 131104 | tf_op jit(solution)/shard_map/ppermute | solution.py:265
  73.3 1.3 %finish.1 = bf16[512,512]{1,0:T(8,128)(2,1)} custom-call(bf16[512,512]{1,0:T(8,128)(2,1)S(1)} %get-tuple-element.23.unsort_ref, bf16[128,512]{1,0:T(8,128)(2,1)S(1)} %get-tuple-element.29.refs_0_, bf16[128,512]{1,0:T(8,128)(2,1)S(1)} %collective-permute-done.5.refs_1_, bf16[128,512]{1,0:T(8,128)(2,1)S(1)} %collective-permute-done.6.refs_2_, ...), custom_call_target="tpu_custom_call" | custom-call | flops 268435456 | bytes 3145728 | tf_op jit(solution)/shard_map/finish/pallas_call | solution.py:247
  (28 shorter events, 1.6 us)
Async XLA Ops:
  0.0 12.2 %copy-start = (bf16[2048,2048]{1,0:T(8,128)(2,1)S(1)}, bf16[2048,2048]{1,0:T(8,128)(2,1)}, u32[]{:S(2)}) copy-start(bf16[2048,2048]{1,0:T(8,128)(2,1)} %w_ref.1) | copy-start | bytes 25165828
  0.0 12.2 %copy-start.3 = (bf16[512,2048]{1,0:T(8,128)(2,1)S(1)}, bf16[512,2048]{1,0:T(8,128)(2,1)}, u32[]{:S(2)}) copy-start(bf16[512,2048]{1,0:T(8,128)(2,1)} %x_ref.1) | copy-start | bytes 6291460
  5.3 17.2 %collective-permute-start.2 = (bf16[512,512]{1,0:T(8,128)(2,1)S(1)}, bf16[512,512]{1,0:T(8,128)(2,1)S(1)}, u32[]{:S(2)}, u32[]{:S(2)}) collective-permute-start(bf16[512,512]{1,0:T(8,128)(2,1)S(1)} %get-tuple-element.27), channel_id=1, source_target_pairs={{0,4},{12,8},{1,5},{13,9},{2,6},{14,10},{3,7},{15,11},{16,20},{28,... | collective-permute-start | bytes 1572872 | tf_op jit(solution)/shard_map/ppermute | solution.py:295
  10.2 15.6 %collective-permute-start = (bf16[128,2176]{1,0:T(8,128)(2,1)S(1)}, bf16[128,2176]{1,0:T(8,128)(2,1)S(1)}, u32[]{:S(2)}, u32[]{:S(2)}) collective-permute-start(bf16[128,2176]{1,0:T(8,128)(2,1)S(1)} %get-tuple-element.25), channel_id=1, source_target_pairs={{0,1},{1,0},{2,3},{3,2},{4,5},{5,4},{6,7},{7,6},{8,9},{9,8},{10,11... | collective-permute-start | bytes 1671176 | tf_op jit(solution)/shard_map/ppermute | solution.py:265
  10.3 15.5 %collective-permute-start.1 = (bf16[128,2176]{1,0:T(8,128)(2,1)S(1)}, bf16[128,2176]{1,0:T(8,128)(2,1)S(1)}, u32[]{:S(2)}, u32[]{:S(2)}) collective-permute-start(bf16[128,2176]{1,0:T(8,128)(2,1)S(1)} %get-tuple-element.26), channel_id=1, source_target_pairs={{0,2},{1,3},{2,0},{3,1},{4,6},{5,7},{6,4},{7,5},{8,10},{9,11},{10,... | collective-permute-start | bytes 1671176 | tf_op jit(solution)/shard_map/ppermute | solution.py:265
  11.9 26.2 %collective-permute-start.7 = (bf16[128,2176]{1,0:T(8,128)(2,1)S(1)}, bf16[128,2176]{1,0:T(8,128)(2,1)S(1)}, u32[]{:S(2)}, u32[]{:S(2)}) collective-permute-start(bf16[128,2176]{1,0:T(8,128)(2,1)S(1)} %get-tuple-element.32), channel_id=1, source_target_pairs={{0,3},{1,2},{2,1},{3,0},{4,7},{5,6},{6,5},{7,4},{8,11},{9,10},{10,... | collective-permute-start | bytes 1671176 | tf_op jit(solution)/shard_map/ppermute | solution.py:265
  12.2 13.6 %copy-start.1 = (bf16[2048,512]{1,0:T(8,128)(2,1)S(1)}, bf16[2048,512]{1,0:T(8,128)(2,1)}, u32[]{:S(2)}) copy-start(bf16[2048,512]{1,0:T(8,128)(2,1)} %down_ref.3) | copy-start | bytes 6291460
  15.6 21.6 %collective-permute-start.11 = (bf16[512,512]{1,0:T(8,128)(2,1)S(1)}, bf16[512,512]{1,0:T(8,128)(2,1)S(1)}, u32[]{:S(2)}, u32[]{:S(2)}) collective-permute-start(bf16[512,512]{1,0:T(8,128)(2,1)S(1)} %get-tuple-element.35), channel_id=1, source_target_pairs={{0,4},{12,8},{1,5},{13,9},{2,6},{14,10},{3,7},{15,11},{16,20},{28,... | collective-permute-start | bytes 1572872 | tf_op jit(solution)/shard_map/ppermute | solution.py:298
  26.9 23.4 %copy-start.2 = (bf16[512,512]{1,0:T(8,128)(2,1)S(1)}, bf16[512,512]{1,0:T(8,128)(2,1)}, u32[]{:S(2)}) copy-start(bf16[512,512]{1,0:T(8,128)(2,1)} %up_ref.3) | copy-start | bytes 1572868
  26.9 6.8 %collective-permute-start.3 = (bf16[192,128]{1,0:T(8,128)(2,1)S(1)}, bf16[192,128]{1,0:T(8,128)(2,1)S(1)}, u32[]{:S(2)}, u32[]{:S(2)}) collective-permute-start(bf16[192,128]{1,0:T(8,128)(2,1)S(1)} %shrink_partial.2), channel_id=1, source_target_pairs={{0,4},{4,0},{8,12},{12,8},{1,5},{5,1},{9,13},{13,9},{2,6},{6,2},{1... | collective-permute-start | bytes 147464 | tf_op jit(solution)/shard_map/ppermute | solution.py:265
  26.9 21.9 %collective-permute-start.14 = (bf16[512,512]{1,0:T(8,128)(2,1)S(1)}, bf16[512,512]{1,0:T(8,128)(2,1)S(1)}, u32[]{:S(2)}, u32[]{:S(2)}) collective-permute-start(bf16[512,512]{1,0:T(8,128)(2,1)S(1)} %add_convert_fusion.2), channel_id=1, source_target_pairs={{4,8},{8,4},{5,9},{9,5},{6,10},{10,6},{7,11},{11,7},{20,24},{24,20... | collective-permute-start | bytes 1572872 | tf_op jit(solution)/shard_map/ppermute | solution.py:300
  33.7 13.6 %collective-permute-start.4 = (bf16[192,128]{1,0:T(8,128)(2,1)S(1)}, bf16[192,128]{1,0:T(8,128)(2,1)S(1)}, u32[]{:S(2)}, u32[]{:S(2)}) collective-permute-start(bf16[192,128]{1,0:T(8,128)(2,1)S(1)} %add_convert_fusion.3.one_ref), channel_id=1, source_target_pairs={{0,8},{4,12},{8,0},{12,4},{1,9},{5,13},{9,1},{13,5},{2,10},{6,14},... | collective-permute-start | bytes 147464 | tf_op jit(solution)/shard_map/ppermute | solution.py:265
  37.4 35.9 %collective-permute-start.12 = (bf16[512,512]{1,0:T(8,128)(2,1)S(1)}, bf16[512,512]{1,0:T(8,128)(2,1)S(1)}, u32[]{:S(2)}, u32[]{:S(2)}) collective-permute-start(bf16[512,512]{1,0:T(8,128)(2,1)S(1)} %add_convert_fusion.1), channel_id=1, source_target_pairs={{4,8},{8,4},{5,9},{9,5},{6,10},{10,6},{7,11},{11,7},{20,24},{24,20... | collective-permute-start | bytes 1572872 | tf_op jit(solution)/shard_map/ppermute | solution.py:313
  47.3 26.0 %collective-permute-start.13 = (bf16[512,512]{1,0:T(8,128)(2,1)S(1)}, bf16[512,512]{1,0:T(8,128)(2,1)S(1)}, u32[]{:S(2)}, u32[]{:S(2)}) collective-permute-start(bf16[512,512]{1,0:T(8,128)(2,1)S(1)} %get-tuple-element.38), channel_id=1, source_target_pairs={{0,4},{12,8},{1,5},{13,9},{2,6},{14,10},{3,7},{15,11},{16,20},{28,... | collective-permute-start | bytes 1572872 | tf_op jit(solution)/shard_map/ppermute | solution.py:312
  49.0 24.3 %collective-permute-start.15 = (bf16[512,512]{1,0:T(8,128)(2,1)S(1)}, bf16[512,512]{1,0:T(8,128)(2,1)S(1)}, u32[]{:S(2)}, u32[]{:S(2)}) collective-permute-start(bf16[512,512]{1,0:T(8,128)(2,1)S(1)} %add_convert_fusion), channel_id=1, source_target_pairs={{4,0},{8,12},{5,1},{9,13},{6,2},{10,14},{7,3},{11,15},{20,16},{24,... | collective-permute-start | bytes 1572872 | tf_op jit(solution)/shard_map/ppermute | solution.py:314
  51.3 9.6 %collective-permute-start.8 = (bf16[64,128]{1,0:T(8,128)(2,1)S(1)}, bf16[64,128]{1,0:T(8,128)(2,1)S(1)}, u32[]{:S(2)}, u32[]{:S(2)}) collective-permute-start(bf16[64,128]{1,0:T(8,128)(2,1)S(1)} %shrink_partial.3), channel_id=1, source_target_pairs={{0,4},{4,0},{8,12},{12,8},{1,5},{5,1},{9,13},{13,9},{2,6},{6,2},{1... | collective-permute-start | bytes 49160 | tf_op jit(solution)/shard_map/ppermute | solution.py:265
  54.0 13.4 %collective-permute-start.5 = (bf16[128,512]{1,0:T(8,128)(2,1)S(1)}, bf16[128,512]{1,0:T(8,128)(2,1)S(1)}, u32[]{:S(2)}, u32[]{:S(2)}) collective-permute-start(bf16[128,512]{1,0:T(8,128)(2,1)S(1)} %get-tuple-element.30), channel_id=1, source_target_pairs={{0,1},{1,0},{2,3},{3,2},{4,5},{5,4},{6,7},{7,6},{8,9},{9,8},{10,11... | collective-permute-start | bytes 393224 | tf_op jit(solution)/shard_map/ppermute | solution.py:265
  60.9 4.7 %collective-permute-start.9 = (bf16[64,128]{1,0:T(8,128)(2,1)S(1)}, bf16[64,128]{1,0:T(8,128)(2,1)S(1)}, u32[]{:S(2)}, u32[]{:S(2)}) collective-permute-start(bf16[64,128]{1,0:T(8,128)(2,1)S(1)} %add_convert_fusion.4.one_ref), channel_id=1, source_target_pairs={{0,8},{4,12},{8,0},{12,4},{1,9},{5,13},{9,1},{13,5},{2,10},{6,14},... | collective-permute-start | bytes 49160 | tf_op jit(solution)/shard_map/ppermute | solution.py:265
  65.6 5.1 %collective-permute-start.6 = (bf16[128,512]{1,0:T(8,128)(2,1)S(1)}, bf16[128,512]{1,0:T(8,128)(2,1)S(1)}, u32[]{:S(2)}, u32[]{:S(2)}) collective-permute-start(bf16[128,512]{1,0:T(8,128)(2,1)S(1)} %get-tuple-element.31), channel_id=1, source_target_pairs={{0,2},{1,3},{2,0},{3,1},{4,6},{5,7},{6,4},{7,5},{8,10},{9,11},{10,... | collective-permute-start | bytes 393224 | tf_op jit(solution)/shard_map/ppermute | solution.py:265
  67.4 5.9 %collective-permute-start.10 = (bf16[128,512]{1,0:T(8,128)(2,1)S(1)}, bf16[128,512]{1,0:T(8,128)(2,1)S(1)}, u32[]{:S(2)}, u32[]{:S(2)}) collective-permute-start(bf16[128,512]{1,0:T(8,128)(2,1)S(1)} %expand.3), channel_id=1, source_target_pairs={{0,3},{1,2},{2,1},{3,0},{4,7},{5,6},{6,5},{7,4},{8,11},{9,10},{10,... | collective-permute-start | bytes 393224 | tf_op jit(solution)/shard_map/ppermute | solution.py:265

commit v3 on v2

v3 whole, which is shorter than its diff:
```python
import functools

import jax
import jax.numpy as jnp
from jax import lax
from jax.experimental import pallas as pl
from jax.experimental.pallas import tpu as pltpu
from jax.sharding import PartitionSpec as P

ADAPTER_RANK = 64
LANES = 128
VMEM_BYTES = 32 * 1024 * 1024

bf16 = jnp.bfloat16
f32 = jnp.float32
i32 = jnp.int32


def params():
    return pltpu.CompilerParams(vmem_limit_bytes=VMEM_BYTES)


def cost(flops, nbytes):
    return pl.CostEstimate(flops=flops, bytes_accessed=nbytes, transcendentals=0)


def dot(a, b, contract=((1,), (0,))):
    return lax.dot_general(a, b, (contract, ((), ())), preferred_element_type=f32)


def in_hbm(a):
    return pltpu.with_memory_space_constraint(a, pltpu.HBM)


def iota(shape, dim):
    return lax.broadcasted_iota(i32, shape, dim)


def places(slots, capacity, holders, me, ids, table):
    rows = ids.shape[1]
    low = (iota((LANES, rows), 0) == (ids & (LANES - 1))).astype(f32).astype(bf16)
    high = iota((table.shape[0], rows), 0) == lax.shift_right_logical(ids, 7)
    found = dot(table.astype(f32).astype(bf16), low)
    slot = jnp.sum(jnp.where(high, found, 0.0), axis=0, keepdims=True).astype(i32)
    holder = lax.div(slot, slots)
    tag = (slot - holder * slots + 1).astype(f32)
    partner = holder ^ me
    mine = iota((max(8, holders), rows), 0) == partner
    earlier = (iota((rows, rows), 0) < iota((rows, rows), 1)).astype(f32).astype(bf16)
    before = dot(mine.astype(f32).astype(bf16), earlier)
    rank = jnp.sum(jnp.where(mine, before, 0.0), axis=0, keepdims=True).astype(i32)
    return partner * capacity + rank, tag


def sort_body(slots, capacity, holders, me_ref, ids_hbm, table_hbm, x_hbm, place_ref, *refs):
    outs, (ids_buf, table_buf, x_buf, small_sem, x_sem) = refs[:holders], refs[holders:]
    rows, features = x_buf.shape
    chunks = x_sem.shape[0]
    step = features // chunks
    small = [
        pltpu.make_async_copy(ids_hbm, ids_buf, small_sem.at[0]),
        pltpu.make_async_copy(table_hbm, table_buf, small_sem.at[1]),
    ]
    copies = []
    for c in range(chunks):
        part = pl.ds(c * step, step)
        copies.append(pltpu.make_async_copy(x_hbm.at[:, part], x_buf.at[:, part], x_sem.at[c]))
    for copy in small + copies:
        copy.start()
    for copy in small:
        copy.wait()
    place, tag = places(slots, capacity, holders, me_ref[0], ids_buf[...], table_buf[...])
    place_ref[...] = jnp.broadcast_to(place, place_ref.shape)
    pick = (iota((holders * capacity, rows), 0) == place).astype(f32).astype(bf16)
    tags = dot(pick, jnp.broadcast_to(tag, (LANES, rows)).astype(bf16), ((1,), (1,))).astype(bf16)
    for j, out in enumerate(outs):
        out[:, features:] = tags[j * capacity:(j + 1) * capacity]
    for c in range(chunks):
        copies[c].wait()
        moved = dot(pick, x_buf[:, c * step:(c + 1) * step]).astype(bf16)
        for j, out in enumerate(outs):
            out[:, c * step:(c + 1) * step] = moved[j * capacity:(j + 1) * capacity]


def sort_rows(me, ids, table, x, holders, slots, capacity):
    rows, features = x.shape
    ids, table = ids.reshape(1, rows), table.reshape(-1, LANES)
    chunks = max(1, features // 512)
    smem, vmem, hbm = (pl.BlockSpec(memory_space=m) for m in (pltpu.SMEM, pltpu.VMEM, pltpu.HBM))
    shapes = [jax.ShapeDtypeStruct((8, rows), i32)]
    shapes += [jax.ShapeDtypeStruct((capacity, features + LANES), bf16)] * holders
    return pl.pallas_call(
        functools.partial(sort_body, slots, capacity, holders),
        out_shape=shapes,
        in_specs=[smem, hbm, hbm, hbm],
        out_specs=[vmem] * len(shapes),
        scratch_shapes=[
            pltpu.VMEM(ids.shape, i32),
            pltpu.VMEM(table.shape, i32),
            pltpu.VMEM((rows, features), bf16),
            pltpu.SemaphoreType.DMA((2,)),
            pltpu.SemaphoreType.DMA((chunks,)),
        ],
        compiler_params=params(),
        cost_estimate=cost(2 * holders * capacity * rows * features, 4 * rows * features),
        name="sort_rows",
    )(me.reshape(1), in_hbm(ids), in_hbm(table), in_hbm(x))


def first_body(z_ref, x_ref, w_hbm, out, w_buf, sem):
    features, width = w_buf.shape
    chunks = sem.shape[0]
    step = features // chunks
    column = pl.multiple_of(jnp.where(z_ref[0] < 2, 3, 0) * width, width)
    copies = []
    for c in range(chunks):
        part = pl.ds(c * step, step)
        copies.append(pltpu.make_async_copy(w_hbm.at[part, pl.ds(column, width)], w_buf.at[part, :], sem.at[c]))
        copies[c].start()
    total = None
    for c in range(chunks):
        copies[c].wait()
        term = dot(x_ref[:, c * step:(c + 1) * step], w_buf[c * step:(c + 1) * step, :])
        total = term if total is None else total + term
    out[...] = total.astype(bf16)


def first_block(z, x, weight, width):
    rows, features = x.shape
    chunks = 4
    smem, vmem, hbm = (pl.BlockSpec(memory_space=m) for m in (pltpu.SMEM, pltpu.VMEM, pltpu.HBM))
    return pl.pallas_call(
        first_body,
        out_shape=jax.ShapeDtypeStruct((rows, width), bf16),
        in_specs=[smem, vmem, hbm],
        out_specs=vmem,
        scratch_shapes=[pltpu.VMEM((features, width), bf16), pltpu.SemaphoreType.DMA((chunks,))],
        compiler_params=params(),
        cost_estimate=cost(2 * rows * features * width, 2 * features * (rows + width)),
        name="first_block",
    )(z.reshape(1), x, in_hbm(weight))


def rest_body(z_ref, place_ref, x_ref, w_hbm, *refs):
    second, third, own, unsort, w_buf, sem = refs
    z = z_ref[0]
    width = own.shape[1]
    blocks = (jnp.where(z < 2, 2, 1), z ^ 1, z)
    copies = []
    for k, block in enumerate(blocks):
        column = pl.multiple_of(block * width, width)
        copies.append(pltpu.make_async_copy(w_hbm.at[:, pl.ds(column, width)], w_buf.at[k], sem.at[k]))
        copies[k].start()
    unsort_matrix(place_ref, unsort)
    x = x_ref[...]
    for k, out in enumerate((second, third, own)):
        copies[k].wait()
        out[...] = dot(x, w_buf[k]).astype(bf16)


def unsort_matrix(place_ref, unsort):
    rows, total = unsort.shape
    place = jnp.broadcast_to(place_ref[0:1, :].astype(f32), (LANES, rows)).T
    lane = iota((rows, LANES), 1).astype(f32)
    for k in range(total // LANES):
        unsort[:, k * LANES:(k + 1) * LANES] = (place == lane + float(k * LANES)).astype(f32).astype(bf16)


def rest(z, place, x, weight, width, total):
    rows, features = x.shape
    smem, vmem, hbm = (pl.BlockSpec(memory_space=m) for m in (pltpu.SMEM, pltpu.VMEM, pltpu.HBM))
    shapes = [jax.ShapeDtypeStruct((rows, width), bf16)] * 3 + [jax.ShapeDtypeStruct((rows, total), bf16)]
    return pl.pallas_call(
        rest_body,
        out_shape=shapes,
        in_specs=[smem, vmem, vmem, hbm],
        out_specs=[vmem] * len(shapes),
        scratch_shapes=[pltpu.VMEM((3, features, width), bf16), pltpu.SemaphoreType.DMA((3,))],
        compiler_params=params(),
        cost_estimate=cost(6 * rows * features * width, 2 * features * (rows + 4 * width)),
        name="rest",
    )(z.reshape(1), place, x, in_hbm(weight))


def unsort_only(place, total):
    return pl.pallas_call(
        unsort_matrix,
        out_shape=jax.ShapeDtypeStruct((place.shape[1], total), bf16),
        compiler_params=params(),
        name="unsort",
    )(place)


def slot_mask(tag, group):
    lane = iota(tag.shape, 1)
    return tag == jnp.where(lane < ADAPTER_RANK, 2 * group + 1, 2 * group + 2).astype(f32)


def shrink_body(kept, down_ref, *refs):
    parts, out = refs[1 if kept else 0:-1], refs[-1]
    features, width = down_ref.shape
    capacity = parts[0].shape[0]
    half = capacity // 2
    first = iota((half, LANES), 1) < ADAPTER_RANK
    if kept:
        out[:kept, :] = refs[0][...]
    for k, part in enumerate(parts):
        full = dot(part[:, :features], down_ref[...])
        tag = part[:, features:].astype(f32)
        total = jnp.zeros((capacity, LANES), f32)
        for group in range(width // LANES):
            total += jnp.where(slot_mask(tag, group), full[:, group * LANES:(group + 1) * LANES], 0.0)
        total += pltpu.roll(total, ADAPTER_RANK, 1)
        spot = slice(kept + k * half, kept + (k + 1) * half)
        out[spot, :] = jnp.where(first, total[:half], total[half:]).astype(bf16)


def shrink_partial(down, parts, done=()):
    features, width = down.shape
    capacity = parts[0].shape[0]
    total = len(parts) * capacity
    kept = sum(d.shape[0] for d in done)
    return pl.pallas_call(
        functools.partial(shrink_body, kept),
        out_shape=jax.ShapeDtypeStruct((kept + total // 2, LANES), bf16),
        compiler_params=params(),
        cost_estimate=cost(2 * total * features * width, 2 * features * (total + width)),
        name="shrink_partial",
    )(down, *done, *parts)


def expand_body(count, one_ref, two_ref, up_ref, *refs):
    tags, outs = refs[:count], refs[count:]
    capacity = outs[0].shape[0]
    half = capacity // 2
    up = up_ref[...]
    first = iota((half, LANES), 1) < ADAPTER_RANK
    for k in range(count):
        part = pl.ds(k * half, half)
        shrink = (one_ref[part, :].astype(f32) + two_ref[part, :].astype(f32)).astype(bf16).astype(f32)
        turned = pltpu.roll(shrink, ADAPTER_RANK, 1)
        rows = jnp.concatenate([jnp.where(first, shrink, turned), jnp.where(first, turned, shrink)], axis=0)
        tag = tags[k][...].astype(f32)
        spread = [
            jnp.where(slot_mask(tag, group), rows, 0.0).astype(bf16) for group in range(up.shape[0] // LANES)
        ]
        outs[k][...] = dot(jnp.concatenate(spread, axis=1), up).astype(bf16)


def expand(one, two, up, parts):
    capacity, width = parts[0].shape
    count = len(parts)
    tag_block = pl.BlockSpec((capacity, LANES), lambda i: (0, width // LANES - 1))
    whole = lambda a: pl.BlockSpec(a.shape, lambda i: (0, 0))
    columns = up.shape[1]
    return pl.pallas_call(
        functools.partial(expand_body, count),
        grid=(1,),
        out_shape=[jax.ShapeDtypeStruct((capacity, columns), bf16)] * count,
        in_specs=[whole(one), whole(two), whole(up)] + [tag_block] * count,
        out_specs=[pl.BlockSpec((capacity, columns), lambda i: (0, 0))] * count,
        compiler_params=params(),
        cost_estimate=cost(2 * count * capacity * up.size, 2 * (up.size + count * capacity * columns)),
        name="expand",
    )(one, two, up, *parts)


def finish_body(count, unsort_ref, *refs):
    deltas, sums, out = refs[:count], refs[count:-1], refs[-1]
    base = sums[0][...].astype(f32)
    for term in sums[1:]:
        base += term[...].astype(f32)
    out[...] = (base + dot(unsort_ref[...], jnp.concatenate([d[...] for d in deltas], axis=0))).astype(bf16)


def finish(unsort, deltas, sums):
    rows, columns = sums[0].shape
    return pl.pallas_call(
        functools.partial(finish_body, len(deltas)),
        out_shape=jax.ShapeDtypeStruct((rows, columns), bf16),
        compiler_params=params(),
        cost_estimate=cost(2 * rows * unsort.shape[1] * columns, 12 * rows * columns),
        name="finish",
    )(unsort, *deltas, *sums)


def both(a, b):
    return (a.astype(f32) + b.astype(f32)).astype(bf16)


def after(value, *others):
    return lax.optimization_barrier((value,) + others)[0]


def swap(value, axis, bit):
    return lax.ppermute(value, axis, [(i, i ^ bit) for i in range(lax.axis_size(axis))])


EDGE = [(0, 1), (3, 2)]
MIDDLE = [(1, 2), (2, 1)]


def tp_sums(mine, *before):
    sums, bit = [mine], 1
    while True:
        other = swap(sums[-1], "tp", bit)
        bit *= 2
        if bit >= lax.axis_size("tp"):
            return sums, other
        sums.append(both(after(sums[-1], *before), other))


def shards(x, ids, table, weight, down, up):
    holders = lax.axis_size("ad")
    capacity = x.shape[0] // 4
    slots = up.shape[0] // ADAPTER_RANK
    width = up.shape[1]
    total = holders * capacity
    me, z = lax.axis_index("ad"), lax.axis_index("tp")
    place, *send = sort_rows(me, ids, table, x, holders, slots, capacity)
    parts = [send[0]] + [swap(send[j], "ad", j) for j in range(1, holders)]
    if lax.axis_size("tp") == 4:
        x = after(x, place)
        first = first_block(z, x, weight, width)
        edge0 = lax.ppermute(first, "tp", EDGE)
        second, third, own, unsort = rest(z, after(place, first), x, weight, width, total)
        edge1 = lax.ppermute(second, "tp", EDGE)
        early = shrink_partial(down, parts[:-1])
        inner0 = both(after(first, early), edge0)
        middle0 = lax.ppermute(inner0, "tp", MIDDLE)
        mine = shrink_partial(down, [after(parts[-1], inner0)], [early])
        inner1, inner2 = both(second, edge1), both(third, middle0)
        steps, other = tp_sums(mine, inner1, inner2)
        middle1 = lax.ppermute(after(inner1, steps[-1]), "tp", MIDDLE)
        last = swap(after(inner2, other), "tp", 1)
        sums = [own, middle1, last]
    else:
        unsort = unsort_only(place, total)
        full = dot(x, weight).astype(bf16)
        sums = [lax.psum_scatter(full, "tp", scatter_dimension=1, tiled=True)]
        steps, other = tp_sums(shrink_partial(down, parts))
    deltas = expand(steps[-1], other, up, parts)
    back = [deltas[0]] + [swap(deltas[j], "ad", j) for j in range(1, holders)]
    return finish(unsort, back, sums)


def solution(mesh):
    in_specs = (
        P(("rep", "ad"), "tp"),
        P(("rep", "ad")),
        P("rep"),
        P("tp", None),
        P(("rep", "tp"), "ad"),
        P(("rep", "ad"), "tp"),
    )
    out_specs = P(("rep", "ad"), "tp")
    return jax.shard_map(shards, mesh=mesh, in_specs=in_specs, out_specs=out_specs, check_vma=False)
```

time: 74.8 us -> 61.2 us (0.82)
  waiting for transfers between devices: 40.8 us -> 24.3 us
  Pallas kernels: 12.3 us -> 15.3 us
  starting transfers between devices: 20.9 us -> 19.1 us
  local copies, waits for them, and re-layouts: 0.02 us -> 1.6 us
    ppermute x10 -> x9, waiting for transfers between devices: 35.3 us -> 10.9 us  [swap(): lax.ppermute(value, axis, [(i, i ^ bit) for i in range(lax.axis_size(axis...]
    ppermute x1, waiting for transfers between devices: 0.01 us -> 9.62 us  [shards(): edge1 = lax.ppermute(second, 'tp', EDGE)]
    pallas_call x4 -> x5, Pallas kernels: 10.3 us -> 13.6 us  [the longest x1 5.5 us: rest(): pl.pallas_call(rest_body, out_shape=shapes, in_specs=[smem, vmem, vmem, h...]
    ppermute x4 -> x2, starting transfers between devices: 4.39 us -> 1.38 us  [the longest x1 0.69 us: shards(): middle0 = lax.ppermute(inner0, 'tp', MIDDLE)]
    ppermute x10 -> x9, starting transfers between devices: 10.2 us -> 12.6 us  [swap(): lax.ppermute(value, axis, [(i, i ^ bit) for i in range(lax.axis_size(axis...]
    ppermute x1, waiting for transfers between devices: 5.54 us -> 3.87 us  [shards(): edge0 = lax.ppermute(first, 'tp', EDGE)]
    unnamed x8 -> x6, local copies, waits for them, and re-layouts: 0.02 us -> 1.6 us
    ppermute x1, starting transfers between devices: 4.96 us -> 3.52 us  [shards(): edge0 = lax.ppermute(first, 'tp', EDGE)]
  transfers between devices with their start and end apart: 16 -> 13, of which waited for: 8 -> 7; matrix products, arithmetic and copies ran while one was open for 1% -> 1% of each run, Pallas kernels for 8% -> 17%
where the time goes in v3:
time: 61.2 us; the launch traced here: 60.9 us
  waiting for transfers between devices  24.3 us (40%)
  starting transfers between devices  19.1 us (31%)
  Pallas kernels  15.3 us (25%)
  local copies, waits for them, and re-layouts  1.6 us (3%)
    ppermute x9, starting transfers between devices, swap(): lax.ppermute(value, axis, [(i, i ^ bit) for i in range(lax.axis_size(axis...  12.6 us
    ppermute x9, waiting for transfers between devices, swap(): lax.ppermute(value, axis, [(i, i ^ bit) for i in range(lax.axis_size(axis...  10.9 us
    ppermute x1, waiting for transfers between devices, shards(): edge1 = lax.ppermute(second, 'tp', EDGE)  9.62 us
    pallas_call x1, Pallas kernels, rest(): pl.pallas_call(rest_body, out_shape=shapes, in_specs=[smem, vmem, vmem, h...  5.5 us
    pallas_call x1, Pallas kernels, sort_rows(): pl.pallas_call(functools.partial(sort_body, slots, capacity, holders), ou...  3.88 us
    ppermute x1, waiting for transfers between devices, shards(): edge0 = lax.ppermute(first, 'tp', EDGE)  3.87 us
    ppermute x1, starting transfers between devices, shards(): edge0 = lax.ppermute(first, 'tp', EDGE)  3.52 us
    pallas_call x1, Pallas kernels, first_block(): pl.pallas_call(first_body, out_shape=jax.ShapeDtypeStruct((rows, width),...  2.59 us
  transfers between devices with their start and end apart: 13, of which 7 were waited for; matrix products, arithmetic and copies ran while one was open for 1% of the time, Pallas kernels for 17%

profile of v3, /device:TPU:0, one launch (start us, length us, event | category | flops | bytes accessed | tf_op | source)
XLA Modules:
  0.0 60.9 jit_solution(2700817709352889400)
XLA Ops:
  0.0 3.9 %sort_rows.1 = (s32[8,512]{1,0:T(8,128)S(1)}, bf16[128,2176]{1,0:T(8,128)(2,1)S(1)}, bf16[128,2176]{1,0:T(8,128)(2,1)S(1)}, bf16[128,2176]{1,0:T(8,128)(2,1)S(1)}, bf16[128,2176]{1,0:T(8,128)(2,1)S(1)}) custom-call(s32[1]{0:T(128)} %bitcast.1.me_ref, s32[1,512]{1,0:T(1,128)} %bitcast.5, s32[32,128]{1,0:T(8,128)} %bitcast.4, bf16[512,2048]{1,0:T(8,128)(2,1)} %x_ref.1), custom_call_target="tpu_custom_call" | custom-call | flops 1073741824 | bytes 4194304 | tf_op jit(solution)/shard_map/sort_rows/pallas_call | solution.py:92
  3.9 0.5 collective-permute-start
  4.4 2.6 %collective-permute-start.1 = (bf16[128,2176]{1,0:T(8,128)(2,1)S(1)}, bf16[128,2176]{1,0:T(8,128)(2,1)S(1)}, u32[]{:S(2)}, u32[]{:S(2)}) collective-permute-start(bf16[128,2176]{1,0:T(8,128)(2,1)S(1)} %get-tuple-element.31), channel_id=1, source_target_pairs={{0,2},{1,3},{2,0},{3,1},{4,6},{5,7},{6,4},{7,5},{8,10},{9,11},{10,... | collective-permute-start | bytes 1671176 | tf_op jit(solution)/shard_map/ppermute | solution.py:296
  7.0 1.6 %copy-done.1 = bf16[512,2048]{1,0:T(8,128)(2,1)S(1)} copy-done((bf16[512,2048]{1,0:T(8,128)(2,1)S(1)}, bf16[512,2048]{1,0:T(8,128)(2,1)}, u32[]{:S(2)}) %copy-start.1) | copy-done | bytes 2097176
  8.6 2.6 %first_block.1 = bf16[512,512]{1,0:T(8,128)(2,1)S(1)} custom-call(s32[1]{0:T(128)} %bitcast.z_ref, bf16[512,2048]{1,0:T(8,128)(2,1)S(1)} %copy-done.1, bf16[2048,2048]{1,0:T(8,128)(2,1)} %w_hbm.3), custom_call_target="tpu_custom_call" | custom-call | flops 1073741824 | bytes 4194304 | tf_op jit(solution)/shard_map/first_block/pallas_call | solution.py:132
  11.2 3.5 %collective-permute-start.3 = (bf16[512,512]{1,0:T(8,128)(2,1)S(1)}, bf16[512,512]{1,0:T(8,128)(2,1)S(1)}, u32[]{:S(2)}, u32[]{:S(2)}) collective-permute-start(bf16[512,512]{1,0:T(8,128)(2,1)S(1)} %first_block.1), channel_id=1, source_target_pairs={{0,4},{12,8},{1,5},{13,9},{2,6},{14,10},{3,7},{15,11},{16,20},{28,... | collective-permute-start | bytes 1572872 | tf_op jit(solution)/shard_map/ppermute | solution.py:325
  14.8 5.5 %rest.1 = (bf16[512,512]{1,0:T(8,128)(2,1)S(1)}, bf16[512,512]{1,0:T(8,128)(2,1)S(1)}, bf16[512,512]{1,0:T(8,128)(2,1)S(1)}, bf16[512,512]{1,0:T(8,128)(2,1)S(1)}) custom-call(s32[1]{0:T(128)} %bitcast.z_ref, s32[8,512]{1,0:T(8,128)S(1)} %get-tuple-element.27.place_ref, bf16[512,2048]{1,0:T(8,128)(2,1)S(1)} %copy-done.1, bf16[2048,2048]{1,0:T(8,128)(2,1)} %w_hbm.3), custom_call_target="tpu_custom_call" | custom-call | flops 3221225472 | bytes 10485760 | tf_op jit(solution)/shard_map/rest/pallas_call | solution.py:173
  20.3 1.6 %collective-permute-start.4 = (bf16[512,512]{1,0:T(8,128)(2,1)S(1)}, bf16[512,512]{1,0:T(8,128)(2,1)S(1)}, u32[]{:S(2)}, u32[]{:S(2)}) collective-permute-start(bf16[512,512]{1,0:T(8,128)(2,1)S(1)} %get-tuple-element.35), channel_id=1, source_target_pairs={{0,4},{12,8},{1,5},{13,9},{2,6},{14,10},{3,7},{15,11},{16,20},{28,... | collective-permute-start | bytes 1572872 | tf_op jit(solution)/shard_map/ppermute | solution.py:327
  21.9 1.1 %shrink_partial.2.refs_0_ = bf16[192,128]{1,0:T(8,128)(2,1)S(1)} custom-call(bf16[2048,512]{1,0:T(8,128)(2,1)S(1)} %copy-done, bf16[128,2176]{1,0:T(8,128)(2,1)S(1)} %get-tuple-element.29.refs_0_, bf16[128,2176]{1,0:T(8,128)(2,1)S(1)} %collective-permute-done.refs_1_, bf16[128,2176]{1,0:T(8,128)(2,1)S(1)} %collective-permute-done.1.refs_2_), custom_call_target="tpu_custom_call" | custom-call | flops 805306368 | bytes 3670016 | tf_op jit(solution)/shard_map/shrink_partial/pallas_call | solution.py:223
  23.0 3.9 %collective-permute-done.3 = bf16[512,512]{1,0:T(8,128)(2,1)S(1)} collective-permute-done((bf16[512,512]{1,0:T(8,128)(2,1)S(1)}, bf16[512,512]{1,0:T(8,128)(2,1)S(1)}, u32[]{:S(2)}, u32[]{:S(2)}) %collective-permute-start.3) | collective-permute-done | bytes 524320 | tf_op jit(solution)/shard_map/ppermute | solution.py:325
  27.1 0.7 %collective-permute-start.5 = (bf16[512,512]{1,0:T(8,128)(2,1)S(1)}, bf16[512,512]{1,0:T(8,128)(2,1)S(1)}, u32[]{:S(2)}, u32[]{:S(2)}) collective-permute-start(bf16[512,512]{1,0:T(8,128)(2,1)S(1)} %add_convert_fusion.2), channel_id=1, source_target_pairs={{4,8},{8,4},{5,9},{9,5},{6,10},{10,6},{7,11},{11,7},{20,24},{24,20... | collective-permute-start | bytes 1572872 | tf_op jit(solution)/shard_map/ppermute | solution.py:330
  27.8 9.6 %collective-permute-done.4 = bf16[512,512]{1,0:T(8,128)(2,1)S(1)} collective-permute-done((bf16[512,512]{1,0:T(8,128)(2,1)S(1)}, bf16[512,512]{1,0:T(8,128)(2,1)S(1)}, u32[]{:S(2)}, u32[]{:S(2)}) %collective-permute-start.4) | collective-permute-done | bytes 524320 | tf_op jit(solution)/shard_map/ppermute | solution.py:327
  38.1 2.5 %collective-permute-start.6 = (bf16[256,128]{1,0:T(8,128)(2,1)S(1)}, bf16[256,128]{1,0:T(8,128)(2,1)S(1)}, u32[]{:S(2)}, u32[]{:S(2)}) collective-permute-start(bf16[256,128]{1,0:T(8,128)(2,1)S(1)} %shrink_partial.3), channel_id=1, source_target_pairs={{0,4},{4,0},{8,12},{12,8},{1,5},{5,1},{9,13},{13,9},{2,6},{6,2},{1... | collective-permute-start | bytes 196616 | tf_op jit(solution)/shard_map/ppermute | solution.py:296
  40.8 2.1 %collective-permute-done.6 = bf16[256,128]{1,0:T(8,128)(2,1)S(1)} collective-permute-done((bf16[256,128]{1,0:T(8,128)(2,1)S(1)}, bf16[256,128]{1,0:T(8,128)(2,1)S(1)}, u32[]{:S(2)}, u32[]{:S(2)}) %collective-permute-start.6) | collective-permute-done | bytes 65568 | tf_op jit(solution)/shard_map/ppermute | solution.py:296
  42.9 3.1 %collective-permute-start.7 = (bf16[256,128]{1,0:T(8,128)(2,1)S(1)}, bf16[256,128]{1,0:T(8,128)(2,1)S(1)}, u32[]{:S(2)}, u32[]{:S(2)}) collective-permute-start(bf16[256,128]{1,0:T(8,128)(2,1)S(1)} %add_convert_fusion.3.one_ref), channel_id=1, source_target_pairs={{0,8},{4,12},{8,0},{12,4},{1,9},{5,13},{9,1},{13,5},{2,10},{6,14},... | collective-permute-start | bytes 196616 | tf_op jit(solution)/shard_map/ppermute | solution.py:296
  46.0 0.7 %collective-permute-start.11 = (bf16[512,512]{1,0:T(8,128)(2,1)S(1)}, bf16[512,512]{1,0:T(8,128)(2,1)S(1)}, u32[]{:S(2)}, u32[]{:S(2)}) collective-permute-start(bf16[512,512]{1,0:T(8,128)(2,1)S(1)} %add_convert_fusion.1), channel_id=1, source_target_pairs={{4,8},{8,4},{5,9},{9,5},{6,10},{10,6},{7,11},{11,7},{20,24},{24,20... | collective-permute-start | bytes 1572872 | tf_op jit(solution)/shard_map/ppermute | solution.py:334
  46.7 1.8 %collective-permute-done.7.two_ref = bf16[256,128]{1,0:T(8,128)(2,1)S(1)} collective-permute-done((bf16[256,128]{1,0:T(8,128)(2,1)S(1)}, bf16[256,128]{1,0:T(8,128)(2,1)S(1)}, u32[]{:S(2)}, u32[]{:S(2)}) %collective-permute-start.7) | collective-permute-done | bytes 65568 | tf_op jit(solution)/shard_map/ppermute | solution.py:296
  48.4 1.8 %collective-permute-start.12 = (bf16[512,512]{1,0:T(8,128)(2,1)S(1)}, bf16[512,512]{1,0:T(8,128)(2,1)S(1)}, u32[]{:S(2)}, u32[]{:S(2)}) collective-permute-start(bf16[512,512]{1,0:T(8,128)(2,1)S(1)} %add_convert_fusion), channel_id=1, source_target_pairs={{0,4},{4,0},{8,12},{12,8},{1,5},{5,1},{9,13},{13,9},{2,6},{6,2},{1... | collective-permute-start | bytes 1572872 | tf_op jit(solution)/shard_map/ppermute | solution.py:296
  50.8 0.6 collective-permute-start.9
  51.4 1.3 %collective-permute-start.10 = (bf16[128,512]{1,0:T(8,128)(2,1)S(1)}, bf16[128,512]{1,0:T(8,128)(2,1)S(1)}, u32[]{:S(2)}, u32[]{:S(2)}) collective-permute-start(bf16[128,512]{1,0:T(8,128)(2,1)S(1)} %get-tuple-element.41), channel_id=1, source_target_pairs={{0,3},{1,2},{2,1},{3,0},{4,7},{5,6},{6,5},{7,4},{8,11},{9,10},{10,... | collective-permute-start | bytes 393224 | tf_op jit(solution)/shard_map/ppermute | solution.py:296
  52.7 4.5 %collective-permute-done.9.refs_2_ = bf16[128,512]{1,0:T(8,128)(2,1)S(1)} collective-permute-done((bf16[128,512]{1,0:T(8,128)(2,1)S(1)}, bf16[128,512]{1,0:T(8,128)(2,1)S(1)}, u32[]{:S(2)}, u32[]{:S(2)}) %collective-permute-start.9) | collective-permute-done | bytes 131104 | tf_op jit(solution)/shard_map/ppermute | solution.py:296
  57.2 1.9 %collective-permute-done.10.refs_3_ = bf16[128,512]{1,0:T(8,128)(2,1)S(1)} collective-permute-done((bf16[128,512]{1,0:T(8,128)(2,1)S(1)}, bf16[128,512]{1,0:T(8,128)(2,1)S(1)}, u32[]{:S(2)}, u32[]{:S(2)}) %collective-permute-start.10) | collective-permute-done | bytes 131104 | tf_op jit(solution)/shard_map/ppermute | solution.py:296
  59.1 0.6 collective-permute-done.12.refs_6_
  59.7 1.3 %finish.1 = bf16[512,512]{1,0:T(8,128)(2,1)} custom-call(bf16[512,512]{1,0:T(8,128)(2,1)S(1)} %get-tuple-element.28.unsort_ref, bf16[128,512]{1,0:T(8,128)(2,1)S(1)} %get-tuple-element.38.refs_0_, bf16[128,512]{1,0:T(8,128)(2,1)S(1)} %collective-permute-done.8.refs_1_, bf16[128,512]{1,0:T(8,128)(2,1)S(1)} %collective-permute-done.9.refs_2_, ...), custom_call_target="tpu_custom_call" | custom-call | flops 268435456 | bytes 3145728 | tf_op jit(solution)/shard_map/finish/pallas_call | solution.py:278
  (19 shorter events, 1.6 us)
Async XLA Ops:
  3.9 18.0 %collective-permute-start = (bf16[128,2176]{1,0:T(8,128)(2,1)S(1)}, bf16[128,2176]{1,0:T(8,128)(2,1)S(1)}, u32[]{:S(2)}, u32[]{:S(2)}) collective-permute-start(bf16[128,2176]{1,0:T(8,128)(2,1)S(1)} %get-tuple-element.30), channel_id=1, source_target_pairs={{0,1},{1,0},{2,3},{3,2},{4,5},{5,4},{6,7},{7,6},{8,9},{9,8},{10,11... | collective-permute-start | bytes 1671176 | tf_op jit(solution)/shard_map/ppermute | solution.py:296
  4.4 17.5 %collective-permute-start.1 = (bf16[128,2176]{1,0:T(8,128)(2,1)S(1)}, bf16[128,2176]{1,0:T(8,128)(2,1)S(1)}, u32[]{:S(2)}, u32[]{:S(2)}) collective-permute-start(bf16[128,2176]{1,0:T(8,128)(2,1)S(1)} %get-tuple-element.31), channel_id=1, source_target_pairs={{0,2},{1,3},{2,0},{3,1},{4,6},{5,7},{6,4},{7,5},{8,10},{9,11},{10,... | collective-permute-start | bytes 1671176 | tf_op jit(solution)/shard_map/ppermute | solution.py:296
  7.0 1.6 %copy-start.1 = (bf16[512,2048]{1,0:T(8,128)(2,1)S(1)}, bf16[512,2048]{1,0:T(8,128)(2,1)}, u32[]{:S(2)}) copy-start(bf16[512,2048]{1,0:T(8,128)(2,1)} %x_ref.1) | copy-start | bytes 6291460
  11.2 15.8 %collective-permute-start.3 = (bf16[512,512]{1,0:T(8,128)(2,1)S(1)}, bf16[512,512]{1,0:T(8,128)(2,1)S(1)}, u32[]{:S(2)}, u32[]{:S(2)}) collective-permute-start(bf16[512,512]{1,0:T(8,128)(2,1)S(1)} %first_block.1), channel_id=1, source_target_pairs={{0,4},{12,8},{1,5},{13,9},{2,6},{14,10},{3,7},{15,11},{16,20},{28,... | collective-permute-start | bytes 1572872 | tf_op jit(solution)/shard_map/ppermute | solution.py:325
  14.7 7.2 %copy-start = (bf16[2048,512]{1,0:T(8,128)(2,1)S(1)}, bf16[2048,512]{1,0:T(8,128)(2,1)}, u32[]{:S(2)}) copy-start(bf16[2048,512]{1,0:T(8,128)(2,1)} %down_ref.3) | copy-start | bytes 6291460
  14.7 22.8 %collective-permute-start.2 = (bf16[128,2176]{1,0:T(8,128)(2,1)S(1)}, bf16[128,2176]{1,0:T(8,128)(2,1)S(1)}, u32[]{:S(2)}, u32[]{:S(2)}) collective-permute-start(bf16[128,2176]{1,0:T(8,128)(2,1)S(1)} %get-tuple-element.32), channel_id=1, source_target_pairs={{0,3},{1,2},{2,1},{3,0},{4,7},{5,6},{6,5},{7,4},{8,11},{9,10},{10,... | collective-permute-start | bytes 1671176 | tf_op jit(solution)/shard_map/ppermute | solution.py:296
  20.3 17.1 %collective-permute-start.4 = (bf16[512,512]{1,0:T(8,128)(2,1)S(1)}, bf16[512,512]{1,0:T(8,128)(2,1)S(1)}, u32[]{:S(2)}, u32[]{:S(2)}) collective-permute-start(bf16[512,512]{1,0:T(8,128)(2,1)S(1)} %get-tuple-element.35), channel_id=1, source_target_pairs={{0,4},{12,8},{1,5},{13,9},{2,6},{14,10},{3,7},{15,11},{16,20},{28,... | collective-permute-start | bytes 1572872 | tf_op jit(solution)/shard_map/ppermute | solution.py:327
  27.1 13.6 %collective-permute-start.5 = (bf16[512,512]{1,0:T(8,128)(2,1)S(1)}, bf16[512,512]{1,0:T(8,128)(2,1)S(1)}, u32[]{:S(2)}, u32[]{:S(2)}) collective-permute-start(bf16[512,512]{1,0:T(8,128)(2,1)S(1)} %add_convert_fusion.2), channel_id=1, source_target_pairs={{4,8},{8,4},{5,9},{9,5},{6,10},{10,6},{7,11},{11,7},{20,24},{24,20... | collective-permute-start | bytes 1572872 | tf_op jit(solution)/shard_map/ppermute | solution.py:330
  37.5 12.7 %copy-start.2 = (bf16[512,512]{1,0:T(8,128)(2,1)S(1)}, bf16[512,512]{1,0:T(8,128)(2,1)}, u32[]{:S(2)}) copy-start(bf16[512,512]{1,0:T(8,128)(2,1)} %up_ref.1) | copy-start | bytes 1572868
  38.1 4.8 %collective-permute-start.6 = (bf16[256,128]{1,0:T(8,128)(2,1)S(1)}, bf16[256,128]{1,0:T(8,128)(2,1)S(1)}, u32[]{:S(2)}, u32[]{:S(2)}) collective-permute-start(bf16[256,128]{1,0:T(8,128)(2,1)S(1)} %shrink_partial.3), channel_id=1, source_target_pairs={{0,4},{4,0},{8,12},{12,8},{1,5},{5,1},{9,13},{13,9},{2,6},{6,2},{1... | collective-permute-start | bytes 196616 | tf_op jit(solution)/shard_map/ppermute | solution.py:296
  42.9 5.6 %collective-permute-start.7 = (bf16[256,128]{1,0:T(8,128)(2,1)S(1)}, bf16[256,128]{1,0:T(8,128)(2,1)S(1)}, u32[]{:S(2)}, u32[]{:S(2)}) collective-permute-start(bf16[256,128]{1,0:T(8,128)(2,1)S(1)} %add_convert_fusion.3.one_ref), channel_id=1, source_target_pairs={{0,8},{4,12},{8,0},{12,4},{1,9},{5,13},{9,1},{13,5},{2,10},{6,14},... | collective-permute-start | bytes 196616 | tf_op jit(solution)/shard_map/ppermute | solution.py:296
  46.0 13.1 %collective-permute-start.11 = (bf16[512,512]{1,0:T(8,128)(2,1)S(1)}, bf16[512,512]{1,0:T(8,128)(2,1)S(1)}, u32[]{:S(2)}, u32[]{:S(2)}) collective-permute-start(bf16[512,512]{1,0:T(8,128)(2,1)S(1)} %add_convert_fusion.1), channel_id=1, source_target_pairs={{4,8},{8,4},{5,9},{9,5},{6,10},{10,6},{7,11},{11,7},{20,24},{24,20... | collective-permute-start | bytes 1572872 | tf_op jit(solution)/shard_map/ppermute | solution.py:334
  48.4 11.2 %collective-permute-start.12 = (bf16[512,512]{1,0:T(8,128)(2,1)S(1)}, bf16[512,512]{1,0:T(8,128)(2,1)S(1)}, u32[]{:S(2)}, u32[]{:S(2)}) collective-permute-start(bf16[512,512]{1,0:T(8,128)(2,1)S(1)} %add_convert_fusion), channel_id=1, source_target_pairs={{0,4},{4,0},{8,12},{12,8},{1,5},{5,1},{9,13},{13,9},{2,6},{6,2},{1... | collective-permute-start | bytes 1572872 | tf_op jit(solution)/shard_map/ppermute | solution.py:296
  50.7 1.9 %collective-permute-start.8 = (bf16[128,512]{1,0:T(8,128)(2,1)S(1)}, bf16[128,512]{1,0:T(8,128)(2,1)S(1)}, u32[]{:S(2)}, u32[]{:S(2)}) collective-permute-start(bf16[128,512]{1,0:T(8,128)(2,1)S(1)} %get-tuple-element.39), channel_id=1, source_target_pairs={{0,1},{1,0},{2,3},{3,2},{4,5},{5,4},{6,7},{7,6},{8,9},{9,8},{10,11... | collective-permute-start | bytes 393224 | tf_op jit(solution)/shard_map/ppermute | solution.py:296
  50.8 6.4 %collective-permute-start.9 = (bf16[128,512]{1,0:T(8,128)(2,1)S(1)}, bf16[128,512]{1,0:T(8,128)(2,1)S(1)}, u32[]{:S(2)}, u32[]{:S(2)}) collective-permute-start(bf16[128,512]{1,0:T(8,128)(2,1)S(1)} %get-tuple-element.40), channel_id=1, source_target_pairs={{0,2},{1,3},{2,0},{3,1},{4,6},{5,7},{6,4},{7,5},{8,10},{9,11},{10,... | collective-permute-start | bytes 393224 | tf_op jit(solution)/shard_map/ppermute | solution.py:296
  51.4 7.7 %collective-permute-start.10 = (bf16[128,512]{1,0:T(8,128)(2,1)S(1)}, bf16[128,512]{1,0:T(8,128)(2,1)S(1)}, u32[]{:S(2)}, u32[]{:S(2)}) collective-permute-start(bf16[128,512]{1,0:T(8,128)(2,1)S(1)} %get-tuple-element.41), channel_id=1, source_target_pairs={{0,3},{1,2},{2,1},{3,0},{4,7},{5,6},{6,5},{7,4},{8,11},{9,10},{10,... | collective-permute-start | bytes 393224 | tf_op jit(solution)/shard_map/ppermute | solution.py:296

commit v4 on v3

--- a/solution.py
+++ b/solution.py
@@ -36,7 +36,7 @@
     return lax.broadcasted_iota(i32, shape, dim)
 
 
-def places(slots, capacity, holders, me, ids, table):
+def places(slots, capacity, holders, me, ids, table, earlier):
     rows = ids.shape[1]
     low = (iota((LANES, rows), 0) == (ids & (LANES - 1))).astype(f32).astype(bf16)
     high = iota((table.shape[0], rows), 0) == lax.shift_right_logical(ids, 7)
@@ -46,15 +46,15 @@
     tag = (slot - holder * slots + 1).astype(f32)
     partner = holder ^ me
     mine = iota((max(8, holders), rows), 0) == partner
-    earlier = (iota((rows, rows), 0) < iota((rows, rows), 1)).astype(f32).astype(bf16)
     before = dot(mine.astype(f32).astype(bf16), earlier)
     rank = jnp.sum(jnp.where(mine, before, 0.0), axis=0, keepdims=True).astype(i32)
     return partner * capacity + rank, tag
 
 
-def sort_body(slots, capacity, holders, me_ref, ids_hbm, table_hbm, x_hbm, place_ref, *refs):
-    outs, (ids_buf, table_buf, x_buf, small_sem, x_sem) = refs[:holders], refs[holders:]
+def sort_body(slots, capacity, holders, me_ref, z_ref, ids_hbm, table_hbm, x_hbm, w_hbm, place_ref, *refs):
+    outs, (x_buf, w_buf, ids_buf, table_buf, small_sem, x_sem, w_sem) = refs[:holders], refs[holders:]
     rows, features = x_buf.shape
+    width = w_buf.shape[1]
     chunks = x_sem.shape[0]
     step = features // chunks
     small = [
@@ -65,11 +65,14 @@
     for c in range(chunks):
         part = pl.ds(c * step, step)
         copies.append(pltpu.make_async_copy(x_hbm.at[:, part], x_buf.at[:, part], x_sem.at[c]))
-    for copy in small + copies:
+    column = pl.multiple_of(jnp.where(z_ref[0] < 2, 3, 0) * width, width)
+    w_copy = pltpu.make_async_copy(w_hbm.at[:, pl.ds(column, width)], w_buf, w_sem)
+    for copy in small + copies + [w_copy]:
         copy.start()
+    earlier = (iota((rows, rows), 0) < iota((rows, rows), 1)).astype(f32).astype(bf16)
     for copy in small:
         copy.wait()
-    place, tag = places(slots, capacity, holders, me_ref[0], ids_buf[...], table_buf[...])
+    place, tag = places(slots, capacity, holders, me_ref[0], ids_buf[...], table_buf[...], earlier)
     place_ref[...] = jnp.broadcast_to(place, place_ref.shape)
     pick = (iota((holders * capacity, rows), 0) == place).astype(f32).astype(bf16)
     tags = dot(pick, jnp.broadcast_to(tag, (LANES, rows)).astype(bf16), ((1,), (1,))).astype(bf16)
@@ -80,65 +83,48 @@
         moved = dot(pick, x_buf[:, c * step:(c + 1) * step]).astype(bf16)
         for j, out in enumerate(outs):
             out[:, c * step:(c + 1) * step] = moved[j * capacity:(j + 1) * capacity]
-
-
-def sort_rows(me, ids, table, x, holders, slots, capacity):
+    w_copy.wait()
+
+
+def sort_rows(me, z, ids, table, x, weight, holders, slots, capacity, width):
     rows, features = x.shape
     ids, table = ids.reshape(1, rows), table.reshape(-1, LANES)
     chunks = max(1, features // 512)
     smem, vmem, hbm = (pl.BlockSpec(memory_space=m) for m in (pltpu.SMEM, pltpu.VMEM, pltpu.HBM))
     shapes = [jax.ShapeDtypeStruct((8, rows), i32)]
     shapes += [jax.ShapeDtypeStruct((capacity, features + LANES), bf16)] * holders
+    shapes += [jax.ShapeDtypeStruct((rows, features), bf16), jax.ShapeDtypeStruct((features, width), bf16)]
     return pl.pallas_call(
         functools.partial(sort_body, slots, capacity, holders),
         out_shape=shapes,
-        in_specs=[smem, hbm, hbm, hbm],
+        in_specs=[smem, smem, hbm, hbm, hbm, hbm],
         out_specs=[vmem] * len(shapes),
         scratch_shapes=[
             pltpu.VMEM(ids.shape, i32),
             pltpu.VMEM(table.shape, i32),
-            pltpu.VMEM((rows, features), bf16),
             pltpu.SemaphoreType.DMA((2,)),
             pltpu.SemaphoreType.DMA((chunks,)),
+            pltpu.SemaphoreType.DMA(()),
         ],
         compiler_params=params(),
         cost_estimate=cost(2 * holders * capacity * rows * features, 4 * rows * features),
         name="sort_rows",
-    )(me.reshape(1), in_hbm(ids), in_hbm(table), in_hbm(x))
-
-
-def first_body(z_ref, x_ref, w_hbm, out, w_buf, sem):
-    features, width = w_buf.shape
-    chunks = sem.shape[0]
-    step = features // chunks
-    column = pl.multiple_of(jnp.where(z_ref[0] < 2, 3, 0) * width, width)
-    copies = []
-    for c in range(chunks):
-        part = pl.ds(c * step, step)
-        copies.append(pltpu.make_async_copy(w_hbm.at[part, pl.ds(column, width)], w_buf.at[part, :], sem.at[c]))
-        copies[c].start()
-    total = None
-    for c in range(chunks):
-        copies[c].wait()
-        term = dot(x_ref[:, c * step:(c + 1) * step], w_buf[c * step:(c + 1) * step, :])
-        total = term if total is None else total + term
-    out[...] = total.astype(bf16)
-
-
-def first_block(z, x, weight, width):
-    rows, features = x.shape
-    chunks = 4
-    smem, vmem, hbm = (pl.BlockSpec(memory_space=m) for m in (pltpu.SMEM, pltpu.VMEM, pltpu.HBM))
+    )(me.reshape(1), z.reshape(1), in_hbm(ids), in_hbm(table), in_hbm(x), in_hbm(weight))
+
+
+def first_body(x_ref, w_ref, out):
+    out[...] = dot(x_ref[...], w_ref[...]).astype(bf16)
+
+
+def first_block(x, w):
+    (rows, features), width = x.shape, w.shape[1]
     return pl.pallas_call(
         first_body,
         out_shape=jax.ShapeDtypeStruct((rows, width), bf16),
-        in_specs=[smem, vmem, hbm],
-        out_specs=vmem,
-        scratch_shapes=[pltpu.VMEM((features, width), bf16), pltpu.SemaphoreType.DMA((chunks,))],
         compiler_params=params(),
         cost_estimate=cost(2 * rows * features * width, 2 * features * (rows + width)),
         name="first_block",
-    )(z.reshape(1), x, in_hbm(weight))
+    )(x, w)
 
 
 def rest_body(z_ref, place_ref, x_ref, w_hbm, *refs):
@@ -260,7 +246,7 @@
         in_specs=[whole(one), whole(two), whole(up)] + [tag_block] * count,
         out_specs=[pl.BlockSpec((capacity, columns), lambda i: (0, 0))] * count,
         compiler_params=params(),
-        cost_estimate=cost(2 * count * capacity * up.size, 2 * (up.size + count * capacity * columns)),
+        cost_estimate=cost(80 * count * capacity * up.size, 80 * (up.size + count * capacity * columns)),
         name="expand",
     )(one, two, up, *parts)
 
@@ -317,11 +303,10 @@
     width = up.shape[1]
     total = holders * capacity
     me, z = lax.axis_index("ad"), lax.axis_index("tp")
-    place, *send = sort_rows(me, ids, table, x, holders, slots, capacity)
+    place, *send, x, w = sort_rows(me, z, ids, table, x, weight, holders, slots, capacity, width)
     parts = [send[0]] + [swap(send[j], "ad", j) for j in range(1, holders)]
     if lax.axis_size("tp") == 4:
-        x = after(x, place)
-        first = first_block(z, x, weight, width)
+        first = first_block(x, w)
         edge0 = lax.ppermute(first, "tp", EDGE)
         second, third, own, unsort = rest(z, after(place, first), x, weight, width, total)
         edge1 = lax.ppermute(second, "tp", EDGE)
@@ -329,10 +314,10 @@
         inner0 = both(after(first, early), edge0)
         middle0 = lax.ppermute(inner0, "tp", MIDDLE)
         mine = shrink_partial(down, [after(parts[-1], inner0)], [early])
-        inner1, inner2 = both(second, edge1), both(third, middle0)
-        steps, other = tp_sums(mine, inner1, inner2)
+        inner1 = both(second, edge1)
+        steps, other = tp_sums(mine, inner1)
         middle1 = lax.ppermute(after(inner1, steps[-1]), "tp", MIDDLE)
-        last = swap(after(inner2, other), "tp", 1)
+        last = swap(both(after(third, steps[-1]), middle0), "tp", 1)
         sums = [own, middle1, last]
     else:
         unsort = unsort_only(place, total)

time: 61.2 us -> 56.2 us (0.918)
  local copies, waits for them, and re-layouts: 1.6 us -> 0.01 us
  waiting for transfers between devices: 24.3 us -> 22.8 us
  Pallas kernels: 15.3 us -> 14 us
    ppermute x1, waiting for transfers between devices: 9.62 us -> 0.33 us  [shards(): edge1 = lax.ppermute(second, 'tp', EDGE)]
    ppermute x9, waiting for transfers between devices: 10.9 us -> 20 us  [swap(): lax.ppermute(value, axis, [(i, i ^ bit) for i in range(lax.axis_size(axis...]
    unnamed x6 -> x4, local copies, waits for them, and re-layouts: 1.6 us -> 0.01 us
    ppermute x1, waiting for transfers between devices: 3.87 us -> 2.47 us  [shards(): edge0 = lax.ppermute(first, 'tp', EDGE)]
    pallas_call x1, Pallas kernels: 2.59 us -> 1.25 us  [first_block(): pl.pallas_call(first_body, out_shape=jax.ShapeDtypeStruct((rows, width),...]
  transfers between devices with their start and end apart: 13 -> 13, of which waited for: 7 -> 9; matrix products, arithmetic and copies ran while one was open for 1% -> 1% of each run, Pallas kernels for 17% -> 16%
where the time goes in v4:
time: 56.2 us; the launch traced here: 56 us
  waiting for transfers between devices  22.8 us (41%)
  starting transfers between devices  18.7 us (33%)
  Pallas kernels  14 us (25%)
    ppermute x9, waiting for transfers between devices, swap(): lax.ppermute(value, axis, [(i, i ^ bit) for i in range(lax.axis_size(axis...  20 us
    ppermute x9, starting transfers between devices, swap(): lax.ppermute(value, axis, [(i, i ^ bit) for i in range(lax.axis_size(axis...  12.2 us
    pallas_call x1, Pallas kernels, rest(): pl.pallas_call(rest_body, out_shape=shapes, in_specs=[smem, vmem, vmem, h...  5.51 us
    pallas_call x1, Pallas kernels, sort_rows(): pl.pallas_call(functools.partial(sort_body, slots, capacity, holders), ou...  3.89 us
    ppermute x1, starting transfers between devices, shards(): edge0 = lax.ppermute(first, 'tp', EDGE)  3.51 us
    ppermute x1, waiting for transfers between devices, shards(): edge0 = lax.ppermute(first, 'tp', EDGE)  2.47 us
    ppermute x1, starting transfers between devices, shards(): edge1 = lax.ppermute(second, 'tp', EDGE)  1.57 us
    pallas_call x2, Pallas kernels, shrink_partial(): pl.pallas_call(functools.partial(shrink_body, kept), out_shape=jax.ShapeD...  1.57 us
  transfers between devices with their start and end apart: 13, of which 9 were waited for; matrix products, arithmetic and copies ran while one was open for 1% of the time, Pallas kernels for 16%

profile of v4, /device:TPU:0, one launch (start us, length us, event | category | flops | bytes accessed | tf_op | source)
XLA Modules:
  0.0 56.0 jit_solution(17149255152054418464)
XLA Ops:
  0.0 3.9 %sort_rows.1 = (s32[8,512]{1,0:T(8,128)S(1)}, bf16[128,2176]{1,0:T(8,128)(2,1)S(1)}, bf16[128,2176]{1,0:T(8,128)(2,1)S(1)}, bf16[128,2176]{1,0:T(8,128)(2,1)S(1)...) custom-call(s32[1]{0:T(128)} %bitcast.1.me_ref, s32[1]{0:T(128)} %bitcast.z_ref, ...), custom_call_target="tpu_custom_call" | custom-call | flops 1073741824 | bytes 4194304 | tf_op jit(solution)/shard_map/sort_rows/pallas_call | solution.py:97
  3.9 0.5 collective-permute-start
  4.4 2.6 %collective-permute-start.1 = (bf16[128,2176]{1,0:T(8,128)(2,1)S(1)}, bf16[128,2176]{1,0:T(8,128)(2,1)S(1)}, u32[]{:S(2)}, u32[]{:S(2)}) collective-permute-start(bf16[128,2176]{1,0:T(8,128)(2,1)S(1)} %get-tuple-element.33), channel_id=1, source_target_pairs={{0,2},{1,3},{2,0},{3,1},{4,6},{5,7},{6,4},{7,5},{8,10},{9,11},{10,... | collective-permute-start | bytes 1671176 | tf_op jit(solution)/shard_map/ppermute | solution.py:282
  7.0 1.3 %first_block.1 = bf16[512,512]{1,0:T(8,128)(2,1)S(1)} custom-call(bf16[512,2048]{1,0:T(8,128)(2,1)S(1)} %get-tuple-element.27.x_ref, bf16[2048,512]{1,0:T(8,128)(2,1)S(1)} %get-tuple-element.28.w_ref), custom_call_target="tpu_custom_call" | custom-call | flops 1073741824 | bytes 4194304 | tf_op jit(solution)/shard_map/first_block/pallas_call | solution.py:121
  8.2 3.5 %collective-permute-start.3 = (bf16[512,512]{1,0:T(8,128)(2,1)S(1)}, bf16[512,512]{1,0:T(8,128)(2,1)S(1)}, u32[]{:S(2)}, u32[]{:S(2)}) collective-permute-start(bf16[512,512]{1,0:T(8,128)(2,1)S(1)} %first_block.1), channel_id=1, source_target_pairs={{0,4},{12,8},{1,5},{13,9},{2,6},{14,10},{3,7},{15,11},{16,20},{28,... | collective-permute-start | bytes 1572872 | tf_op jit(solution)/shard_map/ppermute | solution.py:310
  11.9 5.5 %rest.1 = (bf16[512,512]{1,0:T(8,128)(2,1)S(1)}, bf16[512,512]{1,0:T(8,128)(2,1)S(1)}, bf16[512,512]{1,0:T(8,128)(2,1)S(1)}, bf16[512,512]{1,0:T(8,128)(2,1)S(1)}) custom-call(s32[1]{0:T(128)} %bitcast.z_ref, s32[8,512]{1,0:T(8,128)S(1)} %get-tuple-element.29.place_ref, bf16[512,2048]{1,0:T(8,128)(2,1)S(1)} %get-tuple-element.27.x_ref, bf16[2048,2048]{1,0:T(8,128)(2,1)} %w_hbm.3), custom_call_target="tpu_custom_call" | custom-call | flops 3221225472 | bytes 10485760 | tf_op jit(solution)/shard_map/rest/pallas_call | solution.py:159
  17.4 1.6 %collective-permute-start.4 = (bf16[512,512]{1,0:T(8,128)(2,1)S(1)}, bf16[512,512]{1,0:T(8,128)(2,1)S(1)}, u32[]{:S(2)}, u32[]{:S(2)}) collective-permute-start(bf16[512,512]{1,0:T(8,128)(2,1)S(1)} %get-tuple-element.37), channel_id=1, source_target_pairs={{0,4},{12,8},{1,5},{13,9},{2,6},{14,10},{3,7},{15,11},{16,20},{28,... | collective-permute-start | bytes 1572872 | tf_op jit(solution)/shard_map/ppermute | solution.py:312
  19.0 1.5 %collective-permute-done.1.refs_2_ = bf16[128,2176]{1,0:T(8,128)(2,1)S(1)} collective-permute-done((bf16[128,2176]{1,0:T(8,128)(2,1)S(1)}, bf16[128,2176]{1,0:T(8,128)(2,1)S(1)}, u32[]{:S(2)}, u32[]{:S(2)}) %collective-permute-start.1) | collective-permute-done | bytes 557088 | tf_op jit(solution)/shard_map/ppermute | solution.py:282
  20.5 1.1 %shrink_partial.2.refs_0_ = bf16[192,128]{1,0:T(8,128)(2,1)S(1)} custom-call(bf16[2048,512]{1,0:T(8,128)(2,1)S(1)} %copy-done, bf16[128,2176]{1,0:T(8,128)(2,1)S(1)} %get-tuple-element.31.refs_0_, bf16[128,2176]{1,0:T(8,128)(2,1)S(1)} %collective-permute-done.refs_1_, bf16[128,2176]{1,0:T(8,128)(2,1)S(1)} %collective-permute-done.1.refs_2_), custom_call_target="tpu_custom_call" | custom-call | flops 805306368 | bytes 3670016 | tf_op jit(solution)/shard_map/shrink_partial/pallas_call | solution.py:209
  21.5 2.5 %collective-permute-done.3 = bf16[512,512]{1,0:T(8,128)(2,1)S(1)} collective-permute-done((bf16[512,512]{1,0:T(8,128)(2,1)S(1)}, bf16[512,512]{1,0:T(8,128)(2,1)S(1)}, u32[]{:S(2)}, u32[]{:S(2)}) %collective-permute-start.3) | collective-permute-done | bytes 524320 | tf_op jit(solution)/shard_map/ppermute | solution.py:310
  24.1 0.7 %collective-permute-start.11 = (bf16[512,512]{1,0:T(8,128)(2,1)S(1)}, bf16[512,512]{1,0:T(8,128)(2,1)S(1)}, u32[]{:S(2)}, u32[]{:S(2)}) collective-permute-start(bf16[512,512]{1,0:T(8,128)(2,1)S(1)} %add_convert_fusion.2), channel_id=1, source_target_pairs={{4,8},{8,4},{5,9},{9,5},{6,10},{10,6},{7,11},{11,7},{20,24},{24,20... | collective-permute-start | bytes 1572872 | tf_op jit(solution)/shard_map/ppermute | solution.py:315
  24.8 7.0 %collective-permute-done.2.refs_1_.refs_3_ = bf16[128,2176]{1,0:T(8,128)(2,1)S(1)} collective-permute-done((bf16[128,2176]{1,0:T(8,128)(2,1)S(1)}, bf16[128,2176]{1,0:T(8,128)(2,1)S(1)}, u32[]{:S(2)}, u32[]{:S(2)}) %collective-permute-start.2) | collective-permute-done | bytes 557088 | tf_op jit(solution)/shard_map/ppermute | solution.py:282
  31.9 0.5 shrink_partial.3
  32.4 1.7 %collective-permute-start.5 = (bf16[256,128]{1,0:T(8,128)(2,1)S(1)}, bf16[256,128]{1,0:T(8,128)(2,1)S(1)}, u32[]{:S(2)}, u32[]{:S(2)}) collective-permute-start(bf16[256,128]{1,0:T(8,128)(2,1)S(1)} %shrink_partial.3), channel_id=1, source_target_pairs={{0,4},{4,0},{8,12},{12,8},{1,5},{5,1},{9,13},{13,9},{2,6},{6,2},{1... | collective-permute-start | bytes 196616 | tf_op jit(solution)/shard_map/ppermute | solution.py:282
  34.6 2.4 %collective-permute-done.5 = bf16[256,128]{1,0:T(8,128)(2,1)S(1)} collective-permute-done((bf16[256,128]{1,0:T(8,128)(2,1)S(1)}, bf16[256,128]{1,0:T(8,128)(2,1)S(1)}, u32[]{:S(2)}, u32[]{:S(2)}) %collective-permute-start.5) | collective-permute-done | bytes 65568 | tf_op jit(solution)/shard_map/ppermute | solution.py:282
  37.0 2.8 %collective-permute-start.6 = (bf16[256,128]{1,0:T(8,128)(2,1)S(1)}, bf16[256,128]{1,0:T(8,128)(2,1)S(1)}, u32[]{:S(2)}, u32[]{:S(2)}) collective-permute-start(bf16[256,128]{1,0:T(8,128)(2,1)S(1)} %add_convert_fusion.3.one_ref), channel_id=1, source_target_pairs={{0,8},{4,12},{8,0},{12,4},{1,9},{5,13},{9,1},{13,5},{2,10},{6,14},... | collective-permute-start | bytes 196616 | tf_op jit(solution)/shard_map/ppermute | solution.py:282
  39.8 0.7 %collective-permute-start.10 = (bf16[512,512]{1,0:T(8,128)(2,1)S(1)}, bf16[512,512]{1,0:T(8,128)(2,1)S(1)}, u32[]{:S(2)}, u32[]{:S(2)}) collective-permute-start(bf16[512,512]{1,0:T(8,128)(2,1)S(1)} %add_convert_fusion.1), channel_id=1, source_target_pairs={{4,8},{8,4},{5,9},{9,5},{6,10},{10,6},{7,11},{11,7},{20,24},{24,20... | collective-permute-start | bytes 1572872 | tf_op jit(solution)/shard_map/ppermute | solution.py:319
  40.6 2.6 %collective-permute-start.12 = (bf16[512,512]{1,0:T(8,128)(2,1)S(1)}, bf16[512,512]{1,0:T(8,128)(2,1)S(1)}, u32[]{:S(2)}, u32[]{:S(2)}) collective-permute-start(bf16[512,512]{1,0:T(8,128)(2,1)S(1)} %add_convert_fusion), channel_id=1, source_target_pairs={{0,4},{4,0},{8,12},{12,8},{1,5},{5,1},{9,13},{13,9},{2,6},{6,2},{1... | collective-permute-start | bytes 1572872 | tf_op jit(solution)/shard_map/ppermute | solution.py:282
  43.2 0.5 collective-permute-done.6.two_ref
  44.3 1.6 %collective-permute-start.8 = (bf16[128,512]{1,0:T(8,128)(2,1)S(1)}, bf16[128,512]{1,0:T(8,128)(2,1)S(1)}, u32[]{:S(2)}, u32[]{:S(2)}) collective-permute-start(bf16[128,512]{1,0:T(8,128)(2,1)S(1)} %get-tuple-element.41), channel_id=1, source_target_pairs={{0,2},{1,3},{2,0},{3,1},{4,6},{5,7},{6,4},{7,5},{8,10},{9,11},{10,... | collective-permute-start | bytes 393224 | tf_op jit(solution)/shard_map/ppermute | solution.py:282
  46.2 4.5 %collective-permute-done.8.refs_2_ = bf16[128,512]{1,0:T(8,128)(2,1)S(1)} collective-permute-done((bf16[128,512]{1,0:T(8,128)(2,1)S(1)}, bf16[128,512]{1,0:T(8,128)(2,1)S(1)}, u32[]{:S(2)}, u32[]{:S(2)}) %collective-permute-start.8) | collective-permute-done | bytes 131104 | tf_op jit(solution)/shard_map/ppermute | solution.py:282
  50.7 1.9 %collective-permute-done.9.refs_3_ = bf16[128,512]{1,0:T(8,128)(2,1)S(1)} collective-permute-done((bf16[128,512]{1,0:T(8,128)(2,1)S(1)}, bf16[128,512]{1,0:T(8,128)(2,1)S(1)}, u32[]{:S(2)}, u32[]{:S(2)}) %collective-permute-start.9) | collective-permute-done | bytes 131104 | tf_op jit(solution)/shard_map/ppermute | solution.py:282
  52.6 2.1 %collective-permute-done.12.refs_6_ = bf16[512,512]{1,0:T(8,128)(2,1)S(1)} collective-permute-done((bf16[512,512]{1,0:T(8,128)(2,1)S(1)}, bf16[512,512]{1,0:T(8,128)(2,1)S(1)}, u32[]{:S(2)}, u32[]{:S(2)}) %collective-permute-start.12) | collective-permute-done | bytes 524320 | tf_op jit(solution)/shard_map/ppermute | solution.py:282
  54.7 1.3 %finish.1 = bf16[512,512]{1,0:T(8,128)(2,1)} custom-call(bf16[512,512]{1,0:T(8,128)(2,1)S(1)} %get-tuple-element.30.unsort_ref, bf16[128,512]{1,0:T(8,128)(2,1)S(1)} %get-tuple-element.39.refs_0_, bf16[128,512]{1,0:T(8,128)(2,1)S(1)} %collective-permute-done.7.refs_1_, bf16[128,512]{1,0:T(8,128)(2,1)S(1)} %collective-permute-done.8.refs_2_, ...), custom_call_target="tpu_custom_call" | custom-call | flops 268435456 | bytes 3145728 | tf_op jit(solution)/shard_map/finish/pallas_call | solution.py:264
  (17 shorter events, 1.7 us)
Async XLA Ops:
  3.9 15.1 %collective-permute-start = (bf16[128,2176]{1,0:T(8,128)(2,1)S(1)}, bf16[128,2176]{1,0:T(8,128)(2,1)S(1)}, u32[]{:S(2)}, u32[]{:S(2)}) collective-permute-start(bf16[128,2176]{1,0:T(8,128)(2,1)S(1)} %get-tuple-element.32), channel_id=1, source_target_pairs={{0,1},{1,0},{2,3},{3,2},{4,5},{5,4},{6,7},{7,6},{8,9},{9,8},{10,11... | collective-permute-start | bytes 1671176 | tf_op jit(solution)/shard_map/ppermute | solution.py:282
  4.4 16.0 %collective-permute-start.1 = (bf16[128,2176]{1,0:T(8,128)(2,1)S(1)}, bf16[128,2176]{1,0:T(8,128)(2,1)S(1)}, u32[]{:S(2)}, u32[]{:S(2)}) collective-permute-start(bf16[128,2176]{1,0:T(8,128)(2,1)S(1)} %get-tuple-element.33), channel_id=1, source_target_pairs={{0,2},{1,3},{2,0},{3,1},{4,6},{5,7},{6,4},{7,5},{8,10},{9,11},{10,... | collective-permute-start | bytes 1671176 | tf_op jit(solution)/shard_map/ppermute | solution.py:282
  8.2 15.8 %collective-permute-start.3 = (bf16[512,512]{1,0:T(8,128)(2,1)S(1)}, bf16[512,512]{1,0:T(8,128)(2,1)S(1)}, u32[]{:S(2)}, u32[]{:S(2)}) collective-permute-start(bf16[512,512]{1,0:T(8,128)(2,1)S(1)} %first_block.1), channel_id=1, source_target_pairs={{0,4},{12,8},{1,5},{13,9},{2,6},{14,10},{3,7},{15,11},{16,20},{28,... | collective-permute-start | bytes 1572872 | tf_op jit(solution)/shard_map/ppermute | solution.py:310
  11.8 20.1 %collective-permute-start.2 = (bf16[128,2176]{1,0:T(8,128)(2,1)S(1)}, bf16[128,2176]{1,0:T(8,128)(2,1)S(1)}, u32[]{:S(2)}, u32[]{:S(2)}) collective-permute-start(bf16[128,2176]{1,0:T(8,128)(2,1)S(1)} %get-tuple-element.34), channel_id=1, source_target_pairs={{0,3},{1,2},{2,1},{3,0},{4,7},{5,6},{6,5},{7,4},{8,11},{9,10},{10,... | collective-permute-start | bytes 1671176 | tf_op jit(solution)/shard_map/ppermute | solution.py:282
  11.9 8.6 %copy-start = (bf16[2048,512]{1,0:T(8,128)(2,1)S(1)}, bf16[2048,512]{1,0:T(8,128)(2,1)}, u32[]{:S(2)}) copy-start(bf16[2048,512]{1,0:T(8,128)(2,1)} %down_ref.3) | copy-start | bytes 6291460
  17.4 17.1 %collective-permute-start.4 = (bf16[512,512]{1,0:T(8,128)(2,1)S(1)}, bf16[512,512]{1,0:T(8,128)(2,1)S(1)}, u32[]{:S(2)}, u32[]{:S(2)}) collective-permute-start(bf16[512,512]{1,0:T(8,128)(2,1)S(1)} %get-tuple-element.37), channel_id=1, source_target_pairs={{0,4},{12,8},{1,5},{13,9},{2,6},{14,10},{3,7},{15,11},{16,20},{28,... | collective-permute-start | bytes 1572872 | tf_op jit(solution)/shard_map/ppermute | solution.py:312
  24.1 16.4 %collective-permute-start.11 = (bf16[512,512]{1,0:T(8,128)(2,1)S(1)}, bf16[512,512]{1,0:T(8,128)(2,1)S(1)}, u32[]{:S(2)}, u32[]{:S(2)}) collective-permute-start(bf16[512,512]{1,0:T(8,128)(2,1)S(1)} %add_convert_fusion.2), channel_id=1, source_target_pairs={{4,8},{8,4},{5,9},{9,5},{6,10},{10,6},{7,11},{11,7},{20,24},{24,20... | collective-permute-start | bytes 1572872 | tf_op jit(solution)/shard_map/ppermute | solution.py:315
  32.4 11.3 %copy-start.1 = (bf16[512,512]{1,0:T(8,128)(2,1)S(1)}, bf16[512,512]{1,0:T(8,128)(2,1)}, u32[]{:S(2)}) copy-start(bf16[512,512]{1,0:T(8,128)(2,1)} %up_ref.1) | copy-start | bytes 1572868
  32.4 4.5 %collective-permute-start.5 = (bf16[256,128]{1,0:T(8,128)(2,1)S(1)}, bf16[256,128]{1,0:T(8,128)(2,1)S(1)}, u32[]{:S(2)}, u32[]{:S(2)}) collective-permute-start(bf16[256,128]{1,0:T(8,128)(2,1)S(1)} %shrink_partial.3), channel_id=1, source_target_pairs={{0,4},{4,0},{8,12},{12,8},{1,5},{5,1},{9,13},{13,9},{2,6},{6,2},{1... | collective-permute-start | bytes 196616 | tf_op jit(solution)/shard_map/ppermute | solution.py:282
  37.0 6.7 %collective-permute-start.6 = (bf16[256,128]{1,0:T(8,128)(2,1)S(1)}, bf16[256,128]{1,0:T(8,128)(2,1)S(1)}, u32[]{:S(2)}, u32[]{:S(2)}) collective-permute-start(bf16[256,128]{1,0:T(8,128)(2,1)S(1)} %add_convert_fusion.3.one_ref), channel_id=1, source_target_pairs={{0,8},{4,12},{8,0},{12,4},{1,9},{5,13},{9,1},{13,5},{2,10},{6,14},... | collective-permute-start | bytes 196616 | tf_op jit(solution)/shard_map/ppermute | solution.py:282
  39.8 12.8 %collective-permute-start.10 = (bf16[512,512]{1,0:T(8,128)(2,1)S(1)}, bf16[512,512]{1,0:T(8,128)(2,1)S(1)}, u32[]{:S(2)}, u32[]{:S(2)}) collective-permute-start(bf16[512,512]{1,0:T(8,128)(2,1)S(1)} %add_convert_fusion.1), channel_id=1, source_target_pairs={{4,8},{8,4},{5,9},{9,5},{6,10},{10,6},{7,11},{11,7},{20,24},{24,20... | collective-permute-start | bytes 1572872 | tf_op jit(solution)/shard_map/ppermute | solution.py:319
  40.6 14.1 %collective-permute-start.12 = (bf16[512,512]{1,0:T(8,128)(2,1)S(1)}, bf16[512,512]{1,0:T(8,128)(2,1)S(1)}, u32[]{:S(2)}, u32[]{:S(2)}) collective-permute-start(bf16[512,512]{1,0:T(8,128)(2,1)S(1)} %add_convert_fusion), channel_id=1, source_target_pairs={{0,4},{4,0},{8,12},{12,8},{1,5},{5,1},{9,13},{13,9},{2,6},{6,2},{1... | collective-permute-start | bytes 1572872 | tf_op jit(solution)/shard_map/ppermute | solution.py:282
  44.2 1.9 %collective-permute-start.7 = (bf16[128,512]{1,0:T(8,128)(2,1)S(1)}, bf16[128,512]{1,0:T(8,128)(2,1)S(1)}, u32[]{:S(2)}, u32[]{:S(2)}) collective-permute-start(bf16[128,512]{1,0:T(8,128)(2,1)S(1)} %get-tuple-element.40), channel_id=1, source_target_pairs={{0,1},{1,0},{2,3},{3,2},{4,5},{5,4},{6,7},{7,6},{8,9},{9,8},{10,11... | collective-permute-start | bytes 393224 | tf_op jit(solution)/shard_map/ppermute | solution.py:282
  44.3 6.4 %collective-permute-start.8 = (bf16[128,512]{1,0:T(8,128)(2,1)S(1)}, bf16[128,512]{1,0:T(8,128)(2,1)S(1)}, u32[]{:S(2)}, u32[]{:S(2)}) collective-permute-start(bf16[128,512]{1,0:T(8,128)(2,1)S(1)} %get-tuple-element.41), channel_id=1, source_target_pairs={{0,2},{1,3},{2,0},{3,1},{4,6},{5,7},{6,4},{7,5},{8,10},{9,11},{10,... | collective-permute-start | bytes 393224 | tf_op jit(solution)/shard_map/ppermute | solution.py:282
  45.8 6.7 %collective-permute-start.9 = (bf16[128,512]{1,0:T(8,128)(2,1)S(1)}, bf16[128,512]{1,0:T(8,128)(2,1)S(1)}, u32[]{:S(2)}, u32[]{:S(2)}) collective-permute-start(bf16[128,512]{1,0:T(8,128)(2,1)S(1)} %get-tuple-element.42), channel_id=1, source_target_pairs={{0,3},{1,2},{2,1},{3,0},{4,7},{5,6},{6,5},{7,4},{8,11},{9,10},{10,... | collective-permute-start | bytes 393224 | tf_op jit(solution)/shard_map/ppermute | solution.py:282

commit v5 on v4

--- a/solution.py
+++ b/solution.py
@@ -284,6 +284,7 @@
 
 EDGE = [(0, 1), (3, 2)]
 MIDDLE = [(1, 2), (2, 1)]
+ACROSS = [(1, 3), (2, 0)]
 
 
 def tp_sums(mine, *before):
@@ -312,13 +313,13 @@
         edge1 = lax.ppermute(second, "tp", EDGE)
         early = shrink_partial(down, parts[:-1])
         inner0 = both(after(first, early), edge0)
-        middle0 = lax.ppermute(inner0, "tp", MIDDLE)
+        across = lax.ppermute(inner0, "tp", ACROSS)
         mine = shrink_partial(down, [after(parts[-1], inner0)], [early])
         inner1 = both(second, edge1)
         steps, other = tp_sums(mine, inner1)
-        middle1 = lax.ppermute(after(inner1, steps[-1]), "tp", MIDDLE)
-        last = swap(both(after(third, steps[-1]), middle0), "tp", 1)
-        sums = [own, middle1, last]
+        middle1 = lax.ppermute(after(inner1, steps[-1], across), "tp", MIDDLE)
+        last = swap(after(third, steps[-1]), "tp", 1)
+        sums = [own, across, middle1, last]
     else:
         unsort = unsort_only(place, total)
         full = dot(x, weight).astype(bf16)

time: 56.2 us -> 58.8 us (1.046)
  waiting for transfers between devices: 22.8 us -> 27.3 us
  starting transfers between devices: 18.7 us -> 16.9 us
    ppermute x9, waiting for transfers between devices: 20 us -> 24.5 us  [swap(): lax.ppermute(value, axis, [(i, i ^ bit) for i in range(lax.axis_size(axis...]
    ppermute x9, starting transfers between devices: 12.2 us -> 9.7 us  [swap(): lax.ppermute(value, axis, [(i, i ^ bit) for i in range(lax.axis_size(axis...]
    ppermute x2, starting transfers between devices: 1.38 us -> 2.11 us  [the longest x1 1.42 us: shards(): across = lax.ppermute(inner0, 'tp', ACROSS)]
  transfers between devices with their start and end apart: 13 -> 13, of which waited for: 9 -> 9; matrix products, arithmetic and copies ran while one was open for 1% -> 1% of each run, Pallas kernels for 16% -> 15%
where the time goes in v5:
time: 58.8 us; the launch traced here: 58.6 us
  waiting for transfers between devices  27.3 us (46%)
  starting transfers between devices  16.9 us (29%)
  Pallas kernels  14 us (24%)
    ppermute x9, waiting for transfers between devices, swap(): lax.ppermute(value, axis, [(i, i ^ bit) for i in range(lax.axis_size(axis...  24.5 us
    ppermute x9, starting transfers between devices, swap(): lax.ppermute(value, axis, [(i, i ^ bit) for i in range(lax.axis_size(axis...  9.7 us
    pallas_call x1, Pallas kernels, rest(): pl.pallas_call(rest_body, out_shape=shapes, in_specs=[smem, vmem, vmem, h...  5.51 us
    pallas_call x1, Pallas kernels, sort_rows(): pl.pallas_call(functools.partial(sort_body, slots, capacity, holders), ou...  3.89 us
    ppermute x1, starting transfers between devices, shards(): edge0 = lax.ppermute(first, 'tp', EDGE)  3.51 us
    ppermute x1, waiting for transfers between devices, shards(): edge0 = lax.ppermute(first, 'tp', EDGE)  2.47 us
    ppermute x1, starting transfers between devices, shards(): edge1 = lax.ppermute(second, 'tp', EDGE)  1.57 us
    pallas_call x2, Pallas kernels, shrink_partial(): pl.pallas_call(functools.partial(shrink_body, kept), out_shape=jax.ShapeD...  1.57 us
  transfers between devices with their start and end apart: 13, of which 9 were waited for; matrix products, arithmetic and copies ran while one was open for 1% of the time, Pallas kernels for 15%

profile of v5, /device:TPU:0, one launch (start us, length us, event | category | flops | bytes accessed | tf_op | source)
XLA Modules:
  0.0 58.6 jit_solution(15332857701489357423)
XLA Ops:
  0.0 3.9 %sort_rows.1 = (s32[8,512]{1,0:T(8,128)S(1)}, bf16[128,2176]{1,0:T(8,128)(2,1)S(1)}, bf16[128,2176]{1,0:T(8,128)(2,1)S(1)}, bf16[128,2176]{1,0:T(8,128)(2,1)S(1)...) custom-call(s32[1]{0:T(128)} %bitcast.1.me_ref, s32[1]{0:T(128)} %bitcast.z_ref, ...), custom_call_target="tpu_custom_call" | custom-call | flops 1073741824 | bytes 4194304 | tf_op jit(solution)/shard_map/sort_rows/pallas_call | solution.py:97
  3.9 0.5 collective-permute-start
  4.4 2.6 %collective-permute-start.1 = (bf16[128,2176]{1,0:T(8,128)(2,1)S(1)}, bf16[128,2176]{1,0:T(8,128)(2,1)S(1)}, u32[]{:S(2)}, u32[]{:S(2)}) collective-permute-start(bf16[128,2176]{1,0:T(8,128)(2,1)S(1)} %get-tuple-element.33), channel_id=1, source_target_pairs={{0,2},{1,3},{2,0},{3,1},{4,6},{5,7},{6,4},{7,5},{8,10},{9,11},{10,... | collective-permute-start | bytes 1671176 | tf_op jit(solution)/shard_map/ppermute | solution.py:282
  7.0 1.3 %first_block.1 = bf16[512,512]{1,0:T(8,128)(2,1)S(1)} custom-call(bf16[512,2048]{1,0:T(8,128)(2,1)S(1)} %get-tuple-element.27.x_ref, bf16[2048,512]{1,0:T(8,128)(2,1)S(1)} %get-tuple-element.28.w_ref), custom_call_target="tpu_custom_call" | custom-call | flops 1073741824 | bytes 4194304 | tf_op jit(solution)/shard_map/first_block/pallas_call | solution.py:121
  8.2 3.5 %collective-permute-start.3 = (bf16[512,512]{1,0:T(8,128)(2,1)S(1)}, bf16[512,512]{1,0:T(8,128)(2,1)S(1)}, u32[]{:S(2)}, u32[]{:S(2)}) collective-permute-start(bf16[512,512]{1,0:T(8,128)(2,1)S(1)} %first_block.1), channel_id=1, source_target_pairs={{0,4},{12,8},{1,5},{13,9},{2,6},{14,10},{3,7},{15,11},{16,20},{28,... | collective-permute-start | bytes 1572872 | tf_op jit(solution)/shard_map/ppermute | solution.py:311
  11.9 5.5 %rest.1 = (bf16[512,512]{1,0:T(8,128)(2,1)S(1)}, bf16[512,512]{1,0:T(8,128)(2,1)S(1)}, bf16[512,512]{1,0:T(8,128)(2,1)S(1)}, bf16[512,512]{1,0:T(8,128)(2,1)S(1)}) custom-call(s32[1]{0:T(128)} %bitcast.z_ref, s32[8,512]{1,0:T(8,128)S(1)} %get-tuple-element.29.place_ref, bf16[512,2048]{1,0:T(8,128)(2,1)S(1)} %get-tuple-element.27.x_ref, bf16[2048,2048]{1,0:T(8,128)(2,1)} %w_hbm.3), custom_call_target="tpu_custom_call" | custom-call | flops 3221225472 | bytes 10485760 | tf_op jit(solution)/shard_map/rest/pallas_call | solution.py:159
  17.4 1.6 %collective-permute-start.4 = (bf16[512,512]{1,0:T(8,128)(2,1)S(1)}, bf16[512,512]{1,0:T(8,128)(2,1)S(1)}, u32[]{:S(2)}, u32[]{:S(2)}) collective-permute-start(bf16[512,512]{1,0:T(8,128)(2,1)S(1)} %get-tuple-element.37), channel_id=1, source_target_pairs={{0,4},{12,8},{1,5},{13,9},{2,6},{14,10},{3,7},{15,11},{16,20},{28,... | collective-permute-start | bytes 1572872 | tf_op jit(solution)/shard_map/ppermute | solution.py:313
  19.0 1.5 %collective-permute-done.1.refs_2_ = bf16[128,2176]{1,0:T(8,128)(2,1)S(1)} collective-permute-done((bf16[128,2176]{1,0:T(8,128)(2,1)S(1)}, bf16[128,2176]{1,0:T(8,128)(2,1)S(1)}, u32[]{:S(2)}, u32[]{:S(2)}) %collective-permute-start.1) | collective-permute-done | bytes 557088 | tf_op jit(solution)/shard_map/ppermute | solution.py:282
  20.5 1.1 %shrink_partial.2.refs_0_ = bf16[192,128]{1,0:T(8,128)(2,1)S(1)} custom-call(bf16[2048,512]{1,0:T(8,128)(2,1)S(1)} %copy-done, bf16[128,2176]{1,0:T(8,128)(2,1)S(1)} %get-tuple-element.31.refs_0_, bf16[128,2176]{1,0:T(8,128)(2,1)S(1)} %collective-permute-done.refs_1_, bf16[128,2176]{1,0:T(8,128)(2,1)S(1)} %collective-permute-done.1.refs_2_), custom_call_target="tpu_custom_call" | custom-call | flops 805306368 | bytes 3670016 | tf_op jit(solution)/shard_map/shrink_partial/pallas_call | solution.py:209
  21.5 2.5 %collective-permute-done.3 = bf16[512,512]{1,0:T(8,128)(2,1)S(1)} collective-permute-done((bf16[512,512]{1,0:T(8,128)(2,1)S(1)}, bf16[512,512]{1,0:T(8,128)(2,1)S(1)}, u32[]{:S(2)}, u32[]{:S(2)}) %collective-permute-start.3) | collective-permute-done | bytes 524320 | tf_op jit(solution)/shard_map/ppermute | solution.py:311
  24.1 1.4 %collective-permute-start.10 = (bf16[512,512]{1,0:T(8,128)(2,1)S(1)}, bf16[512,512]{1,0:T(8,128)(2,1)S(1)}, u32[]{:S(2)}, u32[]{:S(2)}) collective-permute-start(bf16[512,512]{1,0:T(8,128)(2,1)S(1)} %add_convert_fusion.1), channel_id=1, source_target_pairs={{4,12},{8,0},{5,13},{9,1},{6,14},{10,2},{7,15},{11,3},{20,28},{24,... | collective-permute-start | bytes 1572872 | tf_op jit(solution)/shard_map/ppermute | solution.py:316
  25.6 6.3 %collective-permute-done.2.refs_1_.refs_3_ = bf16[128,2176]{1,0:T(8,128)(2,1)S(1)} collective-permute-done((bf16[128,2176]{1,0:T(8,128)(2,1)S(1)}, bf16[128,2176]{1,0:T(8,128)(2,1)S(1)}, u32[]{:S(2)}, u32[]{:S(2)}) %collective-permute-start.2) | collective-permute-done | bytes 557088 | tf_op jit(solution)/shard_map/ppermute | solution.py:282
  31.9 0.5 shrink_partial.3
  32.4 1.7 %collective-permute-start.5 = (bf16[256,128]{1,0:T(8,128)(2,1)S(1)}, bf16[256,128]{1,0:T(8,128)(2,1)S(1)}, u32[]{:S(2)}, u32[]{:S(2)}) collective-permute-start(bf16[256,128]{1,0:T(8,128)(2,1)S(1)} %shrink_partial.3), channel_id=1, source_target_pairs={{0,4},{4,0},{8,12},{12,8},{1,5},{5,1},{9,13},{13,9},{2,6},{6,2},{1... | collective-permute-start | bytes 196616 | tf_op jit(solution)/shard_map/ppermute | solution.py:282
  34.6 6.5 %collective-permute-done.5 = bf16[256,128]{1,0:T(8,128)(2,1)S(1)} collective-permute-done((bf16[256,128]{1,0:T(8,128)(2,1)S(1)}, bf16[256,128]{1,0:T(8,128)(2,1)S(1)}, u32[]{:S(2)}, u32[]{:S(2)}) %collective-permute-start.5) | collective-permute-done | bytes 65568 | tf_op jit(solution)/shard_map/ppermute | solution.py:282
  41.5 2.4 %collective-permute-start.12 = (bf16[512,512]{1,0:T(8,128)(2,1)S(1)}, bf16[512,512]{1,0:T(8,128)(2,1)S(1)}, u32[]{:S(2)}, u32[]{:S(2)}) collective-permute-start(bf16[512,512]{1,0:T(8,128)(2,1)S(1)} %get-tuple-element.46), channel_id=1, source_target_pairs={{0,4},{4,0},{8,12},{12,8},{1,5},{5,1},{9,13},{13,9},{2,6},{6,2},{1... | collective-permute-start | bytes 1572872 | tf_op jit(solution)/shard_map/ppermute | solution.py:282
  44.0 0.7 %collective-permute-start.11 = (bf16[512,512]{1,0:T(8,128)(2,1)S(1)}, bf16[512,512]{1,0:T(8,128)(2,1)S(1)}, u32[]{:S(2)}, u32[]{:S(2)}) collective-permute-start(bf16[512,512]{1,0:T(8,128)(2,1)S(1)} %add_convert_fusion), channel_id=1, source_target_pairs={{4,8},{8,4},{5,9},{9,5},{6,10},{10,6},{7,11},{11,7},{20,24},{24,20... | collective-permute-start | bytes 1572872 | tf_op jit(solution)/shard_map/ppermute | solution.py:320
  44.7 2.6 %collective-permute-done.6.two_ref = bf16[256,128]{1,0:T(8,128)(2,1)S(1)} collective-permute-done((bf16[256,128]{1,0:T(8,128)(2,1)S(1)}, bf16[256,128]{1,0:T(8,128)(2,1)S(1)}, u32[]{:S(2)}, u32[]{:S(2)}) %collective-permute-start.6) | collective-permute-done | bytes 65568 | tf_op jit(solution)/shard_map/ppermute | solution.py:282
  47.8 1.0 %collective-permute-start.8 = (bf16[128,512]{1,0:T(8,128)(2,1)S(1)}, bf16[128,512]{1,0:T(8,128)(2,1)S(1)}, u32[]{:S(2)}, u32[]{:S(2)}) collective-permute-start(bf16[128,512]{1,0:T(8,128)(2,1)S(1)} %get-tuple-element.41), channel_id=1, source_target_pairs={{0,2},{1,3},{2,0},{3,1},{4,6},{5,7},{6,4},{7,5},{8,10},{9,11},{10,... | collective-permute-start | bytes 393224 | tf_op jit(solution)/shard_map/ppermute | solution.py:282
  48.9 0.9 %collective-permute-start.9 = (bf16[128,512]{1,0:T(8,128)(2,1)S(1)}, bf16[128,512]{1,0:T(8,128)(2,1)S(1)}, u32[]{:S(2)}, u32[]{:S(2)}) collective-permute-start(bf16[128,512]{1,0:T(8,128)(2,1)S(1)} %get-tuple-element.42), channel_id=1, source_target_pairs={{0,3},{1,2},{2,1},{3,0},{4,7},{5,6},{6,5},{7,4},{8,11},{9,10},{10,... | collective-permute-start | bytes 393224 | tf_op jit(solution)/shard_map/ppermute | solution.py:282
  49.7 4.5 %collective-permute-done.8.refs_2_ = bf16[128,512]{1,0:T(8,128)(2,1)S(1)} collective-permute-done((bf16[128,512]{1,0:T(8,128)(2,1)S(1)}, bf16[128,512]{1,0:T(8,128)(2,1)S(1)}, u32[]{:S(2)}, u32[]{:S(2)}) %collective-permute-start.8) | collective-permute-done | bytes 131104 | tf_op jit(solution)/shard_map/ppermute | solution.py:282
  54.2 1.9 %collective-permute-done.9.refs_3_ = bf16[128,512]{1,0:T(8,128)(2,1)S(1)} collective-permute-done((bf16[128,512]{1,0:T(8,128)(2,1)S(1)}, bf16[128,512]{1,0:T(8,128)(2,1)S(1)}, u32[]{:S(2)}, u32[]{:S(2)}) %collective-permute-start.9) | collective-permute-done | bytes 131104 | tf_op jit(solution)/shard_map/ppermute | solution.py:282
  56.1 1.2 %collective-permute-done.12.refs_7_ = bf16[512,512]{1,0:T(8,128)(2,1)S(1)} collective-permute-done((bf16[512,512]{1,0:T(8,128)(2,1)S(1)}, bf16[512,512]{1,0:T(8,128)(2,1)S(1)}, u32[]{:S(2)}, u32[]{:S(2)}) %collective-permute-start.12) | collective-permute-done | bytes 524320 | tf_op jit(solution)/shard_map/ppermute | solution.py:282
  57.3 1.3 %finish.1 = bf16[512,512]{1,0:T(8,128)(2,1)} custom-call(bf16[512,512]{1,0:T(8,128)(2,1)S(1)} %get-tuple-element.30.unsort_ref, bf16[128,512]{1,0:T(8,128)(2,1)S(1)} %get-tuple-element.39.refs_0_, bf16[128,512]{1,0:T(8,128)(2,1)S(1)} %collective-permute-done.7.refs_1_, bf16[128,512]{1,0:T(8,128)(2,1)S(1)} %collective-permute-done.8.refs_2_, ...), custom_call_target="tpu_custom_call" | custom-call | flops 268435456 | bytes 3145728 | tf_op jit(solution)/shard_map/finish/pallas_call | solution.py:264
  (16 shorter events, 1.7 us)
Async XLA Ops:
  3.9 15.1 %collective-permute-start = (bf16[128,2176]{1,0:T(8,128)(2,1)S(1)}, bf16[128,2176]{1,0:T(8,128)(2,1)S(1)}, u32[]{:S(2)}, u32[]{:S(2)}) collective-permute-start(bf16[128,2176]{1,0:T(8,128)(2,1)S(1)} %get-tuple-element.32), channel_id=1, source_target_pairs={{0,1},{1,0},{2,3},{3,2},{4,5},{5,4},{6,7},{7,6},{8,9},{9,8},{10,11... | collective-permute-start | bytes 1671176 | tf_op jit(solution)/shard_map/ppermute | solution.py:282
  4.4 16.0 %collective-permute-start.1 = (bf16[128,2176]{1,0:T(8,128)(2,1)S(1)}, bf16[128,2176]{1,0:T(8,128)(2,1)S(1)}, u32[]{:S(2)}, u32[]{:S(2)}) collective-permute-start(bf16[128,2176]{1,0:T(8,128)(2,1)S(1)} %get-tuple-element.33), channel_id=1, source_target_pairs={{0,2},{1,3},{2,0},{3,1},{4,6},{5,7},{6,4},{7,5},{8,10},{9,11},{10,... | collective-permute-start | bytes 1671176 | tf_op jit(solution)/shard_map/ppermute | solution.py:282
  8.2 15.8 %collective-permute-start.3 = (bf16[512,512]{1,0:T(8,128)(2,1)S(1)}, bf16[512,512]{1,0:T(8,128)(2,1)S(1)}, u32[]{:S(2)}, u32[]{:S(2)}) collective-permute-start(bf16[512,512]{1,0:T(8,128)(2,1)S(1)} %first_block.1), channel_id=1, source_target_pairs={{0,4},{12,8},{1,5},{13,9},{2,6},{14,10},{3,7},{15,11},{16,20},{28,... | collective-permute-start | bytes 1572872 | tf_op jit(solution)/shard_map/ppermute | solution.py:311
  11.8 20.1 %collective-permute-start.2 = (bf16[128,2176]{1,0:T(8,128)(2,1)S(1)}, bf16[128,2176]{1,0:T(8,128)(2,1)S(1)}, u32[]{:S(2)}, u32[]{:S(2)}) collective-permute-start(bf16[128,2176]{1,0:T(8,128)(2,1)S(1)} %get-tuple-element.34), channel_id=1, source_target_pairs={{0,3},{1,2},{2,1},{3,0},{4,7},{5,6},{6,5},{7,4},{8,11},{9,10},{10,... | collective-permute-start | bytes 1671176 | tf_op jit(solution)/shard_map/ppermute | solution.py:282
  11.9 8.6 %copy-start = (bf16[2048,512]{1,0:T(8,128)(2,1)S(1)}, bf16[2048,512]{1,0:T(8,128)(2,1)}, u32[]{:S(2)}) copy-start(bf16[2048,512]{1,0:T(8,128)(2,1)} %down_ref.3) | copy-start | bytes 6291460
  17.4 17.1 %collective-permute-start.4 = (bf16[512,512]{1,0:T(8,128)(2,1)S(1)}, bf16[512,512]{1,0:T(8,128)(2,1)S(1)}, u32[]{:S(2)}, u32[]{:S(2)}) collective-permute-start(bf16[512,512]{1,0:T(8,128)(2,1)S(1)} %get-tuple-element.37), channel_id=1, source_target_pairs={{0,4},{12,8},{1,5},{13,9},{2,6},{14,10},{3,7},{15,11},{16,20},{28,... | collective-permute-start | bytes 1572872 | tf_op jit(solution)/shard_map/ppermute | solution.py:313
  24.1 23.1 %copy-start.1 = (bf16[512,512]{1,0:T(8,128)(2,1)S(1)}, bf16[512,512]{1,0:T(8,128)(2,1)}, u32[]{:S(2)}) copy-start(bf16[512,512]{1,0:T(8,128)(2,1)} %up_ref.1) | copy-start | bytes 1572868
  24.1 19.8 %collective-permute-start.10 = (bf16[512,512]{1,0:T(8,128)(2,1)S(1)}, bf16[512,512]{1,0:T(8,128)(2,1)S(1)}, u32[]{:S(2)}, u32[]{:S(2)}) collective-permute-start(bf16[512,512]{1,0:T(8,128)(2,1)S(1)} %add_convert_fusion.1), channel_id=1, source_target_pairs={{4,12},{8,0},{5,13},{9,1},{6,14},{10,2},{7,15},{11,3},{20,28},{24,... | collective-permute-start | bytes 1572872 | tf_op jit(solution)/shard_map/ppermute | solution.py:316
  32.4 8.7 %collective-permute-start.5 = (bf16[256,128]{1,0:T(8,128)(2,1)S(1)}, bf16[256,128]{1,0:T(8,128)(2,1)S(1)}, u32[]{:S(2)}, u32[]{:S(2)}) collective-permute-start(bf16[256,128]{1,0:T(8,128)(2,1)S(1)} %shrink_partial.3), channel_id=1, source_target_pairs={{0,4},{4,0},{8,12},{12,8},{1,5},{5,1},{9,13},{13,9},{2,6},{6,2},{1... | collective-permute-start | bytes 196616 | tf_op jit(solution)/shard_map/ppermute | solution.py:282
  41.1 6.2 %collective-permute-start.6 = (bf16[256,128]{1,0:T(8,128)(2,1)S(1)}, bf16[256,128]{1,0:T(8,128)(2,1)S(1)}, u32[]{:S(2)}, u32[]{:S(2)}) collective-permute-start(bf16[256,128]{1,0:T(8,128)(2,1)S(1)} %add_convert_fusion.2.one_ref), channel_id=1, source_target_pairs={{0,8},{4,12},{8,0},{12,4},{1,9},{5,13},{9,1},{13,5},{2,10},{6,14},... | collective-permute-start | bytes 196616 | tf_op jit(solution)/shard_map/ppermute | solution.py:282
  41.5 15.7 %collective-permute-start.12 = (bf16[512,512]{1,0:T(8,128)(2,1)S(1)}, bf16[512,512]{1,0:T(8,128)(2,1)S(1)}, u32[]{:S(2)}, u32[]{:S(2)}) collective-permute-start(bf16[512,512]{1,0:T(8,128)(2,1)S(1)} %get-tuple-element.46), channel_id=1, source_target_pairs={{0,4},{4,0},{8,12},{12,8},{1,5},{5,1},{9,13},{13,9},{2,6},{6,2},{1... | collective-permute-start | bytes 1572872 | tf_op jit(solution)/shard_map/ppermute | solution.py:282
  44.0 13.3 %collective-permute-start.11 = (bf16[512,512]{1,0:T(8,128)(2,1)S(1)}, bf16[512,512]{1,0:T(8,128)(2,1)S(1)}, u32[]{:S(2)}, u32[]{:S(2)}) collective-permute-start(bf16[512,512]{1,0:T(8,128)(2,1)S(1)} %add_convert_fusion), channel_id=1, source_target_pairs={{4,8},{8,4},{5,9},{9,5},{6,10},{10,6},{7,11},{11,7},{20,24},{24,20... | collective-permute-start | bytes 1572872 | tf_op jit(solution)/shard_map/ppermute | solution.py:320
  47.8 1.9 %collective-permute-start.7 = (bf16[128,512]{1,0:T(8,128)(2,1)S(1)}, bf16[128,512]{1,0:T(8,128)(2,1)S(1)}, u32[]{:S(2)}, u32[]{:S(2)}) collective-permute-start(bf16[128,512]{1,0:T(8,128)(2,1)S(1)} %get-tuple-element.40), channel_id=1, source_target_pairs={{0,1},{1,0},{2,3},{3,2},{4,5},{5,4},{6,7},{7,6},{8,9},{9,8},{10,11... | collective-permute-start | bytes 393224 | tf_op jit(solution)/shard_map/ppermute | solution.py:282
  47.8 6.4 %collective-permute-start.8 = (bf16[128,512]{1,0:T(8,128)(2,1)S(1)}, bf16[128,512]{1,0:T(8,128)(2,1)S(1)}, u32[]{:S(2)}, u32[]{:S(2)}) collective-permute-start(bf16[128,512]{1,0:T(8,128)(2,1)S(1)} %get-tuple-element.41), channel_id=1, source_target_pairs={{0,2},{1,3},{2,0},{3,1},{4,6},{5,7},{6,4},{7,5},{8,10},{9,11},{10,... | collective-permute-start | bytes 393224 | tf_op jit(solution)/shard_map/ppermute | solution.py:282
  48.9 7.3 %collective-permute-start.9 = (bf16[128,512]{1,0:T(8,128)(2,1)S(1)}, bf16[128,512]{1,0:T(8,128)(2,1)S(1)}, u32[]{:S(2)}, u32[]{:S(2)}) collective-permute-start(bf16[128,512]{1,0:T(8,128)(2,1)S(1)} %get-tuple-element.42), channel_id=1, source_target_pairs={{0,3},{1,2},{2,1},{3,0},{4,7},{5,6},{6,5},{7,4},{8,11},{9,10},{10,... | collective-permute-start | bytes 393224 | tf_op jit(solution)/shard_map/ppermute | solution.py:282

commit v6 on v5

--- a/solution.py
+++ b/solution.py
@@ -112,15 +112,17 @@
     )(me.reshape(1), z.reshape(1), in_hbm(ids), in_hbm(table), in_hbm(x), in_hbm(weight))
 
 
-def first_body(x_ref, w_ref, out):
-    out[...] = dot(x_ref[...], w_ref[...]).astype(bf16)
+def first_body(x_ref, w_ref, *outs):
+    half = outs[0].shape[0]
+    for k, out in enumerate(outs):
+        out[...] = dot(x_ref[k * half:(k + 1) * half, :], w_ref[...]).astype(bf16)
 
 
 def first_block(x, w):
     (rows, features), width = x.shape, w.shape[1]
     return pl.pallas_call(
         first_body,
-        out_shape=jax.ShapeDtypeStruct((rows, width), bf16),
+        out_shape=[jax.ShapeDtypeStruct((rows // 2, width), bf16)] * 2,
         compiler_params=params(),
         cost_estimate=cost(2 * rows * features * width, 2 * features * (rows + width)),
         name="first_block",
@@ -253,9 +255,15 @@
 
 def finish_body(count, unsort_ref, *refs):
     deltas, sums, out = refs[:count], refs[count:-1], refs[-1]
-    base = sums[0][...].astype(f32)
-    for term in sums[1:]:
-        base += term[...].astype(f32)
+    rows = out.shape[0]
+    base = None
+    at = 0
+    while at < len(sums):
+        if sums[at].shape[0] == rows:
+            term, at = sums[at][...].astype(f32), at + 1
+        else:
+            term, at = jnp.concatenate([sums[at][...], sums[at + 1][...]], axis=0).astype(f32), at + 2
+        base = term if base is None else base + term
     out[...] = (base + dot(unsort_ref[...], jnp.concatenate([d[...] for d in deltas], axis=0))).astype(bf16)
 
 
@@ -308,18 +316,20 @@
     parts = [send[0]] + [swap(send[j], "ad", j) for j in range(1, holders)]
     if lax.axis_size("tp") == 4:
         first = first_block(x, w)
-        edge0 = lax.ppermute(first, "tp", EDGE)
-        second, third, own, unsort = rest(z, after(place, first), x, weight, width, total)
+        edge0 = [lax.ppermute(f, "tp", EDGE) for f in first]
+        second, third, own, unsort = rest(z, after(place, *first), x, weight, width, total)
         edge1 = lax.ppermute(second, "tp", EDGE)
+        inner0 = [both(first[0], edge0[0])]
+        parts[1] = after(parts[1], *inner0)
         early = shrink_partial(down, parts[:-1])
-        inner0 = both(after(first, early), edge0)
-        across = lax.ppermute(inner0, "tp", ACROSS)
-        mine = shrink_partial(down, [after(parts[-1], inner0)], [early])
+        inner0.append(both(after(first[1], early), edge0[1]))
+        across = [lax.ppermute(i, "tp", ACROSS) for i in inner0]
+        mine = shrink_partial(down, [after(parts[-1], *inner0)], [early])
         inner1 = both(second, edge1)
-        steps, other = tp_sums(mine, inner1)
-        middle1 = lax.ppermute(after(inner1, steps[-1], across), "tp", MIDDLE)
+        steps, other = tp_sums(mine, inner1, *across)
+        middle1 = lax.ppermute(after(inner1, steps[-1]), "tp", MIDDLE)
         last = swap(after(third, steps[-1]), "tp", 1)
-        sums = [own, across, middle1, last]
+        sums = [own, *across, middle1, last]
     else:
         unsort = unsort_only(place, total)
         full = dot(x, weight).astype(bf16)

time: 58.8 us -> 58 us (0.986)
  waiting for transfers between devices: 27.3 us -> 23.7 us
  starting transfers between devices: 16.9 us -> 19.6 us
    ppermute x9, waiting for transfers between devices: 24.5 us -> 20.5 us  [swap(): lax.ppermute(value, axis, [(i, i ^ bit) for i in range(lax.axis_size(axis...]
    ppermute x3 -> x5, starting transfers between devices: 5.62 us -> 8.2 us  [the longest x2 4.8 us: shards(): edge0 = [lax.ppermute(f, 'tp', EDGE) for f in first]]
    ppermute x3 -> x5, waiting for transfers between devices: 2.48 us -> 3.23 us  [the longest x2 1.74 us: shards(): across = [lax.ppermute(i, 'tp', ACROSS) for i in inner0]]
  transfers between devices with their start and end apart: 13 -> 15, of which waited for: 9 -> 8; matrix products, arithmetic and copies ran while one was open for 1% -> 0% of each run, Pallas kernels for 15% -> 15%
where the time goes in v6:
time: 58 us; the launch traced here: 57.8 us
  waiting for transfers between devices  23.7 us (41%)
  starting transfers between devices  19.6 us (34%)
  Pallas kernels  14.1 us (24%)
    ppermute x9, waiting for transfers between devices, swap(): lax.ppermute(value, axis, [(i, i ^ bit) for i in range(lax.axis_size(axis...  20.5 us
    ppermute x9, starting transfers between devices, swap(): lax.ppermute(value, axis, [(i, i ^ bit) for i in range(lax.axis_size(axis...  10 us
    pallas_call x1, Pallas kernels, rest(): pl.pallas_call(rest_body, out_shape=shapes, in_specs=[smem, vmem, vmem, h...  5.51 us
    ppermute x2, starting transfers between devices, shards(): edge0 = [lax.ppermute(f, 'tp', EDGE) for f in first]  4.8 us
    pallas_call x1, Pallas kernels, sort_rows(): pl.pallas_call(functools.partial(sort_body, slots, capacity, holders), ou...  3.89 us
    ppermute x2, starting transfers between devices, shards(): across = [lax.ppermute(i, 'tp', ACROSS) for i in inner0]  2.72 us
    ppermute x2, waiting for transfers between devices, shards(): across = [lax.ppermute(i, 'tp', ACROSS) for i in inner0]  1.74 us
    pallas_call x2, Pallas kernels, shrink_partial(): pl.pallas_call(functools.partial(shrink_body, kept), out_shape=jax.ShapeD...  1.59 us
  transfers between devices with their start and end apart: 15, of which 8 were waited for; matrix products, arithmetic and copies ran while one was open for 0% of the time, Pallas kernels for 15%

profile of v6, /device:TPU:0, one launch (start us, length us, event | category | flops | bytes accessed | tf_op | source)
XLA Modules:
  0.0 57.8 jit_solution(2606389823776436562)
XLA Ops:
  0.0 3.9 %sort_rows.1 = (s32[8,512]{1,0:T(8,128)S(1)}, bf16[128,2176]{1,0:T(8,128)(2,1)S(1)}, bf16[128,2176]{1,0:T(8,128)(2,1)S(1)}, bf16[128,2176]{1,0:T(8,128)(2,1)S(1)...) custom-call(s32[1]{0:T(128)} %bitcast.1.me_ref, s32[1]{0:T(128)} %bitcast.z_ref, ...), custom_call_target="tpu_custom_call" | custom-call | flops 1073741824 | bytes 4194304 | tf_op jit(solution)/shard_map/sort_rows/pallas_call | solution.py:97
  3.9 0.5 collective-permute-start
  4.4 2.6 %collective-permute-start.2 = (bf16[128,2176]{1,0:T(8,128)(2,1)S(1)}, bf16[128,2176]{1,0:T(8,128)(2,1)S(1)}, u32[]{:S(2)}, u32[]{:S(2)}) collective-permute-start(bf16[128,2176]{1,0:T(8,128)(2,1)S(1)} %get-tuple-element.39), channel_id=1, source_target_pairs={{0,2},{1,3},{2,0},{3,1},{4,6},{5,7},{6,4},{7,5},{8,10},{9,11},{10,... | collective-permute-start | bytes 1671176 | tf_op jit(solution)/shard_map/ppermute | solution.py:290
  7.0 1.2 %first_block.1 = (bf16[256,512]{1,0:T(8,128)(2,1)S(1)}, bf16[256,512]{1,0:T(8,128)(2,1)S(1)}) custom-call(bf16[512,2048]{1,0:T(8,128)(2,1)S(1)} %get-tuple-element.30.x_ref, bf16[2048,512]{1,0:T(8,128)(2,1)S(1)} %get-tuple-element.31.w_ref), custom_call_target="tpu_custom_call" | custom-call | flops 1073741824 | bytes 4194304 | tf_op jit(solution)/shard_map/first_block/pallas_call | solution.py:123
  8.2 3.5 %collective-permute-start.1 = (bf16[256,512]{1,0:T(8,128)(2,1)S(1)}, bf16[256,512]{1,0:T(8,128)(2,1)S(1)}, u32[]{:S(2)}, u32[]{:S(2)}) collective-permute-start(bf16[256,512]{1,0:T(8,128)(2,1)S(1)} %get-tuple-element.32), channel_id=1, source_target_pairs={{0,4},{12,8},{1,5},{13,9},{2,6},{14,10},{3,7},{15,11},{16,20},{28,... | collective-permute-start | bytes 786440 | tf_op jit(solution)/shard_map/ppermute | solution.py:319
  11.7 1.3 %collective-permute-start.4 = (bf16[256,512]{1,0:T(8,128)(2,1)S(1)}, bf16[256,512]{1,0:T(8,128)(2,1)S(1)}, u32[]{:S(2)}, u32[]{:S(2)}) collective-permute-start(bf16[256,512]{1,0:T(8,128)(2,1)S(1)} %get-tuple-element.41), channel_id=1, source_target_pairs={{0,4},{12,8},{1,5},{13,9},{2,6},{14,10},{3,7},{15,11},{16,20},{28,... | collective-permute-start | bytes 786440 | tf_op jit(solution)/shard_map/ppermute | solution.py:319
  13.1 5.5 %rest.1 = (bf16[512,512]{1,0:T(8,128)(2,1)S(1)}, bf16[512,512]{1,0:T(8,128)(2,1)S(1)}, bf16[512,512]{1,0:T(8,128)(2,1)S(1)}, bf16[512,512]{1,0:T(8,128)(2,1)S(1)}) custom-call(s32[1]{0:T(128)} %bitcast.z_ref, s32[8,512]{1,0:T(8,128)S(1)} %get-tuple-element.34.place_ref, bf16[512,2048]{1,0:T(8,128)(2,1)S(1)} %get-tuple-element.30.x_ref, bf16[2048,2048]{1,0:T(8,128)(2,1)} %w_hbm.3), custom_call_target="tpu_custom_call" | custom-call | flops 3221225472 | bytes 10485760 | tf_op jit(solution)/shard_map/rest/pallas_call | solution.py:161
  18.6 1.3 %collective-permute-start.5 = (bf16[512,512]{1,0:T(8,128)(2,1)S(1)}, bf16[512,512]{1,0:T(8,128)(2,1)S(1)}, u32[]{:S(2)}, u32[]{:S(2)}) collective-permute-start(bf16[512,512]{1,0:T(8,128)(2,1)S(1)} %get-tuple-element.43), channel_id=1, source_target_pairs={{0,4},{12,8},{1,5},{13,9},{2,6},{14,10},{3,7},{15,11},{16,20},{28,... | collective-permute-start | bytes 1572872 | tf_op jit(solution)/shard_map/ppermute | solution.py:321
  20.1 1.3 %collective-permute-start.6 = (bf16[256,512]{1,0:T(8,128)(2,1)S(1)}, bf16[256,512]{1,0:T(8,128)(2,1)S(1)}, u32[]{:S(2)}, u32[]{:S(2)}) collective-permute-start(bf16[256,512]{1,0:T(8,128)(2,1)S(1)} %add_convert_fusion.2), channel_id=1, source_target_pairs={{4,12},{8,0},{5,13},{9,1},{6,14},{10,2},{7,15},{11,3},{20,28},{24,... | collective-permute-start | bytes 786440 | tf_op jit(solution)/shard_map/ppermute | solution.py:326
  21.4 1.1 %shrink_partial.2.refs_0_ = bf16[192,128]{1,0:T(8,128)(2,1)S(1)} custom-call(bf16[2048,512]{1,0:T(8,128)(2,1)S(1)} %copy-done, bf16[128,2176]{1,0:T(8,128)(2,1)S(1)} %get-tuple-element.36.refs_0_, bf16[128,2176]{1,0:T(8,128)(2,1)S(1)} %collective-permute-done.refs_1_, bf16[128,2176]{1,0:T(8,128)(2,1)S(1)} %collective-permute-done.2.refs_2_), custom_call_target="tpu_custom_call" | custom-call | flops 805306368 | bytes 3670016 | tf_op jit(solution)/shard_map/shrink_partial/pallas_call | solution.py:211
  22.5 1.5 %collective-permute-done.4 = bf16[256,512]{1,0:T(8,128)(2,1)S(1)} collective-permute-done((bf16[256,512]{1,0:T(8,128)(2,1)S(1)}, bf16[256,512]{1,0:T(8,128)(2,1)S(1)}, u32[]{:S(2)}, u32[]{:S(2)}) %collective-permute-start.4) | collective-permute-done | bytes 262176 | tf_op jit(solution)/shard_map/ppermute | solution.py:319
  24.1 1.4 %collective-permute-start.7 = (bf16[256,512]{1,0:T(8,128)(2,1)S(1)}, bf16[256,512]{1,0:T(8,128)(2,1)S(1)}, u32[]{:S(2)}, u32[]{:S(2)}) collective-permute-start(bf16[256,512]{1,0:T(8,128)(2,1)S(1)} %add_convert_fusion.1), channel_id=1, source_target_pairs={{4,12},{8,0},{5,13},{9,1},{6,14},{10,2},{7,15},{11,3},{20,28},{24,... | collective-permute-start | bytes 786440 | tf_op jit(solution)/shard_map/ppermute | solution.py:326
  25.5 9.3 %collective-permute-done.3.refs_1_.refs_3_ = bf16[128,2176]{1,0:T(8,128)(2,1)S(1)} collective-permute-done((bf16[128,2176]{1,0:T(8,128)(2,1)S(1)}, bf16[128,2176]{1,0:T(8,128)(2,1)S(1)}, u32[]{:S(2)}, u32[]{:S(2)}) %collective-permute-start.3) | collective-permute-done | bytes 557088 | tf_op jit(solution)/shard_map/ppermute | solution.py:290
  35.6 1.7 %collective-permute-done.7.refs_6_ = bf16[256,512]{1,0:T(8,128)(2,1)S(1)} collective-permute-done((bf16[256,512]{1,0:T(8,128)(2,1)S(1)}, bf16[256,512]{1,0:T(8,128)(2,1)S(1)}, u32[]{:S(2)}, u32[]{:S(2)}) %collective-permute-start.7) | collective-permute-done | bytes 262176 | tf_op jit(solution)/shard_map/ppermute | solution.py:326
  37.3 2.3 %collective-permute-done.8 = bf16[256,128]{1,0:T(8,128)(2,1)S(1)} collective-permute-done((bf16[256,128]{1,0:T(8,128)(2,1)S(1)}, bf16[256,128]{1,0:T(8,128)(2,1)S(1)}, u32[]{:S(2)}, u32[]{:S(2)}) %collective-permute-start.8) | collective-permute-done | bytes 65568 | tf_op jit(solution)/shard_map/ppermute | solution.py:290
  39.7 1.3 %collective-permute-start.9 = (bf16[256,128]{1,0:T(8,128)(2,1)S(1)}, bf16[256,128]{1,0:T(8,128)(2,1)S(1)}, u32[]{:S(2)}, u32[]{:S(2)}) collective-permute-start(bf16[256,128]{1,0:T(8,128)(2,1)S(1)} %add_convert_fusion.3.one_ref), channel_id=1, source_target_pairs={{0,8},{4,12},{8,0},{12,4},{1,9},{5,13},{9,1},{13,5},{2,10},{6,14},... | collective-permute-start | bytes 196616 | tf_op jit(solution)/shard_map/ppermute | solution.py:290
  41.0 0.7 %collective-permute-start.13 = (bf16[512,512]{1,0:T(8,128)(2,1)S(1)}, bf16[512,512]{1,0:T(8,128)(2,1)S(1)}, u32[]{:S(2)}, u32[]{:S(2)}) collective-permute-start(bf16[512,512]{1,0:T(8,128)(2,1)S(1)} %add_convert_fusion), channel_id=1, source_target_pairs={{4,8},{8,4},{5,9},{9,5},{6,10},{10,6},{7,11},{11,7},{20,24},{24,20... | collective-permute-start | bytes 1572872 | tf_op jit(solution)/shard_map/ppermute | solution.py:330
  41.7 3.5 %collective-permute-start.14 = (bf16[512,512]{1,0:T(8,128)(2,1)S(1)}, bf16[512,512]{1,0:T(8,128)(2,1)S(1)}, u32[]{:S(2)}, u32[]{:S(2)}) collective-permute-start(bf16[512,512]{1,0:T(8,128)(2,1)S(1)} %get-tuple-element.52), channel_id=1, source_target_pairs={{0,4},{4,0},{8,12},{12,8},{1,5},{5,1},{9,13},{13,9},{2,6},{6,2},{1... | collective-permute-start | bytes 1572872 | tf_op jit(solution)/shard_map/ppermute | solution.py:290
  46.0 1.0 %collective-permute-start.11 = (bf16[128,512]{1,0:T(8,128)(2,1)S(1)}, bf16[128,512]{1,0:T(8,128)(2,1)S(1)}, u32[]{:S(2)}, u32[]{:S(2)}) collective-permute-start(bf16[128,512]{1,0:T(8,128)(2,1)S(1)} %get-tuple-element.47), channel_id=1, source_target_pairs={{0,2},{1,3},{2,0},{3,1},{4,6},{5,7},{6,4},{7,5},{8,10},{9,11},{10,... | collective-permute-start | bytes 393224 | tf_op jit(solution)/shard_map/ppermute | solution.py:290
  47.0 0.9 %collective-permute-start.12 = (bf16[128,512]{1,0:T(8,128)(2,1)S(1)}, bf16[128,512]{1,0:T(8,128)(2,1)S(1)}, u32[]{:S(2)}, u32[]{:S(2)}) collective-permute-start(bf16[128,512]{1,0:T(8,128)(2,1)S(1)} %get-tuple-element.48), channel_id=1, source_target_pairs={{0,3},{1,2},{2,1},{3,0},{4,7},{5,6},{6,5},{7,4},{8,11},{9,10},{10,... | collective-permute-start | bytes 393224 | tf_op jit(solution)/shard_map/ppermute | solution.py:290
  47.8 4.5 %collective-permute-done.11.refs_2_ = bf16[128,512]{1,0:T(8,128)(2,1)S(1)} collective-permute-done((bf16[128,512]{1,0:T(8,128)(2,1)S(1)}, bf16[128,512]{1,0:T(8,128)(2,1)S(1)}, u32[]{:S(2)}, u32[]{:S(2)}) %collective-permute-start.11) | collective-permute-done | bytes 131104 | tf_op jit(solution)/shard_map/ppermute | solution.py:290
  52.3 1.9 %collective-permute-done.12.refs_3_ = bf16[128,512]{1,0:T(8,128)(2,1)S(1)} collective-permute-done((bf16[128,512]{1,0:T(8,128)(2,1)S(1)}, bf16[128,512]{1,0:T(8,128)(2,1)S(1)}, u32[]{:S(2)}, u32[]{:S(2)}) %collective-permute-start.12) | collective-permute-done | bytes 131104 | tf_op jit(solution)/shard_map/ppermute | solution.py:290
  54.2 2.2 %collective-permute-done.14.refs_8_ = bf16[512,512]{1,0:T(8,128)(2,1)S(1)} collective-permute-done((bf16[512,512]{1,0:T(8,128)(2,1)S(1)}, bf16[512,512]{1,0:T(8,128)(2,1)S(1)}, u32[]{:S(2)}, u32[]{:S(2)}) %collective-permute-start.14) | collective-permute-done | bytes 524320 | tf_op jit(solution)/shard_map/ppermute | solution.py:290
  56.5 1.3 %finish.1 = bf16[512,512]{1,0:T(8,128)(2,1)} custom-call(bf16[512,512]{1,0:T(8,128)(2,1)S(1)} %get-tuple-element.35.unsort_ref, bf16[128,512]{1,0:T(8,128)(2,1)S(1)} %get-tuple-element.45.refs_0_, bf16[128,512]{1,0:T(8,128)(2,1)S(1)} %collective-permute-done.10.refs_1_, bf16[128,512]{1,0:T(8,128)(2,1)S(1)} %collective-permute-done.11.refs_2_, ...), custom_call_target="tpu_custom_call" | custom-call | flops 268435456 | bytes 3145728 | tf_op jit(solution)/shard_map/finish/pallas_call | solution.py:272
  (21 shorter events, 1.7 us)
Async XLA Ops:
  3.9 16.2 %collective-permute-start = (bf16[128,2176]{1,0:T(8,128)(2,1)S(1)}, bf16[128,2176]{1,0:T(8,128)(2,1)S(1)}, u32[]{:S(2)}, u32[]{:S(2)}) collective-permute-start(bf16[128,2176]{1,0:T(8,128)(2,1)S(1)} %get-tuple-element.37), channel_id=1, source_target_pairs={{0,1},{1,0},{2,3},{3,2},{4,5},{5,4},{6,7},{7,6},{8,9},{9,8},{10,11... | collective-permute-start | bytes 1671176 | tf_op jit(solution)/shard_map/ppermute | solution.py:290
  4.4 17.0 %collective-permute-start.2 = (bf16[128,2176]{1,0:T(8,128)(2,1)S(1)}, bf16[128,2176]{1,0:T(8,128)(2,1)S(1)}, u32[]{:S(2)}, u32[]{:S(2)}) collective-permute-start(bf16[128,2176]{1,0:T(8,128)(2,1)S(1)} %get-tuple-element.39), channel_id=1, source_target_pairs={{0,2},{1,3},{2,0},{3,1},{4,6},{5,7},{6,4},{7,5},{8,10},{9,11},{10,... | collective-permute-start | bytes 1671176 | tf_op jit(solution)/shard_map/ppermute | solution.py:290
  8.2 11.7 %collective-permute-start.1 = (bf16[256,512]{1,0:T(8,128)(2,1)S(1)}, bf16[256,512]{1,0:T(8,128)(2,1)S(1)}, u32[]{:S(2)}, u32[]{:S(2)}) collective-permute-start(bf16[256,512]{1,0:T(8,128)(2,1)S(1)} %get-tuple-element.32), channel_id=1, source_target_pairs={{0,4},{12,8},{1,5},{13,9},{2,6},{14,10},{3,7},{15,11},{16,20},{28,... | collective-permute-start | bytes 786440 | tf_op jit(solution)/shard_map/ppermute | solution.py:319
  11.7 12.3 %collective-permute-start.4 = (bf16[256,512]{1,0:T(8,128)(2,1)S(1)}, bf16[256,512]{1,0:T(8,128)(2,1)S(1)}, u32[]{:S(2)}, u32[]{:S(2)}) collective-permute-start(bf16[256,512]{1,0:T(8,128)(2,1)S(1)} %get-tuple-element.41), channel_id=1, source_target_pairs={{0,4},{12,8},{1,5},{13,9},{2,6},{14,10},{3,7},{15,11},{16,20},{28,... | collective-permute-start | bytes 786440 | tf_op jit(solution)/shard_map/ppermute | solution.py:319
  13.1 8.4 %copy-start = (bf16[2048,512]{1,0:T(8,128)(2,1)S(1)}, bf16[2048,512]{1,0:T(8,128)(2,1)}, u32[]{:S(2)}) copy-start(bf16[2048,512]{1,0:T(8,128)(2,1)} %down_ref.3) | copy-start | bytes 6291460
  18.6 16.9 %collective-permute-start.5 = (bf16[512,512]{1,0:T(8,128)(2,1)S(1)}, bf16[512,512]{1,0:T(8,128)(2,1)S(1)}, u32[]{:S(2)}, u32[]{:S(2)}) collective-permute-start(bf16[512,512]{1,0:T(8,128)(2,1)S(1)} %get-tuple-element.43), channel_id=1, source_target_pairs={{0,4},{12,8},{1,5},{13,9},{2,6},{14,10},{3,7},{15,11},{16,20},{28,... | collective-permute-start | bytes 1572872 | tf_op jit(solution)/shard_map/ppermute | solution.py:321
  19.9 14.9 %collective-permute-start.3 = (bf16[128,2176]{1,0:T(8,128)(2,1)S(1)}, bf16[128,2176]{1,0:T(8,128)(2,1)S(1)}, u32[]{:S(2)}, u32[]{:S(2)}) collective-permute-start(bf16[128,2176]{1,0:T(8,128)(2,1)S(1)} %get-tuple-element.40), channel_id=1, source_target_pairs={{0,3},{1,2},{2,1},{3,0},{4,7},{5,6},{6,5},{7,4},{8,11},{9,10},{10,... | collective-permute-start | bytes 1671176 | tf_op jit(solution)/shard_map/ppermute | solution.py:290
  20.1 15.5 %collective-permute-start.6 = (bf16[256,512]{1,0:T(8,128)(2,1)S(1)}, bf16[256,512]{1,0:T(8,128)(2,1)S(1)}, u32[]{:S(2)}, u32[]{:S(2)}) collective-permute-start(bf16[256,512]{1,0:T(8,128)(2,1)S(1)} %add_convert_fusion.2), channel_id=1, source_target_pairs={{4,12},{8,0},{5,13},{9,1},{6,14},{10,2},{7,15},{11,3},{20,28},{24,... | collective-permute-start | bytes 786440 | tf_op jit(solution)/shard_map/ppermute | solution.py:326
  24.1 21.3 %copy-start.1 = (bf16[512,512]{1,0:T(8,128)(2,1)S(1)}, bf16[512,512]{1,0:T(8,128)(2,1)}, u32[]{:S(2)}) copy-start(bf16[512,512]{1,0:T(8,128)(2,1)} %up_ref.1) | copy-start | bytes 1572868
  24.1 13.3 %collective-permute-start.7 = (bf16[256,512]{1,0:T(8,128)(2,1)S(1)}, bf16[256,512]{1,0:T(8,128)(2,1)S(1)}, u32[]{:S(2)}, u32[]{:S(2)}) collective-permute-start(bf16[256,512]{1,0:T(8,128)(2,1)S(1)} %add_convert_fusion.1), channel_id=1, source_target_pairs={{4,12},{8,0},{5,13},{9,1},{6,14},{10,2},{7,15},{11,3},{20,28},{24,... | collective-permute-start | bytes 786440 | tf_op jit(solution)/shard_map/ppermute | solution.py:326
  35.4 4.3 %collective-permute-start.8 = (bf16[256,128]{1,0:T(8,128)(2,1)S(1)}, bf16[256,128]{1,0:T(8,128)(2,1)S(1)}, u32[]{:S(2)}, u32[]{:S(2)}) collective-permute-start(bf16[256,128]{1,0:T(8,128)(2,1)S(1)} %shrink_partial.3), channel_id=1, source_target_pairs={{0,4},{4,0},{8,12},{12,8},{1,5},{5,1},{9,13},{13,9},{2,6},{6,2},{1... | collective-permute-start | bytes 196616 | tf_op jit(solution)/shard_map/ppermute | solution.py:290
  39.7 5.7 %collective-permute-start.9 = (bf16[256,128]{1,0:T(8,128)(2,1)S(1)}, bf16[256,128]{1,0:T(8,128)(2,1)S(1)}, u32[]{:S(2)}, u32[]{:S(2)}) collective-permute-start(bf16[256,128]{1,0:T(8,128)(2,1)S(1)} %add_convert_fusion.3.one_ref), channel_id=1, source_target_pairs={{0,8},{4,12},{8,0},{12,4},{1,9},{5,13},{9,1},{13,5},{2,10},{6,14},... | collective-permute-start | bytes 196616 | tf_op jit(solution)/shard_map/ppermute | solution.py:290
  41.0 13.2 %collective-permute-start.13 = (bf16[512,512]{1,0:T(8,128)(2,1)S(1)}, bf16[512,512]{1,0:T(8,128)(2,1)S(1)}, u32[]{:S(2)}, u32[]{:S(2)}) collective-permute-start(bf16[512,512]{1,0:T(8,128)(2,1)S(1)} %add_convert_fusion), channel_id=1, source_target_pairs={{4,8},{8,4},{5,9},{9,5},{6,10},{10,6},{7,11},{11,7},{20,24},{24,20... | collective-permute-start | bytes 1572872 | tf_op jit(solution)/shard_map/ppermute | solution.py:330
  41.7 14.8 %collective-permute-start.14 = (bf16[512,512]{1,0:T(8,128)(2,1)S(1)}, bf16[512,512]{1,0:T(8,128)(2,1)S(1)}, u32[]{:S(2)}, u32[]{:S(2)}) collective-permute-start(bf16[512,512]{1,0:T(8,128)(2,1)S(1)} %get-tuple-element.52), channel_id=1, source_target_pairs={{0,4},{4,0},{8,12},{12,8},{1,5},{5,1},{9,13},{13,9},{2,6},{6,2},{1... | collective-permute-start | bytes 1572872 | tf_op jit(solution)/shard_map/ppermute | solution.py:290
  45.9 1.9 %collective-permute-start.10 = (bf16[128,512]{1,0:T(8,128)(2,1)S(1)}, bf16[128,512]{1,0:T(8,128)(2,1)S(1)}, u32[]{:S(2)}, u32[]{:S(2)}) collective-permute-start(bf16[128,512]{1,0:T(8,128)(2,1)S(1)} %get-tuple-element.46), channel_id=1, source_target_pairs={{0,1},{1,0},{2,3},{3,2},{4,5},{5,4},{6,7},{7,6},{8,9},{9,8},{10,11... | collective-permute-start | bytes 393224 | tf_op jit(solution)/shard_map/ppermute | solution.py:290
  46.0 6.4 %collective-permute-start.11 = (bf16[128,512]{1,0:T(8,128)(2,1)S(1)}, bf16[128,512]{1,0:T(8,128)(2,1)S(1)}, u32[]{:S(2)}, u32[]{:S(2)}) collective-permute-start(bf16[128,512]{1,0:T(8,128)(2,1)S(1)} %get-tuple-element.47), channel_id=1, source_target_pairs={{0,2},{1,3},{2,0},{3,1},{4,6},{5,7},{6,4},{7,5},{8,10},{9,11},{10,... | collective-permute-start | bytes 393224 | tf_op jit(solution)/shard_map/ppermute | solution.py:290
  47.0 7.3 %collective-permute-start.12 = (bf16[128,512]{1,0:T(8,128)(2,1)S(1)}, bf16[128,512]{1,0:T(8,128)(2,1)S(1)}, u32[]{:S(2)}, u32[]{:S(2)}) collective-permute-start(bf16[128,512]{1,0:T(8,128)(2,1)S(1)} %get-tuple-element.48), channel_id=1, source_target_pairs={{0,3},{1,2},{2,1},{3,0},{4,7},{5,6},{6,5},{7,4},{8,11},{9,10},{10,... | collective-permute-start | bytes 393224 | tf_op jit(solution)/shard_map/ppermute | solution.py:290

commit v7 on v6

--- a/solution.py
+++ b/solution.py
@@ -36,19 +36,32 @@
     return lax.broadcasted_iota(i32, shape, dim)
 
 
-def places(slots, capacity, holders, me, ids, table, earlier):
+def places(slots, capacity, holders, me, ids, table):
     rows = ids.shape[1]
     low = (iota((LANES, rows), 0) == (ids & (LANES - 1))).astype(f32).astype(bf16)
     high = iota((table.shape[0], rows), 0) == lax.shift_right_logical(ids, 7)
     found = dot(table.astype(f32).astype(bf16), low)
     slot = jnp.sum(jnp.where(high, found, 0.0), axis=0, keepdims=True).astype(i32)
-    holder = lax.div(slot, slots)
+    holder = split_slot(slot, slots)
     tag = (slot - holder * slots + 1).astype(f32)
     partner = holder ^ me
     mine = iota((max(8, holders), rows), 0) == partner
-    before = dot(mine.astype(f32).astype(bf16), earlier)
-    rank = jnp.sum(jnp.where(mine, before, 0.0), axis=0, keepdims=True).astype(i32)
-    return partner * capacity + rank, tag
+    ones = mine.astype(f32)
+    groups = [ones[:, k:k + LANES] for k in range(0, rows, LANES)]
+    earlier = (iota((LANES, LANES), 0) < iota((LANES, LANES), 1)).astype(f32).astype(bf16)
+    before = dot(jnp.concatenate(groups, axis=0).astype(bf16), earlier)
+    count = ones.shape[0]
+    ranks, passed = [], jnp.zeros((count, 1), f32)
+    for k, group in enumerate(groups):
+        ranks.append(jnp.sum(group * (before[k * count:(k + 1) * count] + passed), axis=0, keepdims=True))
+        passed += jnp.sum(group, axis=1, keepdims=True)
+    return partner * capacity + jnp.concatenate(ranks, axis=1).astype(i32), tag
+
+
+def split_slot(slot, slots):
+    if slots & (slots - 1):
+        return lax.div(slot, slots)
+    return lax.shift_right_logical(slot, slots.bit_length() - 1)
 
 
 def sort_body(slots, capacity, holders, me_ref, z_ref, ids_hbm, table_hbm, x_hbm, w_hbm, place_ref, *refs):
@@ -69,10 +82,9 @@
     w_copy = pltpu.make_async_copy(w_hbm.at[:, pl.ds(column, width)], w_buf, w_sem)
     for copy in small + copies + [w_copy]:
         copy.start()
-    earlier = (iota((rows, rows), 0) < iota((rows, rows), 1)).astype(f32).astype(bf16)
     for copy in small:
         copy.wait()
-    place, tag = places(slots, capacity, holders, me_ref[0], ids_buf[...], table_buf[...], earlier)
+    place, tag = places(slots, capacity, holders, me_ref[0], ids_buf[...], table_buf[...])
     place_ref[...] = jnp.broadcast_to(place, place_ref.shape)
     pick = (iota((holders * capacity, rows), 0) == place).astype(f32).astype(bf16)
     tags = dot(pick, jnp.broadcast_to(tag, (LANES, rows)).astype(bf16), ((1,), (1,))).astype(bf16)
@@ -130,7 +142,7 @@
 
 
 def rest_body(z_ref, place_ref, x_ref, w_hbm, *refs):
-    second, third, own, unsort, w_buf, sem = refs
+    second, upper, lower, own, unsort, w_buf, sem = refs
     z = z_ref[0]
     width = own.shape[1]
     blocks = (jnp.where(z < 2, 2, 1), z ^ 1, z)
@@ -141,9 +153,11 @@
         copies[k].start()
     unsort_matrix(place_ref, unsort)
     x = x_ref[...]
-    for k, out in enumerate((second, third, own)):
+    half = upper.shape[0]
+    for k, outs in enumerate(((second,), (upper, lower), (own,))):
         copies[k].wait()
-        out[...] = dot(x, w_buf[k]).astype(bf16)
+        for i, out in enumerate(outs):
+            out[...] = dot(x[i * half:] if len(outs) == 1 else x[i * half:(i + 1) * half], w_buf[k]).astype(bf16)
 
 
 def unsort_matrix(place_ref, unsort):
@@ -157,7 +171,8 @@
 def rest(z, place, x, weight, width, total):
     rows, features = x.shape
     smem, vmem, hbm = (pl.BlockSpec(memory_space=m) for m in (pltpu.SMEM, pltpu.VMEM, pltpu.HBM))
-    shapes = [jax.ShapeDtypeStruct((rows, width), bf16)] * 3 + [jax.ShapeDtypeStruct((rows, total), bf16)]
+    shapes = [jax.ShapeDtypeStruct((r, width), bf16) for r in (rows, rows // 2, rows // 2, rows)]
+    shapes.append(jax.ShapeDtypeStruct((rows, total), bf16))
     return pl.pallas_call(
         rest_body,
         out_shape=shapes,
@@ -253,29 +268,33 @@
     )(one, two, up, *parts)
 
 
-def finish_body(count, unsort_ref, *refs):
+def finish_body(count, halves, unsort_ref, *refs):
     deltas, sums, out = refs[:count], refs[count:-1], refs[-1]
     rows = out.shape[0]
-    base = None
-    at = 0
-    while at < len(sums):
-        if sums[at].shape[0] == rows:
-            term, at = sums[at][...].astype(f32), at + 1
-        else:
-            term, at = jnp.concatenate([sums[at][...], sums[at + 1][...]], axis=0).astype(f32), at + 2
-        base = term if base is None else base + term
-    out[...] = (base + dot(unsort_ref[...], jnp.concatenate([d[...] for d in deltas], axis=0))).astype(bf16)
-
-
-def finish(unsort, deltas, sums):
+    whole = sums[:len(sums) - len(halves)]
+    parts = [[], []]
+    for ref, half in zip(sums[len(whole):], halves):
+        parts[half].append(ref)
+    sorted_deltas = jnp.concatenate([d[...] for d in deltas], axis=0)
+    for half in range(2):
+        part = slice(half * rows // 2, (half + 1) * rows // 2)
+        total = dot(unsort_ref[part, :], sorted_deltas)
+        terms = [ref[part, :].astype(f32) for ref in whole] + [ref[...].astype(f32) for ref in parts[half]]
+        base = terms[0]
+        for term in terms[1:]:
+            base += term
+        out[part, :] = (base + total).astype(bf16)
+
+
+def finish(unsort, deltas, sums, halves=()):
     rows, columns = sums[0].shape
     return pl.pallas_call(
-        functools.partial(finish_body, len(deltas)),
+        functools.partial(finish_body, len(deltas), [which for part, which in halves]),
         out_shape=jax.ShapeDtypeStruct((rows, columns), bf16),
         compiler_params=params(),
         cost_estimate=cost(2 * rows * unsort.shape[1] * columns, 12 * rows * columns),
         name="finish",
-    )(unsort, *deltas, *sums)
+    )(unsort, *deltas, *sums, *[part for part, which in halves])
 
 
 def both(a, b):
@@ -292,7 +311,7 @@
 
 EDGE = [(0, 1), (3, 2)]
 MIDDLE = [(1, 2), (2, 1)]
-ACROSS = [(1, 3), (2, 0)]
+OUTER = [(1, 0), (2, 3)]
 
 
 def tp_sums(mine, *before):
@@ -317,27 +336,31 @@
     if lax.axis_size("tp") == 4:
         first = first_block(x, w)
         edge0 = [lax.ppermute(f, "tp", EDGE) for f in first]
-        second, third, own, unsort = rest(z, after(place, *first), x, weight, width, total)
+        second, *third, own, unsort = rest(z, after(place, parts[1], *first), x, weight, width, total)
         edge1 = lax.ppermute(second, "tp", EDGE)
-        inner0 = [both(first[0], edge0[0])]
-        parts[1] = after(parts[1], *inner0)
-        early = shrink_partial(down, parts[:-1])
+        inner0 = [both(after(first[0], second), edge0[0])]
+        early = shrink_partial(down, parts[:2] + [after(parts[2], *inner0)])
         inner0.append(both(after(first[1], early), edge0[1]))
-        across = [lax.ppermute(i, "tp", ACROSS) for i in inner0]
-        mine = shrink_partial(down, [after(parts[-1], *inner0)], [early])
+        middle0 = [lax.ppermute(i, "tp", MIDDLE) for i in inner0]
+        inner2 = [both(after(third[0], inner0[1]), middle0[0]), both(third[1], middle0[1])]
+        outer = lax.ppermute(inner2[0], "tp", OUTER)
+        mine = shrink_partial(down, [after(parts[-1], inner2[0])], [early])
+        edge2 = lax.ppermute(after(third[0], mine), "tp", EDGE)
         inner1 = both(second, edge1)
-        steps, other = tp_sums(mine, inner1, *across)
+        steps, other = tp_sums(mine, inner1, inner2[1], outer)
         middle1 = lax.ppermute(after(inner1, steps[-1]), "tp", MIDDLE)
-        last = swap(after(third, steps[-1]), "tp", 1)
-        sums = [own, *across, middle1, last]
+        last = swap(after(inner2[1], steps[-1]), "tp", 1)
+        other = after(other, edge2)
+        sums, halves = [own, middle1], [(edge2, 0), (outer, 0), (last, 1)]
     else:
         unsort = unsort_only(place, total)
         full = dot(x, weight).astype(bf16)
         sums = [lax.psum_scatter(full, "tp", scatter_dimension=1, tiled=True)]
+        halves = []
         steps, other = tp_sums(shrink_partial(down, parts))
     deltas = expand(steps[-1], other, up, parts)
     back = [deltas[0]] + [swap(deltas[j], "ad", j) for j in range(1, holders)]
-    return finish(unsort, back, sums)
+    return finish(unsort, back, sums, halves)
 
 
 def solution(mesh):

time: 58 us -> 57 us (0.983)
  the two profiles are of different devices: /device:TPU:0 before, /device:TPU:13 now
where the time goes in v7:
time: 57 us; the launch traced here: 56.7 us
  starting transfers between devices  24.6 us (43%)
  waiting for transfers between devices  17.5 us (31%)
  Pallas kernels  14 us (25%)
    ppermute x9, waiting for transfers between devices, swap(): lax.ppermute(value, axis, [(i, i ^ bit) for i in range(lax.axis_size(axis...  15.6 us
    ppermute x9, starting transfers between devices, swap(): lax.ppermute(value, axis, [(i, i ^ bit) for i in range(lax.axis_size(axis...  9.53 us
    ppermute x2, starting transfers between devices, shards(): middle0 = [lax.ppermute(i, 'tp', MIDDLE) for i in inner0]  6.41 us
    pallas_call x1, Pallas kernels, rest(): pl.pallas_call(rest_body, out_shape=shapes, in_specs=[smem, vmem, vmem, h...  5.51 us
    pallas_call x1, Pallas kernels, sort_rows(): pl.pallas_call(functools.partial(sort_body, slots, capacity, holders), ou...  3.91 us
    ppermute x2, starting transfers between devices, shards(): edge0 = [lax.ppermute(f, 'tp', EDGE) for f in first]  2.58 us
    ppermute x1, starting transfers between devices, shards(): middle1 = lax.ppermute(after(inner1, steps[-1]), 'tp', MIDDLE)  2.06 us
    pallas_call x2, Pallas kernels, shrink_partial(): pl.pallas_call(functools.partial(shrink_body, kept), out_shape=jax.ShapeD...  1.6 us
  transfers between devices with their start and end apart: 17, of which 8 were waited for; matrix products, arithmetic and copies ran while one was open for 1% of the time, Pallas kernels for 16%

profile of v7, /device:TPU:13, one launch (start us, length us, event | category | flops | bytes accessed | tf_op | source)
XLA Modules:
  0.0 56.7 jit_solution(10881846335040766425)
XLA Ops:
  0.0 3.9 %sort_rows.1 = (s32[8,512]{1,0:T(8,128)S(1)}, bf16[128,2176]{1,0:T(8,128)(2,1)S(1)}, bf16[128,2176]{1,0:T(8,128)(2,1)S(1)}, bf16[128,2176]{1,0:T(8,128)(2,1)S(1)...) custom-call(s32[1]{0:T(128)} %bitcast.1.me_ref, s32[1]{0:T(128)} %bitcast.z_ref, ...), custom_call_target="tpu_custom_call" | custom-call | flops 1073741824 | bytes 4194304 | tf_op jit(solution)/shard_map/sort_rows/pallas_call | solution.py:109
  3.9 0.7 %collective-permute-start = (bf16[128,2176]{1,0:T(8,128)(2,1)S(1)}, bf16[128,2176]{1,0:T(8,128)(2,1)S(1)}, u32[]{:S(2)}, u32[]{:S(2)}) collective-permute-start(bf16[128,2176]{1,0:T(8,128)(2,1)S(1)} %get-tuple-element.35), channel_id=1, source_target_pairs={{0,1},{1,0},{2,3},{3,2},{4,5},{5,4},{6,7},{7,6},{8,9},{9,8},{10,11... | collective-permute-start | bytes 1671176 | tf_op jit(solution)/shard_map/ppermute | solution.py:309
  4.7 1.2 %collective-permute-start.1 = (bf16[128,2176]{1,0:T(8,128)(2,1)S(1)}, bf16[128,2176]{1,0:T(8,128)(2,1)S(1)}, u32[]{:S(2)}, u32[]{:S(2)}) collective-permute-start(bf16[128,2176]{1,0:T(8,128)(2,1)S(1)} %get-tuple-element.43), channel_id=1, source_target_pairs={{0,2},{1,3},{2,0},{3,1},{4,6},{5,7},{6,4},{7,5},{8,10},{9,11},{10,... | collective-permute-start | bytes 1671176 | tf_op jit(solution)/shard_map/ppermute | solution.py:309
  5.9 1.2 %first_block.1 = (bf16[256,512]{1,0:T(8,128)(2,1)S(1)}, bf16[256,512]{1,0:T(8,128)(2,1)S(1)}) custom-call(bf16[512,2048]{1,0:T(8,128)(2,1)S(1)} %get-tuple-element.36.x_ref, bf16[2048,512]{1,0:T(8,128)(2,1)S(1)} %get-tuple-element.37.w_ref), custom_call_target="tpu_custom_call" | custom-call | flops 1073741824 | bytes 4194304 | tf_op jit(solution)/shard_map/first_block/pallas_call | solution.py:135
  7.1 1.3 %collective-permute-start.2 = (bf16[256,512]{1,0:T(8,128)(2,1)S(1)}, bf16[256,512]{1,0:T(8,128)(2,1)S(1)}, u32[]{:S(2)}, u32[]{:S(2)}) collective-permute-start(bf16[256,512]{1,0:T(8,128)(2,1)S(1)} %get-tuple-element.45), channel_id=1, source_target_pairs={{0,4},{12,8},{1,5},{13,9},{2,6},{14,10},{3,7},{15,11},{16,20},{28,... | collective-permute-start | bytes 786440 | tf_op jit(solution)/shard_map/ppermute | solution.py:338
  8.4 1.3 %collective-permute-start.4 = (bf16[256,512]{1,0:T(8,128)(2,1)S(1)}, bf16[256,512]{1,0:T(8,128)(2,1)S(1)}, u32[]{:S(2)}, u32[]{:S(2)}) collective-permute-start(bf16[256,512]{1,0:T(8,128)(2,1)S(1)} %get-tuple-element.49), channel_id=1, source_target_pairs={{0,4},{12,8},{1,5},{13,9},{2,6},{14,10},{3,7},{15,11},{16,20},{28,... | collective-permute-start | bytes 786440 | tf_op jit(solution)/shard_map/ppermute | solution.py:338
  10.3 5.5 %rest.1 = (bf16[512,512]{1,0:T(8,128)(2,1)S(1)}, bf16[256,512]{1,0:T(8,128)(2,1)S(1)}, bf16[256,512]{1,0:T(8,128)(2,1)S(1)}, bf16[512,512]{1,0:T(8,128)(2,1)S(1)}, bf16[512,512]{1,0:T(8,128)(2,1)S(1)}) custom-call(s32[1]{0:T(128)} %bitcast.z_ref, s32[8,512]{1,0:T(8,128)S(1)} %get-tuple-element.40.place_ref, bf16[512,2048]{1,0:T(8,128)(2,1)S(1)} %get-tuple-element.36.x_ref, ...), custom_call_target="tpu_custom_call" | custom-call | flops 3221225472 | bytes 10485760 | tf_op jit(solution)/shard_map/rest/pallas_call | solution.py:176
  15.8 1.3 %collective-permute-start.6 = (bf16[512,512]{1,0:T(8,128)(2,1)S(1)}, bf16[512,512]{1,0:T(8,128)(2,1)S(1)}, u32[]{:S(2)}, u32[]{:S(2)}) collective-permute-start(bf16[512,512]{1,0:T(8,128)(2,1)S(1)} %get-tuple-element.44), channel_id=1, source_target_pairs={{0,4},{12,8},{1,5},{13,9},{2,6},{14,10},{3,7},{15,11},{16,20},{28,... | collective-permute-start | bytes 1572872 | tf_op jit(solution)/shard_map/ppermute | solution.py:340
  17.2 3.2 %collective-permute-start.5 = (bf16[256,512]{1,0:T(8,128)(2,1)S(1)}, bf16[256,512]{1,0:T(8,128)(2,1)S(1)}, u32[]{:S(2)}, u32[]{:S(2)}) collective-permute-start(bf16[256,512]{1,0:T(8,128)(2,1)S(1)} %add_convert_fusion.4), channel_id=1, source_target_pairs={{4,8},{8,4},{5,9},{9,5},{6,10},{10,6},{7,11},{11,7},{20,24},{24,20... | collective-permute-start | bytes 786440 | tf_op jit(solution)/shard_map/ppermute | solution.py:344
  20.4 1.1 %shrink_partial.2.refs_0_ = bf16[192,128]{1,0:T(8,128)(2,1)S(1)} custom-call(bf16[2048,512]{1,0:T(8,128)(2,1)S(1)} %copy-done, bf16[128,2176]{1,0:T(8,128)(2,1)S(1)} %get-tuple-element.42.refs_0_, bf16[128,2176]{1,0:T(8,128)(2,1)S(1)} %collective-permute-done.refs_1_, bf16[128,2176]{1,0:T(8,128)(2,1)S(1)} %collective-permute-done.1.refs_2_), custom_call_target="tpu_custom_call" | custom-call | flops 805306368 | bytes 3670016 | tf_op jit(solution)/shard_map/shrink_partial/pallas_call | solution.py:226
  22.3 3.2 %collective-permute-start.7 = (bf16[256,512]{1,0:T(8,128)(2,1)S(1)}, bf16[256,512]{1,0:T(8,128)(2,1)S(1)}, u32[]{:S(2)}, u32[]{:S(2)}) collective-permute-start(bf16[256,512]{1,0:T(8,128)(2,1)S(1)} %add_convert_fusion.3), channel_id=1, source_target_pairs={{4,8},{8,4},{5,9},{9,5},{6,10},{10,6},{7,11},{11,7},{20,24},{24,20... | collective-permute-start | bytes 786440 | tf_op jit(solution)/shard_map/ppermute | solution.py:344
  25.6 1.4 %collective-permute-start.8 = (bf16[256,512]{1,0:T(8,128)(2,1)S(1)}, bf16[256,512]{1,0:T(8,128)(2,1)S(1)}, u32[]{:S(2)}, u32[]{:S(2)}) collective-permute-start(bf16[256,512]{1,0:T(8,128)(2,1)S(1)} %add_convert_fusion.2), channel_id=1, source_target_pairs={{4,0},{8,12},{5,1},{9,13},{6,2},{10,14},{7,3},{11,15},{20,16},{24,... | collective-permute-start | bytes 786440 | tf_op jit(solution)/shard_map/ppermute | solution.py:346
  27.0 4.2 %collective-permute-done.3.refs_1_.refs_3_ = bf16[128,2176]{1,0:T(8,128)(2,1)S(1)} collective-permute-done((bf16[128,2176]{1,0:T(8,128)(2,1)S(1)}, bf16[128,2176]{1,0:T(8,128)(2,1)S(1)}, u32[]{:S(2)}, u32[]{:S(2)}) %collective-permute-start.3) | collective-permute-done | bytes 557088 | tf_op jit(solution)/shard_map/ppermute | solution.py:309
  31.9 1.3 %collective-permute-start.11 = (bf16[256,512]{1,0:T(8,128)(2,1)S(1)}, bf16[256,512]{1,0:T(8,128)(2,1)S(1)}, u32[]{:S(2)}, u32[]{:S(2)}) collective-permute-start(bf16[256,512]{1,0:T(8,128)(2,1)S(1)} %get-tuple-element.54), channel_id=1, source_target_pairs={{0,4},{12,8},{1,5},{13,9},{2,6},{14,10},{3,7},{15,11},{16,20},{28,... | collective-permute-start | bytes 786440 | tf_op jit(solution)/shard_map/ppermute | solution.py:348
  33.6 2.1 %collective-permute-done.9 = bf16[256,128]{1,0:T(8,128)(2,1)S(1)} collective-permute-done((bf16[256,128]{1,0:T(8,128)(2,1)S(1)}, bf16[256,128]{1,0:T(8,128)(2,1)S(1)}, u32[]{:S(2)}, u32[]{:S(2)}) %collective-permute-start.9) | collective-permute-done | bytes 65568 | tf_op jit(solution)/shard_map/ppermute | solution.py:309
  35.7 1.9 %collective-permute-start.10 = (bf16[256,128]{1,0:T(8,128)(2,1)S(1)}, bf16[256,128]{1,0:T(8,128)(2,1)S(1)}, u32[]{:S(2)}, u32[]{:S(2)}) collective-permute-start(bf16[256,128]{1,0:T(8,128)(2,1)S(1)} %add_convert_fusion.5.one_ref), channel_id=1, source_target_pairs={{0,8},{4,12},{8,0},{12,4},{1,9},{5,13},{9,1},{13,5},{2,10},{6,14},... | collective-permute-start | bytes 196616 | tf_op jit(solution)/shard_map/ppermute | solution.py:309
  38.2 2.1 %collective-permute-start.15 = (bf16[512,512]{1,0:T(8,128)(2,1)S(1)}, bf16[512,512]{1,0:T(8,128)(2,1)S(1)}, u32[]{:S(2)}, u32[]{:S(2)}) collective-permute-start(bf16[512,512]{1,0:T(8,128)(2,1)S(1)} %add_convert_fusion), channel_id=1, source_target_pairs={{4,8},{8,4},{5,9},{9,5},{6,10},{10,6},{7,11},{11,7},{20,24},{24,20... | collective-permute-start | bytes 1572872 | tf_op jit(solution)/shard_map/ppermute | solution.py:351
  40.3 1.0 %collective-permute-done.11.refs_6_ = bf16[256,512]{1,0:T(8,128)(2,1)S(1)} collective-permute-done((bf16[256,512]{1,0:T(8,128)(2,1)S(1)}, bf16[256,512]{1,0:T(8,128)(2,1)S(1)}, u32[]{:S(2)}, u32[]{:S(2)}) %collective-permute-start.11) | collective-permute-done | bytes 262176 | tf_op jit(solution)/shard_map/ppermute | solution.py:348
  41.3 2.9 %collective-permute-done.10.two_ref = bf16[256,128]{1,0:T(8,128)(2,1)S(1)} collective-permute-done((bf16[256,128]{1,0:T(8,128)(2,1)S(1)}, bf16[256,128]{1,0:T(8,128)(2,1)S(1)}, u32[]{:S(2)}, u32[]{:S(2)}) %collective-permute-start.10) | collective-permute-done | bytes 65568 | tf_op jit(solution)/shard_map/ppermute | solution.py:309
  44.7 2.7 %collective-permute-start.12 = (bf16[128,512]{1,0:T(8,128)(2,1)S(1)}, bf16[128,512]{1,0:T(8,128)(2,1)S(1)}, u32[]{:S(2)}, u32[]{:S(2)}) collective-permute-start(bf16[128,512]{1,0:T(8,128)(2,1)S(1)} %get-tuple-element.57), channel_id=1, source_target_pairs={{0,1},{1,0},{2,3},{3,2},{4,5},{5,4},{6,7},{7,6},{8,9},{9,8},{10,11... | collective-permute-start | bytes 393224 | tf_op jit(solution)/shard_map/ppermute | solution.py:309
  47.4 1.2 %collective-permute-start.13 = (bf16[128,512]{1,0:T(8,128)(2,1)S(1)}, bf16[128,512]{1,0:T(8,128)(2,1)S(1)}, u32[]{:S(2)}, u32[]{:S(2)}) collective-permute-start(bf16[128,512]{1,0:T(8,128)(2,1)S(1)} %get-tuple-element.58), channel_id=1, source_target_pairs={{0,2},{1,3},{2,0},{3,1},{4,6},{5,7},{6,4},{7,5},{8,10},{9,11},{10,... | collective-permute-start | bytes 393224 | tf_op jit(solution)/shard_map/ppermute | solution.py:309
  49.1 3.4 %collective-permute-done.13.refs_2_ = bf16[128,512]{1,0:T(8,128)(2,1)S(1)} collective-permute-done((bf16[128,512]{1,0:T(8,128)(2,1)S(1)}, bf16[128,512]{1,0:T(8,128)(2,1)S(1)}, u32[]{:S(2)}, u32[]{:S(2)}) %collective-permute-start.13) | collective-permute-done | bytes 131104 | tf_op jit(solution)/shard_map/ppermute | solution.py:309
  52.5 3.0 %collective-permute-done.14.refs_3_ = bf16[128,512]{1,0:T(8,128)(2,1)S(1)} collective-permute-done((bf16[128,512]{1,0:T(8,128)(2,1)S(1)}, bf16[128,512]{1,0:T(8,128)(2,1)S(1)}, u32[]{:S(2)}, u32[]{:S(2)}) %collective-permute-start.14) | collective-permute-done | bytes 131104 | tf_op jit(solution)/shard_map/ppermute | solution.py:309
  55.5 1.3 %finish.1 = bf16[512,512]{1,0:T(8,128)(2,1)} custom-call(bf16[512,512]{1,0:T(8,128)(2,1)S(1)} %get-tuple-element.41.unsort_ref, bf16[128,512]{1,0:T(8,128)(2,1)S(1)} %get-tuple-element.56.refs_0_, bf16[128,512]{1,0:T(8,128)(2,1)S(1)} %collective-permute-done.12.refs_1_, bf16[128,512]{1,0:T(8,128)(2,1)S(1)} %collective-permute-done.13.refs_2_, ...), custom_call_target="tpu_custom_call" | custom-call | flops 268435456 | bytes 3145728 | tf_op jit(solution)/shard_map/finish/pallas_call | solution.py:291
  (27 shorter events, 4.1 us)
Async XLA Ops:
  3.9 6.4 %collective-permute-start = (bf16[128,2176]{1,0:T(8,128)(2,1)S(1)}, bf16[128,2176]{1,0:T(8,128)(2,1)S(1)}, u32[]{:S(2)}, u32[]{:S(2)}) collective-permute-start(bf16[128,2176]{1,0:T(8,128)(2,1)S(1)} %get-tuple-element.35), channel_id=1, source_target_pairs={{0,1},{1,0},{2,3},{3,2},{4,5},{5,4},{6,7},{7,6},{8,9},{9,8},{10,11... | collective-permute-start | bytes 1671176 | tf_op jit(solution)/shard_map/ppermute | solution.py:309
  4.7 15.7 %collective-permute-start.1 = (bf16[128,2176]{1,0:T(8,128)(2,1)S(1)}, bf16[128,2176]{1,0:T(8,128)(2,1)S(1)}, u32[]{:S(2)}, u32[]{:S(2)}) collective-permute-start(bf16[128,2176]{1,0:T(8,128)(2,1)S(1)} %get-tuple-element.43), channel_id=1, source_target_pairs={{0,2},{1,3},{2,0},{3,1},{4,6},{5,7},{6,4},{7,5},{8,10},{9,11},{10,... | collective-permute-start | bytes 1671176 | tf_op jit(solution)/shard_map/ppermute | solution.py:309
  7.1 10.0 %collective-permute-start.2 = (bf16[256,512]{1,0:T(8,128)(2,1)S(1)}, bf16[256,512]{1,0:T(8,128)(2,1)S(1)}, u32[]{:S(2)}, u32[]{:S(2)}) collective-permute-start(bf16[256,512]{1,0:T(8,128)(2,1)S(1)} %get-tuple-element.45), channel_id=1, source_target_pairs={{0,4},{12,8},{1,5},{13,9},{2,6},{14,10},{3,7},{15,11},{16,20},{28,... | collective-permute-start | bytes 786440 | tf_op jit(solution)/shard_map/ppermute | solution.py:338
  8.4 13.8 %collective-permute-start.4 = (bf16[256,512]{1,0:T(8,128)(2,1)S(1)}, bf16[256,512]{1,0:T(8,128)(2,1)S(1)}, u32[]{:S(2)}, u32[]{:S(2)}) collective-permute-start(bf16[256,512]{1,0:T(8,128)(2,1)S(1)} %get-tuple-element.49), channel_id=1, source_target_pairs={{0,4},{12,8},{1,5},{13,9},{2,6},{14,10},{3,7},{15,11},{16,20},{28,... | collective-permute-start | bytes 786440 | tf_op jit(solution)/shard_map/ppermute | solution.py:338
  9.7 21.5 %collective-permute-start.3 = (bf16[128,2176]{1,0:T(8,128)(2,1)S(1)}, bf16[128,2176]{1,0:T(8,128)(2,1)S(1)}, u32[]{:S(2)}, u32[]{:S(2)}) collective-permute-start(bf16[128,2176]{1,0:T(8,128)(2,1)S(1)} %get-tuple-element.47), channel_id=1, source_target_pairs={{0,3},{1,2},{2,1},{3,0},{4,7},{5,6},{6,5},{7,4},{8,11},{9,10},{10,... | collective-permute-start | bytes 1671176 | tf_op jit(solution)/shard_map/ppermute | solution.py:309
  10.3 10.1 %copy-start = (bf16[2048,512]{1,0:T(8,128)(2,1)S(1)}, bf16[2048,512]{1,0:T(8,128)(2,1)}, u32[]{:S(2)}) copy-start(bf16[2048,512]{1,0:T(8,128)(2,1)} %down_ref.3) | copy-start | bytes 6291460
  15.8 17.6 %collective-permute-start.6 = (bf16[512,512]{1,0:T(8,128)(2,1)S(1)}, bf16[512,512]{1,0:T(8,128)(2,1)S(1)}, u32[]{:S(2)}, u32[]{:S(2)}) collective-permute-start(bf16[512,512]{1,0:T(8,128)(2,1)S(1)} %get-tuple-element.44), channel_id=1, source_target_pairs={{0,4},{12,8},{1,5},{13,9},{2,6},{14,10},{3,7},{15,11},{16,20},{28,... | collective-permute-start | bytes 1572872 | tf_op jit(solution)/shard_map/ppermute | solution.py:340
  17.2 8.3 %collective-permute-start.5 = (bf16[256,512]{1,0:T(8,128)(2,1)S(1)}, bf16[256,512]{1,0:T(8,128)(2,1)S(1)}, u32[]{:S(2)}, u32[]{:S(2)}) collective-permute-start(bf16[256,512]{1,0:T(8,128)(2,1)S(1)} %add_convert_fusion.4), channel_id=1, source_target_pairs={{4,8},{8,4},{5,9},{9,5},{6,10},{10,6},{7,11},{11,7},{20,24},{24,20... | collective-permute-start | bytes 786440 | tf_op jit(solution)/shard_map/ppermute | solution.py:344
  22.3 10.9 %collective-permute-start.7 = (bf16[256,512]{1,0:T(8,128)(2,1)S(1)}, bf16[256,512]{1,0:T(8,128)(2,1)S(1)}, u32[]{:S(2)}, u32[]{:S(2)}) collective-permute-start(bf16[256,512]{1,0:T(8,128)(2,1)S(1)} %add_convert_fusion.3), channel_id=1, source_target_pairs={{4,8},{8,4},{5,9},{9,5},{6,10},{10,6},{7,11},{11,7},{20,24},{24,20... | collective-permute-start | bytes 786440 | tf_op jit(solution)/shard_map/ppermute | solution.py:344
  25.6 18.7 %copy-start.1 = (bf16[512,512]{1,0:T(8,128)(2,1)S(1)}, bf16[512,512]{1,0:T(8,128)(2,1)}, u32[]{:S(2)}) copy-start(bf16[512,512]{1,0:T(8,128)(2,1)} %up_ref.1) | copy-start | bytes 1572868
  25.6 8.0 %collective-permute-start.8 = (bf16[256,512]{1,0:T(8,128)(2,1)S(1)}, bf16[256,512]{1,0:T(8,128)(2,1)S(1)}, u32[]{:S(2)}, u32[]{:S(2)}) collective-permute-start(bf16[256,512]{1,0:T(8,128)(2,1)S(1)} %add_convert_fusion.2), channel_id=1, source_target_pairs={{4,0},{8,12},{5,1},{9,13},{6,2},{10,14},{7,3},{11,15},{20,16},{24,... | collective-permute-start | bytes 786440 | tf_op jit(solution)/shard_map/ppermute | solution.py:346
  31.8 3.9 %collective-permute-start.9 = (bf16[256,128]{1,0:T(8,128)(2,1)S(1)}, bf16[256,128]{1,0:T(8,128)(2,1)S(1)}, u32[]{:S(2)}, u32[]{:S(2)}) collective-permute-start(bf16[256,128]{1,0:T(8,128)(2,1)S(1)} %shrink_partial.3), channel_id=1, source_target_pairs={{0,4},{4,0},{8,12},{12,8},{1,5},{5,1},{9,13},{13,9},{2,6},{6,2},{1... | collective-permute-start | bytes 196616 | tf_op jit(solution)/shard_map/ppermute | solution.py:309
  31.9 9.4 %collective-permute-start.11 = (bf16[256,512]{1,0:T(8,128)(2,1)S(1)}, bf16[256,512]{1,0:T(8,128)(2,1)S(1)}, u32[]{:S(2)}, u32[]{:S(2)}) collective-permute-start(bf16[256,512]{1,0:T(8,128)(2,1)S(1)} %get-tuple-element.54), channel_id=1, source_target_pairs={{0,4},{12,8},{1,5},{13,9},{2,6},{14,10},{3,7},{15,11},{16,20},{28,... | collective-permute-start | bytes 786440 | tf_op jit(solution)/shard_map/ppermute | solution.py:348
  35.7 8.5 %collective-permute-start.10 = (bf16[256,128]{1,0:T(8,128)(2,1)S(1)}, bf16[256,128]{1,0:T(8,128)(2,1)S(1)}, u32[]{:S(2)}, u32[]{:S(2)}) collective-permute-start(bf16[256,128]{1,0:T(8,128)(2,1)S(1)} %add_convert_fusion.5.one_ref), channel_id=1, source_target_pairs={{0,8},{4,12},{8,0},{12,4},{1,9},{5,13},{9,1},{13,5},{2,10},{6,14},... | collective-permute-start | bytes 196616 | tf_op jit(solution)/shard_map/ppermute | solution.py:309
  37.6 17.9 %collective-permute-start.16 = (bf16[256,512]{1,0:T(8,128)(2,1)S(1)}, bf16[256,512]{1,0:T(8,128)(2,1)S(1)}, u32[]{:S(2)}, u32[]{:S(2)}) collective-permute-start(bf16[256,512]{1,0:T(8,128)(2,1)S(1)} %add_convert_fusion.1), channel_id=1, source_target_pairs={{0,4},{4,0},{8,12},{12,8},{1,5},{5,1},{9,13},{13,9},{2,6},{6,2},{1... | collective-permute-start | bytes 786440 | tf_op jit(solution)/shard_map/ppermute | solution.py:309
  38.2 17.2 %collective-permute-start.15 = (bf16[512,512]{1,0:T(8,128)(2,1)S(1)}, bf16[512,512]{1,0:T(8,128)(2,1)S(1)}, u32[]{:S(2)}, u32[]{:S(2)}) collective-permute-start(bf16[512,512]{1,0:T(8,128)(2,1)S(1)} %add_convert_fusion), channel_id=1, source_target_pairs={{4,8},{8,4},{5,9},{9,5},{6,10},{10,6},{7,11},{11,7},{20,24},{24,20... | collective-permute-start | bytes 1572872 | tf_op jit(solution)/shard_map/ppermute | solution.py:351
  44.7 4.4 %collective-permute-start.12 = (bf16[128,512]{1,0:T(8,128)(2,1)S(1)}, bf16[128,512]{1,0:T(8,128)(2,1)S(1)}, u32[]{:S(2)}, u32[]{:S(2)}) collective-permute-start(bf16[128,512]{1,0:T(8,128)(2,1)S(1)} %get-tuple-element.57), channel_id=1, source_target_pairs={{0,1},{1,0},{2,3},{3,2},{4,5},{5,4},{6,7},{7,6},{8,9},{9,8},{10,11... | collective-permute-start | bytes 393224 | tf_op jit(solution)/shard_map/ppermute | solution.py:309
  47.4 5.1 %collective-permute-start.13 = (bf16[128,512]{1,0:T(8,128)(2,1)S(1)}, bf16[128,512]{1,0:T(8,128)(2,1)S(1)}, u32[]{:S(2)}, u32[]{:S(2)}) collective-permute-start(bf16[128,512]{1,0:T(8,128)(2,1)S(1)} %get-tuple-element.58), channel_id=1, source_target_pairs={{0,2},{1,3},{2,0},{3,1},{4,6},{5,7},{6,4},{7,5},{8,10},{9,11},{10,... | collective-permute-start | bytes 393224 | tf_op jit(solution)/shard_map/ppermute | solution.py:309
  48.6 6.8 %collective-permute-start.14 = (bf16[128,512]{1,0:T(8,128)(2,1)S(1)}, bf16[128,512]{1,0:T(8,128)(2,1)S(1)}, u32[]{:S(2)}, u32[]{:S(2)}) collective-permute-start(bf16[128,512]{1,0:T(8,128)(2,1)S(1)} %get-tuple-element.59), channel_id=1, source_target_pairs={{0,3},{1,2},{2,1},{3,0},{4,7},{5,6},{6,5},{7,4},{8,11},{9,10},{10,... | collective-permute-start | bytes 393224 | tf_op jit(solution)/shard_map/ppermute | solution.py:309

commit v8 on v7

--- a/solution.py
+++ b/solution.py
@@ -142,7 +142,7 @@
 
 
 def rest_body(z_ref, place_ref, x_ref, w_hbm, *refs):
-    second, upper, lower, own, unsort, w_buf, sem = refs
+    *second, upper, lower, own, unsort, w_buf, sem = refs
     z = z_ref[0]
     width = own.shape[1]
     blocks = (jnp.where(z < 2, 2, 1), z ^ 1, z)
@@ -152,12 +152,12 @@
         copies.append(pltpu.make_async_copy(w_hbm.at[:, pl.ds(column, width)], w_buf.at[k], sem.at[k]))
         copies[k].start()
     unsort_matrix(place_ref, unsort)
-    x = x_ref[...]
-    half = upper.shape[0]
-    for k, outs in enumerate(((second,), (upper, lower), (own,))):
+    for k, outs in enumerate((second, (upper, lower), (own,))):
         copies[k].wait()
-        for i, out in enumerate(outs):
-            out[...] = dot(x[i * half:] if len(outs) == 1 else x[i * half:(i + 1) * half], w_buf[k]).astype(bf16)
+        at = 0
+        for out in outs:
+            out[...] = dot(x_ref[at:at + out.shape[0], :], w_buf[k]).astype(bf16)
+            at += out.shape[0]
 
 
 def unsort_matrix(place_ref, unsort):
@@ -171,7 +171,7 @@
 def rest(z, place, x, weight, width, total):
     rows, features = x.shape
     smem, vmem, hbm = (pl.BlockSpec(memory_space=m) for m in (pltpu.SMEM, pltpu.VMEM, pltpu.HBM))
-    shapes = [jax.ShapeDtypeStruct((r, width), bf16) for r in (rows, rows // 2, rows // 2, rows)]
+    shapes = [jax.ShapeDtypeStruct((r, width), bf16) for r in (rows // 2, rows // 2, rows // 4, rows - rows // 4, rows)]
     shapes.append(jax.ShapeDtypeStruct((rows, total), bf16))
     return pl.pallas_call(
         rest_body,
@@ -268,33 +268,35 @@
     )(one, two, up, *parts)
 
 
-def finish_body(count, halves, unsort_ref, *refs):
-    deltas, sums, out = refs[:count], refs[count:-1], refs[-1]
+def finish_body(count, pieces, unsort_ref, *refs):
+    deltas, rest, out = refs[:count], refs[count:-1], refs[-1]
     rows = out.shape[0]
-    whole = sums[:len(sums) - len(halves)]
-    parts = [[], []]
-    for ref, half in zip(sums[len(whole):], halves):
-        parts[half].append(ref)
+    step = rows // 4
     sorted_deltas = jnp.concatenate([d[...] for d in deltas], axis=0)
-    for half in range(2):
-        part = slice(half * rows // 2, (half + 1) * rows // 2)
-        total = dot(unsort_ref[part, :], sorted_deltas)
-        terms = [ref[part, :].astype(f32) for ref in whole] + [ref[...].astype(f32) for ref in parts[half]]
-        base = terms[0]
-        for term in terms[1:]:
-            base += term
-        out[part, :] = (base + total).astype(bf16)
-
-
-def finish(unsort, deltas, sums, halves=()):
-    rows, columns = sums[0].shape
-    return pl.pallas_call(
-        functools.partial(finish_body, len(deltas), [which for part, which in halves]),
+    for start in range(0, rows, step):
+        total = dot(unsort_ref[start:start + step, :], sorted_deltas)
+        base, at = None, 0
+        for number in pieces:
+            first = start
+            for ref in rest[at:at + number]:
+                if 0 <= first < ref.shape[0]:
+                    term = ref[first:first + step, :].astype(f32)
+                    base = term if base is None else base + term
+                first -= ref.shape[0]
+            at += number
+        out[start:start + step, :] = (base + total).astype(bf16)
+
+
+def finish(unsort, deltas, terms):
+    rows, total = unsort.shape
+    columns = deltas[0].shape[1]
+    return pl.pallas_call(
+        functools.partial(finish_body, len(deltas), [len(t) for t in terms]),
         out_shape=jax.ShapeDtypeStruct((rows, columns), bf16),
         compiler_params=params(),
-        cost_estimate=cost(2 * rows * unsort.shape[1] * columns, 12 * rows * columns),
+        cost_estimate=cost(2 * rows * total * columns, 12 * rows * columns),
         name="finish",
-    )(unsort, *deltas, *sums, *[part for part, which in halves])
+    )(unsort, *deltas, *[piece for t in terms for piece in t])
 
 
 def both(a, b):
@@ -336,31 +338,35 @@
     if lax.axis_size("tp") == 4:
         first = first_block(x, w)
         edge0 = [lax.ppermute(f, "tp", EDGE) for f in first]
-        second, *third, own, unsort = rest(z, after(place, parts[1], *first), x, weight, width, total)
-        edge1 = lax.ppermute(second, "tp", EDGE)
-        inner0 = [both(after(first[0], second), edge0[0])]
+        *blocks, own, unsort = rest(z, after(place, parts[1], *first), x, weight, width, total)
+        second, third = blocks[:2], blocks[2:]
+        edge1 = [lax.ppermute(s, "tp", EDGE) for s in second]
+        inner0 = [both(after(first[0], own), edge0[0])]
         early = shrink_partial(down, parts[:2] + [after(parts[2], *inner0)])
         inner0.append(both(after(first[1], early), edge0[1]))
         middle0 = [lax.ppermute(i, "tp", MIDDLE) for i in inner0]
-        inner2 = [both(after(third[0], inner0[1]), middle0[0]), both(third[1], middle0[1])]
+        quarter = third[0].shape[0]
+        inner2 = [both(after(third[0], inner0[1]), middle0[0][:quarter])]
         outer = lax.ppermute(inner2[0], "tp", OUTER)
-        mine = shrink_partial(down, [after(parts[-1], inner2[0])], [early])
+        inner1 = [both(after(second[0], inner2[0]), edge1[0])]
+        middle1 = [lax.ppermute(inner1[0], "tp", MIDDLE)]
+        mine = shrink_partial(down, [after(parts[-1], *inner1)], [early])
         edge2 = lax.ppermute(after(third[0], mine), "tp", EDGE)
-        inner1 = both(second, edge1)
-        steps, other = tp_sums(mine, inner1, inner2[1], outer)
-        middle1 = lax.ppermute(after(inner1, steps[-1]), "tp", MIDDLE)
+        inner1.append(both(second[1], edge1[1]))
+        inner2.append(both(third[1], jnp.concatenate([middle0[0][quarter:], middle0[1]], axis=0)))
+        steps, other = tp_sums(mine, inner1[1], inner2[1], outer)
         last = swap(after(inner2[1], steps[-1]), "tp", 1)
+        middle1.append(lax.ppermute(after(inner1[1], steps[-1], middle1[0]), "tp", MIDDLE))
         other = after(other, edge2)
-        sums, halves = [own, middle1], [(edge2, 0), (outer, 0), (last, 1)]
+        sums = [[own], middle1, [edge2, last], [outer]]
     else:
         unsort = unsort_only(place, total)
         full = dot(x, weight).astype(bf16)
-        sums = [lax.psum_scatter(full, "tp", scatter_dimension=1, tiled=True)]
-        halves = []
+        sums = [[lax.psum_scatter(full, "tp", scatter_dimension=1, tiled=True)]]
         steps, other = tp_sums(shrink_partial(down, parts))
     deltas = expand(steps[-1], other, up, parts)
     back = [deltas[0]] + [swap(deltas[j], "ad", j) for j in range(1, holders)]
-    return finish(unsort, back, sums, halves)
+    return finish(unsort, back, sums)
 
 
 def solution(mesh):

time: 57 us -> 60.7 us (1.065)
  the two profiles are of different devices: /device:TPU:13 before, /device:TPU:17 now
where the time goes in v8:
time: 60.7 us; the launch traced here: 60.5 us
  starting transfers between devices  31.9 us (53%)
  Pallas kernels  14.1 us (23%)
  waiting for transfers between devices  13.9 us (23%)
    ppermute x9, starting transfers between devices, swap(): lax.ppermute(value, axis, [(i, i ^ bit) for i in range(lax.axis_size(axis...  12 us
    ppermute x9, waiting for transfers between devices, swap(): lax.ppermute(value, axis, [(i, i ^ bit) for i in range(lax.axis_size(axis...  10.8 us
    pallas_call x1, Pallas kernels, rest(): pl.pallas_call(rest_body, out_shape=shapes, in_specs=[smem, vmem, vmem, h...  5.53 us
    ppermute x2, starting transfers between devices, shards(): middle0 = [lax.ppermute(i, 'tp', MIDDLE) for i in inner0]  4.24 us
    ppermute x1, starting transfers between devices, shards(): outer = lax.ppermute(inner2[0], 'tp', OUTER)  4.01 us
    pallas_call x1, Pallas kernels, sort_rows(): pl.pallas_call(functools.partial(sort_body, slots, capacity, holders), ou...  3.9 us
    ppermute x1, starting transfers between devices, shards(): middle1 = [lax.ppermute(inner1[0], 'tp', MIDDLE)]  3.25 us
    ppermute x2, starting transfers between devices, shards(): edge0 = [lax.ppermute(f, 'tp', EDGE) for f in first]  2.58 us
  transfers between devices with their start and end apart: 19, of which 9 were waited for; matrix products, arithmetic and copies ran while one was open for 1% of the time, Pallas kernels for 15%

profile of v8, /device:TPU:17, one launch (start us, length us, event | category | flops | bytes accessed | tf_op | source)
XLA Modules:
  0.0 60.5 jit_solution(12972473984676900956)
XLA Ops:
  0.0 3.9 %sort_rows.1 = (s32[8,512]{1,0:T(8,128)S(1)}, bf16[128,2176]{1,0:T(8,128)(2,1)S(1)}, bf16[128,2176]{1,0:T(8,128)(2,1)S(1)}, bf16[128,2176]{1,0:T(8,128)(2,1)S(1)...) custom-call(s32[1]{0:T(128)} %bitcast.1.me_ref, s32[1]{0:T(128)} %bitcast.z_ref, ...), custom_call_target="tpu_custom_call" | custom-call | flops 1073741824 | bytes 4194304 | tf_op jit(solution)/shard_map/sort_rows/pallas_call | solution.py:109
  4.7 1.2 %collective-permute-start.1 = (bf16[128,2176]{1,0:T(8,128)(2,1)S(1)}, bf16[128,2176]{1,0:T(8,128)(2,1)S(1)}, u32[]{:S(2)}, u32[]{:S(2)}) collective-permute-start(bf16[128,2176]{1,0:T(8,128)(2,1)S(1)} %get-tuple-element.45), channel_id=1, source_target_pairs={{0,2},{1,3},{2,0},{3,1},{4,6},{5,7},{6,4},{7,5},{8,10},{9,11},{10,... | collective-permute-start | bytes 1671176 | tf_op jit(solution)/shard_map/ppermute | solution.py:311
  5.9 1.2 %first_block.1 = (bf16[256,512]{1,0:T(8,128)(2,1)S(1)}, bf16[256,512]{1,0:T(8,128)(2,1)S(1)}) custom-call(bf16[512,2048]{1,0:T(8,128)(2,1)S(1)} %get-tuple-element.38.x_ref, bf16[2048,512]{1,0:T(8,128)(2,1)S(1)} %get-tuple-element.39.w_ref), custom_call_target="tpu_custom_call" | custom-call | flops 1073741824 | bytes 4194304 | tf_op jit(solution)/shard_map/first_block/pallas_call | solution.py:135
  7.1 1.3 %collective-permute-start.2 = (bf16[256,512]{1,0:T(8,128)(2,1)S(1)}, bf16[256,512]{1,0:T(8,128)(2,1)S(1)}, u32[]{:S(2)}, u32[]{:S(2)}) collective-permute-start(bf16[256,512]{1,0:T(8,128)(2,1)S(1)} %get-tuple-element.47), channel_id=1, source_target_pairs={{0,4},{12,8},{1,5},{13,9},{2,6},{14,10},{3,7},{15,11},{16,20},{28,... | collective-permute-start | bytes 786440 | tf_op jit(solution)/shard_map/ppermute | solution.py:340
  8.4 1.3 %collective-permute-start.4 = (bf16[256,512]{1,0:T(8,128)(2,1)S(1)}, bf16[256,512]{1,0:T(8,128)(2,1)S(1)}, u32[]{:S(2)}, u32[]{:S(2)}) collective-permute-start(bf16[256,512]{1,0:T(8,128)(2,1)S(1)} %get-tuple-element.52), channel_id=1, source_target_pairs={{0,4},{12,8},{1,5},{13,9},{2,6},{14,10},{3,7},{15,11},{16,20},{28,... | collective-permute-start | bytes 786440 | tf_op jit(solution)/shard_map/ppermute | solution.py:340
  10.3 5.5 %rest.1 = (bf16[256,512]{1,0:T(8,128)(2,1)S(1)}, bf16[256,512]{1,0:T(8,128)(2,1)S(1)}, bf16[128,512]{1,0:T(8,128)(2,1)S(1)}, bf16[384,512]{1,0:T(8,128)(2,1)S(1)...) custom-call(s32[1]{0:T(128)} %bitcast.z_ref, s32[8,512]{1,0:T(8,128)S(1)} %get-tuple-element.42.place_ref, ...), custom_call_target="tpu_custom_call" | custom-call | flops 3221225472 | bytes 10485760 | tf_op jit(solution)/shard_map/rest/pallas_call | solution.py:176
  16.6 2.1 %collective-permute-start.5 = (bf16[256,512]{1,0:T(8,128)(2,1)S(1)}, bf16[256,512]{1,0:T(8,128)(2,1)S(1)}, u32[]{:S(2)}, u32[]{:S(2)}) collective-permute-start(bf16[256,512]{1,0:T(8,128)(2,1)S(1)} %add_convert_fusion.4), channel_id=1, source_target_pairs={{4,8},{8,4},{5,9},{9,5},{6,10},{10,6},{7,11},{11,7},{20,24},{24,20... | collective-permute-start | bytes 786440 | tf_op jit(solution)/shard_map/ppermute | solution.py:347
  18.9 1.1 %shrink_partial.2.refs_0_ = bf16[192,128]{1,0:T(8,128)(2,1)S(1)} custom-call(bf16[2048,512]{1,0:T(8,128)(2,1)S(1)} %copy-done, bf16[128,2176]{1,0:T(8,128)(2,1)S(1)} %get-tuple-element.44.refs_0_, bf16[128,2176]{1,0:T(8,128)(2,1)S(1)} %collective-permute-done.refs_1_, bf16[128,2176]{1,0:T(8,128)(2,1)S(1)} %collective-permute-done.1.refs_2_), custom_call_target="tpu_custom_call" | custom-call | flops 805306368 | bytes 3670016 | tf_op jit(solution)/shard_map/shrink_partial/pallas_call | solution.py:226
  19.9 1.3 %collective-permute-start.6 = (bf16[256,512]{1,0:T(8,128)(2,1)S(1)}, bf16[256,512]{1,0:T(8,128)(2,1)S(1)}, u32[]{:S(2)}, u32[]{:S(2)}) collective-permute-start(bf16[256,512]{1,0:T(8,128)(2,1)S(1)} %get-tuple-element.54), channel_id=1, source_target_pairs={{0,4},{12,8},{1,5},{13,9},{2,6},{14,10},{3,7},{15,11},{16,20},{28,... | collective-permute-start | bytes 786440 | tf_op jit(solution)/shard_map/ppermute | solution.py:343
  22.3 2.2 %collective-permute-start.8 = (bf16[256,512]{1,0:T(8,128)(2,1)S(1)}, bf16[256,512]{1,0:T(8,128)(2,1)S(1)}, u32[]{:S(2)}, u32[]{:S(2)}) collective-permute-start(bf16[256,512]{1,0:T(8,128)(2,1)S(1)} %add_convert_fusion.3), channel_id=1, source_target_pairs={{4,8},{8,4},{5,9},{9,5},{6,10},{10,6},{7,11},{11,7},{20,24},{24,20... | collective-permute-start | bytes 786440 | tf_op jit(solution)/shard_map/ppermute | solution.py:347
  24.4 1.3 %collective-permute-start.7 = (bf16[256,512]{1,0:T(8,128)(2,1)S(1)}, bf16[256,512]{1,0:T(8,128)(2,1)S(1)}, u32[]{:S(2)}, u32[]{:S(2)}) collective-permute-start(bf16[256,512]{1,0:T(8,128)(2,1)S(1)} %get-tuple-element.56), channel_id=1, source_target_pairs={{0,4},{12,8},{1,5},{13,9},{2,6},{14,10},{3,7},{15,11},{16,20},{28,... | collective-permute-start | bytes 786440 | tf_op jit(solution)/shard_map/ppermute | solution.py:343
  25.8 4.0 %collective-permute-start.9 = (bf16[128,512]{1,0:T(8,128)(2,1)S(1)}, bf16[128,512]{1,0:T(8,128)(2,1)S(1)}, u32[]{:S(2)}, u32[]{:S(2)}) collective-permute-start(bf16[128,512]{1,0:T(8,128)(2,1)S(1)} %add_convert_fusion.5), channel_id=1, source_target_pairs={{4,0},{8,12},{5,1},{9,13},{6,2},{10,14},{7,3},{11,15},{20,16},{24,... | collective-permute-start | bytes 393224 | tf_op jit(solution)/shard_map/ppermute | solution.py:350
  29.9 3.3 %collective-permute-start.16 = (bf16[256,512]{1,0:T(8,128)(2,1)S(1)}, bf16[256,512]{1,0:T(8,128)(2,1)S(1)}, u32[]{:S(2)}, u32[]{:S(2)}) collective-permute-start(bf16[256,512]{1,0:T(8,128)(2,1)S(1)} %add_convert_fusion.2), channel_id=1, source_target_pairs={{4,8},{8,4},{5,9},{9,5},{6,10},{10,6},{7,11},{11,7},{20,24},{24,20... | collective-permute-start | bytes 786440 | tf_op jit(solution)/shard_map/ppermute | solution.py:352
  33.9 1.3 %collective-permute-start.12 = (bf16[128,512]{1,0:T(8,128)(2,1)S(1)}, bf16[128,512]{1,0:T(8,128)(2,1)S(1)}, u32[]{:S(2)}, u32[]{:S(2)}) collective-permute-start(bf16[128,512]{1,0:T(8,128)(2,1)S(1)} %get-tuple-element.59), channel_id=1, source_target_pairs={{0,4},{12,8},{1,5},{13,9},{2,6},{14,10},{3,7},{15,11},{16,20},{28,... | collective-permute-start | bytes 393224 | tf_op jit(solution)/shard_map/ppermute | solution.py:354
  35.4 1.5 %collective-permute-done.10 = bf16[256,128]{1,0:T(8,128)(2,1)S(1)} collective-permute-done((bf16[256,128]{1,0:T(8,128)(2,1)S(1)}, bf16[256,128]{1,0:T(8,128)(2,1)S(1)}, u32[]{:S(2)}, u32[]{:S(2)}) %collective-permute-start.10) | collective-permute-done | bytes 65568 | tf_op jit(solution)/shard_map/ppermute | solution.py:311
  36.9 2.4 %collective-permute-start.11 = (bf16[256,128]{1,0:T(8,128)(2,1)S(1)}, bf16[256,128]{1,0:T(8,128)(2,1)S(1)}, u32[]{:S(2)}, u32[]{:S(2)}) collective-permute-start(bf16[256,128]{1,0:T(8,128)(2,1)S(1)} %add_convert_fusion.6.one_ref), channel_id=1, source_target_pairs={{0,8},{4,12},{8,0},{12,4},{1,9},{5,13},{9,1},{13,5},{2,10},{6,14},... | collective-permute-start | bytes 196616 | tf_op jit(solution)/shard_map/ppermute | solution.py:311
  39.3 1.3 %collective-permute-done.12.refs_7_ = bf16[128,512]{1,0:T(8,128)(2,1)S(1)} collective-permute-done((bf16[128,512]{1,0:T(8,128)(2,1)S(1)}, bf16[128,512]{1,0:T(8,128)(2,1)S(1)}, u32[]{:S(2)}, u32[]{:S(2)}) %collective-permute-start.12) | collective-permute-done | bytes 131104 | tf_op jit(solution)/shard_map/ppermute | solution.py:354
  40.6 2.8 %collective-permute-done.11.two_ref = bf16[256,128]{1,0:T(8,128)(2,1)S(1)} collective-permute-done((bf16[256,128]{1,0:T(8,128)(2,1)S(1)}, bf16[256,128]{1,0:T(8,128)(2,1)S(1)}, u32[]{:S(2)}, u32[]{:S(2)}) %collective-permute-start.11) | collective-permute-done | bytes 65568 | tf_op jit(solution)/shard_map/ppermute | solution.py:311
  43.4 1.9 %collective-permute-start.17 = (bf16[256,512]{1,0:T(8,128)(2,1)S(1)}, bf16[256,512]{1,0:T(8,128)(2,1)S(1)}, u32[]{:S(2)}, u32[]{:S(2)}) collective-permute-start(bf16[256,512]{1,0:T(8,128)(2,1)S(1)} %add_convert_fusion.1), channel_id=1, source_target_pairs={{4,8},{8,4},{5,9},{9,5},{6,10},{10,6},{7,11},{11,7},{20,24},{24,20... | collective-permute-start | bytes 786440 | tf_op jit(solution)/shard_map/ppermute | solution.py:359
  45.8 5.3 %collective-permute-start.13 = (bf16[128,512]{1,0:T(8,128)(2,1)S(1)}, bf16[128,512]{1,0:T(8,128)(2,1)S(1)}, u32[]{:S(2)}, u32[]{:S(2)}) collective-permute-start(bf16[128,512]{1,0:T(8,128)(2,1)S(1)} %get-tuple-element.62), channel_id=1, source_target_pairs={{0,1},{1,0},{2,3},{3,2},{4,5},{5,4},{6,7},{7,6},{8,9},{9,8},{10,11... | collective-permute-start | bytes 393224 | tf_op jit(solution)/shard_map/ppermute | solution.py:311
  51.8 1.1 %collective-permute-start.15 = (bf16[128,512]{1,0:T(8,128)(2,1)S(1)}, bf16[128,512]{1,0:T(8,128)(2,1)S(1)}, u32[]{:S(2)}, u32[]{:S(2)}) collective-permute-start(bf16[128,512]{1,0:T(8,128)(2,1)S(1)} %get-tuple-element.64), channel_id=1, source_target_pairs={{0,3},{1,2},{2,1},{3,0},{4,7},{5,6},{6,5},{7,4},{8,11},{9,10},{10,... | collective-permute-start | bytes 393224 | tf_op jit(solution)/shard_map/ppermute | solution.py:311
  52.8 3.4 %collective-permute-done.14.refs_2_ = bf16[128,512]{1,0:T(8,128)(2,1)S(1)} collective-permute-done((bf16[128,512]{1,0:T(8,128)(2,1)S(1)}, bf16[128,512]{1,0:T(8,128)(2,1)S(1)}, u32[]{:S(2)}, u32[]{:S(2)}) %collective-permute-start.14) | collective-permute-done | bytes 131104 | tf_op jit(solution)/shard_map/ppermute | solution.py:311
  56.2 3.0 %collective-permute-done.15.refs_3_ = bf16[128,512]{1,0:T(8,128)(2,1)S(1)} collective-permute-done((bf16[128,512]{1,0:T(8,128)(2,1)S(1)}, bf16[128,512]{1,0:T(8,128)(2,1)S(1)}, u32[]{:S(2)}, u32[]{:S(2)}) %collective-permute-start.15) | collective-permute-done | bytes 131104 | tf_op jit(solution)/shard_map/ppermute | solution.py:311
  59.2 1.3 %finish.1 = bf16[512,512]{1,0:T(8,128)(2,1)} custom-call(bf16[512,512]{1,0:T(8,128)(2,1)S(1)} %get-tuple-element.43.unsort_ref, bf16[128,512]{1,0:T(8,128)(2,1)S(1)} %get-tuple-element.61.refs_0_, bf16[128,512]{1,0:T(8,128)(2,1)S(1)} %collective-permute-done.13.refs_1_, bf16[128,512]{1,0:T(8,128)(2,1)S(1)} %collective-permute-done.14.refs_2_, ...), custom_call_target="tpu_custom_call" | custom-call | flops 268435456 | bytes 3145728 | tf_op jit(solution)/shard_map/finish/pallas_call | solution.py:293
  (33 shorter events, 5.4 us)
Async XLA Ops:
  3.9 6.4 %collective-permute-start = (bf16[128,2176]{1,0:T(8,128)(2,1)S(1)}, bf16[128,2176]{1,0:T(8,128)(2,1)S(1)}, u32[]{:S(2)}, u32[]{:S(2)}) collective-permute-start(bf16[128,2176]{1,0:T(8,128)(2,1)S(1)} %get-tuple-element.37), channel_id=1, source_target_pairs={{0,1},{1,0},{2,3},{3,2},{4,5},{5,4},{6,7},{7,6},{8,9},{9,8},{10,11... | collective-permute-start | bytes 1671176 | tf_op jit(solution)/shard_map/ppermute | solution.py:311
  4.7 14.2 %collective-permute-start.1 = (bf16[128,2176]{1,0:T(8,128)(2,1)S(1)}, bf16[128,2176]{1,0:T(8,128)(2,1)S(1)}, u32[]{:S(2)}, u32[]{:S(2)}) collective-permute-start(bf16[128,2176]{1,0:T(8,128)(2,1)S(1)} %get-tuple-element.45), channel_id=1, source_target_pairs={{0,2},{1,3},{2,0},{3,1},{4,6},{5,7},{6,4},{7,5},{8,10},{9,11},{10,... | collective-permute-start | bytes 1671176 | tf_op jit(solution)/shard_map/ppermute | solution.py:311
  7.1 9.4 %collective-permute-start.2 = (bf16[256,512]{1,0:T(8,128)(2,1)S(1)}, bf16[256,512]{1,0:T(8,128)(2,1)S(1)}, u32[]{:S(2)}, u32[]{:S(2)}) collective-permute-start(bf16[256,512]{1,0:T(8,128)(2,1)S(1)} %get-tuple-element.47), channel_id=1, source_target_pairs={{0,4},{12,8},{1,5},{13,9},{2,6},{14,10},{3,7},{15,11},{16,20},{28,... | collective-permute-start | bytes 786440 | tf_op jit(solution)/shard_map/ppermute | solution.py:340
  8.4 13.8 %collective-permute-start.4 = (bf16[256,512]{1,0:T(8,128)(2,1)S(1)}, bf16[256,512]{1,0:T(8,128)(2,1)S(1)}, u32[]{:S(2)}, u32[]{:S(2)}) collective-permute-start(bf16[256,512]{1,0:T(8,128)(2,1)S(1)} %get-tuple-element.52), channel_id=1, source_target_pairs={{0,4},{12,8},{1,5},{13,9},{2,6},{14,10},{3,7},{15,11},{16,20},{28,... | collective-permute-start | bytes 786440 | tf_op jit(solution)/shard_map/ppermute | solution.py:340
  9.7 23.4 %collective-permute-start.3 = (bf16[128,2176]{1,0:T(8,128)(2,1)S(1)}, bf16[128,2176]{1,0:T(8,128)(2,1)S(1)}, u32[]{:S(2)}, u32[]{:S(2)}) collective-permute-start(bf16[128,2176]{1,0:T(8,128)(2,1)S(1)} %get-tuple-element.49), channel_id=1, source_target_pairs={{0,3},{1,2},{2,1},{3,0},{4,7},{5,6},{6,5},{7,4},{8,11},{9,10},{10,... | collective-permute-start | bytes 1671176 | tf_op jit(solution)/shard_map/ppermute | solution.py:311
  10.3 8.6 %copy-start = (bf16[2048,512]{1,0:T(8,128)(2,1)S(1)}, bf16[2048,512]{1,0:T(8,128)(2,1)}, u32[]{:S(2)}) copy-start(bf16[2048,512]{1,0:T(8,128)(2,1)} %down_ref.3) | copy-start | bytes 6291460
  16.6 9.1 %collective-permute-start.5 = (bf16[256,512]{1,0:T(8,128)(2,1)S(1)}, bf16[256,512]{1,0:T(8,128)(2,1)S(1)}, u32[]{:S(2)}, u32[]{:S(2)}) collective-permute-start(bf16[256,512]{1,0:T(8,128)(2,1)S(1)} %add_convert_fusion.4), channel_id=1, source_target_pairs={{4,8},{8,4},{5,9},{9,5},{6,10},{10,6},{7,11},{11,7},{20,24},{24,20... | collective-permute-start | bytes 786440 | tf_op jit(solution)/shard_map/ppermute | solution.py:347
  19.9 9.8 %collective-permute-start.6 = (bf16[256,512]{1,0:T(8,128)(2,1)S(1)}, bf16[256,512]{1,0:T(8,128)(2,1)S(1)}, u32[]{:S(2)}, u32[]{:S(2)}) collective-permute-start(bf16[256,512]{1,0:T(8,128)(2,1)S(1)} %get-tuple-element.54), channel_id=1, source_target_pairs={{0,4},{12,8},{1,5},{13,9},{2,6},{14,10},{3,7},{15,11},{16,20},{28,... | collective-permute-start | bytes 786440 | tf_op jit(solution)/shard_map/ppermute | solution.py:343
  22.3 13.0 %collective-permute-start.8 = (bf16[256,512]{1,0:T(8,128)(2,1)S(1)}, bf16[256,512]{1,0:T(8,128)(2,1)S(1)}, u32[]{:S(2)}, u32[]{:S(2)}) collective-permute-start(bf16[256,512]{1,0:T(8,128)(2,1)S(1)} %add_convert_fusion.3), channel_id=1, source_target_pairs={{4,8},{8,4},{5,9},{9,5},{6,10},{10,6},{7,11},{11,7},{20,24},{24,20... | collective-permute-start | bytes 786440 | tf_op jit(solution)/shard_map/ppermute | solution.py:347
  24.4 9.5 %collective-permute-start.7 = (bf16[256,512]{1,0:T(8,128)(2,1)S(1)}, bf16[256,512]{1,0:T(8,128)(2,1)S(1)}, u32[]{:S(2)}, u32[]{:S(2)}) collective-permute-start(bf16[256,512]{1,0:T(8,128)(2,1)S(1)} %get-tuple-element.56), channel_id=1, source_target_pairs={{0,4},{12,8},{1,5},{13,9},{2,6},{14,10},{3,7},{15,11},{16,20},{28,... | collective-permute-start | bytes 786440 | tf_op jit(solution)/shard_map/ppermute | solution.py:343
  25.8 9.6 %collective-permute-start.9 = (bf16[128,512]{1,0:T(8,128)(2,1)S(1)}, bf16[128,512]{1,0:T(8,128)(2,1)S(1)}, u32[]{:S(2)}, u32[]{:S(2)}) collective-permute-start(bf16[128,512]{1,0:T(8,128)(2,1)S(1)} %add_convert_fusion.5), channel_id=1, source_target_pairs={{4,0},{8,12},{5,1},{9,13},{6,2},{10,14},{7,3},{11,15},{20,16},{24,... | collective-permute-start | bytes 393224 | tf_op jit(solution)/shard_map/ppermute | solution.py:350
  29.9 15.4 %copy-start.1 = (bf16[512,512]{1,0:T(8,128)(2,1)S(1)}, bf16[512,512]{1,0:T(8,128)(2,1)}, u32[]{:S(2)}) copy-start(bf16[512,512]{1,0:T(8,128)(2,1)} %up_ref.1) | copy-start | bytes 1572868
  29.9 13.5 %collective-permute-start.16 = (bf16[256,512]{1,0:T(8,128)(2,1)S(1)}, bf16[256,512]{1,0:T(8,128)(2,1)S(1)}, u32[]{:S(2)}, u32[]{:S(2)}) collective-permute-start(bf16[256,512]{1,0:T(8,128)(2,1)S(1)} %add_convert_fusion.2), channel_id=1, source_target_pairs={{4,8},{8,4},{5,9},{9,5},{6,10},{10,6},{7,11},{11,7},{20,24},{24,20... | collective-permute-start | bytes 786440 | tf_op jit(solution)/shard_map/ppermute | solution.py:352
  33.7 3.2 %collective-permute-start.10 = (bf16[256,128]{1,0:T(8,128)(2,1)S(1)}, bf16[256,128]{1,0:T(8,128)(2,1)S(1)}, u32[]{:S(2)}, u32[]{:S(2)}) collective-permute-start(bf16[256,128]{1,0:T(8,128)(2,1)S(1)} %shrink_partial.3), channel_id=1, source_target_pairs={{0,4},{4,0},{8,12},{12,8},{1,5},{5,1},{9,13},{13,9},{2,6},{6,2},{1... | collective-permute-start | bytes 196616 | tf_op jit(solution)/shard_map/ppermute | solution.py:311
  33.9 6.7 %collective-permute-start.12 = (bf16[128,512]{1,0:T(8,128)(2,1)S(1)}, bf16[128,512]{1,0:T(8,128)(2,1)S(1)}, u32[]{:S(2)}, u32[]{:S(2)}) collective-permute-start(bf16[128,512]{1,0:T(8,128)(2,1)S(1)} %get-tuple-element.59), channel_id=1, source_target_pairs={{0,4},{12,8},{1,5},{13,9},{2,6},{14,10},{3,7},{15,11},{16,20},{28,... | collective-permute-start | bytes 393224 | tf_op jit(solution)/shard_map/ppermute | solution.py:354
  36.9 6.5 %collective-permute-start.11 = (bf16[256,128]{1,0:T(8,128)(2,1)S(1)}, bf16[256,128]{1,0:T(8,128)(2,1)S(1)}, u32[]{:S(2)}, u32[]{:S(2)}) collective-permute-start(bf16[256,128]{1,0:T(8,128)(2,1)S(1)} %add_convert_fusion.6.one_ref), channel_id=1, source_target_pairs={{0,8},{4,12},{8,0},{12,4},{1,9},{5,13},{9,1},{13,5},{2,10},{6,14},... | collective-permute-start | bytes 196616 | tf_op jit(solution)/shard_map/ppermute | solution.py:311
  39.3 19.8 %collective-permute-start.18 = (bf16[384,512]{1,0:T(8,128)(2,1)S(1)}, bf16[384,512]{1,0:T(8,128)(2,1)S(1)}, u32[]{:S(2)}, u32[]{:S(2)}) collective-permute-start(bf16[384,512]{1,0:T(8,128)(2,1)S(1)} %add_convert_fusion), channel_id=1, source_target_pairs={{0,4},{4,0},{8,12},{12,8},{1,5},{5,1},{9,13},{13,9},{2,6},{6,2},{1... | collective-permute-start | bytes 1179656 | tf_op jit(solution)/shard_map/ppermute | solution.py:311
  43.4 15.8 %collective-permute-start.17 = (bf16[256,512]{1,0:T(8,128)(2,1)S(1)}, bf16[256,512]{1,0:T(8,128)(2,1)S(1)}, u32[]{:S(2)}, u32[]{:S(2)}) collective-permute-start(bf16[256,512]{1,0:T(8,128)(2,1)S(1)} %add_convert_fusion.1), channel_id=1, source_target_pairs={{4,8},{8,4},{5,9},{9,5},{6,10},{10,6},{7,11},{11,7},{20,24},{24,20... | collective-permute-start | bytes 786440 | tf_op jit(solution)/shard_map/ppermute | solution.py:359
  45.8 7.0 %collective-permute-start.13 = (bf16[128,512]{1,0:T(8,128)(2,1)S(1)}, bf16[128,512]{1,0:T(8,128)(2,1)S(1)}, u32[]{:S(2)}, u32[]{:S(2)}) collective-permute-start(bf16[128,512]{1,0:T(8,128)(2,1)S(1)} %get-tuple-element.62), channel_id=1, source_target_pairs={{0,1},{1,0},{2,3},{3,2},{4,5},{5,4},{6,7},{7,6},{8,9},{9,8},{10,11... | collective-permute-start | bytes 393224 | tf_op jit(solution)/shard_map/ppermute | solution.py:311
  51.1 5.1 %collective-permute-start.14 = (bf16[128,512]{1,0:T(8,128)(2,1)S(1)}, bf16[128,512]{1,0:T(8,128)(2,1)S(1)}, u32[]{:S(2)}, u32[]{:S(2)}) collective-permute-start(bf16[128,512]{1,0:T(8,128)(2,1)S(1)} %get-tuple-element.63), channel_id=1, source_target_pairs={{0,2},{1,3},{2,0},{3,1},{4,6},{5,7},{6,4},{7,5},{8,10},{9,11},{10,... | collective-permute-start | bytes 393224 | tf_op jit(solution)/shard_map/ppermute | solution.py:311
  51.8 7.4 %collective-permute-start.15 = (bf16[128,512]{1,0:T(8,128)(2,1)S(1)}, bf16[128,512]{1,0:T(8,128)(2,1)S(1)}, u32[]{:S(2)}, u32[]{:S(2)}) collective-permute-start(bf16[128,512]{1,0:T(8,128)(2,1)S(1)} %get-tuple-element.64), channel_id=1, source_target_pairs={{0,3},{1,2},{2,1},{3,0},{4,7},{5,6},{6,5},{7,4},{8,11},{9,10},{10,... | collective-permute-start | bytes 393224 | tf_op jit(solution)/shard_map/ppermute | solution.py:311

commit v9 on v4

--- a/solution.py
+++ b/solution.py
@@ -9,6 +9,7 @@
 
 ADAPTER_RANK = 64
 LANES = 128
+NEAR = 2
 VMEM_BYTES = 32 * 1024 * 1024
 
 bf16 = jnp.bfloat16
@@ -36,66 +37,80 @@
     return lax.broadcasted_iota(i32, shape, dim)
 
 
-def places(slots, capacity, holders, me, ids, table, earlier):
+def places(slots, capacity, holders, me, ids, table):
     rows = ids.shape[1]
     low = (iota((LANES, rows), 0) == (ids & (LANES - 1))).astype(f32).astype(bf16)
     high = iota((table.shape[0], rows), 0) == lax.shift_right_logical(ids, 7)
     found = dot(table.astype(f32).astype(bf16), low)
     slot = jnp.sum(jnp.where(high, found, 0.0), axis=0, keepdims=True).astype(i32)
-    holder = lax.div(slot, slots)
+    holder = split_slot(slot, slots)
     tag = (slot - holder * slots + 1).astype(f32)
     partner = holder ^ me
     mine = iota((max(8, holders), rows), 0) == partner
-    before = dot(mine.astype(f32).astype(bf16), earlier)
-    rank = jnp.sum(jnp.where(mine, before, 0.0), axis=0, keepdims=True).astype(i32)
-    return partner * capacity + rank, tag
-
-
-def sort_body(slots, capacity, holders, me_ref, z_ref, ids_hbm, table_hbm, x_hbm, w_hbm, place_ref, *refs):
-    outs, (x_buf, w_buf, ids_buf, table_buf, small_sem, x_sem, w_sem) = refs[:holders], refs[holders:]
-    rows, features = x_buf.shape
+    ones = mine.astype(f32)
+    groups = [ones[:, k:k + LANES] for k in range(0, rows, LANES)]
+    earlier = (iota((LANES, LANES), 0) < iota((LANES, LANES), 1)).astype(f32).astype(bf16)
+    before = dot(jnp.concatenate(groups, axis=0).astype(bf16), earlier)
+    count = ones.shape[0]
+    ranks, passed = [], jnp.zeros((count, 1), f32)
+    for k, group in enumerate(groups):
+        ranks.append(jnp.sum(group * (before[k * count:(k + 1) * count] + passed), axis=0, keepdims=True))
+        passed += jnp.sum(group, axis=1, keepdims=True)
+    return partner * capacity + jnp.concatenate(ranks, axis=1).astype(i32), tag
+
+
+def split_slot(slot, slots):
+    if slots & (slots - 1):
+        return lax.div(slot, slots)
+    return lax.shift_right_logical(slot, slots.bit_length() - 1)
+
+
+def pick_rows(start, place, tag, x, outs):
+    rows, features = x.shape
+    capacity = outs[0].shape[0]
+    pick = iota((len(outs) * capacity, rows), 0) + start * capacity == place
+    pick = pick.astype(f32).astype(bf16)
+    tags = dot(pick, jnp.broadcast_to(tag, (LANES, rows)).astype(bf16), ((1,), (1,))).astype(bf16)
+    step = min(512, features)
+    for c in range(0, features, step):
+        moved = dot(pick, x[:, c:c + step]).astype(bf16)
+        for j, out in enumerate(outs):
+            out[:, c:c + step] = moved[j * capacity:(j + 1) * capacity]
+    for j, out in enumerate(outs):
+        out[:, features:] = tags[j * capacity:(j + 1) * capacity]
+
+
+def far_body(slots, capacity, holders, me_ref, z_ref, ids_hbm, table_hbm, x_hbm, w_hbm, places_ref, *refs):
+    outs, (x_buf, w_buf, ids_buf, table_buf, small_sem, x_sem, w_sem) = refs[:holders - NEAR], refs[holders - NEAR:]
     width = w_buf.shape[1]
-    chunks = x_sem.shape[0]
-    step = features // chunks
     small = [
         pltpu.make_async_copy(ids_hbm, ids_buf, small_sem.at[0]),
         pltpu.make_async_copy(table_hbm, table_buf, small_sem.at[1]),
     ]
-    copies = []
-    for c in range(chunks):
-        part = pl.ds(c * step, step)
-        copies.append(pltpu.make_async_copy(x_hbm.at[:, part], x_buf.at[:, part], x_sem.at[c]))
+    x_copy = pltpu.make_async_copy(x_hbm, x_buf, x_sem)
     column = pl.multiple_of(jnp.where(z_ref[0] < 2, 3, 0) * width, width)
     w_copy = pltpu.make_async_copy(w_hbm.at[:, pl.ds(column, width)], w_buf, w_sem)
-    for copy in small + copies + [w_copy]:
+    for copy in small + [x_copy, w_copy]:
         copy.start()
-    earlier = (iota((rows, rows), 0) < iota((rows, rows), 1)).astype(f32).astype(bf16)
     for copy in small:
         copy.wait()
-    place, tag = places(slots, capacity, holders, me_ref[0], ids_buf[...], table_buf[...], earlier)
-    place_ref[...] = jnp.broadcast_to(place, place_ref.shape)
-    pick = (iota((holders * capacity, rows), 0) == place).astype(f32).astype(bf16)
-    tags = dot(pick, jnp.broadcast_to(tag, (LANES, rows)).astype(bf16), ((1,), (1,))).astype(bf16)
-    for j, out in enumerate(outs):
-        out[:, features:] = tags[j * capacity:(j + 1) * capacity]
-    for c in range(chunks):
-        copies[c].wait()
-        moved = dot(pick, x_buf[:, c * step:(c + 1) * step]).astype(bf16)
-        for j, out in enumerate(outs):
-            out[:, c * step:(c + 1) * step] = moved[j * capacity:(j + 1) * capacity]
+    place, tag = places(slots, capacity, holders, me_ref[0], ids_buf[...], table_buf[...])
+    row = iota(places_ref.shape, 0)
+    places_ref[...] = jnp.where(row == 0, place, jnp.where(row == 1, tag.astype(i32), 0))
+    x_copy.wait()
+    pick_rows(NEAR, place, tag, x_buf, outs)
     w_copy.wait()
 
 
-def sort_rows(me, z, ids, table, x, weight, holders, slots, capacity, width):
+def far_rows(me, z, ids, table, x, weight, holders, slots, capacity, width):
     rows, features = x.shape
     ids, table = ids.reshape(1, rows), table.reshape(-1, LANES)
-    chunks = max(1, features // 512)
     smem, vmem, hbm = (pl.BlockSpec(memory_space=m) for m in (pltpu.SMEM, pltpu.VMEM, pltpu.HBM))
     shapes = [jax.ShapeDtypeStruct((8, rows), i32)]
-    shapes += [jax.ShapeDtypeStruct((capacity, features + LANES), bf16)] * holders
+    shapes += [jax.ShapeDtypeStruct((capacity, features + LANES), bf16)] * (holders - NEAR)
     shapes += [jax.ShapeDtypeStruct((rows, features), bf16), jax.ShapeDtypeStruct((features, width), bf16)]
     return pl.pallas_call(
-        functools.partial(sort_body, slots, capacity, holders),
+        functools.partial(far_body, slots, capacity, holders),
         out_shape=shapes,
         in_specs=[smem, smem, hbm, hbm, hbm, hbm],
         out_specs=[vmem] * len(shapes),
@@ -103,13 +118,28 @@
             pltpu.VMEM(ids.shape, i32),
             pltpu.VMEM(table.shape, i32),
             pltpu.SemaphoreType.DMA((2,)),
-            pltpu.SemaphoreType.DMA((chunks,)),
+            pltpu.SemaphoreType.DMA(()),
             pltpu.SemaphoreType.DMA(()),
         ],
         compiler_params=params(),
         cost_estimate=cost(2 * holders * capacity * rows * features, 4 * rows * features),
-        name="sort_rows",
+        name="far_rows",
     )(me.reshape(1), z.reshape(1), in_hbm(ids), in_hbm(table), in_hbm(x), in_hbm(weight))
+
+
+def near_body(places_ref, x_ref, *outs):
+    pick_rows(0, places_ref[0:1, :], places_ref[1:2, :].astype(f32), x_ref, outs)
+
+
+def near_rows(spots, x, capacity):
+    rows, features = x.shape
+    return pl.pallas_call(
+        near_body,
+        out_shape=[jax.ShapeDtypeStruct((capacity, features + LANES), bf16)] * NEAR,
+        compiler_params=params(),
+        cost_estimate=cost(2 * NEAR * capacity * rows * features, 4 * rows * features),
+        name="near_rows",
+    )(spots, x)
 
 
 def first_body(x_ref, w_ref, out):
@@ -127,21 +157,20 @@
     )(x, w)
 
 
-def rest_body(z_ref, place_ref, x_ref, w_hbm, *refs):
-    second, third, own, unsort, w_buf, sem = refs
+def rest_body(z_ref, spots_ref, x_ref, w_hbm, *refs):
+    near, (second, third, own, unsort, w_buf, sem) = refs[:NEAR], refs[NEAR:]
     z = z_ref[0]
     width = own.shape[1]
-    blocks = (jnp.where(z < 2, 2, 1), z ^ 1, z)
     copies = []
-    for k, block in enumerate(blocks):
+    for k, block in enumerate((jnp.where(z < 2, 2, 1), z ^ 1, z)):
         column = pl.multiple_of(block * width, width)
         copies.append(pltpu.make_async_copy(w_hbm.at[:, pl.ds(column, width)], w_buf.at[k], sem.at[k]))
         copies[k].start()
-    unsort_matrix(place_ref, unsort)
-    x = x_ref[...]
+    near_body(spots_ref, x_ref, *near)
+    unsort_matrix(spots_ref, unsort)
     for k, out in enumerate((second, third, own)):
         copies[k].wait()
-        out[...] = dot(x, w_buf[k]).astype(bf16)
+        out[...] = dot(x_ref[...], w_buf[k]).astype(bf16)
 
 
 def unsort_matrix(place_ref, unsort):
@@ -152,10 +181,11 @@
         unsort[:, k * LANES:(k + 1) * LANES] = (place == lane + float(k * LANES)).astype(f32).astype(bf16)
 
 
-def rest(z, place, x, weight, width, total):
+def rest(z, spots, x, weight, width, total, capacity):
     rows, features = x.shape
     smem, vmem, hbm = (pl.BlockSpec(memory_space=m) for m in (pltpu.SMEM, pltpu.VMEM, pltpu.HBM))
-    shapes = [jax.ShapeDtypeStruct((rows, width), bf16)] * 3 + [jax.ShapeDtypeStruct((rows, total), bf16)]
+    shapes = [jax.ShapeDtypeStruct((capacity, features + LANES), bf16)] * NEAR
+    shapes += [jax.ShapeDtypeStruct((rows, width), bf16)] * 3 + [jax.ShapeDtypeStruct((rows, total), bf16)]
     return pl.pallas_call(
         rest_body,
         out_shape=shapes,
@@ -165,7 +195,7 @@
         compiler_params=params(),
         cost_estimate=cost(6 * rows * features * width, 2 * features * (rows + 4 * width)),
         name="rest",
-    )(z.reshape(1), place, x, in_hbm(weight))
+    )(z.reshape(1), spots, x, in_hbm(weight))
 
 
 def unsort_only(place, total):
@@ -303,29 +333,37 @@
     width = up.shape[1]
     total = holders * capacity
     me, z = lax.axis_index("ad"), lax.axis_index("tp")
-    place, *send, x, w = sort_rows(me, z, ids, table, x, weight, holders, slots, capacity, width)
-    parts = [send[0]] + [swap(send[j], "ad", j) for j in range(1, holders)]
-    if lax.axis_size("tp") == 4:
+    spots, *far, x, w = far_rows(me, z, ids, table, x, weight, holders, slots, capacity, width)
+    far = [swap(rows, "ad", j + NEAR) for j, rows in enumerate(far)]
+    if lax.axis_size("tp") == 4 and holders == 4:
         first = first_block(x, w)
         edge0 = lax.ppermute(first, "tp", EDGE)
-        second, third, own, unsort = rest(z, after(place, first), x, weight, width, total)
+        *near, second, third, own, unsort = rest(z, after(spots, first), x, weight, width, total, capacity)
+        near = [near[0], swap(near[1], "ad", 1)]
         edge1 = lax.ppermute(second, "tp", EDGE)
-        early = shrink_partial(down, parts[:-1])
+        early = shrink_partial(down, [near[0], far[0]])
         inner0 = both(after(first, early), edge0)
         middle0 = lax.ppermute(inner0, "tp", MIDDLE)
-        mine = shrink_partial(down, [after(parts[-1], inner0)], [early])
-        inner1 = both(second, edge1)
-        steps, other = tp_sums(mine, inner1)
+        early = shrink_partial(down, [after(near[1], inner0)], [early])
+        mine = shrink_partial(down, [after(far[1], early)], [early])
+        parts, order = [near[0], far[0], near[1], far[1]], (0, 2, 1, 3)
+        inner1, inner2 = both(after(second, mine), edge1), both(third, middle0)
+        steps, other = tp_sums(mine, inner1, inner2)
+        last = swap(after(inner2, steps[-1]), "tp", 1)
         middle1 = lax.ppermute(after(inner1, steps[-1]), "tp", MIDDLE)
-        last = swap(both(after(third, steps[-1]), middle0), "tp", 1)
         sums = [own, middle1, last]
     else:
-        unsort = unsort_only(place, total)
+        near = near_rows(spots, x, capacity)
+        near = [near[0], swap(near[1], "ad", 1)]
+        parts, order = near + far, range(holders)
+        unsort = unsort_only(spots, total)
         full = dot(x, weight).astype(bf16)
         sums = [lax.psum_scatter(full, "tp", scatter_dimension=1, tiled=True)]
         steps, other = tp_sums(shrink_partial(down, parts))
     deltas = expand(steps[-1], other, up, parts)
-    back = [deltas[0]] + [swap(deltas[j], "ad", j) for j in range(1, holders)]
+    back = [None] * holders
+    for j, delta in zip(order, deltas):
+        back[j] = swap(delta, "ad", j) if j else delta
     return finish(unsort, back, sums)
 
 

time: 56.2 us -> 53.7 us (0.956)
  starting transfers between devices: 18.7 us -> 16.7 us
  Pallas kernels: 14 us -> 12.8 us
    ppermute x9, starting transfers between devices: 12.2 us -> 10.5 us  [swap(): lax.ppermute(value, axis, [(i, i ^ bit) for i in range(lax.axis_size(axis...]
    pallas_call x1, Pallas kernels: 3.89 us -> 2.46 us  [far_rows(): pl.pallas_call(functools.partial(far_body, slots, capacity, holders), out...]
    ppermute x9, waiting for transfers between devices: 20 us -> 18.5 us  [swap(): lax.ppermute(value, axis, [(i, i ^ bit) for i in range(lax.axis_size(axis...]
    ppermute x1, waiting for transfers between devices: 2.47 us -> 3.68 us  [shards(): edge0 = lax.ppermute(first, 'tp', EDGE)]
    pallas_call x2 -> x3, Pallas kernels: 1.57 us -> 1.82 us  [shrink_partial(): pl.pallas_call(functools.partial(shrink_body, kept), out_shape=jax.ShapeD...]
  transfers between devices with their start and end apart: 13 -> 13, of which waited for: 9 -> 9; matrix products, arithmetic and copies ran while one was open for 1% -> 1% of each run, Pallas kernels for 16% -> 17%
where the time goes in v9:
time: 53.7 us; the launch traced here: 53.3 us
  waiting for transfers between devices  23.1 us (43%)
  starting transfers between devices  16.7 us (31%)
  Pallas kernels  12.8 us (24%)
    ppermute x9, waiting for transfers between devices, swap(): lax.ppermute(value, axis, [(i, i ^ bit) for i in range(lax.axis_size(axis...  18.5 us
    ppermute x9, starting transfers between devices, swap(): lax.ppermute(value, axis, [(i, i ^ bit) for i in range(lax.axis_size(axis...  10.5 us
    pallas_call x1, Pallas kernels, rest(): pl.pallas_call(rest_body, out_shape=shapes, in_specs=[smem, vmem, vmem, h...  5.54 us
    ppermute x1, waiting for transfers between devices, shards(): edge0 = lax.ppermute(first, 'tp', EDGE)  3.68 us
    ppermute x1, starting transfers between devices, shards(): edge0 = lax.ppermute(first, 'tp', EDGE)  3.52 us
    pallas_call x1, Pallas kernels, far_rows(): pl.pallas_call(functools.partial(far_body, slots, capacity, holders), out...  2.46 us
    pallas_call x3, Pallas kernels, shrink_partial(): pl.pallas_call(functools.partial(shrink_body, kept), out_shape=jax.ShapeD...  1.82 us
    ppermute x1, starting transfers between devices, shards(): edge1 = lax.ppermute(second, 'tp', EDGE)  1.31 us
  transfers between devices with their start and end apart: 13, of which 9 were waited for; matrix products, arithmetic and copies ran while one was open for 1% of the time, Pallas kernels for 17%

profile of v9, /device:TPU:0, one launch (start us, length us, event | category | flops | bytes accessed | tf_op | source)
XLA Modules:
  0.0 53.3 jit_solution(1996019535920013187)
XLA Ops:
  0.0 2.5 %far_rows.1 = (s32[8,512]{1,0:T(8,128)S(1)}, bf16[128,2176]{1,0:T(8,128)(2,1)S(1)}, bf16[128,2176]{1,0:T(8,128)(2,1)S(1)}, bf16[512,2048]{1,0:T(8,128)(2,1)S(1)}, bf16[2048,512]{1,0:T(8,128)(2,1)S(1)}) custom-call(s32[1]{0:T(128)} %bitcast.1.me_ref, s32[1]{0:T(128)} %bitcast.z_ref, s32[1,512]{1,0:T(1,128)} %bitcast.5, s32[32,128]{1,0:T(8,128)} %bitcast.4, ...), custom_call_target="tpu_custom_call" | custom-call | flops 1073741824 | bytes 4194304 | tf_op jit(solution)/shard_map/far_rows/pallas_call | solution.py:112
  2.5 3.0 %collective-permute-start = (bf16[128,2176]{1,0:T(8,128)(2,1)S(1)}, bf16[128,2176]{1,0:T(8,128)(2,1)S(1)}, u32[]{:S(2)}, u32[]{:S(2)}) collective-permute-start(bf16[128,2176]{1,0:T(8,128)(2,1)S(1)} %get-tuple-element.34), channel_id=1, source_target_pairs={{0,2},{1,3},{2,0},{3,1},{4,6},{5,7},{6,4},{7,5},{8,10},{9,11},{10,... | collective-permute-start | bytes 1671176 | tf_op jit(solution)/shard_map/ppermute | solution.py:312
  5.5 1.3 %first_block.1 = bf16[512,512]{1,0:T(8,128)(2,1)S(1)} custom-call(bf16[512,2048]{1,0:T(8,128)(2,1)S(1)} %get-tuple-element.29.x_ref, bf16[2048,512]{1,0:T(8,128)(2,1)S(1)} %get-tuple-element.30.w_ref), custom_call_target="tpu_custom_call" | custom-call | flops 1073741824 | bytes 4194304 | tf_op jit(solution)/shard_map/first_block/pallas_call | solution.py:151
  6.7 3.5 %collective-permute-start.2 = (bf16[512,512]{1,0:T(8,128)(2,1)S(1)}, bf16[512,512]{1,0:T(8,128)(2,1)S(1)}, u32[]{:S(2)}, u32[]{:S(2)}) collective-permute-start(bf16[512,512]{1,0:T(8,128)(2,1)S(1)} %first_block.1), channel_id=1, source_target_pairs={{0,4},{12,8},{1,5},{13,9},{2,6},{14,10},{3,7},{15,11},{16,20},{28,... | collective-permute-start | bytes 1572872 | tf_op jit(solution)/shard_map/ppermute | solution.py:340
  10.3 5.5 %rest.1 = (bf16[128,2176]{1,0:T(8,128)(2,1)S(1)}, bf16[128,2176]{1,0:T(8,128)(2,1)S(1)}, bf16[512,512]{1,0:T(8,128)(2,1)S(1)}, bf16[512,512]{1,0:T(8,128)(2,1)S(...) custom-call(s32[1]{0:T(128)} %bitcast.z_ref, s32[8,512]{1,0:T(8,128)S(1)} %get-tuple-element.31.spots_ref, ...), custom_call_target="tpu_custom_call" | custom-call | flops 3221225472 | bytes 10485760 | tf_op jit(solution)/shard_map/rest/pallas_call | solution.py:189
  15.9 0.6 %collective-permute-start.3 = (bf16[128,2176]{1,0:T(8,128)(2,1)S(1)}, bf16[128,2176]{1,0:T(8,128)(2,1)S(1)}, u32[]{:S(2)}, u32[]{:S(2)}) collective-permute-start(bf16[128,2176]{1,0:T(8,128)(2,1)S(1)} %get-tuple-element.38), channel_id=1, source_target_pairs={{0,3},{1,2},{2,1},{3,0},{4,7},{5,6},{6,5},{7,4},{8,11},{9,10},{10,... | collective-permute-start | bytes 1671176 | tf_op jit(solution)/shard_map/ppermute | solution.py:312
  16.5 1.3 %collective-permute-start.4 = (bf16[512,512]{1,0:T(8,128)(2,1)S(1)}, bf16[512,512]{1,0:T(8,128)(2,1)S(1)}, u32[]{:S(2)}, u32[]{:S(2)}) collective-permute-start(bf16[512,512]{1,0:T(8,128)(2,1)S(1)} %get-tuple-element.41), channel_id=1, source_target_pairs={{0,4},{12,8},{1,5},{13,9},{2,6},{14,10},{3,7},{15,11},{16,20},{28,... | collective-permute-start | bytes 1572872 | tf_op jit(solution)/shard_map/ppermute | solution.py:343
  18.1 0.8 %shrink_partial.3.refs_0_ = bf16[128,128]{1,0:T(8,128)(2,1)S(1)} custom-call(bf16[2048,512]{1,0:T(8,128)(2,1)S(1)} %copy-done, bf16[128,2176]{1,0:T(8,128)(2,1)S(1)} %get-tuple-element.33.refs_0_, bf16[128,2176]{1,0:T(8,128)(2,1)S(1)} %collective-permute-done.refs_1_), custom_call_target="tpu_custom_call" | custom-call | flops 536870912 | bytes 3145728 | tf_op jit(solution)/shard_map/shrink_partial/pallas_call | solution.py:239
  18.9 3.7 %collective-permute-done.2 = bf16[512,512]{1,0:T(8,128)(2,1)S(1)} collective-permute-done((bf16[512,512]{1,0:T(8,128)(2,1)S(1)}, bf16[512,512]{1,0:T(8,128)(2,1)S(1)}, u32[]{:S(2)}, u32[]{:S(2)}) %collective-permute-start.2) | collective-permute-done | bytes 524320 | tf_op jit(solution)/shard_map/ppermute | solution.py:340
  22.7 0.7 %collective-permute-start.5 = (bf16[512,512]{1,0:T(8,128)(2,1)S(1)}, bf16[512,512]{1,0:T(8,128)(2,1)S(1)}, u32[]{:S(2)}, u32[]{:S(2)}) collective-permute-start(bf16[512,512]{1,0:T(8,128)(2,1)S(1)} %add_convert_fusion.2), channel_id=1, source_target_pairs={{4,8},{8,4},{5,9},{9,5},{6,10},{10,6},{7,11},{11,7},{20,24},{24,20... | collective-permute-start | bytes 1572872 | tf_op jit(solution)/shard_map/ppermute | solution.py:346
  23.4 0.5 shrink_partial.4.refs_0_
  23.9 6.4 %collective-permute-done.3.refs_1_.refs_3_ = bf16[128,2176]{1,0:T(8,128)(2,1)S(1)} collective-permute-done((bf16[128,2176]{1,0:T(8,128)(2,1)S(1)}, bf16[128,2176]{1,0:T(8,128)(2,1)S(1)}, u32[]{:S(2)}, u32[]{:S(2)}) %collective-permute-start.3) | collective-permute-done | bytes 557088 | tf_op jit(solution)/shard_map/ppermute | solution.py:312
  30.8 0.6 %collective-permute-start.6 = (bf16[256,128]{1,0:T(8,128)(2,1)S(1)}, bf16[256,128]{1,0:T(8,128)(2,1)S(1)}, u32[]{:S(2)}, u32[]{:S(2)}) collective-permute-start(bf16[256,128]{1,0:T(8,128)(2,1)S(1)} %shrink_partial.5), channel_id=1, source_target_pairs={{0,4},{4,0},{8,12},{12,8},{1,5},{5,1},{9,13},{13,9},{2,6},{6,2},{1... | collective-permute-start | bytes 196616 | tf_op jit(solution)/shard_map/ppermute | solution.py:312
  31.5 0.9 %collective-permute-done.4 = bf16[512,512]{1,0:T(8,128)(2,1)S(1)} collective-permute-done((bf16[512,512]{1,0:T(8,128)(2,1)S(1)}, bf16[512,512]{1,0:T(8,128)(2,1)S(1)}, u32[]{:S(2)}, u32[]{:S(2)}) %collective-permute-start.4) | collective-permute-done | bytes 524320 | tf_op jit(solution)/shard_map/ppermute | solution.py:343
  32.6 2.7 %collective-permute-done.6 = bf16[256,128]{1,0:T(8,128)(2,1)S(1)} collective-permute-done((bf16[256,128]{1,0:T(8,128)(2,1)S(1)}, bf16[256,128]{1,0:T(8,128)(2,1)S(1)}, u32[]{:S(2)}, u32[]{:S(2)}) %collective-permute-start.6) | collective-permute-done | bytes 65568 | tf_op jit(solution)/shard_map/ppermute | solution.py:312
  35.3 4.0 %collective-permute-start.7 = (bf16[256,128]{1,0:T(8,128)(2,1)S(1)}, bf16[256,128]{1,0:T(8,128)(2,1)S(1)}, u32[]{:S(2)}, u32[]{:S(2)}) collective-permute-start(bf16[256,128]{1,0:T(8,128)(2,1)S(1)} %add_convert_fusion.3.one_ref), channel_id=1, source_target_pairs={{0,8},{4,12},{8,0},{12,4},{1,9},{5,13},{9,1},{13,5},{2,10},{6,14},... | collective-permute-start | bytes 196616 | tf_op jit(solution)/shard_map/ppermute | solution.py:312
  39.3 0.7 %collective-permute-start.11 = (bf16[512,512]{1,0:T(8,128)(2,1)S(1)}, bf16[512,512]{1,0:T(8,128)(2,1)S(1)}, u32[]{:S(2)}, u32[]{:S(2)}) collective-permute-start(bf16[512,512]{1,0:T(8,128)(2,1)S(1)} %add_convert_fusion.1), channel_id=1, source_target_pairs={{4,8},{8,4},{5,9},{9,5},{6,10},{10,6},{7,11},{11,7},{20,24},{24,20... | collective-permute-start | bytes 1572872 | tf_op jit(solution)/shard_map/ppermute | solution.py:353
  40.0 1.9 %collective-permute-done.7.two_ref = bf16[256,128]{1,0:T(8,128)(2,1)S(1)} collective-permute-done((bf16[256,128]{1,0:T(8,128)(2,1)S(1)}, bf16[256,128]{1,0:T(8,128)(2,1)S(1)}, u32[]{:S(2)}, u32[]{:S(2)}) %collective-permute-start.7) | collective-permute-done | bytes 65568 | tf_op jit(solution)/shard_map/ppermute | solution.py:312
  42.5 0.6 %collective-permute-start.8 = (bf16[128,512]{1,0:T(8,128)(2,1)S(1)}, bf16[128,512]{1,0:T(8,128)(2,1)S(1)}, u32[]{:S(2)}, u32[]{:S(2)}) collective-permute-start(bf16[128,512]{1,0:T(8,128)(2,1)S(1)} %get-tuple-element.45), channel_id=1, source_target_pairs={{0,1},{1,0},{2,3},{3,2},{4,5},{5,4},{6,7},{7,6},{8,9},{9,8},{10,11... | collective-permute-start | bytes 393224 | tf_op jit(solution)/shard_map/ppermute | solution.py:312
  43.1 1.5 %collective-permute-start.9 = (bf16[128,512]{1,0:T(8,128)(2,1)S(1)}, bf16[128,512]{1,0:T(8,128)(2,1)S(1)}, u32[]{:S(2)}, u32[]{:S(2)}) collective-permute-start(bf16[128,512]{1,0:T(8,128)(2,1)S(1)} %get-tuple-element.46), channel_id=1, source_target_pairs={{0,2},{1,3},{2,0},{3,1},{4,6},{5,7},{6,4},{7,5},{8,10},{9,11},{10,... | collective-permute-start | bytes 393224 | tf_op jit(solution)/shard_map/ppermute | solution.py:312
  44.6 3.4 %collective-permute-done.10.refs_3_ = bf16[128,512]{1,0:T(8,128)(2,1)S(1)} collective-permute-done((bf16[128,512]{1,0:T(8,128)(2,1)S(1)}, bf16[128,512]{1,0:T(8,128)(2,1)S(1)}, u32[]{:S(2)}, u32[]{:S(2)}) %collective-permute-start.10) | collective-permute-done | bytes 131104 | tf_op jit(solution)/shard_map/ppermute | solution.py:312
  48.0 1.5 %collective-permute-done.9.refs_2_ = bf16[128,512]{1,0:T(8,128)(2,1)S(1)} collective-permute-done((bf16[128,512]{1,0:T(8,128)(2,1)S(1)}, bf16[128,512]{1,0:T(8,128)(2,1)S(1)}, u32[]{:S(2)}, u32[]{:S(2)}) %collective-permute-start.9) | collective-permute-done | bytes 131104 | tf_op jit(solution)/shard_map/ppermute | solution.py:312
  49.5 2.5 %collective-permute-done.12.refs_6_ = bf16[512,512]{1,0:T(8,128)(2,1)S(1)} collective-permute-done((bf16[512,512]{1,0:T(8,128)(2,1)S(1)}, bf16[512,512]{1,0:T(8,128)(2,1)S(1)}, u32[]{:S(2)}, u32[]{:S(2)}) %collective-permute-start.12) | collective-permute-done | bytes 524320 | tf_op jit(solution)/shard_map/ppermute | solution.py:312
  52.0 1.3 %finish.1 = bf16[512,512]{1,0:T(8,128)(2,1)} custom-call(bf16[512,512]{1,0:T(8,128)(2,1)S(1)} %get-tuple-element.32.unsort_ref, bf16[128,512]{1,0:T(8,128)(2,1)S(1)} %get-tuple-element.44.refs_0_, bf16[128,512]{1,0:T(8,128)(2,1)S(1)} %collective-permute-done.8.refs_1_, bf16[128,512]{1,0:T(8,128)(2,1)S(1)} %collective-permute-done.9.refs_2_, ...), custom_call_target="tpu_custom_call" | custom-call | flops 268435456 | bytes 3145728 | tf_op jit(solution)/shard_map/finish/pallas_call | solution.py:294
  (18 shorter events, 1.9 us)
Async XLA Ops:
  2.5 15.6 %collective-permute-start = (bf16[128,2176]{1,0:T(8,128)(2,1)S(1)}, bf16[128,2176]{1,0:T(8,128)(2,1)S(1)}, u32[]{:S(2)}, u32[]{:S(2)}) collective-permute-start(bf16[128,2176]{1,0:T(8,128)(2,1)S(1)} %get-tuple-element.34), channel_id=1, source_target_pairs={{0,2},{1,3},{2,0},{3,1},{4,6},{5,7},{6,4},{7,5},{8,10},{9,11},{10,... | collective-permute-start | bytes 1671176 | tf_op jit(solution)/shard_map/ppermute | solution.py:312
  6.7 15.8 %collective-permute-start.2 = (bf16[512,512]{1,0:T(8,128)(2,1)S(1)}, bf16[512,512]{1,0:T(8,128)(2,1)S(1)}, u32[]{:S(2)}, u32[]{:S(2)}) collective-permute-start(bf16[512,512]{1,0:T(8,128)(2,1)S(1)} %first_block.1), channel_id=1, source_target_pairs={{0,4},{12,8},{1,5},{13,9},{2,6},{14,10},{3,7},{15,11},{16,20},{28,... | collective-permute-start | bytes 1572872 | tf_op jit(solution)/shard_map/ppermute | solution.py:340
  10.2 7.8 %copy-start = (bf16[2048,512]{1,0:T(8,128)(2,1)S(1)}, bf16[2048,512]{1,0:T(8,128)(2,1)}, u32[]{:S(2)}) copy-start(bf16[2048,512]{1,0:T(8,128)(2,1)} %down_ref.5) | copy-start | bytes 6291460
  15.8 7.6 %collective-permute-start.1 = (bf16[128,2176]{1,0:T(8,128)(2,1)S(1)}, bf16[128,2176]{1,0:T(8,128)(2,1)S(1)}, u32[]{:S(2)}, u32[]{:S(2)}) collective-permute-start(bf16[128,2176]{1,0:T(8,128)(2,1)S(1)} %get-tuple-element.35), channel_id=1, source_target_pairs={{0,1},{1,0},{2,3},{3,2},{4,5},{5,4},{6,7},{7,6},{8,9},{9,8},{10,11... | collective-permute-start | bytes 1671176 | tf_op jit(solution)/shard_map/ppermute | solution.py:312
  15.9 14.4 %collective-permute-start.3 = (bf16[128,2176]{1,0:T(8,128)(2,1)S(1)}, bf16[128,2176]{1,0:T(8,128)(2,1)S(1)}, u32[]{:S(2)}, u32[]{:S(2)}) collective-permute-start(bf16[128,2176]{1,0:T(8,128)(2,1)S(1)} %get-tuple-element.38), channel_id=1, source_target_pairs={{0,3},{1,2},{2,1},{3,0},{4,7},{5,6},{6,5},{7,4},{8,11},{9,10},{10,... | collective-permute-start | bytes 1671176 | tf_op jit(solution)/shard_map/ppermute | solution.py:312
  16.5 15.8 %collective-permute-start.4 = (bf16[512,512]{1,0:T(8,128)(2,1)S(1)}, bf16[512,512]{1,0:T(8,128)(2,1)S(1)}, u32[]{:S(2)}, u32[]{:S(2)}) collective-permute-start(bf16[512,512]{1,0:T(8,128)(2,1)S(1)} %get-tuple-element.41), channel_id=1, source_target_pairs={{0,4},{12,8},{1,5},{13,9},{2,6},{14,10},{3,7},{15,11},{16,20},{28,... | collective-permute-start | bytes 1572872 | tf_op jit(solution)/shard_map/ppermute | solution.py:343
  22.7 9.8 %collective-permute-start.5 = (bf16[512,512]{1,0:T(8,128)(2,1)S(1)}, bf16[512,512]{1,0:T(8,128)(2,1)S(1)}, u32[]{:S(2)}, u32[]{:S(2)}) collective-permute-start(bf16[512,512]{1,0:T(8,128)(2,1)S(1)} %add_convert_fusion.2), channel_id=1, source_target_pairs={{4,8},{8,4},{5,9},{9,5},{6,10},{10,6},{7,11},{11,7},{20,24},{24,20... | collective-permute-start | bytes 1572872 | tf_op jit(solution)/shard_map/ppermute | solution.py:346
  30.8 11.1 %copy-start.1 = (bf16[512,512]{1,0:T(8,128)(2,1)S(1)}, bf16[512,512]{1,0:T(8,128)(2,1)}, u32[]{:S(2)}) copy-start(bf16[512,512]{1,0:T(8,128)(2,1)} %up_ref.1) | copy-start | bytes 1572868
  30.8 4.5 %collective-permute-start.6 = (bf16[256,128]{1,0:T(8,128)(2,1)S(1)}, bf16[256,128]{1,0:T(8,128)(2,1)S(1)}, u32[]{:S(2)}, u32[]{:S(2)}) collective-permute-start(bf16[256,128]{1,0:T(8,128)(2,1)S(1)} %shrink_partial.5), channel_id=1, source_target_pairs={{0,4},{4,0},{8,12},{12,8},{1,5},{5,1},{9,13},{13,9},{2,6},{6,2},{1... | collective-permute-start | bytes 196616 | tf_op jit(solution)/shard_map/ppermute | solution.py:312
  35.3 6.6 %collective-permute-start.7 = (bf16[256,128]{1,0:T(8,128)(2,1)S(1)}, bf16[256,128]{1,0:T(8,128)(2,1)S(1)}, u32[]{:S(2)}, u32[]{:S(2)}) collective-permute-start(bf16[256,128]{1,0:T(8,128)(2,1)S(1)} %add_convert_fusion.3.one_ref), channel_id=1, source_target_pairs={{0,8},{4,12},{8,0},{12,4},{1,9},{5,13},{9,1},{13,5},{2,10},{6,14},... | collective-permute-start | bytes 196616 | tf_op jit(solution)/shard_map/ppermute | solution.py:312
  39.3 12.7 %collective-permute-start.12 = (bf16[512,512]{1,0:T(8,128)(2,1)S(1)}, bf16[512,512]{1,0:T(8,128)(2,1)S(1)}, u32[]{:S(2)}, u32[]{:S(2)}) collective-permute-start(bf16[512,512]{1,0:T(8,128)(2,1)S(1)} %add_convert_fusion), channel_id=1, source_target_pairs={{0,4},{4,0},{8,12},{12,8},{1,5},{5,1},{9,13},{13,9},{2,6},{6,2},{1... | collective-permute-start | bytes 1572872 | tf_op jit(solution)/shard_map/ppermute | solution.py:312
  39.3 12.7 %collective-permute-start.11 = (bf16[512,512]{1,0:T(8,128)(2,1)S(1)}, bf16[512,512]{1,0:T(8,128)(2,1)S(1)}, u32[]{:S(2)}, u32[]{:S(2)}) collective-permute-start(bf16[512,512]{1,0:T(8,128)(2,1)S(1)} %add_convert_fusion.1), channel_id=1, source_target_pairs={{4,8},{8,4},{5,9},{9,5},{6,10},{10,6},{7,11},{11,7},{20,24},{24,20... | collective-permute-start | bytes 1572872 | tf_op jit(solution)/shard_map/ppermute | solution.py:353
  42.4 5.6 %collective-permute-start.10 = (bf16[128,512]{1,0:T(8,128)(2,1)S(1)}, bf16[128,512]{1,0:T(8,128)(2,1)S(1)}, u32[]{:S(2)}, u32[]{:S(2)}) collective-permute-start(bf16[128,512]{1,0:T(8,128)(2,1)S(1)} %get-tuple-element.47), channel_id=1, source_target_pairs={{0,3},{1,2},{2,1},{3,0},{4,7},{5,6},{6,5},{7,4},{8,11},{9,10},{10,... | collective-permute-start | bytes 393224 | tf_op jit(solution)/shard_map/ppermute | solution.py:312
  42.5 5.5 %collective-permute-start.8 = (bf16[128,512]{1,0:T(8,128)(2,1)S(1)}, bf16[128,512]{1,0:T(8,128)(2,1)S(1)}, u32[]{:S(2)}, u32[]{:S(2)}) collective-permute-start(bf16[128,512]{1,0:T(8,128)(2,1)S(1)} %get-tuple-element.45), channel_id=1, source_target_pairs={{0,1},{1,0},{2,3},{3,2},{4,5},{5,4},{6,7},{7,6},{8,9},{9,8},{10,11... | collective-permute-start | bytes 393224 | tf_op jit(solution)/shard_map/ppermute | solution.py:312
  43.1 6.4 %collective-permute-start.9 = (bf16[128,512]{1,0:T(8,128)(2,1)S(1)}, bf16[128,512]{1,0:T(8,128)(2,1)S(1)}, u32[]{:S(2)}, u32[]{:S(2)}) collective-permute-start(bf16[128,512]{1,0:T(8,128)(2,1)S(1)} %get-tuple-element.46), channel_id=1, source_target_pairs={{0,2},{1,3},{2,0},{3,1},{4,6},{5,7},{6,4},{7,5},{8,10},{9,11},{10,... | collective-permute-start | bytes 393224 | tf_op jit(solution)/shard_map/ppermute | solution.py:312

commit v10 on v9

--- a/solution.py
+++ b/solution.py
@@ -245,7 +245,9 @@
     )(down, *done, *parts)
 
 
-def expand_body(count, one_ref, two_ref, up_ref, *refs):
+def expand_body(terms, up_ref, *refs):
+    shares, refs = refs[:terms], refs[terms:]
+    count = len(refs) // 2
     tags, outs = refs[:count], refs[count:]
     capacity = outs[0].shape[0]
     half = capacity // 2
@@ -253,7 +255,10 @@
     first = iota((half, LANES), 1) < ADAPTER_RANK
     for k in range(count):
         part = pl.ds(k * half, half)
-        shrink = (one_ref[part, :].astype(f32) + two_ref[part, :].astype(f32)).astype(bf16).astype(f32)
+        shrink = shares[0][part, :].astype(f32)
+        for share in shares[1:]:
+            shrink += share[part, :].astype(f32)
+        shrink = shrink.astype(bf16).astype(f32)
         turned = pltpu.roll(shrink, ADAPTER_RANK, 1)
         rows = jnp.concatenate([jnp.where(first, shrink, turned), jnp.where(first, turned, shrink)], axis=0)
         tag = tags[k][...].astype(f32)
@@ -263,41 +268,39 @@
         outs[k][...] = dot(jnp.concatenate(spread, axis=1), up).astype(bf16)
 
 
-def expand(one, two, up, parts):
+def expand(shares, up, parts):
     capacity, width = parts[0].shape
     count = len(parts)
     tag_block = pl.BlockSpec((capacity, LANES), lambda i: (0, width // LANES - 1))
     whole = lambda a: pl.BlockSpec(a.shape, lambda i: (0, 0))
     columns = up.shape[1]
     return pl.pallas_call(
-        functools.partial(expand_body, count),
+        functools.partial(expand_body, len(shares)),
         grid=(1,),
         out_shape=[jax.ShapeDtypeStruct((capacity, columns), bf16)] * count,
-        in_specs=[whole(one), whole(two), whole(up)] + [tag_block] * count,
+        in_specs=[whole(up)] + [whole(s) for s in shares] + [tag_block] * count,
         out_specs=[pl.BlockSpec((capacity, columns), lambda i: (0, 0))] * count,
         compiler_params=params(),
         cost_estimate=cost(80 * count * capacity * up.size, 80 * (up.size + count * capacity * columns)),
         name="expand",
-    )(one, two, up, *parts)
-
-
-def finish_body(count, unsort_ref, *refs):
-    deltas, sums, out = refs[:count], refs[count:-1], refs[-1]
-    base = sums[0][...].astype(f32)
-    for term in sums[1:]:
-        base += term[...].astype(f32)
-    out[...] = (base + dot(unsort_ref[...], jnp.concatenate([d[...] for d in deltas], axis=0))).astype(bf16)
-
-
-def finish(unsort, deltas, sums):
-    rows, columns = sums[0].shape
-    return pl.pallas_call(
-        functools.partial(finish_body, len(deltas)),
-        out_shape=jax.ShapeDtypeStruct((rows, columns), bf16),
+    )(up, *shares, *parts)
+
+
+def deltas_body(unsort_ref, own_ref, *refs):
+    deltas, out = refs[:-1], refs[-1]
+    placed = dot(unsort_ref[...], jnp.concatenate([d[...] for d in deltas], axis=0))
+    out[...] = own_ref[...].astype(f32) + placed
+
+
+def with_deltas(unsort, deltas, own):
+    rows, columns = own.shape
+    return pl.pallas_call(
+        deltas_body,
+        out_shape=jax.ShapeDtypeStruct((rows, columns), f32),
         compiler_params=params(),
         cost_estimate=cost(2 * rows * unsort.shape[1] * columns, 12 * rows * columns),
-        name="finish",
-    )(unsort, *deltas, *sums)
+        name="with_deltas",
+    )(unsort, own, *deltas)
 
 
 def both(a, b):
@@ -316,14 +319,14 @@
 MIDDLE = [(1, 2), (2, 1)]
 
 
-def tp_sums(mine, *before):
+def tp_sums(mine):
     sums, bit = [mine], 1
     while True:
         other = swap(sums[-1], "tp", bit)
         bit *= 2
         if bit >= lax.axis_size("tp"):
-            return sums, other
-        sums.append(both(after(sums[-1], *before), other))
+            return [sums[-1], other]
+        sums.append(both(sums[-1], other))
 
 
 def shards(x, ids, table, weight, down, up):
@@ -347,24 +350,26 @@
         early = shrink_partial(down, [after(near[1], inner0)], [early])
         mine = shrink_partial(down, [after(far[1], early)], [early])
         parts, order = [near[0], far[0], near[1], far[1]], (0, 2, 1, 3)
-        inner1, inner2 = both(after(second, mine), edge1), both(third, middle0)
-        steps, other = tp_sums(mine, inner1, inner2)
-        last = swap(after(inner2, steps[-1]), "tp", 1)
-        middle1 = lax.ppermute(after(inner1, steps[-1]), "tp", MIDDLE)
-        sums = [own, middle1, last]
+        shares = [mine] + [swap(mine, "tp", bit) for bit in (2, 3, 1)]
+        middle1 = lax.ppermute(both(after(second, mine), edge1), "tp", MIDDLE)
+        last = swap(both(after(third, mine), middle0), "tp", 1)
+        sums = [middle1, last]
     else:
         near = near_rows(spots, x, capacity)
         near = [near[0], swap(near[1], "ad", 1)]
         parts, order = near + far, range(holders)
         unsort = unsort_only(spots, total)
         full = dot(x, weight).astype(bf16)
-        sums = [lax.psum_scatter(full, "tp", scatter_dimension=1, tiled=True)]
-        steps, other = tp_sums(shrink_partial(down, parts))
-    deltas = expand(steps[-1], other, up, parts)
+        own, sums = lax.psum_scatter(full, "tp", scatter_dimension=1, tiled=True), []
+        shares = tp_sums(shrink_partial(down, parts))
+    deltas = expand(shares, up, parts)
     back = [None] * holders
     for j, delta in zip(order, deltas):
         back[j] = swap(delta, "ad", j) if j else delta
-    return finish(unsort, back, sums)
+    total = with_deltas(unsort, back, own)
+    for term in sums:
+        total += term.astype(f32)
+    return total.astype(bf16)
 
 
 def solution(mesh):

time: 53.7 us -> 55 us (1.024)
  starting transfers between devices: 16.7 us -> 23.8 us
  waiting for transfers between devices: 23.1 us -> 17.3 us
  other arithmetic: 0.44 us -> 1.46 us
  Pallas kernels: 12.8 us -> 12 us
    ppermute x9 -> x10, starting transfers between devices: 10.5 us -> 17.5 us  [swap(): lax.ppermute(value, axis, [(i, i ^ bit) for i in range(lax.axis_size(axis...]
    ppermute x9 -> x10, waiting for transfers between devices: 18.5 us -> 13.6 us  [swap(): lax.ppermute(value, axis, [(i, i ^ bit) for i in range(lax.axis_size(axis...]
    convert_element_type x0 -> x1, other arithmetic: none -> 1.04 us  [shards(): return total.astype(bf16)]
    ppermute x1, waiting for transfers between devices: 0.87 us -> 0.01 us  [shards(): edge1 = lax.ppermute(second, 'tp', EDGE)]
    pallas_call x2, Pallas kernels: 1.75 us -> 0.93 us  [the longest x1 0.5 us: expand(): pl.pallas_call(functools.partial(expand_body, len(shares)), grid=(1,), ou...]
  transfers between devices with their start and end apart: 13 -> 14, of which waited for: 9 -> 6; matrix products, arithmetic and copies ran while one was open for 1% -> 1% of each run, Pallas kernels for 17% -> 17%
where the time goes in v10:
time: 55 us; the launch traced here: 54.7 us
  starting transfers between devices  23.8 us (43%)
  waiting for transfers between devices  17.3 us (31%)
  Pallas kernels  12 us (22%)
  other arithmetic  1.46 us (3%)
    ppermute x10, starting transfers between devices, swap(): lax.ppermute(value, axis, [(i, i ^ bit) for i in range(lax.axis_size(axis...  17.5 us
    ppermute x10, waiting for transfers between devices, swap(): lax.ppermute(value, axis, [(i, i ^ bit) for i in range(lax.axis_size(axis...  13.6 us
    pallas_call x1, Pallas kernels, rest(): pl.pallas_call(rest_body, out_shape=shapes, in_specs=[smem, vmem, vmem, h...  5.54 us
    ppermute x1, waiting for transfers between devices, shards(): edge0 = lax.ppermute(first, 'tp', EDGE)  3.68 us
    ppermute x1, starting transfers between devices, shards(): edge0 = lax.ppermute(first, 'tp', EDGE)  3.52 us
    pallas_call x1, Pallas kernels, far_rows(): pl.pallas_call(functools.partial(far_body, slots, capacity, holders), out...  2.46 us
    pallas_call x3, Pallas kernels, shrink_partial(): pl.pallas_call(functools.partial(shrink_body, kept), out_shape=jax.ShapeD...  1.82 us
    ppermute x1, starting transfers between devices, shards(): edge1 = lax.ppermute(second, 'tp', EDGE)  1.31 us
  transfers between devices with their start and end apart: 14, of which 6 were waited for; matrix products, arithmetic and copies ran while one was open for 1% of the time, Pallas kernels for 17%

profile of v10, /device:TPU:0, one launch (start us, length us, event | category | flops | bytes accessed | tf_op | source)
XLA Modules:
  0.0 54.7 jit_solution(11209628327795400854)
XLA Ops:
  0.0 2.5 %far_rows.1 = (s32[8,512]{1,0:T(8,128)S(1)}, bf16[128,2176]{1,0:T(8,128)(2,1)S(1)}, bf16[128,2176]{1,0:T(8,128)(2,1)S(1)}, bf16[512,2048]{1,0:T(8,128)(2,1)S(1)}, bf16[2048,512]{1,0:T(8,128)(2,1)S(1)}) custom-call(s32[1]{0:T(128)} %bitcast.1.me_ref, s32[1]{0:T(128)} %bitcast.z_ref, s32[1,512]{1,0:T(1,128)} %bitcast.5, s32[32,128]{1,0:T(8,128)} %bitcast.4, ...), custom_call_target="tpu_custom_call" | custom-call | flops 1073741824 | bytes 4194304 | tf_op jit(solution)/shard_map/far_rows/pallas_call | solution.py:112
  2.5 3.0 %collective-permute-start = (bf16[128,2176]{1,0:T(8,128)(2,1)S(1)}, bf16[128,2176]{1,0:T(8,128)(2,1)S(1)}, u32[]{:S(2)}, u32[]{:S(2)}) collective-permute-start(bf16[128,2176]{1,0:T(8,128)(2,1)S(1)} %get-tuple-element.33), channel_id=1, source_target_pairs={{0,2},{1,3},{2,0},{3,1},{4,6},{5,7},{6,4},{7,5},{8,10},{9,11},{10,... | collective-permute-start | bytes 1671176 | tf_op jit(solution)/shard_map/ppermute | solution.py:315
  5.5 1.3 %first_block.1 = bf16[512,512]{1,0:T(8,128)(2,1)S(1)} custom-call(bf16[512,2048]{1,0:T(8,128)(2,1)S(1)} %get-tuple-element.27.x_ref, bf16[2048,512]{1,0:T(8,128)(2,1)S(1)} %get-tuple-element.28.w_ref), custom_call_target="tpu_custom_call" | custom-call | flops 1073741824 | bytes 4194304 | tf_op jit(solution)/shard_map/first_block/pallas_call | solution.py:151
  6.7 3.5 %collective-permute-start.2 = (bf16[512,512]{1,0:T(8,128)(2,1)S(1)}, bf16[512,512]{1,0:T(8,128)(2,1)S(1)}, u32[]{:S(2)}, u32[]{:S(2)}) collective-permute-start(bf16[512,512]{1,0:T(8,128)(2,1)S(1)} %first_block.1), channel_id=1, source_target_pairs={{0,4},{12,8},{1,5},{13,9},{2,6},{14,10},{3,7},{15,11},{16,20},{28,... | collective-permute-start | bytes 1572872 | tf_op jit(solution)/shard_map/ppermute | solution.py:343
  10.3 5.5 %rest.1 = (bf16[128,2176]{1,0:T(8,128)(2,1)S(1)}, bf16[128,2176]{1,0:T(8,128)(2,1)S(1)}, bf16[512,512]{1,0:T(8,128)(2,1)S(1)}, bf16[512,512]{1,0:T(8,128)(2,1)S(...) custom-call(s32[1]{0:T(128)} %bitcast.z_ref, s32[8,512]{1,0:T(8,128)S(1)} %get-tuple-element.29.spots_ref, ...), custom_call_target="tpu_custom_call" | custom-call | flops 3221225472 | bytes 10485760 | tf_op jit(solution)/shard_map/rest/pallas_call | solution.py:189
  15.9 0.6 %collective-permute-start.3 = (bf16[128,2176]{1,0:T(8,128)(2,1)S(1)}, bf16[128,2176]{1,0:T(8,128)(2,1)S(1)}, u32[]{:S(2)}, u32[]{:S(2)}) collective-permute-start(bf16[128,2176]{1,0:T(8,128)(2,1)S(1)} %get-tuple-element.37), channel_id=1, source_target_pairs={{0,3},{1,2},{2,1},{3,0},{4,7},{5,6},{6,5},{7,4},{8,11},{9,10},{10,... | collective-permute-start | bytes 1671176 | tf_op jit(solution)/shard_map/ppermute | solution.py:315
  16.5 1.3 %collective-permute-start.10 = (bf16[512,512]{1,0:T(8,128)(2,1)S(1)}, bf16[512,512]{1,0:T(8,128)(2,1)S(1)}, u32[]{:S(2)}, u32[]{:S(2)}) collective-permute-start(bf16[512,512]{1,0:T(8,128)(2,1)S(1)} %get-tuple-element.44), channel_id=1, source_target_pairs={{0,4},{12,8},{1,5},{13,9},{2,6},{14,10},{3,7},{15,11},{16,20},{28,... | collective-permute-start | bytes 1572872 | tf_op jit(solution)/shard_map/ppermute | solution.py:346
  18.1 0.8 %shrink_partial.3.refs_0_ = bf16[128,128]{1,0:T(8,128)(2,1)S(1)} custom-call(bf16[2048,512]{1,0:T(8,128)(2,1)S(1)} %copy-done, bf16[128,2176]{1,0:T(8,128)(2,1)S(1)} %get-tuple-element.32.refs_0_.refs_4_, bf16[128,2176]{1,0:T(8,128)(2,1)S(1)} %collective-permute-done.refs_1_.refs_5_), custom_call_target="tpu_custom_call" | custom-call | flops 536870912 | bytes 3145728 | tf_op jit(solution)/shard_map/shrink_partial/pallas_call | solution.py:239
  18.9 3.7 %collective-permute-done.2 = bf16[512,512]{1,0:T(8,128)(2,1)S(1)} collective-permute-done((bf16[512,512]{1,0:T(8,128)(2,1)S(1)}, bf16[512,512]{1,0:T(8,128)(2,1)S(1)}, u32[]{:S(2)}, u32[]{:S(2)}) %collective-permute-start.2) | collective-permute-done | bytes 524320 | tf_op jit(solution)/shard_map/ppermute | solution.py:343
  22.7 0.7 %collective-permute-start.12 = (bf16[512,512]{1,0:T(8,128)(2,1)S(1)}, bf16[512,512]{1,0:T(8,128)(2,1)S(1)}, u32[]{:S(2)}, u32[]{:S(2)}) collective-permute-start(bf16[512,512]{1,0:T(8,128)(2,1)S(1)} %add_convert_fusion.3), channel_id=1, source_target_pairs={{4,8},{8,4},{5,9},{9,5},{6,10},{10,6},{7,11},{11,7},{20,24},{24,20... | collective-permute-start | bytes 1572872 | tf_op jit(solution)/shard_map/ppermute | solution.py:349
  23.4 0.5 shrink_partial.4.refs_0_
  23.9 6.4 %collective-permute-done.3.refs_1_.refs_7_ = bf16[128,2176]{1,0:T(8,128)(2,1)S(1)} collective-permute-done((bf16[128,2176]{1,0:T(8,128)(2,1)S(1)}, bf16[128,2176]{1,0:T(8,128)(2,1)S(1)}, u32[]{:S(2)}, u32[]{:S(2)}) %collective-permute-start.3) | collective-permute-done | bytes 557088 | tf_op jit(solution)/shard_map/ppermute | solution.py:315
  30.3 0.5 shrink_partial.5.refs_0_
  30.8 1.6 %collective-permute-start.4 = (bf16[256,128]{1,0:T(8,128)(2,1)S(1)}, bf16[256,128]{1,0:T(8,128)(2,1)S(1)}, u32[]{:S(2)}, u32[]{:S(2)}) collective-permute-start(bf16[256,128]{1,0:T(8,128)(2,1)S(1)} %shrink_partial.5.refs_0_), channel_id=1, source_target_pairs={{0,8},{4,12},{8,0},{12,4},{1,9},{5,13},{9,1},{13,5},{2,10},{6,14},... | collective-permute-start | bytes 196616 | tf_op jit(solution)/shard_map/ppermute | solution.py:315
  32.5 1.6 %collective-permute-start.5 = (bf16[256,128]{1,0:T(8,128)(2,1)S(1)}, bf16[256,128]{1,0:T(8,128)(2,1)S(1)}, u32[]{:S(2)}, u32[]{:S(2)}) collective-permute-start(bf16[256,128]{1,0:T(8,128)(2,1)S(1)} %shrink_partial.5.refs_0_), channel_id=1, source_target_pairs={{0,12},{4,8},{8,4},{12,0},{1,13},{5,9},{9,5},{13,1},{2,14},{6,10},... | collective-permute-start | bytes 196616 | tf_op jit(solution)/shard_map/ppermute | solution.py:315
  34.1 0.5 collective-permute-start.6
  34.7 0.7 %collective-permute-start.11 = (bf16[512,512]{1,0:T(8,128)(2,1)S(1)}, bf16[512,512]{1,0:T(8,128)(2,1)S(1)}, u32[]{:S(2)}, u32[]{:S(2)}) collective-permute-start(bf16[512,512]{1,0:T(8,128)(2,1)S(1)} %add_convert_fusion.2), channel_id=1, source_target_pairs={{4,8},{8,4},{5,9},{9,5},{6,10},{10,6},{7,11},{11,7},{20,24},{24,20... | collective-permute-start | bytes 1572872 | tf_op jit(solution)/shard_map/ppermute | solution.py:354
  35.6 8.2 %collective-permute-start.13 = (bf16[512,512]{1,0:T(8,128)(2,1)S(1)}, bf16[512,512]{1,0:T(8,128)(2,1)S(1)}, u32[]{:S(2)}, u32[]{:S(2)}) collective-permute-start(bf16[512,512]{1,0:T(8,128)(2,1)S(1)} %add_convert_fusion.1), channel_id=1, source_target_pairs={{0,4},{4,0},{8,12},{12,8},{1,5},{5,1},{9,13},{13,9},{2,6},{6,2},{1... | collective-permute-start | bytes 1572872 | tf_op jit(solution)/shard_map/ppermute | solution.py:315
  43.7 0.6 %collective-permute-done.4.refs_1_ = bf16[256,128]{1,0:T(8,128)(2,1)S(1)} collective-permute-done((bf16[256,128]{1,0:T(8,128)(2,1)S(1)}, bf16[256,128]{1,0:T(8,128)(2,1)S(1)}, u32[]{:S(2)}, u32[]{:S(2)}) %collective-permute-start.4) | collective-permute-done | bytes 65568 | tf_op jit(solution)/shard_map/ppermute | solution.py:315
  44.4 0.5 expand.1
  45.0 1.8 %collective-permute-start.9 = (bf16[128,512]{1,0:T(8,128)(2,1)S(1)}, bf16[128,512]{1,0:T(8,128)(2,1)S(1)}, u32[]{:S(2)}, u32[]{:S(2)}) collective-permute-start(bf16[128,512]{1,0:T(8,128)(2,1)S(1)} %get-tuple-element.42), channel_id=1, source_target_pairs={{0,3},{1,2},{2,1},{3,0},{4,7},{5,6},{6,5},{7,4},{8,11},{9,10},{10,... | collective-permute-start | bytes 393224 | tf_op jit(solution)/shard_map/ppermute | solution.py:315
  46.8 4.5 %collective-permute-done.8.refs_2_ = bf16[128,512]{1,0:T(8,128)(2,1)S(1)} collective-permute-done((bf16[128,512]{1,0:T(8,128)(2,1)S(1)}, bf16[128,512]{1,0:T(8,128)(2,1)S(1)}, u32[]{:S(2)}, u32[]{:S(2)}) %collective-permute-start.8) | collective-permute-done | bytes 131104 | tf_op jit(solution)/shard_map/ppermute | solution.py:315
  51.3 1.9 %collective-permute-done.9.refs_3_ = bf16[128,512]{1,0:T(8,128)(2,1)S(1)} collective-permute-done((bf16[128,512]{1,0:T(8,128)(2,1)S(1)}, bf16[128,512]{1,0:T(8,128)(2,1)S(1)}, u32[]{:S(2)}, u32[]{:S(2)}) %collective-permute-start.9) | collective-permute-done | bytes 131104 | tf_op jit(solution)/shard_map/ppermute | solution.py:315
  53.7 1.0 %add_convert_fusion = bf16[512,512]{1,0:T(8,128)(2,1)} fusion(bf16[512,512]{1,0:T(8,128)(2,1)S(1)} %collective-permute-done.13, f32[512,512]{1,0:T(8,128)S(1)} %with_deltas.1, bf16[512,512]{1,0:T(8,128)(2,1)S(1)} %collective-permute-done.11), kind=kLoop, calls=%fused_computation | loop fusion | flops 1310720 | bytes 2621440 | tf_op jit(solution)/shard_map/convert_element_type | solution.py:372
  (20 shorter events, 1.3 us)
Async XLA Ops:
  2.5 15.6 %collective-permute-start = (bf16[128,2176]{1,0:T(8,128)(2,1)S(1)}, bf16[128,2176]{1,0:T(8,128)(2,1)S(1)}, u32[]{:S(2)}, u32[]{:S(2)}) collective-permute-start(bf16[128,2176]{1,0:T(8,128)(2,1)S(1)} %get-tuple-element.33), channel_id=1, source_target_pairs={{0,2},{1,3},{2,0},{3,1},{4,6},{5,7},{6,4},{7,5},{8,10},{9,11},{10,... | collective-permute-start | bytes 1671176 | tf_op jit(solution)/shard_map/ppermute | solution.py:315
  6.7 15.8 %collective-permute-start.2 = (bf16[512,512]{1,0:T(8,128)(2,1)S(1)}, bf16[512,512]{1,0:T(8,128)(2,1)S(1)}, u32[]{:S(2)}, u32[]{:S(2)}) collective-permute-start(bf16[512,512]{1,0:T(8,128)(2,1)S(1)} %first_block.1), channel_id=1, source_target_pairs={{0,4},{12,8},{1,5},{13,9},{2,6},{14,10},{3,7},{15,11},{16,20},{28,... | collective-permute-start | bytes 1572872 | tf_op jit(solution)/shard_map/ppermute | solution.py:343
  10.2 7.8 %copy-start = (bf16[2048,512]{1,0:T(8,128)(2,1)S(1)}, bf16[2048,512]{1,0:T(8,128)(2,1)}, u32[]{:S(2)}) copy-start(bf16[2048,512]{1,0:T(8,128)(2,1)} %down_ref.5) | copy-start | bytes 6291460
  15.8 7.6 %collective-permute-start.1 = (bf16[128,2176]{1,0:T(8,128)(2,1)S(1)}, bf16[128,2176]{1,0:T(8,128)(2,1)S(1)}, u32[]{:S(2)}, u32[]{:S(2)}) collective-permute-start(bf16[128,2176]{1,0:T(8,128)(2,1)S(1)} %get-tuple-element.34), channel_id=1, source_target_pairs={{0,1},{1,0},{2,3},{3,2},{4,5},{5,4},{6,7},{7,6},{8,9},{9,8},{10,11... | collective-permute-start | bytes 1671176 | tf_op jit(solution)/shard_map/ppermute | solution.py:315
  15.9 14.4 %collective-permute-start.3 = (bf16[128,2176]{1,0:T(8,128)(2,1)S(1)}, bf16[128,2176]{1,0:T(8,128)(2,1)S(1)}, u32[]{:S(2)}, u32[]{:S(2)}) collective-permute-start(bf16[128,2176]{1,0:T(8,128)(2,1)S(1)} %get-tuple-element.37), channel_id=1, source_target_pairs={{0,3},{1,2},{2,1},{3,0},{4,7},{5,6},{6,5},{7,4},{8,11},{9,10},{10,... | collective-permute-start | bytes 1671176 | tf_op jit(solution)/shard_map/ppermute | solution.py:315
  16.5 18.1 %collective-permute-start.10 = (bf16[512,512]{1,0:T(8,128)(2,1)S(1)}, bf16[512,512]{1,0:T(8,128)(2,1)S(1)}, u32[]{:S(2)}, u32[]{:S(2)}) collective-permute-start(bf16[512,512]{1,0:T(8,128)(2,1)S(1)} %get-tuple-element.44), channel_id=1, source_target_pairs={{0,4},{12,8},{1,5},{13,9},{2,6},{14,10},{3,7},{15,11},{16,20},{28,... | collective-permute-start | bytes 1572872 | tf_op jit(solution)/shard_map/ppermute | solution.py:346
  22.7 12.7 %collective-permute-start.12 = (bf16[512,512]{1,0:T(8,128)(2,1)S(1)}, bf16[512,512]{1,0:T(8,128)(2,1)S(1)}, u32[]{:S(2)}, u32[]{:S(2)}) collective-permute-start(bf16[512,512]{1,0:T(8,128)(2,1)S(1)} %add_convert_fusion.3), channel_id=1, source_target_pairs={{4,8},{8,4},{5,9},{9,5},{6,10},{10,6},{7,11},{11,7},{20,24},{24,20... | collective-permute-start | bytes 1572872 | tf_op jit(solution)/shard_map/ppermute | solution.py:349
  30.8 13.5 %copy-start.1 = (bf16[512,512]{1,0:T(8,128)(2,1)S(1)}, bf16[512,512]{1,0:T(8,128)(2,1)}, u32[]{:S(2)}) copy-start(bf16[512,512]{1,0:T(8,128)(2,1)} %up_ref.1) | copy-start | bytes 1572868
  30.8 13.5 %collective-permute-start.4 = (bf16[256,128]{1,0:T(8,128)(2,1)S(1)}, bf16[256,128]{1,0:T(8,128)(2,1)S(1)}, u32[]{:S(2)}, u32[]{:S(2)}) collective-permute-start(bf16[256,128]{1,0:T(8,128)(2,1)S(1)} %shrink_partial.5.refs_0_), channel_id=1, source_target_pairs={{0,8},{4,12},{8,0},{12,4},{1,9},{5,13},{9,1},{13,5},{2,10},{6,14},... | collective-permute-start | bytes 196616 | tf_op jit(solution)/shard_map/ppermute | solution.py:315
  32.5 11.9 %collective-permute-start.5 = (bf16[256,128]{1,0:T(8,128)(2,1)S(1)}, bf16[256,128]{1,0:T(8,128)(2,1)S(1)}, u32[]{:S(2)}, u32[]{:S(2)}) collective-permute-start(bf16[256,128]{1,0:T(8,128)(2,1)S(1)} %shrink_partial.5.refs_0_), channel_id=1, source_target_pairs={{0,12},{4,8},{8,4},{12,0},{1,13},{5,9},{9,5},{13,1},{2,14},{6,10},... | collective-permute-start | bytes 196616 | tf_op jit(solution)/shard_map/ppermute | solution.py:315
  34.1 10.3 %collective-permute-start.6 = (bf16[256,128]{1,0:T(8,128)(2,1)S(1)}, bf16[256,128]{1,0:T(8,128)(2,1)S(1)}, u32[]{:S(2)}, u32[]{:S(2)}) collective-permute-start(bf16[256,128]{1,0:T(8,128)(2,1)S(1)} %shrink_partial.5.refs_0_), channel_id=1, source_target_pairs={{0,4},{4,0},{8,12},{12,8},{1,5},{5,1},{9,13},{13,9},{2,6},{6,2},{1... | collective-permute-start | bytes 196616 | tf_op jit(solution)/shard_map/ppermute | solution.py:315
  34.7 19.0 %collective-permute-start.11 = (bf16[512,512]{1,0:T(8,128)(2,1)S(1)}, bf16[512,512]{1,0:T(8,128)(2,1)S(1)}, u32[]{:S(2)}, u32[]{:S(2)}) collective-permute-start(bf16[512,512]{1,0:T(8,128)(2,1)S(1)} %add_convert_fusion.2), channel_id=1, source_target_pairs={{4,8},{8,4},{5,9},{9,5},{6,10},{10,6},{7,11},{11,7},{20,24},{24,20... | collective-permute-start | bytes 1572872 | tf_op jit(solution)/shard_map/ppermute | solution.py:354
  35.6 18.1 %collective-permute-start.13 = (bf16[512,512]{1,0:T(8,128)(2,1)S(1)}, bf16[512,512]{1,0:T(8,128)(2,1)S(1)}, u32[]{:S(2)}, u32[]{:S(2)}) collective-permute-start(bf16[512,512]{1,0:T(8,128)(2,1)S(1)} %add_convert_fusion.1), channel_id=1, source_target_pairs={{0,4},{4,0},{8,12},{12,8},{1,5},{5,1},{9,13},{13,9},{2,6},{6,2},{1... | collective-permute-start | bytes 1572872 | tf_op jit(solution)/shard_map/ppermute | solution.py:315
  44.9 1.9 %collective-permute-start.7 = (bf16[128,512]{1,0:T(8,128)(2,1)S(1)}, bf16[128,512]{1,0:T(8,128)(2,1)S(1)}, u32[]{:S(2)}, u32[]{:S(2)}) collective-permute-start(bf16[128,512]{1,0:T(8,128)(2,1)S(1)} %get-tuple-element.40), channel_id=1, source_target_pairs={{0,1},{1,0},{2,3},{3,2},{4,5},{5,4},{6,7},{7,6},{8,9},{9,8},{10,11... | collective-permute-start | bytes 393224 | tf_op jit(solution)/shard_map/ppermute | solution.py:315
  45.0 6.4 %collective-permute-start.8 = (bf16[128,512]{1,0:T(8,128)(2,1)S(1)}, bf16[128,512]{1,0:T(8,128)(2,1)S(1)}, u32[]{:S(2)}, u32[]{:S(2)}) collective-permute-start(bf16[128,512]{1,0:T(8,128)(2,1)S(1)} %get-tuple-element.41), channel_id=1, source_target_pairs={{0,2},{1,3},{2,0},{3,1},{4,6},{5,7},{6,4},{7,5},{8,10},{9,11},{10,... | collective-permute-start | bytes 393224 | tf_op jit(solution)/shard_map/ppermute | solution.py:315
  45.0 8.2 %collective-permute-start.9 = (bf16[128,512]{1,0:T(8,128)(2,1)S(1)}, bf16[128,512]{1,0:T(8,128)(2,1)S(1)}, u32[]{:S(2)}, u32[]{:S(2)}) collective-permute-start(bf16[128,512]{1,0:T(8,128)(2,1)S(1)} %get-tuple-element.42), channel_id=1, source_target_pairs={{0,3},{1,2},{2,1},{3,0},{4,7},{5,6},{6,5},{7,4},{8,11},{9,10},{10,... | collective-permute-start | bytes 393224 | tf_op jit(solution)/shard_map/ppermute | solution.py:315

commit v11 on v9

--- a/solution.py
+++ b/solution.py
@@ -281,23 +281,52 @@
     )(one, two, up, *parts)
 
 
-def finish_body(count, unsort_ref, *refs):
-    deltas, sums, out = refs[:count], refs[count:-1], refs[-1]
-    base = sums[0][...].astype(f32)
-    for term in sums[1:]:
-        base += term[...].astype(f32)
-    out[...] = (base + dot(unsort_ref[...], jnp.concatenate([d[...] for d in deltas], axis=0))).astype(bf16)
-
-
-def finish(unsort, deltas, sums):
-    rows, columns = sums[0].shape
-    return pl.pallas_call(
-        functools.partial(finish_body, len(deltas)),
-        out_shape=jax.ShapeDtypeStruct((rows, columns), bf16),
+def deltas_body(unsort_ref, own_ref, *refs):
+    deltas, out = refs[:-1], refs[-1]
+    placed = dot(unsort_ref[...], jnp.concatenate([d[...] for d in deltas], axis=0))
+    out[...] = own_ref[...].astype(f32) + placed
+
+
+def with_deltas(unsort, deltas, own):
+    rows, columns = own.shape
+    return pl.pallas_call(
+        deltas_body,
+        out_shape=jax.ShapeDtypeStruct((rows, columns), f32),
         compiler_params=params(),
         cost_estimate=cost(2 * rows * unsort.shape[1] * columns, 12 * rows * columns),
+        name="with_deltas",
+    )(unsort, own, *deltas)
+
+
+def finish_body(start_ref, *refs):
+    terms, (out_hbm, out_buf, sem) = refs[:-3], refs[-3:]
+    pieces = sem.shape[0]
+    step = out_buf.shape[0] // pieces
+    copies = []
+    for k in range(pieces):
+        part = pl.ds(k * step, step)
+        total = start_ref[part, :]
+        for term in terms:
+            total += term[part, :].astype(f32)
+        out_buf[part, :] = total.astype(bf16)
+        copies.append(pltpu.make_async_copy(out_buf.at[part, :], out_hbm.at[part, :], sem.at[k]))
+        copies[k].start()
+    for copy in copies:
+        copy.wait()
+
+
+def finish(start, terms):
+    vmem, hbm = (pl.BlockSpec(memory_space=m) for m in (pltpu.VMEM, pltpu.HBM))
+    return pl.pallas_call(
+        finish_body,
+        out_shape=jax.ShapeDtypeStruct(start.shape, bf16),
+        in_specs=[vmem] * (1 + len(terms)),
+        out_specs=hbm,
+        scratch_shapes=[pltpu.VMEM(start.shape, bf16), pltpu.SemaphoreType.DMA((4,))],
+        compiler_params=params(),
+        cost_estimate=cost(start.size, 8 * start.size),
         name="finish",
-    )(unsort, *deltas, *sums)
+    )(start, *terms)
 
 
 def both(a, b):
@@ -347,24 +376,25 @@
         early = shrink_partial(down, [after(near[1], inner0)], [early])
         mine = shrink_partial(down, [after(far[1], early)], [early])
         parts, order = [near[0], far[0], near[1], far[1]], (0, 2, 1, 3)
-        inner1, inner2 = both(after(second, mine), edge1), both(third, middle0)
-        steps, other = tp_sums(mine, inner1, inner2)
-        last = swap(after(inner2, steps[-1]), "tp", 1)
-        middle1 = lax.ppermute(after(inner1, steps[-1]), "tp", MIDDLE)
-        sums = [own, middle1, last]
+        inner1 = both(after(second, mine), edge1)
+        steps, other = tp_sums(mine, inner1)
+        inner2 = both(after(third, steps[-1]), middle0)
+        last = swap(inner2, "tp", 1)
+        middle1 = lax.ppermute(after(inner1, inner2), "tp", MIDDLE)
+        sums = [middle1, last]
     else:
         near = near_rows(spots, x, capacity)
         near = [near[0], swap(near[1], "ad", 1)]
         parts, order = near + far, range(holders)
         unsort = unsort_only(spots, total)
         full = dot(x, weight).astype(bf16)
-        sums = [lax.psum_scatter(full, "tp", scatter_dimension=1, tiled=True)]
+        own, sums = lax.psum_scatter(full, "tp", scatter_dimension=1, tiled=True), []
         steps, other = tp_sums(shrink_partial(down, parts))
     deltas = expand(steps[-1], other, up, parts)
     back = [None] * holders
     for j, delta in zip(order, deltas):
         back[j] = swap(delta, "ad", j) if j else delta
-    return finish(unsort, back, sums)
+    return finish(with_deltas(unsort, back, own), sums)
 
 
 def solution(mesh):

time: 53.7 us -> 53.2 us (level)
    ppermute x9, starting transfers between devices: 10.5 us -> 9.95 us  [swap(): lax.ppermute(value, axis, [(i, i ^ bit) for i in range(lax.axis_size(axis...]
    pallas_call x1 -> x2, Pallas kernels: 1.26 us -> 1.3 us  [the longest x1 0.86 us: finish(): pl.pallas_call(finish_body, out_shape=jax.ShapeDtypeStruct(start.shape, b...]
  transfers between devices with their start and end apart: 13 -> 13, of which waited for: 9 -> 9; matrix products, arithmetic and copies ran while one was open for 1% -> 1% of each run, Pallas kernels for 17% -> 18%
where the time goes in v11:
time: 53.2 us; the launch traced here: 53 us
  waiting for transfers between devices  23.4 us (44%)
  starting transfers between devices  16.2 us (30%)
  Pallas kernels  12.9 us (24%)
    ppermute x9, waiting for transfers between devices, swap(): lax.ppermute(value, axis, [(i, i ^ bit) for i in range(lax.axis_size(axis...  18.8 us
    ppermute x9, starting transfers between devices, swap(): lax.ppermute(value, axis, [(i, i ^ bit) for i in range(lax.axis_size(axis...  9.95 us
    pallas_call x1, Pallas kernels, rest(): pl.pallas_call(rest_body, out_shape=shapes, in_specs=[smem, vmem, vmem, h...  5.54 us
    ppermute x1, waiting for transfers between devices, shards(): edge0 = lax.ppermute(first, 'tp', EDGE)  3.68 us
    ppermute x1, starting transfers between devices, shards(): edge0 = lax.ppermute(first, 'tp', EDGE)  3.52 us
    pallas_call x1, Pallas kernels, far_rows(): pl.pallas_call(functools.partial(far_body, slots, capacity, holders), out...  2.46 us
    pallas_call x3, Pallas kernels, shrink_partial(): pl.pallas_call(functools.partial(shrink_body, kept), out_shape=jax.ShapeD...  1.82 us
    ppermute x1, starting transfers between devices, shards(): edge1 = lax.ppermute(second, 'tp', EDGE)  1.31 us
  transfers between devices with their start and end apart: 13, of which 9 were waited for; matrix products, arithmetic and copies ran while one was open for 1% of the time, Pallas kernels for 18%

profile of v11, /device:TPU:0, one launch (start us, length us, event | category | flops | bytes accessed | tf_op | source)
XLA Modules:
  0.0 53.0 jit_solution(4619744051670745313)
XLA Ops:
  0.0 2.5 %far_rows.1 = (s32[8,512]{1,0:T(8,128)S(1)}, bf16[128,2176]{1,0:T(8,128)(2,1)S(1)}, bf16[128,2176]{1,0:T(8,128)(2,1)S(1)}, bf16[512,2048]{1,0:T(8,128)(2,1)S(1)}, bf16[2048,512]{1,0:T(8,128)(2,1)S(1)}) custom-call(s32[1]{0:T(128)} %bitcast.1.me_ref, s32[1]{0:T(128)} %bitcast.z_ref, s32[1,512]{1,0:T(1,128)} %bitcast.5, s32[32,128]{1,0:T(8,128)} %bitcast.4, ...), custom_call_target="tpu_custom_call" | custom-call | flops 1073741824 | bytes 4194304 | tf_op jit(solution)/shard_map/far_rows/pallas_call | solution.py:112
  2.5 3.0 %collective-permute-start = (bf16[128,2176]{1,0:T(8,128)(2,1)S(1)}, bf16[128,2176]{1,0:T(8,128)(2,1)S(1)}, u32[]{:S(2)}, u32[]{:S(2)}) collective-permute-start(bf16[128,2176]{1,0:T(8,128)(2,1)S(1)} %get-tuple-element.35), channel_id=1, source_target_pairs={{0,2},{1,3},{2,0},{3,1},{4,6},{5,7},{6,4},{7,5},{8,10},{9,11},{10,... | collective-permute-start | bytes 1671176 | tf_op jit(solution)/shard_map/ppermute | solution.py:341
  5.5 1.3 %first_block.1 = bf16[512,512]{1,0:T(8,128)(2,1)S(1)} custom-call(bf16[512,2048]{1,0:T(8,128)(2,1)S(1)} %get-tuple-element.29.x_ref, bf16[2048,512]{1,0:T(8,128)(2,1)S(1)} %get-tuple-element.30.w_ref), custom_call_target="tpu_custom_call" | custom-call | flops 1073741824 | bytes 4194304 | tf_op jit(solution)/shard_map/first_block/pallas_call | solution.py:151
  6.7 3.5 %collective-permute-start.2 = (bf16[512,512]{1,0:T(8,128)(2,1)S(1)}, bf16[512,512]{1,0:T(8,128)(2,1)S(1)}, u32[]{:S(2)}, u32[]{:S(2)}) collective-permute-start(bf16[512,512]{1,0:T(8,128)(2,1)S(1)} %first_block.1), channel_id=1, source_target_pairs={{0,4},{12,8},{1,5},{13,9},{2,6},{14,10},{3,7},{15,11},{16,20},{28,... | collective-permute-start | bytes 1572872 | tf_op jit(solution)/shard_map/ppermute | solution.py:369
  10.3 5.5 %rest.1 = (bf16[128,2176]{1,0:T(8,128)(2,1)S(1)}, bf16[128,2176]{1,0:T(8,128)(2,1)S(1)}, bf16[512,512]{1,0:T(8,128)(2,1)S(1)}, bf16[512,512]{1,0:T(8,128)(2,1)S(...) custom-call(s32[1]{0:T(128)} %bitcast.z_ref, s32[8,512]{1,0:T(8,128)S(1)} %get-tuple-element.31.spots_ref, ...), custom_call_target="tpu_custom_call" | custom-call | flops 3221225472 | bytes 10485760 | tf_op jit(solution)/shard_map/rest/pallas_call | solution.py:189
  15.9 0.6 %collective-permute-start.3 = (bf16[128,2176]{1,0:T(8,128)(2,1)S(1)}, bf16[128,2176]{1,0:T(8,128)(2,1)S(1)}, u32[]{:S(2)}, u32[]{:S(2)}) collective-permute-start(bf16[128,2176]{1,0:T(8,128)(2,1)S(1)} %get-tuple-element.39), channel_id=1, source_target_pairs={{0,3},{1,2},{2,1},{3,0},{4,7},{5,6},{6,5},{7,4},{8,11},{9,10},{10,... | collective-permute-start | bytes 1671176 | tf_op jit(solution)/shard_map/ppermute | solution.py:341
  16.5 1.3 %collective-permute-start.4 = (bf16[512,512]{1,0:T(8,128)(2,1)S(1)}, bf16[512,512]{1,0:T(8,128)(2,1)S(1)}, u32[]{:S(2)}, u32[]{:S(2)}) collective-permute-start(bf16[512,512]{1,0:T(8,128)(2,1)S(1)} %get-tuple-element.42), channel_id=1, source_target_pairs={{0,4},{12,8},{1,5},{13,9},{2,6},{14,10},{3,7},{15,11},{16,20},{28,... | collective-permute-start | bytes 1572872 | tf_op jit(solution)/shard_map/ppermute | solution.py:372
  18.1 0.8 %shrink_partial.3.refs_0_ = bf16[128,128]{1,0:T(8,128)(2,1)S(1)} custom-call(bf16[2048,512]{1,0:T(8,128)(2,1)S(1)} %copy-done, bf16[128,2176]{1,0:T(8,128)(2,1)S(1)} %get-tuple-element.34.refs_0_, bf16[128,2176]{1,0:T(8,128)(2,1)S(1)} %collective-permute-done.refs_1_), custom_call_target="tpu_custom_call" | custom-call | flops 536870912 | bytes 3145728 | tf_op jit(solution)/shard_map/shrink_partial/pallas_call | solution.py:239
  18.9 3.7 %collective-permute-done.2 = bf16[512,512]{1,0:T(8,128)(2,1)S(1)} collective-permute-done((bf16[512,512]{1,0:T(8,128)(2,1)S(1)}, bf16[512,512]{1,0:T(8,128)(2,1)S(1)}, u32[]{:S(2)}, u32[]{:S(2)}) %collective-permute-start.2) | collective-permute-done | bytes 524320 | tf_op jit(solution)/shard_map/ppermute | solution.py:369
  22.7 0.7 %collective-permute-start.10 = (bf16[512,512]{1,0:T(8,128)(2,1)S(1)}, bf16[512,512]{1,0:T(8,128)(2,1)S(1)}, u32[]{:S(2)}, u32[]{:S(2)}) collective-permute-start(bf16[512,512]{1,0:T(8,128)(2,1)S(1)} %add_convert_fusion.2), channel_id=1, source_target_pairs={{4,8},{8,4},{5,9},{9,5},{6,10},{10,6},{7,11},{11,7},{20,24},{24,20... | collective-permute-start | bytes 1572872 | tf_op jit(solution)/shard_map/ppermute | solution.py:375
  23.4 0.5 shrink_partial.4.refs_0_
  23.9 6.4 %collective-permute-done.3.refs_1_.refs_3_ = bf16[128,2176]{1,0:T(8,128)(2,1)S(1)} collective-permute-done((bf16[128,2176]{1,0:T(8,128)(2,1)S(1)}, bf16[128,2176]{1,0:T(8,128)(2,1)S(1)}, u32[]{:S(2)}, u32[]{:S(2)}) %collective-permute-start.3) | collective-permute-done | bytes 557088 | tf_op jit(solution)/shard_map/ppermute | solution.py:341
  30.8 0.6 %collective-permute-start.5 = (bf16[256,128]{1,0:T(8,128)(2,1)S(1)}, bf16[256,128]{1,0:T(8,128)(2,1)S(1)}, u32[]{:S(2)}, u32[]{:S(2)}) collective-permute-start(bf16[256,128]{1,0:T(8,128)(2,1)S(1)} %shrink_partial.5), channel_id=1, source_target_pairs={{0,4},{4,0},{8,12},{12,8},{1,5},{5,1},{9,13},{13,9},{2,6},{6,2},{1... | collective-permute-start | bytes 196616 | tf_op jit(solution)/shard_map/ppermute | solution.py:341
  31.5 0.9 %collective-permute-done.4 = bf16[512,512]{1,0:T(8,128)(2,1)S(1)} collective-permute-done((bf16[512,512]{1,0:T(8,128)(2,1)S(1)}, bf16[512,512]{1,0:T(8,128)(2,1)S(1)}, u32[]{:S(2)}, u32[]{:S(2)}) %collective-permute-start.4) | collective-permute-done | bytes 524320 | tf_op jit(solution)/shard_map/ppermute | solution.py:372
  32.5 2.8 %collective-permute-done.5 = bf16[256,128]{1,0:T(8,128)(2,1)S(1)} collective-permute-done((bf16[256,128]{1,0:T(8,128)(2,1)S(1)}, bf16[256,128]{1,0:T(8,128)(2,1)S(1)}, u32[]{:S(2)}, u32[]{:S(2)}) %collective-permute-start.5) | collective-permute-done | bytes 65568 | tf_op jit(solution)/shard_map/ppermute | solution.py:341
  35.3 2.2 %collective-permute-start.6 = (bf16[256,128]{1,0:T(8,128)(2,1)S(1)}, bf16[256,128]{1,0:T(8,128)(2,1)S(1)}, u32[]{:S(2)}, u32[]{:S(2)}) collective-permute-start(bf16[256,128]{1,0:T(8,128)(2,1)S(1)} %add_convert_fusion.3.one_ref), channel_id=1, source_target_pairs={{0,8},{4,12},{8,0},{12,4},{1,9},{5,13},{9,1},{13,5},{2,10},{6,14},... | collective-permute-start | bytes 196616 | tf_op jit(solution)/shard_map/ppermute | solution.py:341
  37.7 1.4 %collective-permute-start.12 = (bf16[512,512]{1,0:T(8,128)(2,1)S(1)}, bf16[512,512]{1,0:T(8,128)(2,1)S(1)}, u32[]{:S(2)}, u32[]{:S(2)}) collective-permute-start(bf16[512,512]{1,0:T(8,128)(2,1)S(1)} %add_convert_fusion), channel_id=1, source_target_pairs={{0,4},{4,0},{8,12},{12,8},{1,5},{5,1},{9,13},{13,9},{2,6},{6,2},{1... | collective-permute-start | bytes 1572872 | tf_op jit(solution)/shard_map/ppermute | solution.py:341
  39.2 0.7 %collective-permute-start.11 = (bf16[512,512]{1,0:T(8,128)(2,1)S(1)}, bf16[512,512]{1,0:T(8,128)(2,1)S(1)}, u32[]{:S(2)}, u32[]{:S(2)}) collective-permute-start(bf16[512,512]{1,0:T(8,128)(2,1)S(1)} %add_convert_fusion.1), channel_id=1, source_target_pairs={{4,8},{8,4},{5,9},{9,5},{6,10},{10,6},{7,11},{11,7},{20,24},{24,20... | collective-permute-start | bytes 1572872 | tf_op jit(solution)/shard_map/ppermute | solution.py:383
  39.9 1.9 %collective-permute-done.6.two_ref = bf16[256,128]{1,0:T(8,128)(2,1)S(1)} collective-permute-done((bf16[256,128]{1,0:T(8,128)(2,1)S(1)}, bf16[256,128]{1,0:T(8,128)(2,1)S(1)}, u32[]{:S(2)}, u32[]{:S(2)}) %collective-permute-start.6) | collective-permute-done | bytes 65568 | tf_op jit(solution)/shard_map/ppermute | solution.py:341
  42.4 1.4 %collective-permute-start.8 = (bf16[128,512]{1,0:T(8,128)(2,1)S(1)}, bf16[128,512]{1,0:T(8,128)(2,1)S(1)}, u32[]{:S(2)}, u32[]{:S(2)}) collective-permute-start(bf16[128,512]{1,0:T(8,128)(2,1)S(1)} %get-tuple-element.46), channel_id=1, source_target_pairs={{0,2},{1,3},{2,0},{3,1},{4,6},{5,7},{6,4},{7,5},{8,10},{9,11},{10,... | collective-permute-start | bytes 393224 | tf_op jit(solution)/shard_map/ppermute | solution.py:341
  44.2 4.5 %collective-permute-done.8.refs_2_ = bf16[128,512]{1,0:T(8,128)(2,1)S(1)} collective-permute-done((bf16[128,512]{1,0:T(8,128)(2,1)S(1)}, bf16[128,512]{1,0:T(8,128)(2,1)S(1)}, u32[]{:S(2)}, u32[]{:S(2)}) %collective-permute-start.8) | collective-permute-done | bytes 131104 | tf_op jit(solution)/shard_map/ppermute | solution.py:341
  48.7 1.9 %collective-permute-done.9.refs_3_ = bf16[128,512]{1,0:T(8,128)(2,1)S(1)} collective-permute-done((bf16[128,512]{1,0:T(8,128)(2,1)S(1)}, bf16[128,512]{1,0:T(8,128)(2,1)S(1)}, u32[]{:S(2)}, u32[]{:S(2)}) %collective-permute-start.9) | collective-permute-done | bytes 131104 | tf_op jit(solution)/shard_map/ppermute | solution.py:341
  51.1 1.1 %collective-permute-done.12.refs_1_ = bf16[512,512]{1,0:T(8,128)(2,1)S(1)} collective-permute-done((bf16[512,512]{1,0:T(8,128)(2,1)S(1)}, bf16[512,512]{1,0:T(8,128)(2,1)S(1)}, u32[]{:S(2)}, u32[]{:S(2)}) %collective-permute-start.12) | collective-permute-done | bytes 524320 | tf_op jit(solution)/shard_map/ppermute | solution.py:341
  52.2 0.9 %finish.1 = bf16[512,512]{1,0:T(8,128)(2,1)} custom-call(f32[512,512]{1,0:T(8,128)S(1)} %with_deltas.1.start_ref, bf16[512,512]{1,0:T(8,128)(2,1)S(1)} %collective-permute-done.11.refs_0_, bf16[512,512]{1,0:T(8,128)(2,1)S(1)} %collective-permute-done.12.refs_1_), custom_call_target="tpu_custom_call" | custom-call | flops 262144 | bytes 2097152 | tf_op jit(solution)/shard_map/finish/pallas_call | solution.py:320
  (19 shorter events, 2.8 us)
Async XLA Ops:
  2.5 15.6 %collective-permute-start = (bf16[128,2176]{1,0:T(8,128)(2,1)S(1)}, bf16[128,2176]{1,0:T(8,128)(2,1)S(1)}, u32[]{:S(2)}, u32[]{:S(2)}) collective-permute-start(bf16[128,2176]{1,0:T(8,128)(2,1)S(1)} %get-tuple-element.35), channel_id=1, source_target_pairs={{0,2},{1,3},{2,0},{3,1},{4,6},{5,7},{6,4},{7,5},{8,10},{9,11},{10,... | collective-permute-start | bytes 1671176 | tf_op jit(solution)/shard_map/ppermute | solution.py:341
  6.7 15.8 %collective-permute-start.2 = (bf16[512,512]{1,0:T(8,128)(2,1)S(1)}, bf16[512,512]{1,0:T(8,128)(2,1)S(1)}, u32[]{:S(2)}, u32[]{:S(2)}) collective-permute-start(bf16[512,512]{1,0:T(8,128)(2,1)S(1)} %first_block.1), channel_id=1, source_target_pairs={{0,4},{12,8},{1,5},{13,9},{2,6},{14,10},{3,7},{15,11},{16,20},{28,... | collective-permute-start | bytes 1572872 | tf_op jit(solution)/shard_map/ppermute | solution.py:369
  10.2 7.8 %copy-start = (bf16[2048,512]{1,0:T(8,128)(2,1)S(1)}, bf16[2048,512]{1,0:T(8,128)(2,1)}, u32[]{:S(2)}) copy-start(bf16[2048,512]{1,0:T(8,128)(2,1)} %down_ref.5) | copy-start | bytes 6291460
  15.8 7.6 %collective-permute-start.1 = (bf16[128,2176]{1,0:T(8,128)(2,1)S(1)}, bf16[128,2176]{1,0:T(8,128)(2,1)S(1)}, u32[]{:S(2)}, u32[]{:S(2)}) collective-permute-start(bf16[128,2176]{1,0:T(8,128)(2,1)S(1)} %get-tuple-element.36), channel_id=1, source_target_pairs={{0,1},{1,0},{2,3},{3,2},{4,5},{5,4},{6,7},{7,6},{8,9},{9,8},{10,11... | collective-permute-start | bytes 1671176 | tf_op jit(solution)/shard_map/ppermute | solution.py:341
  15.9 14.4 %collective-permute-start.3 = (bf16[128,2176]{1,0:T(8,128)(2,1)S(1)}, bf16[128,2176]{1,0:T(8,128)(2,1)S(1)}, u32[]{:S(2)}, u32[]{:S(2)}) collective-permute-start(bf16[128,2176]{1,0:T(8,128)(2,1)S(1)} %get-tuple-element.39), channel_id=1, source_target_pairs={{0,3},{1,2},{2,1},{3,0},{4,7},{5,6},{6,5},{7,4},{8,11},{9,10},{10,... | collective-permute-start | bytes 1671176 | tf_op jit(solution)/shard_map/ppermute | solution.py:341
  16.5 15.8 %collective-permute-start.4 = (bf16[512,512]{1,0:T(8,128)(2,1)S(1)}, bf16[512,512]{1,0:T(8,128)(2,1)S(1)}, u32[]{:S(2)}, u32[]{:S(2)}) collective-permute-start(bf16[512,512]{1,0:T(8,128)(2,1)S(1)} %get-tuple-element.42), channel_id=1, source_target_pairs={{0,4},{12,8},{1,5},{13,9},{2,6},{14,10},{3,7},{15,11},{16,20},{28,... | collective-permute-start | bytes 1572872 | tf_op jit(solution)/shard_map/ppermute | solution.py:372
  22.7 14.9 %collective-permute-start.10 = (bf16[512,512]{1,0:T(8,128)(2,1)S(1)}, bf16[512,512]{1,0:T(8,128)(2,1)S(1)}, u32[]{:S(2)}, u32[]{:S(2)}) collective-permute-start(bf16[512,512]{1,0:T(8,128)(2,1)S(1)} %add_convert_fusion.2), channel_id=1, source_target_pairs={{4,8},{8,4},{5,9},{9,5},{6,10},{10,6},{7,11},{11,7},{20,24},{24,20... | collective-permute-start | bytes 1572872 | tf_op jit(solution)/shard_map/ppermute | solution.py:375
  30.8 10.9 %copy-start.1 = (bf16[512,512]{1,0:T(8,128)(2,1)S(1)}, bf16[512,512]{1,0:T(8,128)(2,1)}, u32[]{:S(2)}) copy-start(bf16[512,512]{1,0:T(8,128)(2,1)} %up_ref.1) | copy-start | bytes 1572868
  30.8 4.5 %collective-permute-start.5 = (bf16[256,128]{1,0:T(8,128)(2,1)S(1)}, bf16[256,128]{1,0:T(8,128)(2,1)S(1)}, u32[]{:S(2)}, u32[]{:S(2)}) collective-permute-start(bf16[256,128]{1,0:T(8,128)(2,1)S(1)} %shrink_partial.5), channel_id=1, source_target_pairs={{0,4},{4,0},{8,12},{12,8},{1,5},{5,1},{9,13},{13,9},{2,6},{6,2},{1... | collective-permute-start | bytes 196616 | tf_op jit(solution)/shard_map/ppermute | solution.py:341
  35.3 6.4 %collective-permute-start.6 = (bf16[256,128]{1,0:T(8,128)(2,1)S(1)}, bf16[256,128]{1,0:T(8,128)(2,1)S(1)}, u32[]{:S(2)}, u32[]{:S(2)}) collective-permute-start(bf16[256,128]{1,0:T(8,128)(2,1)S(1)} %add_convert_fusion.3.one_ref), channel_id=1, source_target_pairs={{0,8},{4,12},{8,0},{12,4},{1,9},{5,13},{9,1},{13,5},{2,10},{6,14},... | collective-permute-start | bytes 196616 | tf_op jit(solution)/shard_map/ppermute | solution.py:341
  37.7 14.4 %collective-permute-start.12 = (bf16[512,512]{1,0:T(8,128)(2,1)S(1)}, bf16[512,512]{1,0:T(8,128)(2,1)S(1)}, u32[]{:S(2)}, u32[]{:S(2)}) collective-permute-start(bf16[512,512]{1,0:T(8,128)(2,1)S(1)} %add_convert_fusion), channel_id=1, source_target_pairs={{0,4},{4,0},{8,12},{12,8},{1,5},{5,1},{9,13},{13,9},{2,6},{6,2},{1... | collective-permute-start | bytes 1572872 | tf_op jit(solution)/shard_map/ppermute | solution.py:341
  39.2 11.9 %collective-permute-start.11 = (bf16[512,512]{1,0:T(8,128)(2,1)S(1)}, bf16[512,512]{1,0:T(8,128)(2,1)S(1)}, u32[]{:S(2)}, u32[]{:S(2)}) collective-permute-start(bf16[512,512]{1,0:T(8,128)(2,1)S(1)} %add_convert_fusion.1), channel_id=1, source_target_pairs={{4,8},{8,4},{5,9},{9,5},{6,10},{10,6},{7,11},{11,7},{20,24},{24,20... | collective-permute-start | bytes 1572872 | tf_op jit(solution)/shard_map/ppermute | solution.py:383
  42.3 1.9 %collective-permute-start.7 = (bf16[128,512]{1,0:T(8,128)(2,1)S(1)}, bf16[128,512]{1,0:T(8,128)(2,1)S(1)}, u32[]{:S(2)}, u32[]{:S(2)}) collective-permute-start(bf16[128,512]{1,0:T(8,128)(2,1)S(1)} %get-tuple-element.45), channel_id=1, source_target_pairs={{0,1},{1,0},{2,3},{3,2},{4,5},{5,4},{6,7},{7,6},{8,9},{9,8},{10,11... | collective-permute-start | bytes 393224 | tf_op jit(solution)/shard_map/ppermute | solution.py:341
  42.4 6.4 %collective-permute-start.8 = (bf16[128,512]{1,0:T(8,128)(2,1)S(1)}, bf16[128,512]{1,0:T(8,128)(2,1)S(1)}, u32[]{:S(2)}, u32[]{:S(2)}) collective-permute-start(bf16[128,512]{1,0:T(8,128)(2,1)S(1)} %get-tuple-element.46), channel_id=1, source_target_pairs={{0,2},{1,3},{2,0},{3,1},{4,6},{5,7},{6,4},{7,5},{8,10},{9,11},{10,... | collective-permute-start | bytes 393224 | tf_op jit(solution)/shard_map/ppermute | solution.py:341
  43.8 6.9 %collective-permute-start.9 = (bf16[128,512]{1,0:T(8,128)(2,1)S(1)}, bf16[128,512]{1,0:T(8,128)(2,1)S(1)}, u32[]{:S(2)}, u32[]{:S(2)}) collective-permute-start(bf16[128,512]{1,0:T(8,128)(2,1)S(1)} %get-tuple-element.47), channel_id=1, source_target_pairs={{0,3},{1,2},{2,1},{3,0},{4,7},{5,6},{6,5},{7,4},{8,11},{9,10},{10,... | collective-permute-start | bytes 393224 | tf_op jit(solution)/shard_map/ppermute | solution.py:341

commit v12 on v11

--- a/solution.py
+++ b/solution.py
@@ -276,26 +276,28 @@
         in_specs=[whole(one), whole(two), whole(up)] + [tag_block] * count,
         out_specs=[pl.BlockSpec((capacity, columns), lambda i: (0, 0))] * count,
         compiler_params=params(),
-        cost_estimate=cost(80 * count * capacity * up.size, 80 * (up.size + count * capacity * columns)),
+        cost_estimate=cost(30 * count * capacity * up.size, 30 * (up.size + count * capacity * columns)),
         name="expand",
     )(one, two, up, *parts)
 
 
-def deltas_body(unsort_ref, own_ref, *refs):
-    deltas, out = refs[:-1], refs[-1]
-    placed = dot(unsort_ref[...], jnp.concatenate([d[...] for d in deltas], axis=0))
-    out[...] = own_ref[...].astype(f32) + placed
-
-
-def with_deltas(unsort, deltas, own):
-    rows, columns = own.shape
-    return pl.pallas_call(
-        deltas_body,
+def deltas_body(count, unsort_ref, *refs):
+    deltas, bases, out = refs[:count], refs[count:-1], refs[-1]
+    total = dot(unsort_ref[...], jnp.concatenate([d[...] for d in deltas], axis=0))
+    for base in bases:
+        total += base[...].astype(f32)
+    out[...] = total
+
+
+def with_deltas(unsort, deltas, bases):
+    rows, columns = bases[0].shape
+    return pl.pallas_call(
+        functools.partial(deltas_body, len(deltas)),
         out_shape=jax.ShapeDtypeStruct((rows, columns), f32),
         compiler_params=params(),
-        cost_estimate=cost(2 * rows * unsort.shape[1] * columns, 12 * rows * columns),
+        cost_estimate=cost(2 * rows * unsort.shape[1] * columns, 2 * 6 * rows * columns),
         name="with_deltas",
-    )(unsort, own, *deltas)
+    )(unsort, *deltas, *bases)
 
 
 def finish_body(start_ref, *refs):
@@ -346,11 +348,11 @@
 
 
 def tp_sums(mine, *before):
-    sums, bit = [mine], 1
+    sums, bit = [mine], lax.axis_size("tp") // 2
     while True:
         other = swap(sums[-1], "tp", bit)
-        bit *= 2
-        if bit >= lax.axis_size("tp"):
+        bit //= 2
+        if not bit:
             return sums, other
         sums.append(both(after(sums[-1], *before), other))
 
@@ -378,23 +380,23 @@
         parts, order = [near[0], far[0], near[1], far[1]], (0, 2, 1, 3)
         inner1 = both(after(second, mine), edge1)
         steps, other = tp_sums(mine, inner1)
+        middle1 = lax.ppermute(inner1, "tp", MIDDLE)
         inner2 = both(after(third, steps[-1]), middle0)
         last = swap(inner2, "tp", 1)
-        middle1 = lax.ppermute(after(inner1, inner2), "tp", MIDDLE)
-        sums = [middle1, last]
+        bases, sums = [own, middle1], [last]
     else:
         near = near_rows(spots, x, capacity)
         near = [near[0], swap(near[1], "ad", 1)]
         parts, order = near + far, range(holders)
         unsort = unsort_only(spots, total)
         full = dot(x, weight).astype(bf16)
-        own, sums = lax.psum_scatter(full, "tp", scatter_dimension=1, tiled=True), []
+        bases, sums = [lax.psum_scatter(full, "tp", scatter_dimension=1, tiled=True)], []
         steps, other = tp_sums(shrink_partial(down, parts))
     deltas = expand(steps[-1], other, up, parts)
     back = [None] * holders
     for j, delta in zip(order, deltas):
         back[j] = swap(delta, "ad", j) if j else delta
-    return finish(with_deltas(unsort, back, own), sums)
+    return finish(with_deltas(unsort, back, bases), sums)
 
 
 def solution(mesh):

time: 53.2 us -> 57.4 us (1.079)
  waiting for transfers between devices: 23.4 us -> 28.1 us
  starting transfers between devices: 16.2 us -> 15.6 us
    ppermute x9, waiting for transfers between devices: 18.8 us -> 24.4 us  [swap(): lax.ppermute(value, axis, [(i, i ^ bit) for i in range(lax.axis_size(axis...]
    ppermute x1, waiting for transfers between devices: 0.87 us -> 0.01 us  [shards(): edge1 = lax.ppermute(second, 'tp', EDGE)]
  transfers between devices with their start and end apart: 13 -> 13, of which waited for: 9 -> 7; matrix products, arithmetic and copies ran while one was open for 1% -> 1% of each run, Pallas kernels for 18% -> 17%
where the time goes in v12:
time: 57.4 us; the launch traced here: 57.2 us
  waiting for transfers between devices  28.1 us (49%)
  starting transfers between devices  15.6 us (27%)
  Pallas kernels  12.9 us (22%)
    ppermute x9, waiting for transfers between devices, swap(): lax.ppermute(value, axis, [(i, i ^ bit) for i in range(lax.axis_size(axis...  24.4 us
    ppermute x9, starting transfers between devices, swap(): lax.ppermute(value, axis, [(i, i ^ bit) for i in range(lax.axis_size(axis...  9.42 us
    pallas_call x1, Pallas kernels, rest(): pl.pallas_call(rest_body, out_shape=shapes, in_specs=[smem, vmem, vmem, h...  5.54 us
    ppermute x1, waiting for transfers between devices, shards(): edge0 = lax.ppermute(first, 'tp', EDGE)  3.68 us
    ppermute x1, starting transfers between devices, shards(): edge0 = lax.ppermute(first, 'tp', EDGE)  3.52 us
    pallas_call x1, Pallas kernels, far_rows(): pl.pallas_call(functools.partial(far_body, slots, capacity, holders), out...  2.46 us
    pallas_call x3, Pallas kernels, shrink_partial(): pl.pallas_call(functools.partial(shrink_body, kept), out_shape=jax.ShapeD...  1.82 us
    ppermute x1, starting transfers between devices, shards(): edge1 = lax.ppermute(second, 'tp', EDGE)  1.31 us
  transfers between devices with their start and end apart: 13, of which 7 were waited for; matrix products, arithmetic and copies ran while one was open for 1% of the time, Pallas kernels for 17%

profile of v12, /device:TPU:0, one launch (start us, length us, event | category | flops | bytes accessed | tf_op | source)
XLA Modules:
  0.0 57.2 jit_solution(14332898213331489922)
XLA Ops:
  0.0 2.5 %far_rows.1 = (s32[8,512]{1,0:T(8,128)S(1)}, bf16[128,2176]{1,0:T(8,128)(2,1)S(1)}, bf16[128,2176]{1,0:T(8,128)(2,1)S(1)}, bf16[512,2048]{1,0:T(8,128)(2,1)S(1)}, bf16[2048,512]{1,0:T(8,128)(2,1)S(1)}) custom-call(s32[1]{0:T(128)} %bitcast.1.me_ref, s32[1]{0:T(128)} %bitcast.z_ref, s32[1,512]{1,0:T(1,128)} %bitcast.5, s32[32,128]{1,0:T(8,128)} %bitcast.4, ...), custom_call_target="tpu_custom_call" | custom-call | flops 1073741824 | bytes 4194304 | tf_op jit(solution)/shard_map/far_rows/pallas_call | solution.py:112
  2.5 3.0 %collective-permute-start = (bf16[128,2176]{1,0:T(8,128)(2,1)S(1)}, bf16[128,2176]{1,0:T(8,128)(2,1)S(1)}, u32[]{:S(2)}, u32[]{:S(2)}) collective-permute-start(bf16[128,2176]{1,0:T(8,128)(2,1)S(1)} %get-tuple-element.33), channel_id=1, source_target_pairs={{0,2},{1,3},{2,0},{3,1},{4,6},{5,7},{6,4},{7,5},{8,10},{9,11},{10,... | collective-permute-start | bytes 1671176 | tf_op jit(solution)/shard_map/ppermute | solution.py:343
  5.5 1.3 %first_block.1 = bf16[512,512]{1,0:T(8,128)(2,1)S(1)} custom-call(bf16[512,2048]{1,0:T(8,128)(2,1)S(1)} %get-tuple-element.28.x_ref, bf16[2048,512]{1,0:T(8,128)(2,1)S(1)} %get-tuple-element.29.w_ref), custom_call_target="tpu_custom_call" | custom-call | flops 1073741824 | bytes 4194304 | tf_op jit(solution)/shard_map/first_block/pallas_call | solution.py:151
  6.7 3.5 %collective-permute-start.2 = (bf16[512,512]{1,0:T(8,128)(2,1)S(1)}, bf16[512,512]{1,0:T(8,128)(2,1)S(1)}, u32[]{:S(2)}, u32[]{:S(2)}) collective-permute-start(bf16[512,512]{1,0:T(8,128)(2,1)S(1)} %first_block.1), channel_id=1, source_target_pairs={{0,4},{12,8},{1,5},{13,9},{2,6},{14,10},{3,7},{15,11},{16,20},{28,... | collective-permute-start | bytes 1572872 | tf_op jit(solution)/shard_map/ppermute | solution.py:371
  10.3 5.5 %rest.1 = (bf16[128,2176]{1,0:T(8,128)(2,1)S(1)}, bf16[128,2176]{1,0:T(8,128)(2,1)S(1)}, bf16[512,512]{1,0:T(8,128)(2,1)S(1)}, bf16[512,512]{1,0:T(8,128)(2,1)S(...) custom-call(s32[1]{0:T(128)} %bitcast.z_ref, s32[8,512]{1,0:T(8,128)S(1)} %get-tuple-element.30.spots_ref, ...), custom_call_target="tpu_custom_call" | custom-call | flops 3221225472 | bytes 10485760 | tf_op jit(solution)/shard_map/rest/pallas_call | solution.py:189
  15.9 0.6 %collective-permute-start.3 = (bf16[128,2176]{1,0:T(8,128)(2,1)S(1)}, bf16[128,2176]{1,0:T(8,128)(2,1)S(1)}, u32[]{:S(2)}, u32[]{:S(2)}) collective-permute-start(bf16[128,2176]{1,0:T(8,128)(2,1)S(1)} %get-tuple-element.37), channel_id=1, source_target_pairs={{0,3},{1,2},{2,1},{3,0},{4,7},{5,6},{6,5},{7,4},{8,11},{9,10},{10,... | collective-permute-start | bytes 1671176 | tf_op jit(solution)/shard_map/ppermute | solution.py:343
  16.5 1.3 %collective-permute-start.4 = (bf16[512,512]{1,0:T(8,128)(2,1)S(1)}, bf16[512,512]{1,0:T(8,128)(2,1)S(1)}, u32[]{:S(2)}, u32[]{:S(2)}) collective-permute-start(bf16[512,512]{1,0:T(8,128)(2,1)S(1)} %get-tuple-element.40), channel_id=1, source_target_pairs={{0,4},{12,8},{1,5},{13,9},{2,6},{14,10},{3,7},{15,11},{16,20},{28,... | collective-permute-start | bytes 1572872 | tf_op jit(solution)/shard_map/ppermute | solution.py:374
  18.1 0.8 %shrink_partial.3.refs_0_ = bf16[128,128]{1,0:T(8,128)(2,1)S(1)} custom-call(bf16[2048,512]{1,0:T(8,128)(2,1)S(1)} %copy-done, bf16[128,2176]{1,0:T(8,128)(2,1)S(1)} %get-tuple-element.32.refs_0_, bf16[128,2176]{1,0:T(8,128)(2,1)S(1)} %collective-permute-done.refs_1_), custom_call_target="tpu_custom_call" | custom-call | flops 536870912 | bytes 3145728 | tf_op jit(solution)/shard_map/shrink_partial/pallas_call | solution.py:239
  18.9 3.7 %collective-permute-done.2 = bf16[512,512]{1,0:T(8,128)(2,1)S(1)} collective-permute-done((bf16[512,512]{1,0:T(8,128)(2,1)S(1)}, bf16[512,512]{1,0:T(8,128)(2,1)S(1)}, u32[]{:S(2)}, u32[]{:S(2)}) %collective-permute-start.2) | collective-permute-done | bytes 524320 | tf_op jit(solution)/shard_map/ppermute | solution.py:371
  22.7 0.7 %collective-permute-start.11 = (bf16[512,512]{1,0:T(8,128)(2,1)S(1)}, bf16[512,512]{1,0:T(8,128)(2,1)S(1)}, u32[]{:S(2)}, u32[]{:S(2)}) collective-permute-start(bf16[512,512]{1,0:T(8,128)(2,1)S(1)} %add_convert_fusion.2), channel_id=1, source_target_pairs={{4,8},{8,4},{5,9},{9,5},{6,10},{10,6},{7,11},{11,7},{20,24},{24,20... | collective-permute-start | bytes 1572872 | tf_op jit(solution)/shard_map/ppermute | solution.py:377
  23.4 0.5 shrink_partial.4.refs_0_
  23.9 6.4 %collective-permute-done.3.refs_1_.refs_3_ = bf16[128,2176]{1,0:T(8,128)(2,1)S(1)} collective-permute-done((bf16[128,2176]{1,0:T(8,128)(2,1)S(1)}, bf16[128,2176]{1,0:T(8,128)(2,1)S(1)}, u32[]{:S(2)}, u32[]{:S(2)}) %collective-permute-start.3) | collective-permute-done | bytes 557088 | tf_op jit(solution)/shard_map/ppermute | solution.py:343
  30.3 0.5 shrink_partial.5
  30.8 1.6 %collective-permute-start.5 = (bf16[256,128]{1,0:T(8,128)(2,1)S(1)}, bf16[256,128]{1,0:T(8,128)(2,1)S(1)}, u32[]{:S(2)}, u32[]{:S(2)}) collective-permute-start(bf16[256,128]{1,0:T(8,128)(2,1)S(1)} %shrink_partial.5), channel_id=1, source_target_pairs={{0,8},{4,12},{8,0},{12,4},{1,9},{5,13},{9,1},{13,5},{2,10},{6,14},... | collective-permute-start | bytes 196616 | tf_op jit(solution)/shard_map/ppermute | solution.py:343
  32.6 0.7 %collective-permute-start.10 = (bf16[512,512]{1,0:T(8,128)(2,1)S(1)}, bf16[512,512]{1,0:T(8,128)(2,1)S(1)}, u32[]{:S(2)}, u32[]{:S(2)}) collective-permute-start(bf16[512,512]{1,0:T(8,128)(2,1)S(1)} %add_convert_fusion.1), channel_id=1, source_target_pairs={{4,8},{8,4},{5,9},{9,5},{6,10},{10,6},{7,11},{11,7},{20,24},{24,20... | collective-permute-start | bytes 1572872 | tf_op jit(solution)/shard_map/ppermute | solution.py:383
  33.3 8.6 %collective-permute-done.5 = bf16[256,128]{1,0:T(8,128)(2,1)S(1)} collective-permute-done((bf16[256,128]{1,0:T(8,128)(2,1)S(1)}, bf16[256,128]{1,0:T(8,128)(2,1)S(1)}, u32[]{:S(2)}, u32[]{:S(2)}) %collective-permute-start.5) | collective-permute-done | bytes 65568 | tf_op jit(solution)/shard_map/ppermute | solution.py:343
  42.3 1.9 %collective-permute-start.12 = (bf16[512,512]{1,0:T(8,128)(2,1)S(1)}, bf16[512,512]{1,0:T(8,128)(2,1)S(1)}, u32[]{:S(2)}, u32[]{:S(2)}) collective-permute-start(bf16[512,512]{1,0:T(8,128)(2,1)S(1)} %add_convert_fusion), channel_id=1, source_target_pairs={{0,4},{4,0},{8,12},{12,8},{1,5},{5,1},{9,13},{13,9},{2,6},{6,2},{1... | collective-permute-start | bytes 1572872 | tf_op jit(solution)/shard_map/ppermute | solution.py:343
  44.3 2.8 %collective-permute-done.6.two_ref = bf16[256,128]{1,0:T(8,128)(2,1)S(1)} collective-permute-done((bf16[256,128]{1,0:T(8,128)(2,1)S(1)}, bf16[256,128]{1,0:T(8,128)(2,1)S(1)}, u32[]{:S(2)}, u32[]{:S(2)}) %collective-permute-start.6) | collective-permute-done | bytes 65568 | tf_op jit(solution)/shard_map/ppermute | solution.py:343
  47.1 0.5 expand.1
  47.7 1.8 %collective-permute-start.9 = (bf16[128,512]{1,0:T(8,128)(2,1)S(1)}, bf16[128,512]{1,0:T(8,128)(2,1)S(1)}, u32[]{:S(2)}, u32[]{:S(2)}) collective-permute-start(bf16[128,512]{1,0:T(8,128)(2,1)S(1)} %get-tuple-element.45), channel_id=1, source_target_pairs={{0,3},{1,2},{2,1},{3,0},{4,7},{5,6},{6,5},{7,4},{8,11},{9,10},{10,... | collective-permute-start | bytes 393224 | tf_op jit(solution)/shard_map/ppermute | solution.py:343
  49.5 4.5 %collective-permute-done.8.refs_2_ = bf16[128,512]{1,0:T(8,128)(2,1)S(1)} collective-permute-done((bf16[128,512]{1,0:T(8,128)(2,1)S(1)}, bf16[128,512]{1,0:T(8,128)(2,1)S(1)}, u32[]{:S(2)}, u32[]{:S(2)}) %collective-permute-start.8) | collective-permute-done | bytes 131104 | tf_op jit(solution)/shard_map/ppermute | solution.py:343
  54.0 1.9 %collective-permute-done.9.refs_3_ = bf16[128,512]{1,0:T(8,128)(2,1)S(1)} collective-permute-done((bf16[128,512]{1,0:T(8,128)(2,1)S(1)}, bf16[128,512]{1,0:T(8,128)(2,1)S(1)}, u32[]{:S(2)}, u32[]{:S(2)}) %collective-permute-start.9) | collective-permute-done | bytes 131104 | tf_op jit(solution)/shard_map/ppermute | solution.py:343
  55.9 0.4 with_deltas.1.start_ref
  56.4 0.8 %finish.1 = bf16[512,512]{1,0:T(8,128)(2,1)} custom-call(f32[512,512]{1,0:T(8,128)S(1)} %with_deltas.1.start_ref, bf16[512,512]{1,0:T(8,128)(2,1)S(1)} %collective-permute-done.12.refs_0_), custom_call_target="tpu_custom_call" | custom-call | flops 262144 | bytes 2097152 | tf_op jit(solution)/shard_map/finish/pallas_call | solution.py:322
  (19 shorter events, 1.1 us)
Async XLA Ops:
  2.5 15.6 %collective-permute-start = (bf16[128,2176]{1,0:T(8,128)(2,1)S(1)}, bf16[128,2176]{1,0:T(8,128)(2,1)S(1)}, u32[]{:S(2)}, u32[]{:S(2)}) collective-permute-start(bf16[128,2176]{1,0:T(8,128)(2,1)S(1)} %get-tuple-element.33), channel_id=1, source_target_pairs={{0,2},{1,3},{2,0},{3,1},{4,6},{5,7},{6,4},{7,5},{8,10},{9,11},{10,... | collective-permute-start | bytes 1671176 | tf_op jit(solution)/shard_map/ppermute | solution.py:343
  6.7 15.8 %collective-permute-start.2 = (bf16[512,512]{1,0:T(8,128)(2,1)S(1)}, bf16[512,512]{1,0:T(8,128)(2,1)S(1)}, u32[]{:S(2)}, u32[]{:S(2)}) collective-permute-start(bf16[512,512]{1,0:T(8,128)(2,1)S(1)} %first_block.1), channel_id=1, source_target_pairs={{0,4},{12,8},{1,5},{13,9},{2,6},{14,10},{3,7},{15,11},{16,20},{28,... | collective-permute-start | bytes 1572872 | tf_op jit(solution)/shard_map/ppermute | solution.py:371
  10.2 7.8 %copy-start = (bf16[2048,512]{1,0:T(8,128)(2,1)S(1)}, bf16[2048,512]{1,0:T(8,128)(2,1)}, u32[]{:S(2)}) copy-start(bf16[2048,512]{1,0:T(8,128)(2,1)} %down_ref.5) | copy-start | bytes 6291460
  15.8 7.6 %collective-permute-start.1 = (bf16[128,2176]{1,0:T(8,128)(2,1)S(1)}, bf16[128,2176]{1,0:T(8,128)(2,1)S(1)}, u32[]{:S(2)}, u32[]{:S(2)}) collective-permute-start(bf16[128,2176]{1,0:T(8,128)(2,1)S(1)} %get-tuple-element.34), channel_id=1, source_target_pairs={{0,1},{1,0},{2,3},{3,2},{4,5},{5,4},{6,7},{7,6},{8,9},{9,8},{10,11... | collective-permute-start | bytes 1671176 | tf_op jit(solution)/shard_map/ppermute | solution.py:343
  15.9 14.4 %collective-permute-start.3 = (bf16[128,2176]{1,0:T(8,128)(2,1)S(1)}, bf16[128,2176]{1,0:T(8,128)(2,1)S(1)}, u32[]{:S(2)}, u32[]{:S(2)}) collective-permute-start(bf16[128,2176]{1,0:T(8,128)(2,1)S(1)} %get-tuple-element.37), channel_id=1, source_target_pairs={{0,3},{1,2},{2,1},{3,0},{4,7},{5,6},{6,5},{7,4},{8,11},{9,10},{10,... | collective-permute-start | bytes 1671176 | tf_op jit(solution)/shard_map/ppermute | solution.py:343
  16.5 15.9 %collective-permute-start.4 = (bf16[512,512]{1,0:T(8,128)(2,1)S(1)}, bf16[512,512]{1,0:T(8,128)(2,1)S(1)}, u32[]{:S(2)}, u32[]{:S(2)}) collective-permute-start(bf16[512,512]{1,0:T(8,128)(2,1)S(1)} %get-tuple-element.40), channel_id=1, source_target_pairs={{0,4},{12,8},{1,5},{13,9},{2,6},{14,10},{3,7},{15,11},{16,20},{28,... | collective-permute-start | bytes 1572872 | tf_op jit(solution)/shard_map/ppermute | solution.py:374
  22.7 19.5 %collective-permute-start.11 = (bf16[512,512]{1,0:T(8,128)(2,1)S(1)}, bf16[512,512]{1,0:T(8,128)(2,1)S(1)}, u32[]{:S(2)}, u32[]{:S(2)}) collective-permute-start(bf16[512,512]{1,0:T(8,128)(2,1)S(1)} %add_convert_fusion.2), channel_id=1, source_target_pairs={{4,8},{8,4},{5,9},{9,5},{6,10},{10,6},{7,11},{11,7},{20,24},{24,20... | collective-permute-start | bytes 1572872 | tf_op jit(solution)/shard_map/ppermute | solution.py:377
  30.8 16.2 %copy-start.1 = (bf16[512,512]{1,0:T(8,128)(2,1)S(1)}, bf16[512,512]{1,0:T(8,128)(2,1)}, u32[]{:S(2)}) copy-start(bf16[512,512]{1,0:T(8,128)(2,1)} %up_ref.1) | copy-start | bytes 1572868
  30.8 11.1 %collective-permute-start.5 = (bf16[256,128]{1,0:T(8,128)(2,1)S(1)}, bf16[256,128]{1,0:T(8,128)(2,1)S(1)}, u32[]{:S(2)}, u32[]{:S(2)}) collective-permute-start(bf16[256,128]{1,0:T(8,128)(2,1)S(1)} %shrink_partial.5), channel_id=1, source_target_pairs={{0,8},{4,12},{8,0},{12,4},{1,9},{5,13},{9,1},{13,5},{2,10},{6,14},... | collective-permute-start | bytes 196616 | tf_op jit(solution)/shard_map/ppermute | solution.py:343
  32.6 23.3 %collective-permute-start.10 = (bf16[512,512]{1,0:T(8,128)(2,1)S(1)}, bf16[512,512]{1,0:T(8,128)(2,1)S(1)}, u32[]{:S(2)}, u32[]{:S(2)}) collective-permute-start(bf16[512,512]{1,0:T(8,128)(2,1)S(1)} %add_convert_fusion.1), channel_id=1, source_target_pairs={{4,8},{8,4},{5,9},{9,5},{6,10},{10,6},{7,11},{11,7},{20,24},{24,20... | collective-permute-start | bytes 1572872 | tf_op jit(solution)/shard_map/ppermute | solution.py:383
  42.0 5.1 %collective-permute-start.6 = (bf16[256,128]{1,0:T(8,128)(2,1)S(1)}, bf16[256,128]{1,0:T(8,128)(2,1)S(1)}, u32[]{:S(2)}, u32[]{:S(2)}) collective-permute-start(bf16[256,128]{1,0:T(8,128)(2,1)S(1)} %add_convert_fusion.3.one_ref), channel_id=1, source_target_pairs={{0,4},{4,0},{8,12},{12,8},{1,5},{5,1},{9,13},{13,9},{2,6},{6,2},{1... | collective-permute-start | bytes 196616 | tf_op jit(solution)/shard_map/ppermute | solution.py:343
  42.3 14.0 %collective-permute-start.12 = (bf16[512,512]{1,0:T(8,128)(2,1)S(1)}, bf16[512,512]{1,0:T(8,128)(2,1)S(1)}, u32[]{:S(2)}, u32[]{:S(2)}) collective-permute-start(bf16[512,512]{1,0:T(8,128)(2,1)S(1)} %add_convert_fusion), channel_id=1, source_target_pairs={{0,4},{4,0},{8,12},{12,8},{1,5},{5,1},{9,13},{13,9},{2,6},{6,2},{1... | collective-permute-start | bytes 1572872 | tf_op jit(solution)/shard_map/ppermute | solution.py:343
  47.6 1.9 %collective-permute-start.7 = (bf16[128,512]{1,0:T(8,128)(2,1)S(1)}, bf16[128,512]{1,0:T(8,128)(2,1)S(1)}, u32[]{:S(2)}, u32[]{:S(2)}) collective-permute-start(bf16[128,512]{1,0:T(8,128)(2,1)S(1)} %get-tuple-element.43), channel_id=1, source_target_pairs={{0,1},{1,0},{2,3},{3,2},{4,5},{5,4},{6,7},{7,6},{8,9},{9,8},{10,11... | collective-permute-start | bytes 393224 | tf_op jit(solution)/shard_map/ppermute | solution.py:343
  47.6 6.4 %collective-permute-start.8 = (bf16[128,512]{1,0:T(8,128)(2,1)S(1)}, bf16[128,512]{1,0:T(8,128)(2,1)S(1)}, u32[]{:S(2)}, u32[]{:S(2)}) collective-permute-start(bf16[128,512]{1,0:T(8,128)(2,1)S(1)} %get-tuple-element.44), channel_id=1, source_target_pairs={{0,2},{1,3},{2,0},{3,1},{4,6},{5,7},{6,4},{7,5},{8,10},{9,11},{10,... | collective-permute-start | bytes 393224 | tf_op jit(solution)/shard_map/ppermute | solution.py:343
  47.7 8.2 %collective-permute-start.9 = (bf16[128,512]{1,0:T(8,128)(2,1)S(1)}, bf16[128,512]{1,0:T(8,128)(2,1)S(1)}, u32[]{:S(2)}, u32[]{:S(2)}) collective-permute-start(bf16[128,512]{1,0:T(8,128)(2,1)S(1)} %get-tuple-element.45), channel_id=1, source_target_pairs={{0,3},{1,2},{2,1},{3,0},{4,7},{5,6},{6,5},{7,4},{8,11},{9,10},{10,... | collective-permute-start | bytes 393224 | tf_op jit(solution)/shard_map/ppermute | solution.py:343

commit v13 on v11

--- a/solution.py
+++ b/solution.py
@@ -10,6 +10,7 @@
 ADAPTER_RANK = 64
 LANES = 128
 NEAR = 2
+TAG_ROWS = 16
 VMEM_BYTES = 32 * 1024 * 1024
 
 bf16 = jnp.bfloat16
@@ -67,17 +68,29 @@
 
 def pick_rows(start, place, tag, x, outs):
     rows, features = x.shape
-    capacity = outs[0].shape[0]
-    pick = iota((len(outs) * capacity, rows), 0) + start * capacity == place
+    pick = iota((len(outs) * LANES, rows), 0) + start * LANES == place
     pick = pick.astype(f32).astype(bf16)
-    tags = dot(pick, jnp.broadcast_to(tag, (LANES, rows)).astype(bf16), ((1,), (1,))).astype(bf16)
+    tags = dot(jnp.broadcast_to(tag, (TAG_ROWS, rows)).astype(bf16), pick, ((1,), (1,))).astype(bf16)
     step = min(512, features)
     for c in range(0, features, step):
         moved = dot(pick, x[:, c:c + step]).astype(bf16)
         for j, out in enumerate(outs):
-            out[:, c:c + step] = moved[j * capacity:(j + 1) * capacity]
+            for i in range(0, step, LANES):
+                out[c + i:c + i + LANES, :] = moved[j * LANES:(j + 1) * LANES, i:i + LANES]
     for j, out in enumerate(outs):
-        out[:, features:] = tags[j * capacity:(j + 1) * capacity]
+        out[features:, :] = tags[:, j * LANES:(j + 1) * LANES]
+
+
+def part_rows(part, features):
+    return jnp.concatenate([part[c:c + LANES, :] for c in range(0, features, LANES)], axis=1)
+
+
+def tag_lanes(tags):
+    return jnp.broadcast_to(tags[0:1, :].astype(f32), (LANES, LANES)).T
+
+
+def part_shape(features):
+    return jax.ShapeDtypeStruct((features + TAG_ROWS, LANES), bf16)
 
 
 def far_body(slots, capacity, holders, me_ref, z_ref, ids_hbm, table_hbm, x_hbm, w_hbm, places_ref, *refs):
@@ -107,7 +120,7 @@
     ids, table = ids.reshape(1, rows), table.reshape(-1, LANES)
     smem, vmem, hbm = (pl.BlockSpec(memory_space=m) for m in (pltpu.SMEM, pltpu.VMEM, pltpu.HBM))
     shapes = [jax.ShapeDtypeStruct((8, rows), i32)]
-    shapes += [jax.ShapeDtypeStruct((capacity, features + LANES), bf16)] * (holders - NEAR)
+    shapes += [part_shape(features)] * (holders - NEAR)
     shapes += [jax.ShapeDtypeStruct((rows, features), bf16), jax.ShapeDtypeStruct((features, width), bf16)]
     return pl.pallas_call(
         functools.partial(far_body, slots, capacity, holders),
@@ -135,7 +148,7 @@
     rows, features = x.shape
     return pl.pallas_call(
         near_body,
-        out_shape=[jax.ShapeDtypeStruct((capacity, features + LANES), bf16)] * NEAR,
+        out_shape=[part_shape(features)] * NEAR,
         compiler_params=params(),
         cost_estimate=cost(2 * NEAR * capacity * rows * features, 4 * rows * features),
         name="near_rows",
@@ -184,7 +197,7 @@
 def rest(z, spots, x, weight, width, total, capacity):
     rows, features = x.shape
     smem, vmem, hbm = (pl.BlockSpec(memory_space=m) for m in (pltpu.SMEM, pltpu.VMEM, pltpu.HBM))
-    shapes = [jax.ShapeDtypeStruct((capacity, features + LANES), bf16)] * NEAR
+    shapes = [part_shape(features)] * NEAR
     shapes += [jax.ShapeDtypeStruct((rows, width), bf16)] * 3 + [jax.ShapeDtypeStruct((rows, total), bf16)]
     return pl.pallas_call(
         rest_body,
@@ -215,15 +228,14 @@
 def shrink_body(kept, down_ref, *refs):
     parts, out = refs[1 if kept else 0:-1], refs[-1]
     features, width = down_ref.shape
-    capacity = parts[0].shape[0]
-    half = capacity // 2
+    half = LANES // 2
     first = iota((half, LANES), 1) < ADAPTER_RANK
     if kept:
         out[:kept, :] = refs[0][...]
     for k, part in enumerate(parts):
-        full = dot(part[:, :features], down_ref[...])
-        tag = part[:, features:].astype(f32)
-        total = jnp.zeros((capacity, LANES), f32)
+        tag = tag_lanes(part[features:, :])
+        full = dot(part_rows(part, features), down_ref[...])
+        total = jnp.zeros((LANES, LANES), f32)
         for group in range(width // LANES):
             total += jnp.where(slot_mask(tag, group), full[:, group * LANES:(group + 1) * LANES], 0.0)
         total += pltpu.roll(total, ADAPTER_RANK, 1)
@@ -233,8 +245,7 @@
 
 def shrink_partial(down, parts, done=()):
     features, width = down.shape
-    capacity = parts[0].shape[0]
-    total = len(parts) * capacity
+    total = len(parts) * LANES
     kept = sum(d.shape[0] for d in done)
     return pl.pallas_call(
         functools.partial(shrink_body, kept),
@@ -256,7 +267,7 @@
         shrink = (one_ref[part, :].astype(f32) + two_ref[part, :].astype(f32)).astype(bf16).astype(f32)
         turned = pltpu.roll(shrink, ADAPTER_RANK, 1)
         rows = jnp.concatenate([jnp.where(first, shrink, turned), jnp.where(first, turned, shrink)], axis=0)
-        tag = tags[k][...].astype(f32)
+        tag = tag_lanes(tags[k][...])
         spread = [
             jnp.where(slot_mask(tag, group), rows, 0.0).astype(bf16) for group in range(up.shape[0] // LANES)
         ]
@@ -264,9 +275,9 @@
 
 
 def expand(one, two, up, parts):
-    capacity, width = parts[0].shape
-    count = len(parts)
-    tag_block = pl.BlockSpec((capacity, LANES), lambda i: (0, width // LANES - 1))
+    capacity, count = LANES, len(parts)
+    last = parts[0].shape[0] // TAG_ROWS - 1
+    tag_block = pl.BlockSpec((TAG_ROWS, LANES), lambda i: (last, 0))
     whole = lambda a: pl.BlockSpec(a.shape, lambda i: (0, 0))
     columns = up.shape[1]
     return pl.pallas_call(
@@ -358,6 +369,7 @@
 def shards(x, ids, table, weight, down, up):
     holders = lax.axis_size("ad")
     capacity = x.shape[0] // 4
+    assert capacity == LANES
     slots = up.shape[0] // ADAPTER_RANK
     width = up.shape[1]
     total = holders * capacity

time: 53.2 us -> 52.2 us (0.981)
  starting transfers between devices: 16.2 us -> 15.3 us
    ppermute x9, waiting for transfers between devices: 18.8 us -> 16.5 us  [swap(): lax.ppermute(value, axis, [(i, i ^ bit) for i in range(lax.axis_size(axis...]
    ppermute x1, waiting for transfers between devices: 0.87 us -> 2.71 us  [shards(): edge1 = lax.ppermute(second, 'tp', EDGE)]
    ppermute x9, starting transfers between devices: 9.95 us -> 9.11 us  [swap(): lax.ppermute(value, axis, [(i, i ^ bit) for i in range(lax.axis_size(axis...]
  transfers between devices with their start and end apart: 13 -> 13, of which waited for: 9 -> 8; matrix products, arithmetic and copies ran while one was open for 1% -> 1% of each run, Pallas kernels for 18% -> 18%
where the time goes in v13:
time: 52.2 us; the launch traced here: 52 us
  waiting for transfers between devices  23.1 us (44%)
  starting transfers between devices  15.3 us (29%)
  Pallas kernels  12.9 us (25%)
    ppermute x9, waiting for transfers between devices, swap(): lax.ppermute(value, axis, [(i, i ^ bit) for i in range(lax.axis_size(axis...  16.5 us
    ppermute x9, starting transfers between devices, swap(): lax.ppermute(value, axis, [(i, i ^ bit) for i in range(lax.axis_size(axis...  9.11 us
    pallas_call x1, Pallas kernels, rest(): pl.pallas_call(rest_body, out_shape=shapes, in_specs=[smem, vmem, vmem, h...  5.55 us
    ppermute x1, waiting for transfers between devices, shards(): edge0 = lax.ppermute(first, 'tp', EDGE)  3.89 us
    ppermute x1, starting transfers between devices, shards(): edge0 = lax.ppermute(first, 'tp', EDGE)  3.51 us
    ppermute x1, waiting for transfers between devices, shards(): edge1 = lax.ppermute(second, 'tp', EDGE)  2.71 us
    pallas_call x1, Pallas kernels, far_rows(): pl.pallas_call(functools.partial(far_body, slots, capacity, holders), out...  2.44 us
    pallas_call x3, Pallas kernels, shrink_partial(): pl.pallas_call(functools.partial(shrink_body, kept), out_shape=jax.ShapeD...  1.84 us
  transfers between devices with their start and end apart: 13, of which 8 were waited for; matrix products, arithmetic and copies ran while one was open for 1% of the time, Pallas kernels for 18%

profile of v13, /device:TPU:0, one launch (start us, length us, event | category | flops | bytes accessed | tf_op | source)
XLA Modules:
  0.0 52.0 jit_solution(1130782482936743981)
XLA Ops:
  0.0 2.4 %far_rows.1 = (s32[8,512]{1,0:T(8,128)S(1)}, bf16[2064,128]{1,0:T(8,128)(2,1)S(1)}, bf16[2064,128]{1,0:T(8,128)(2,1)S(1)}, bf16[512,2048]{1,0:T(8,128)(2,1)S(1)}, bf16[2048,512]{1,0:T(8,128)(2,1)S(1)}) custom-call(s32[1]{0:T(128)} %bitcast.1.me_ref, s32[1]{0:T(128)} %bitcast.z_ref, s32[1,512]{1,0:T(1,128)} %bitcast.5, s32[32,128]{1,0:T(8,128)} %bitcast.4, ...), custom_call_target="tpu_custom_call" | custom-call | flops 1073741824 | bytes 4194304 | tf_op jit(solution)/shard_map/far_rows/pallas_call | solution.py:125
  2.4 3.0 %collective-permute-start = (bf16[2064,128]{1,0:T(8,128)(2,1)S(1)}, bf16[2064,128]{1,0:T(8,128)(2,1)S(1)}, u32[]{:S(2)}, u32[]{:S(2)}) collective-permute-start(bf16[2064,128]{1,0:T(8,128)(2,1)S(1)} %get-tuple-element.35), channel_id=1, source_target_pairs={{0,2},{1,3},{2,0},{3,1},{4,6},{5,7},{6,4},{7,5},{8,10},{9,11},{10,... | collective-permute-start | bytes 1585160 | tf_op jit(solution)/shard_map/ppermute | solution.py:352
  5.5 1.2 %first_block.1 = bf16[512,512]{1,0:T(8,128)(2,1)S(1)} custom-call(bf16[512,2048]{1,0:T(8,128)(2,1)S(1)} %get-tuple-element.29.x_ref, bf16[2048,512]{1,0:T(8,128)(2,1)S(1)} %get-tuple-element.30.w_ref), custom_call_target="tpu_custom_call" | custom-call | flops 1073741824 | bytes 4194304 | tf_op jit(solution)/shard_map/first_block/pallas_call | solution.py:164
  6.7 3.5 %collective-permute-start.2 = (bf16[512,512]{1,0:T(8,128)(2,1)S(1)}, bf16[512,512]{1,0:T(8,128)(2,1)S(1)}, u32[]{:S(2)}, u32[]{:S(2)}) collective-permute-start(bf16[512,512]{1,0:T(8,128)(2,1)S(1)} %first_block.1), channel_id=1, source_target_pairs={{0,4},{12,8},{1,5},{13,9},{2,6},{14,10},{3,7},{15,11},{16,20},{28,... | collective-permute-start | bytes 1572872 | tf_op jit(solution)/shard_map/ppermute | solution.py:381
  10.2 5.5 %rest.1 = (bf16[2064,128]{1,0:T(8,128)(2,1)S(1)}, bf16[2064,128]{1,0:T(8,128)(2,1)S(1)}, bf16[512,512]{1,0:T(8,128)(2,1)S(1)}, bf16[512,512]{1,0:T(8,128)(2,1)S(...) custom-call(s32[1]{0:T(128)} %bitcast.z_ref, s32[8,512]{1,0:T(8,128)S(1)} %get-tuple-element.31.spots_ref, ...), custom_call_target="tpu_custom_call" | custom-call | flops 3221225472 | bytes 10485760 | tf_op jit(solution)/shard_map/rest/pallas_call | solution.py:202
  15.9 0.6 %collective-permute-start.3 = (bf16[2064,128]{1,0:T(8,128)(2,1)S(1)}, bf16[2064,128]{1,0:T(8,128)(2,1)S(1)}, u32[]{:S(2)}, u32[]{:S(2)}) collective-permute-start(bf16[2064,128]{1,0:T(8,128)(2,1)S(1)} %get-tuple-element.39), channel_id=1, source_target_pairs={{0,3},{1,2},{2,1},{3,0},{4,7},{5,6},{6,5},{7,4},{8,11},{9,10},{10,... | collective-permute-start | bytes 1585160 | tf_op jit(solution)/shard_map/ppermute | solution.py:352
  16.5 1.3 %collective-permute-start.4 = (bf16[512,512]{1,0:T(8,128)(2,1)S(1)}, bf16[512,512]{1,0:T(8,128)(2,1)S(1)}, u32[]{:S(2)}, u32[]{:S(2)}) collective-permute-start(bf16[512,512]{1,0:T(8,128)(2,1)S(1)} %get-tuple-element.42), channel_id=1, source_target_pairs={{0,4},{12,8},{1,5},{13,9},{2,6},{14,10},{3,7},{15,11},{16,20},{28,... | collective-permute-start | bytes 1572872 | tf_op jit(solution)/shard_map/ppermute | solution.py:384
  17.9 0.8 %shrink_partial.3.refs_0_ = bf16[128,128]{1,0:T(8,128)(2,1)S(1)} custom-call(bf16[2048,512]{1,0:T(8,128)(2,1)S(1)} %copy-done, bf16[2064,128]{1,0:T(8,128)(2,1)S(1)} %get-tuple-element.34.refs_0_, bf16[2064,128]{1,0:T(8,128)(2,1)S(1)} %collective-permute-done.refs_1_), custom_call_target="tpu_custom_call" | custom-call | flops 536870912 | bytes 3145728 | tf_op jit(solution)/shard_map/shrink_partial/pallas_call | solution.py:250
  18.7 3.9 %collective-permute-done.2 = bf16[512,512]{1,0:T(8,128)(2,1)S(1)} collective-permute-done((bf16[512,512]{1,0:T(8,128)(2,1)S(1)}, bf16[512,512]{1,0:T(8,128)(2,1)S(1)}, u32[]{:S(2)}, u32[]{:S(2)}) %collective-permute-start.2) | collective-permute-done | bytes 524320 | tf_op jit(solution)/shard_map/ppermute | solution.py:381
  22.7 0.7 %collective-permute-start.10 = (bf16[512,512]{1,0:T(8,128)(2,1)S(1)}, bf16[512,512]{1,0:T(8,128)(2,1)S(1)}, u32[]{:S(2)}, u32[]{:S(2)}) collective-permute-start(bf16[512,512]{1,0:T(8,128)(2,1)S(1)} %add_convert_fusion.2), channel_id=1, source_target_pairs={{4,8},{8,4},{5,9},{9,5},{6,10},{10,6},{7,11},{11,7},{20,24},{24,20... | collective-permute-start | bytes 1572872 | tf_op jit(solution)/shard_map/ppermute | solution.py:387
  23.4 0.5 %shrink_partial.4.refs_0_ = bf16[192,128]{1,0:T(8,128)(2,1)S(1)} custom-call(bf16[2048,512]{1,0:T(8,128)(2,1)S(1)} %copy-done, bf16[128,128]{1,0:T(8,128)(2,1)S(1)} %shrink_partial.3.refs_0_, bf16[2064,128]{1,0:T(8,128)(2,1)S(1)} %collective-permute-done.1.refs_1_.refs_2_), custom_call_target="tpu_custom_call" | custom-call | flops 268435456 | bytes 2621440 | tf_op jit(solution)/shard_map/shrink_partial/pallas_call | solution.py:250
  23.9 5.7 %collective-permute-done.3.refs_1_.refs_3_ = bf16[2064,128]{1,0:T(8,128)(2,1)S(1)} collective-permute-done((bf16[2064,128]{1,0:T(8,128)(2,1)S(1)}, bf16[2064,128]{1,0:T(8,128)(2,1)S(1)}, u32[]{:S(2)}, u32[]{:S(2)}) %collective-permute-start.3) | collective-permute-done | bytes 528416 | tf_op jit(solution)/shard_map/ppermute | solution.py:352
  29.7 0.5 %shrink_partial.5 = bf16[256,128]{1,0:T(8,128)(2,1)S(1)} custom-call(bf16[2048,512]{1,0:T(8,128)(2,1)S(1)} %copy-done, bf16[192,128]{1,0:T(8,128)(2,1)S(1)} %shrink_partial.4.refs_0_, bf16[2064,128]{1,0:T(8,128)(2,1)S(1)} %collective-permute-done.3.refs_1_.refs_3_), custom_call_target="tpu_custom_call" | custom-call | flops 268435456 | bytes 2621440 | tf_op jit(solution)/shard_map/shrink_partial/pallas_call | solution.py:250
  30.3 2.7 %collective-permute-done.4 = bf16[512,512]{1,0:T(8,128)(2,1)S(1)} collective-permute-done((bf16[512,512]{1,0:T(8,128)(2,1)S(1)}, bf16[512,512]{1,0:T(8,128)(2,1)S(1)}, u32[]{:S(2)}, u32[]{:S(2)}) %collective-permute-start.4) | collective-permute-done | bytes 524320 | tf_op jit(solution)/shard_map/ppermute | solution.py:384
  33.2 1.6 %collective-permute-done.5 = bf16[256,128]{1,0:T(8,128)(2,1)S(1)} collective-permute-done((bf16[256,128]{1,0:T(8,128)(2,1)S(1)}, bf16[256,128]{1,0:T(8,128)(2,1)S(1)}, u32[]{:S(2)}, u32[]{:S(2)}) %collective-permute-start.5) | collective-permute-done | bytes 65568 | tf_op jit(solution)/shard_map/ppermute | solution.py:352
  34.7 2.6 %collective-permute-start.6 = (bf16[256,128]{1,0:T(8,128)(2,1)S(1)}, bf16[256,128]{1,0:T(8,128)(2,1)S(1)}, u32[]{:S(2)}, u32[]{:S(2)}) collective-permute-start(bf16[256,128]{1,0:T(8,128)(2,1)S(1)} %add_convert_fusion.3.one_ref), channel_id=1, source_target_pairs={{0,8},{4,12},{8,0},{12,4},{1,9},{5,13},{9,1},{13,5},{2,10},{6,14},... | collective-permute-start | bytes 196616 | tf_op jit(solution)/shard_map/ppermute | solution.py:352
  37.4 0.8 %collective-permute-start.12 = (bf16[512,512]{1,0:T(8,128)(2,1)S(1)}, bf16[512,512]{1,0:T(8,128)(2,1)S(1)}, u32[]{:S(2)}, u32[]{:S(2)}) collective-permute-start(bf16[512,512]{1,0:T(8,128)(2,1)S(1)} %add_convert_fusion), channel_id=1, source_target_pairs={{0,4},{4,0},{8,12},{12,8},{1,5},{5,1},{9,13},{13,9},{2,6},{6,2},{1... | collective-permute-start | bytes 1572872 | tf_op jit(solution)/shard_map/ppermute | solution.py:352
  38.3 0.7 %collective-permute-start.11 = (bf16[512,512]{1,0:T(8,128)(2,1)S(1)}, bf16[512,512]{1,0:T(8,128)(2,1)S(1)}, u32[]{:S(2)}, u32[]{:S(2)}) collective-permute-start(bf16[512,512]{1,0:T(8,128)(2,1)S(1)} %add_convert_fusion.1), channel_id=1, source_target_pairs={{4,8},{8,4},{5,9},{9,5},{6,10},{10,6},{7,11},{11,7},{20,24},{24,20... | collective-permute-start | bytes 1572872 | tf_op jit(solution)/shard_map/ppermute | solution.py:395
  39.0 1.2 %collective-permute-done.6.two_ref = bf16[256,128]{1,0:T(8,128)(2,1)S(1)} collective-permute-done((bf16[256,128]{1,0:T(8,128)(2,1)S(1)}, bf16[256,128]{1,0:T(8,128)(2,1)S(1)}, u32[]{:S(2)}, u32[]{:S(2)}) %collective-permute-start.6) | collective-permute-done | bytes 65568 | tf_op jit(solution)/shard_map/ppermute | solution.py:352
  40.7 1.7 %collective-permute-start.8 = (bf16[128,512]{1,0:T(8,128)(2,1)S(1)}, bf16[128,512]{1,0:T(8,128)(2,1)S(1)}, u32[]{:S(2)}, u32[]{:S(2)}) collective-permute-start(bf16[128,512]{1,0:T(8,128)(2,1)S(1)} %get-tuple-element.46), channel_id=1, source_target_pairs={{0,2},{1,3},{2,0},{3,1},{4,6},{5,7},{6,4},{7,5},{8,10},{9,11},{10,... | collective-permute-start | bytes 393224 | tf_op jit(solution)/shard_map/ppermute | solution.py:352
  42.6 4.5 %collective-permute-done.8.refs_2_ = bf16[128,512]{1,0:T(8,128)(2,1)S(1)} collective-permute-done((bf16[128,512]{1,0:T(8,128)(2,1)S(1)}, bf16[128,512]{1,0:T(8,128)(2,1)S(1)}, u32[]{:S(2)}, u32[]{:S(2)}) %collective-permute-start.8) | collective-permute-done | bytes 131104 | tf_op jit(solution)/shard_map/ppermute | solution.py:352
  47.1 1.9 %collective-permute-done.9.refs_3_ = bf16[128,512]{1,0:T(8,128)(2,1)S(1)} collective-permute-done((bf16[128,512]{1,0:T(8,128)(2,1)S(1)}, bf16[128,512]{1,0:T(8,128)(2,1)S(1)}, u32[]{:S(2)}, u32[]{:S(2)}) %collective-permute-start.9) | collective-permute-done | bytes 131104 | tf_op jit(solution)/shard_map/ppermute | solution.py:352
  49.5 1.6 %collective-permute-done.12.refs_1_ = bf16[512,512]{1,0:T(8,128)(2,1)S(1)} collective-permute-done((bf16[512,512]{1,0:T(8,128)(2,1)S(1)}, bf16[512,512]{1,0:T(8,128)(2,1)S(1)}, u32[]{:S(2)}, u32[]{:S(2)}) %collective-permute-start.12) | collective-permute-done | bytes 524320 | tf_op jit(solution)/shard_map/ppermute | solution.py:352
  51.1 0.9 %finish.1 = bf16[512,512]{1,0:T(8,128)(2,1)} custom-call(f32[512,512]{1,0:T(8,128)S(1)} %with_deltas.1.start_ref, bf16[512,512]{1,0:T(8,128)(2,1)S(1)} %collective-permute-done.11.refs_0_, bf16[512,512]{1,0:T(8,128)(2,1)S(1)} %collective-permute-done.12.refs_1_), custom_call_target="tpu_custom_call" | custom-call | flops 262144 | bytes 2097152 | tf_op jit(solution)/shard_map/finish/pallas_call | solution.py:331
  (19 shorter events, 1.8 us)
Async XLA Ops:
  2.4 15.4 %collective-permute-start = (bf16[2064,128]{1,0:T(8,128)(2,1)S(1)}, bf16[2064,128]{1,0:T(8,128)(2,1)S(1)}, u32[]{:S(2)}, u32[]{:S(2)}) collective-permute-start(bf16[2064,128]{1,0:T(8,128)(2,1)S(1)} %get-tuple-element.35), channel_id=1, source_target_pairs={{0,2},{1,3},{2,0},{3,1},{4,6},{5,7},{6,4},{7,5},{8,10},{9,11},{10,... | collective-permute-start | bytes 1585160 | tf_op jit(solution)/shard_map/ppermute | solution.py:352
  6.7 15.8 %collective-permute-start.2 = (bf16[512,512]{1,0:T(8,128)(2,1)S(1)}, bf16[512,512]{1,0:T(8,128)(2,1)S(1)}, u32[]{:S(2)}, u32[]{:S(2)}) collective-permute-start(bf16[512,512]{1,0:T(8,128)(2,1)S(1)} %first_block.1), channel_id=1, source_target_pairs={{0,4},{12,8},{1,5},{13,9},{2,6},{14,10},{3,7},{15,11},{16,20},{28,... | collective-permute-start | bytes 1572872 | tf_op jit(solution)/shard_map/ppermute | solution.py:381
  10.2 7.6 %copy-start = (bf16[2048,512]{1,0:T(8,128)(2,1)S(1)}, bf16[2048,512]{1,0:T(8,128)(2,1)}, u32[]{:S(2)}) copy-start(bf16[2048,512]{1,0:T(8,128)(2,1)} %down_ref.5) | copy-start | bytes 6291460
  15.8 7.6 %collective-permute-start.1 = (bf16[2064,128]{1,0:T(8,128)(2,1)S(1)}, bf16[2064,128]{1,0:T(8,128)(2,1)S(1)}, u32[]{:S(2)}, u32[]{:S(2)}) collective-permute-start(bf16[2064,128]{1,0:T(8,128)(2,1)S(1)} %get-tuple-element.36), channel_id=1, source_target_pairs={{0,1},{1,0},{2,3},{3,2},{4,5},{5,4},{6,7},{7,6},{8,9},{9,8},{10,11... | collective-permute-start | bytes 1585160 | tf_op jit(solution)/shard_map/ppermute | solution.py:352
  15.9 13.8 %collective-permute-start.3 = (bf16[2064,128]{1,0:T(8,128)(2,1)S(1)}, bf16[2064,128]{1,0:T(8,128)(2,1)S(1)}, u32[]{:S(2)}, u32[]{:S(2)}) collective-permute-start(bf16[2064,128]{1,0:T(8,128)(2,1)S(1)} %get-tuple-element.39), channel_id=1, source_target_pairs={{0,3},{1,2},{2,1},{3,0},{4,7},{5,6},{6,5},{7,4},{8,11},{9,10},{10,... | collective-permute-start | bytes 1585160 | tf_op jit(solution)/shard_map/ppermute | solution.py:352
  16.5 16.5 %collective-permute-start.4 = (bf16[512,512]{1,0:T(8,128)(2,1)S(1)}, bf16[512,512]{1,0:T(8,128)(2,1)S(1)}, u32[]{:S(2)}, u32[]{:S(2)}) collective-permute-start(bf16[512,512]{1,0:T(8,128)(2,1)S(1)} %get-tuple-element.42), channel_id=1, source_target_pairs={{0,4},{12,8},{1,5},{13,9},{2,6},{14,10},{3,7},{15,11},{16,20},{28,... | collective-permute-start | bytes 1572872 | tf_op jit(solution)/shard_map/ppermute | solution.py:384
  22.7 14.6 %collective-permute-start.10 = (bf16[512,512]{1,0:T(8,128)(2,1)S(1)}, bf16[512,512]{1,0:T(8,128)(2,1)S(1)}, u32[]{:S(2)}, u32[]{:S(2)}) collective-permute-start(bf16[512,512]{1,0:T(8,128)(2,1)S(1)} %add_convert_fusion.2), channel_id=1, source_target_pairs={{4,8},{8,4},{5,9},{9,5},{6,10},{10,6},{7,11},{11,7},{20,24},{24,20... | collective-permute-start | bytes 1572872 | tf_op jit(solution)/shard_map/ppermute | solution.py:387
  30.2 9.9 %copy-start.1 = (bf16[512,512]{1,0:T(8,128)(2,1)S(1)}, bf16[512,512]{1,0:T(8,128)(2,1)}, u32[]{:S(2)}) copy-start(bf16[512,512]{1,0:T(8,128)(2,1)} %up_ref.1) | copy-start | bytes 1572868
  30.2 4.5 %collective-permute-start.5 = (bf16[256,128]{1,0:T(8,128)(2,1)S(1)}, bf16[256,128]{1,0:T(8,128)(2,1)S(1)}, u32[]{:S(2)}, u32[]{:S(2)}) collective-permute-start(bf16[256,128]{1,0:T(8,128)(2,1)S(1)} %shrink_partial.5), channel_id=1, source_target_pairs={{0,4},{4,0},{8,12},{12,8},{1,5},{5,1},{9,13},{13,9},{2,6},{6,2},{1... | collective-permute-start | bytes 196616 | tf_op jit(solution)/shard_map/ppermute | solution.py:352
  34.7 5.4 %collective-permute-start.6 = (bf16[256,128]{1,0:T(8,128)(2,1)S(1)}, bf16[256,128]{1,0:T(8,128)(2,1)S(1)}, u32[]{:S(2)}, u32[]{:S(2)}) collective-permute-start(bf16[256,128]{1,0:T(8,128)(2,1)S(1)} %add_convert_fusion.3.one_ref), channel_id=1, source_target_pairs={{0,8},{4,12},{8,0},{12,4},{1,9},{5,13},{9,1},{13,5},{2,10},{6,14},... | collective-permute-start | bytes 196616 | tf_op jit(solution)/shard_map/ppermute | solution.py:352
  37.4 13.6 %collective-permute-start.12 = (bf16[512,512]{1,0:T(8,128)(2,1)S(1)}, bf16[512,512]{1,0:T(8,128)(2,1)S(1)}, u32[]{:S(2)}, u32[]{:S(2)}) collective-permute-start(bf16[512,512]{1,0:T(8,128)(2,1)S(1)} %add_convert_fusion), channel_id=1, source_target_pairs={{0,4},{4,0},{8,12},{12,8},{1,5},{5,1},{9,13},{13,9},{2,6},{6,2},{1... | collective-permute-start | bytes 1572872 | tf_op jit(solution)/shard_map/ppermute | solution.py:352
  38.3 11.2 %collective-permute-start.11 = (bf16[512,512]{1,0:T(8,128)(2,1)S(1)}, bf16[512,512]{1,0:T(8,128)(2,1)S(1)}, u32[]{:S(2)}, u32[]{:S(2)}) collective-permute-start(bf16[512,512]{1,0:T(8,128)(2,1)S(1)} %add_convert_fusion.1), channel_id=1, source_target_pairs={{4,8},{8,4},{5,9},{9,5},{6,10},{10,6},{7,11},{11,7},{20,24},{24,20... | collective-permute-start | bytes 1572872 | tf_op jit(solution)/shard_map/ppermute | solution.py:395
  40.7 1.9 %collective-permute-start.7 = (bf16[128,512]{1,0:T(8,128)(2,1)S(1)}, bf16[128,512]{1,0:T(8,128)(2,1)S(1)}, u32[]{:S(2)}, u32[]{:S(2)}) collective-permute-start(bf16[128,512]{1,0:T(8,128)(2,1)S(1)} %get-tuple-element.45), channel_id=1, source_target_pairs={{0,1},{1,0},{2,3},{3,2},{4,5},{5,4},{6,7},{7,6},{8,9},{9,8},{10,11... | collective-permute-start | bytes 393224 | tf_op jit(solution)/shard_map/ppermute | solution.py:352
  40.7 6.4 %collective-permute-start.8 = (bf16[128,512]{1,0:T(8,128)(2,1)S(1)}, bf16[128,512]{1,0:T(8,128)(2,1)S(1)}, u32[]{:S(2)}, u32[]{:S(2)}) collective-permute-start(bf16[128,512]{1,0:T(8,128)(2,1)S(1)} %get-tuple-element.46), channel_id=1, source_target_pairs={{0,2},{1,3},{2,0},{3,1},{4,6},{5,7},{6,4},{7,5},{8,10},{9,11},{10,... | collective-permute-start | bytes 393224 | tf_op jit(solution)/shard_map/ppermute | solution.py:352
  42.5 6.6 %collective-permute-start.9 = (bf16[128,512]{1,0:T(8,128)(2,1)S(1)}, bf16[128,512]{1,0:T(8,128)(2,1)S(1)}, u32[]{:S(2)}, u32[]{:S(2)}) collective-permute-start(bf16[128,512]{1,0:T(8,128)(2,1)S(1)} %get-tuple-element.47), channel_id=1, source_target_pairs={{0,3},{1,2},{2,1},{3,0},{4,7},{5,6},{6,5},{7,4},{8,11},{9,10},{10,... | collective-permute-start | bytes 393224 | tf_op jit(solution)/shard_map/ppermute | solution.py:352

commit v14 on v13

--- a/solution.py
+++ b/solution.py
@@ -375,16 +375,16 @@
     total = holders * capacity
     me, z = lax.axis_index("ad"), lax.axis_index("tp")
     spots, *far, x, w = far_rows(me, z, ids, table, x, weight, holders, slots, capacity, width)
-    far = [swap(rows, "ad", j + NEAR) for j, rows in enumerate(far)]
     if lax.axis_size("tp") == 4 and holders == 4:
         first = first_block(x, w)
         edge0 = lax.ppermute(first, "tp", EDGE)
+        far = [swap(after(rows, first), "ad", j + NEAR) for j, rows in enumerate(far)]
         *near, second, third, own, unsort = rest(z, after(spots, first), x, weight, width, total, capacity)
         near = [near[0], swap(near[1], "ad", 1)]
         edge1 = lax.ppermute(second, "tp", EDGE)
-        early = shrink_partial(down, [near[0], far[0]])
-        inner0 = both(after(first, early), edge0)
+        inner0 = both(first, edge0)
         middle0 = lax.ppermute(inner0, "tp", MIDDLE)
+        early = shrink_partial(down, [near[0], after(far[0], inner0)])
         early = shrink_partial(down, [after(near[1], inner0)], [early])
         mine = shrink_partial(down, [after(far[1], early)], [early])
         parts, order = [near[0], far[0], near[1], far[1]], (0, 2, 1, 3)
@@ -395,6 +395,7 @@
         middle1 = lax.ppermute(after(inner1, inner2), "tp", MIDDLE)
         sums = [middle1, last]
     else:
+        far = [swap(rows, "ad", j + NEAR) for j, rows in enumerate(far)]
         near = near_rows(spots, x, capacity)
         near = [near[0], swap(near[1], "ad", 1)]
         parts, order = near + far, range(holders)

time: 52.2 us -> 55.5 us (1.063)
  waiting for transfers between devices: 23.1 us -> 26.7 us
    ppermute x9, waiting for transfers between devices: 16.5 us -> 23.6 us  [swap(): lax.ppermute(value, axis, [(i, i ^ bit) for i in range(lax.axis_size(axis...]
    ppermute x1, waiting for transfers between devices: 2.71 us -> 0.01 us  [shards(): edge1 = lax.ppermute(second, 'tp', EDGE)]
    ppermute x9, starting transfers between devices: 9.11 us -> 7.45 us  [swap(): lax.ppermute(value, axis, [(i, i ^ bit) for i in range(lax.axis_size(axis...]
    ppermute x1, starting transfers between devices: 3.51 us -> 4.96 us  [shards(): edge0 = lax.ppermute(first, 'tp', EDGE)]
    ppermute x1, waiting for transfers between devices: 3.89 us -> 3.12 us  [shards(): edge0 = lax.ppermute(first, 'tp', EDGE)]
  transfers between devices with their start and end apart: 13 -> 13, of which waited for: 8 -> 8; matrix products, arithmetic and copies ran while one was open for 1% -> 1% of each run, Pallas kernels for 18% -> 15%
where the time goes in v14:
time: 55.5 us; the launch traced here: 55.3 us
  waiting for transfers between devices  26.7 us (48%)
  starting transfers between devices  15.1 us (27%)
  Pallas kernels  12.9 us (23%)
    ppermute x9, waiting for transfers between devices, swap(): lax.ppermute(value, axis, [(i, i ^ bit) for i in range(lax.axis_size(axis...  23.6 us
    ppermute x9, starting transfers between devices, swap(): lax.ppermute(value, axis, [(i, i ^ bit) for i in range(lax.axis_size(axis...  7.45 us
    pallas_call x1, Pallas kernels, rest(): pl.pallas_call(rest_body, out_shape=shapes, in_specs=[smem, vmem, vmem, h...  5.54 us
    ppermute x1, starting transfers between devices, shards(): edge0 = lax.ppermute(first, 'tp', EDGE)  4.96 us
    ppermute x1, waiting for transfers between devices, shards(): edge0 = lax.ppermute(first, 'tp', EDGE)  3.12 us
    pallas_call x1, Pallas kernels, far_rows(): pl.pallas_call(functools.partial(far_body, slots, capacity, holders), out...  2.44 us
    pallas_call x3, Pallas kernels, shrink_partial(): pl.pallas_call(functools.partial(shrink_body, kept), out_shape=jax.ShapeD...  1.83 us
    ppermute x1, starting transfers between devices, shards(): edge1 = lax.ppermute(second, 'tp', EDGE)  1.31 us
  transfers between devices with their start and end apart: 13, of which 8 were waited for; matrix products, arithmetic and copies ran while one was open for 1% of the time, Pallas kernels for 15%

profile of v14, /device:TPU:0, one launch (start us, length us, event | category | flops | bytes accessed | tf_op | source)
XLA Modules:
  0.0 55.3 jit_solution(11165822141245844648)
XLA Ops:
  0.0 2.4 %far_rows.1 = (s32[8,512]{1,0:T(8,128)S(1)}, bf16[2064,128]{1,0:T(8,128)(2,1)S(1)}, bf16[2064,128]{1,0:T(8,128)(2,1)S(1)}, bf16[512,2048]{1,0:T(8,128)(2,1)S(1)}, bf16[2048,512]{1,0:T(8,128)(2,1)S(1)}) custom-call(s32[1]{0:T(128)} %bitcast.1.me_ref, s32[1]{0:T(128)} %bitcast.z_ref, s32[1,512]{1,0:T(1,128)} %bitcast.5, s32[32,128]{1,0:T(8,128)} %bitcast.4, ...), custom_call_target="tpu_custom_call" | custom-call | flops 1073741824 | bytes 4194304 | tf_op jit(solution)/shard_map/far_rows/pallas_call | solution.py:125
  2.4 1.3 %first_block.1 = bf16[512,512]{1,0:T(8,128)(2,1)S(1)} custom-call(bf16[512,2048]{1,0:T(8,128)(2,1)S(1)} %get-tuple-element.31.x_ref, bf16[2048,512]{1,0:T(8,128)(2,1)S(1)} %get-tuple-element.32.w_ref), custom_call_target="tpu_custom_call" | custom-call | flops 1073741824 | bytes 4194304 | tf_op jit(solution)/shard_map/first_block/pallas_call | solution.py:164
  3.7 5.0 %collective-permute-start.1 = (bf16[512,512]{1,0:T(8,128)(2,1)S(1)}, bf16[512,512]{1,0:T(8,128)(2,1)S(1)}, u32[]{:S(2)}, u32[]{:S(2)}) collective-permute-start(bf16[512,512]{1,0:T(8,128)(2,1)S(1)} %first_block.1), channel_id=1, source_target_pairs={{0,4},{12,8},{1,5},{13,9},{2,6},{14,10},{3,7},{15,11},{16,20},{28,... | collective-permute-start | bytes 1572872 | tf_op jit(solution)/shard_map/ppermute | solution.py:380
  8.7 1.6 %collective-permute-start = (bf16[2064,128]{1,0:T(8,128)(2,1)S(1)}, bf16[2064,128]{1,0:T(8,128)(2,1)S(1)}, u32[]{:S(2)}, u32[]{:S(2)}) collective-permute-start(bf16[2064,128]{1,0:T(8,128)(2,1)S(1)} %get-tuple-element.38), channel_id=1, source_target_pairs={{0,2},{1,3},{2,0},{3,1},{4,6},{5,7},{6,4},{7,5},{8,10},{9,11},{10,... | collective-permute-start | bytes 1585160 | tf_op jit(solution)/shard_map/ppermute | solution.py:352
  10.2 5.5 %rest.1 = (bf16[2064,128]{1,0:T(8,128)(2,1)S(1)}, bf16[2064,128]{1,0:T(8,128)(2,1)S(1)}, bf16[512,512]{1,0:T(8,128)(2,1)S(1)}, bf16[512,512]{1,0:T(8,128)(2,1)S(...) custom-call(s32[1]{0:T(128)} %bitcast.z_ref, s32[8,512]{1,0:T(8,128)S(1)} %get-tuple-element.33.spots_ref, ...), custom_call_target="tpu_custom_call" | custom-call | flops 3221225472 | bytes 10485760 | tf_op jit(solution)/shard_map/rest/pallas_call | solution.py:202
  15.9 0.7 %collective-permute-start.3 = (bf16[2064,128]{1,0:T(8,128)(2,1)S(1)}, bf16[2064,128]{1,0:T(8,128)(2,1)S(1)}, u32[]{:S(2)}, u32[]{:S(2)}) collective-permute-start(bf16[2064,128]{1,0:T(8,128)(2,1)S(1)} %get-tuple-element.43), channel_id=1, source_target_pairs={{0,3},{1,2},{2,1},{3,0},{4,7},{5,6},{6,5},{7,4},{8,11},{9,10},{10,... | collective-permute-start | bytes 1585160 | tf_op jit(solution)/shard_map/ppermute | solution.py:352
  16.5 1.3 %collective-permute-start.4 = (bf16[512,512]{1,0:T(8,128)(2,1)S(1)}, bf16[512,512]{1,0:T(8,128)(2,1)S(1)}, u32[]{:S(2)}, u32[]{:S(2)}) collective-permute-start(bf16[512,512]{1,0:T(8,128)(2,1)S(1)} %get-tuple-element.46), channel_id=1, source_target_pairs={{0,4},{12,8},{1,5},{13,9},{2,6},{14,10},{3,7},{15,11},{16,20},{28,... | collective-permute-start | bytes 1572872 | tf_op jit(solution)/shard_map/ppermute | solution.py:384
  17.8 3.1 %collective-permute-done.1 = bf16[512,512]{1,0:T(8,128)(2,1)S(1)} collective-permute-done((bf16[512,512]{1,0:T(8,128)(2,1)S(1)}, bf16[512,512]{1,0:T(8,128)(2,1)S(1)}, u32[]{:S(2)}, u32[]{:S(2)}) %collective-permute-start.1) | collective-permute-done | bytes 524320 | tf_op jit(solution)/shard_map/ppermute | solution.py:380
  21.1 0.7 %collective-permute-start.10 = (bf16[512,512]{1,0:T(8,128)(2,1)S(1)}, bf16[512,512]{1,0:T(8,128)(2,1)S(1)}, u32[]{:S(2)}, u32[]{:S(2)}) collective-permute-start(bf16[512,512]{1,0:T(8,128)(2,1)S(1)} %add_convert_fusion.2), channel_id=1, source_target_pairs={{4,8},{8,4},{5,9},{9,5},{6,10},{10,6},{7,11},{11,7},{20,24},{24,20... | collective-permute-start | bytes 1572872 | tf_op jit(solution)/shard_map/ppermute | solution.py:386
  21.8 1.9 %collective-permute-done.refs_1_ = bf16[2064,128]{1,0:T(8,128)(2,1)S(1)} collective-permute-done((bf16[2064,128]{1,0:T(8,128)(2,1)S(1)}, bf16[2064,128]{1,0:T(8,128)(2,1)S(1)}, u32[]{:S(2)}, u32[]{:S(2)}) %collective-permute-start) | collective-permute-done | bytes 528416 | tf_op jit(solution)/shard_map/ppermute | solution.py:352
  23.7 0.8 %shrink_partial.3.refs_0_ = bf16[128,128]{1,0:T(8,128)(2,1)S(1)} custom-call(bf16[2048,512]{1,0:T(8,128)(2,1)S(1)} %copy-done, bf16[2064,128]{1,0:T(8,128)(2,1)S(1)} %get-tuple-element.36.refs_0_, bf16[2064,128]{1,0:T(8,128)(2,1)S(1)} %collective-permute-done.refs_1_), custom_call_target="tpu_custom_call" | custom-call | flops 536870912 | bytes 3145728 | tf_op jit(solution)/shard_map/shrink_partial/pallas_call | solution.py:250
  24.5 0.5 shrink_partial.4.refs_0_
  25.0 7.5 %collective-permute-done.3.refs_1_.refs_3_ = bf16[2064,128]{1,0:T(8,128)(2,1)S(1)} collective-permute-done((bf16[2064,128]{1,0:T(8,128)(2,1)S(1)}, bf16[2064,128]{1,0:T(8,128)(2,1)S(1)}, u32[]{:S(2)}, u32[]{:S(2)}) %collective-permute-start.3) | collective-permute-done | bytes 528416 | tf_op jit(solution)/shard_map/ppermute | solution.py:352
  33.3 4.6 %collective-permute-done.5 = bf16[256,128]{1,0:T(8,128)(2,1)S(1)} collective-permute-done((bf16[256,128]{1,0:T(8,128)(2,1)S(1)}, bf16[256,128]{1,0:T(8,128)(2,1)S(1)}, u32[]{:S(2)}, u32[]{:S(2)}) %collective-permute-start.5) | collective-permute-done | bytes 65568 | tf_op jit(solution)/shard_map/ppermute | solution.py:352
  38.0 1.1 %collective-permute-start.6 = (bf16[256,128]{1,0:T(8,128)(2,1)S(1)}, bf16[256,128]{1,0:T(8,128)(2,1)S(1)}, u32[]{:S(2)}, u32[]{:S(2)}) collective-permute-start(bf16[256,128]{1,0:T(8,128)(2,1)S(1)} %add_convert_fusion.3.one_ref), channel_id=1, source_target_pairs={{0,8},{4,12},{8,0},{12,4},{1,9},{5,13},{9,1},{13,5},{2,10},{6,14},... | collective-permute-start | bytes 196616 | tf_op jit(solution)/shard_map/ppermute | solution.py:352
  39.3 2.0 %collective-permute-start.12 = (bf16[512,512]{1,0:T(8,128)(2,1)S(1)}, bf16[512,512]{1,0:T(8,128)(2,1)S(1)}, u32[]{:S(2)}, u32[]{:S(2)}) collective-permute-start(bf16[512,512]{1,0:T(8,128)(2,1)S(1)} %add_convert_fusion), channel_id=1, source_target_pairs={{0,4},{4,0},{8,12},{12,8},{1,5},{5,1},{9,13},{13,9},{2,6},{6,2},{1... | collective-permute-start | bytes 1572872 | tf_op jit(solution)/shard_map/ppermute | solution.py:352
  41.3 0.7 %collective-permute-start.11 = (bf16[512,512]{1,0:T(8,128)(2,1)S(1)}, bf16[512,512]{1,0:T(8,128)(2,1)S(1)}, u32[]{:S(2)}, u32[]{:S(2)}) collective-permute-start(bf16[512,512]{1,0:T(8,128)(2,1)S(1)} %add_convert_fusion.1), channel_id=1, source_target_pairs={{4,8},{8,4},{5,9},{9,5},{6,10},{10,6},{7,11},{11,7},{20,24},{24,20... | collective-permute-start | bytes 1572872 | tf_op jit(solution)/shard_map/ppermute | solution.py:395
  42.0 2.2 %collective-permute-done.6.two_ref = bf16[256,128]{1,0:T(8,128)(2,1)S(1)} collective-permute-done((bf16[256,128]{1,0:T(8,128)(2,1)S(1)}, bf16[256,128]{1,0:T(8,128)(2,1)S(1)}, u32[]{:S(2)}, u32[]{:S(2)}) %collective-permute-start.6) | collective-permute-done | bytes 65568 | tf_op jit(solution)/shard_map/ppermute | solution.py:352
  44.8 1.1 %collective-permute-start.8 = (bf16[128,512]{1,0:T(8,128)(2,1)S(1)}, bf16[128,512]{1,0:T(8,128)(2,1)S(1)}, u32[]{:S(2)}, u32[]{:S(2)}) collective-permute-start(bf16[128,512]{1,0:T(8,128)(2,1)S(1)} %get-tuple-element.50), channel_id=1, source_target_pairs={{0,2},{1,3},{2,0},{3,1},{4,6},{5,7},{6,4},{7,5},{8,10},{9,11},{10,... | collective-permute-start | bytes 393224 | tf_op jit(solution)/shard_map/ppermute | solution.py:352
  45.9 0.7 %collective-permute-start.9 = (bf16[128,512]{1,0:T(8,128)(2,1)S(1)}, bf16[128,512]{1,0:T(8,128)(2,1)S(1)}, u32[]{:S(2)}, u32[]{:S(2)}) collective-permute-start(bf16[128,512]{1,0:T(8,128)(2,1)S(1)} %get-tuple-element.51), channel_id=1, source_target_pairs={{0,3},{1,2},{2,1},{3,0},{4,7},{5,6},{6,5},{7,4},{8,11},{9,10},{10,... | collective-permute-start | bytes 393224 | tf_op jit(solution)/shard_map/ppermute | solution.py:352
  46.7 4.5 %collective-permute-done.8.refs_2_ = bf16[128,512]{1,0:T(8,128)(2,1)S(1)} collective-permute-done((bf16[128,512]{1,0:T(8,128)(2,1)S(1)}, bf16[128,512]{1,0:T(8,128)(2,1)S(1)}, u32[]{:S(2)}, u32[]{:S(2)}) %collective-permute-start.8) | collective-permute-done | bytes 131104 | tf_op jit(solution)/shard_map/ppermute | solution.py:352
  51.2 1.9 %collective-permute-done.9.refs_3_ = bf16[128,512]{1,0:T(8,128)(2,1)S(1)} collective-permute-done((bf16[128,512]{1,0:T(8,128)(2,1)S(1)}, bf16[128,512]{1,0:T(8,128)(2,1)S(1)}, u32[]{:S(2)}, u32[]{:S(2)}) %collective-permute-start.9) | collective-permute-done | bytes 131104 | tf_op jit(solution)/shard_map/ppermute | solution.py:352
  53.5 0.9 %collective-permute-done.12.refs_1_ = bf16[512,512]{1,0:T(8,128)(2,1)S(1)} collective-permute-done((bf16[512,512]{1,0:T(8,128)(2,1)S(1)}, bf16[512,512]{1,0:T(8,128)(2,1)S(1)}, u32[]{:S(2)}, u32[]{:S(2)}) %collective-permute-start.12) | collective-permute-done | bytes 524320 | tf_op jit(solution)/shard_map/ppermute | solution.py:352
  54.4 0.9 %finish.1 = bf16[512,512]{1,0:T(8,128)(2,1)} custom-call(f32[512,512]{1,0:T(8,128)S(1)} %with_deltas.1.start_ref, bf16[512,512]{1,0:T(8,128)(2,1)S(1)} %collective-permute-done.11.refs_0_, bf16[512,512]{1,0:T(8,128)(2,1)S(1)} %collective-permute-done.12.refs_1_), custom_call_target="tpu_custom_call" | custom-call | flops 262144 | bytes 2097152 | tf_op jit(solution)/shard_map/finish/pallas_call | solution.py:331
  (19 shorter events, 2.1 us)
Async XLA Ops:
  3.7 17.2 %collective-permute-start.1 = (bf16[512,512]{1,0:T(8,128)(2,1)S(1)}, bf16[512,512]{1,0:T(8,128)(2,1)S(1)}, u32[]{:S(2)}, u32[]{:S(2)}) collective-permute-start(bf16[512,512]{1,0:T(8,128)(2,1)S(1)} %first_block.1), channel_id=1, source_target_pairs={{0,4},{12,8},{1,5},{13,9},{2,6},{14,10},{3,7},{15,11},{16,20},{28,... | collective-permute-start | bytes 1572872 | tf_op jit(solution)/shard_map/ppermute | solution.py:380
  8.7 15.0 %collective-permute-start = (bf16[2064,128]{1,0:T(8,128)(2,1)S(1)}, bf16[2064,128]{1,0:T(8,128)(2,1)S(1)}, u32[]{:S(2)}, u32[]{:S(2)}) collective-permute-start(bf16[2064,128]{1,0:T(8,128)(2,1)S(1)} %get-tuple-element.38), channel_id=1, source_target_pairs={{0,2},{1,3},{2,0},{3,1},{4,6},{5,7},{6,4},{7,5},{8,10},{9,11},{10,... | collective-permute-start | bytes 1585160 | tf_op jit(solution)/shard_map/ppermute | solution.py:352
  10.2 13.4 %copy-start = (bf16[2048,512]{1,0:T(8,128)(2,1)S(1)}, bf16[2048,512]{1,0:T(8,128)(2,1)}, u32[]{:S(2)}) copy-start(bf16[2048,512]{1,0:T(8,128)(2,1)} %down_ref.5) | copy-start | bytes 6291460
  15.8 7.9 %collective-permute-start.2 = (bf16[2064,128]{1,0:T(8,128)(2,1)S(1)}, bf16[2064,128]{1,0:T(8,128)(2,1)S(1)}, u32[]{:S(2)}, u32[]{:S(2)}) collective-permute-start(bf16[2064,128]{1,0:T(8,128)(2,1)S(1)} %get-tuple-element.40), channel_id=1, source_target_pairs={{0,1},{1,0},{2,3},{3,2},{4,5},{5,4},{6,7},{7,6},{8,9},{9,8},{10,11... | collective-permute-start | bytes 1585160 | tf_op jit(solution)/shard_map/ppermute | solution.py:352
  15.9 16.7 %collective-permute-start.3 = (bf16[2064,128]{1,0:T(8,128)(2,1)S(1)}, bf16[2064,128]{1,0:T(8,128)(2,1)S(1)}, u32[]{:S(2)}, u32[]{:S(2)}) collective-permute-start(bf16[2064,128]{1,0:T(8,128)(2,1)S(1)} %get-tuple-element.43), channel_id=1, source_target_pairs={{0,3},{1,2},{2,1},{3,0},{4,7},{5,6},{6,5},{7,4},{8,11},{9,10},{10,... | collective-permute-start | bytes 1585160 | tf_op jit(solution)/shard_map/ppermute | solution.py:352
  16.5 16.7 %collective-permute-start.4 = (bf16[512,512]{1,0:T(8,128)(2,1)S(1)}, bf16[512,512]{1,0:T(8,128)(2,1)S(1)}, u32[]{:S(2)}, u32[]{:S(2)}) collective-permute-start(bf16[512,512]{1,0:T(8,128)(2,1)S(1)} %get-tuple-element.46), channel_id=1, source_target_pairs={{0,4},{12,8},{1,5},{13,9},{2,6},{14,10},{3,7},{15,11},{16,20},{28,... | collective-permute-start | bytes 1572872 | tf_op jit(solution)/shard_map/ppermute | solution.py:384
  21.1 18.0 %collective-permute-start.10 = (bf16[512,512]{1,0:T(8,128)(2,1)S(1)}, bf16[512,512]{1,0:T(8,128)(2,1)S(1)}, u32[]{:S(2)}, u32[]{:S(2)}) collective-permute-start(bf16[512,512]{1,0:T(8,128)(2,1)S(1)} %add_convert_fusion.2), channel_id=1, source_target_pairs={{4,8},{8,4},{5,9},{9,5},{6,10},{10,6},{7,11},{11,7},{20,24},{24,20... | collective-permute-start | bytes 1572872 | tf_op jit(solution)/shard_map/ppermute | solution.py:386
  33.1 11.2 %copy-start.1 = (bf16[512,512]{1,0:T(8,128)(2,1)S(1)}, bf16[512,512]{1,0:T(8,128)(2,1)}, u32[]{:S(2)}) copy-start(bf16[512,512]{1,0:T(8,128)(2,1)} %up_ref.1) | copy-start | bytes 1572868
  33.1 4.9 %collective-permute-start.5 = (bf16[256,128]{1,0:T(8,128)(2,1)S(1)}, bf16[256,128]{1,0:T(8,128)(2,1)S(1)}, u32[]{:S(2)}, u32[]{:S(2)}) collective-permute-start(bf16[256,128]{1,0:T(8,128)(2,1)S(1)} %shrink_partial.5), channel_id=1, source_target_pairs={{0,4},{4,0},{8,12},{12,8},{1,5},{5,1},{9,13},{13,9},{2,6},{6,2},{1... | collective-permute-start | bytes 196616 | tf_op jit(solution)/shard_map/ppermute | solution.py:352
  38.0 6.2 %collective-permute-start.6 = (bf16[256,128]{1,0:T(8,128)(2,1)S(1)}, bf16[256,128]{1,0:T(8,128)(2,1)S(1)}, u32[]{:S(2)}, u32[]{:S(2)}) collective-permute-start(bf16[256,128]{1,0:T(8,128)(2,1)S(1)} %add_convert_fusion.3.one_ref), channel_id=1, source_target_pairs={{0,8},{4,12},{8,0},{12,4},{1,9},{5,13},{9,1},{13,5},{2,10},{6,14},... | collective-permute-start | bytes 196616 | tf_op jit(solution)/shard_map/ppermute | solution.py:352
  39.3 15.2 %collective-permute-start.12 = (bf16[512,512]{1,0:T(8,128)(2,1)S(1)}, bf16[512,512]{1,0:T(8,128)(2,1)S(1)}, u32[]{:S(2)}, u32[]{:S(2)}) collective-permute-start(bf16[512,512]{1,0:T(8,128)(2,1)S(1)} %add_convert_fusion), channel_id=1, source_target_pairs={{0,4},{4,0},{8,12},{12,8},{1,5},{5,1},{9,13},{13,9},{2,6},{6,2},{1... | collective-permute-start | bytes 1572872 | tf_op jit(solution)/shard_map/ppermute | solution.py:352
  41.3 12.2 %collective-permute-start.11 = (bf16[512,512]{1,0:T(8,128)(2,1)S(1)}, bf16[512,512]{1,0:T(8,128)(2,1)S(1)}, u32[]{:S(2)}, u32[]{:S(2)}) collective-permute-start(bf16[512,512]{1,0:T(8,128)(2,1)S(1)} %add_convert_fusion.1), channel_id=1, source_target_pairs={{4,8},{8,4},{5,9},{9,5},{6,10},{10,6},{7,11},{11,7},{20,24},{24,20... | collective-permute-start | bytes 1572872 | tf_op jit(solution)/shard_map/ppermute | solution.py:395
  44.7 1.9 %collective-permute-start.7 = (bf16[128,512]{1,0:T(8,128)(2,1)S(1)}, bf16[128,512]{1,0:T(8,128)(2,1)S(1)}, u32[]{:S(2)}, u32[]{:S(2)}) collective-permute-start(bf16[128,512]{1,0:T(8,128)(2,1)S(1)} %get-tuple-element.49), channel_id=1, source_target_pairs={{0,1},{1,0},{2,3},{3,2},{4,5},{5,4},{6,7},{7,6},{8,9},{9,8},{10,11... | collective-permute-start | bytes 393224 | tf_op jit(solution)/shard_map/ppermute | solution.py:352
  44.8 6.4 %collective-permute-start.8 = (bf16[128,512]{1,0:T(8,128)(2,1)S(1)}, bf16[128,512]{1,0:T(8,128)(2,1)S(1)}, u32[]{:S(2)}, u32[]{:S(2)}) collective-permute-start(bf16[128,512]{1,0:T(8,128)(2,1)S(1)} %get-tuple-element.50), channel_id=1, source_target_pairs={{0,2},{1,3},{2,0},{3,1},{4,6},{5,7},{6,4},{7,5},{8,10},{9,11},{10,... | collective-permute-start | bytes 393224 | tf_op jit(solution)/shard_map/ppermute | solution.py:352
  45.9 7.2 %collective-permute-start.9 = (bf16[128,512]{1,0:T(8,128)(2,1)S(1)}, bf16[128,512]{1,0:T(8,128)(2,1)S(1)}, u32[]{:S(2)}, u32[]{:S(2)}) collective-permute-start(bf16[128,512]{1,0:T(8,128)(2,1)S(1)} %get-tuple-element.51), channel_id=1, source_target_pairs={{0,3},{1,2},{2,1},{3,0},{4,7},{5,6},{6,5},{7,4},{8,11},{9,10},{10,... | collective-permute-start | bytes 393224 | tf_op jit(solution)/shard_map/ppermute | solution.py:352

commit v15 on v13

--- a/solution.py
+++ b/solution.py
@@ -380,14 +380,13 @@
         first = first_block(x, w)
         edge0 = lax.ppermute(first, "tp", EDGE)
         *near, second, third, own, unsort = rest(z, after(spots, first), x, weight, width, total, capacity)
-        near = [near[0], swap(near[1], "ad", 1)]
         edge1 = lax.ppermute(second, "tp", EDGE)
         early = shrink_partial(down, [near[0], far[0]])
+        partner = swap(after(near[1], early), "ad", 1)
         inner0 = both(after(first, early), edge0)
         middle0 = lax.ppermute(inner0, "tp", MIDDLE)
-        early = shrink_partial(down, [after(near[1], inner0)], [early])
-        mine = shrink_partial(down, [after(far[1], early)], [early])
-        parts, order = [near[0], far[0], near[1], far[1]], (0, 2, 1, 3)
+        mine = shrink_partial(down, [after(partner, inner0), after(far[1], inner0)], [early])
+        parts, order = [near[0], far[0], partner, far[1]], (0, 2, 1, 3)
         inner1 = both(after(second, mine), edge1)
         steps, other = tp_sums(mine, inner1)
         inner2 = both(after(third, steps[-1]), middle0)

time: 52.2 us -> 55.2 us (1.057)
  starting transfers between devices: 15.3 us -> 19.3 us
  waiting for transfers between devices: 23.1 us -> 22.3 us
    ppermute x1, waiting for transfers between devices: 3.89 us -> 0.01 us  [shards(): edge0 = lax.ppermute(first, 'tp', EDGE)]
    ppermute x1, starting transfers between devices: 1.31 us -> 4.09 us  [shards(): edge1 = lax.ppermute(second, 'tp', EDGE)]
    ppermute x1, waiting for transfers between devices: 2.71 us -> 4.94 us  [shards(): edge1 = lax.ppermute(second, 'tp', EDGE)]
    ppermute x9, starting transfers between devices: 9.11 us -> 10.4 us  [swap(): lax.ppermute(value, axis, [(i, i ^ bit) for i in range(lax.axis_size(axis...]
    ppermute x9, waiting for transfers between devices: 16.5 us -> 17.3 us  [swap(): lax.ppermute(value, axis, [(i, i ^ bit) for i in range(lax.axis_size(axis...]
    pallas_call x3 -> x2, Pallas kernels: 1.84 us -> 1.58 us  [shrink_partial(): pl.pallas_call(functools.partial(shrink_body, kept), out_shape=jax.ShapeD...]
  transfers between devices with their start and end apart: 13 -> 13, of which waited for: 8 -> 8; matrix products, arithmetic and copies ran while one was open for 1% -> 1% of each run, Pallas kernels for 18% -> 17%
where the time goes in v15:
time: 55.2 us; the launch traced here: 54.9 us
  waiting for transfers between devices  22.3 us (40%)
  starting transfers between devices  19.3 us (35%)
  Pallas kernels  12.6 us (23%)
    ppermute x9, waiting for transfers between devices, swap(): lax.ppermute(value, axis, [(i, i ^ bit) for i in range(lax.axis_size(axis...  17.3 us
    ppermute x9, starting transfers between devices, swap(): lax.ppermute(value, axis, [(i, i ^ bit) for i in range(lax.axis_size(axis...  10.4 us
    pallas_call x1, Pallas kernels, rest(): pl.pallas_call(rest_body, out_shape=shapes, in_specs=[smem, vmem, vmem, h...  5.54 us
    ppermute x1, waiting for transfers between devices, shards(): edge1 = lax.ppermute(second, 'tp', EDGE)  4.94 us
    ppermute x1, starting transfers between devices, shards(): edge1 = lax.ppermute(second, 'tp', EDGE)  4.09 us
    ppermute x1, starting transfers between devices, shards(): edge0 = lax.ppermute(first, 'tp', EDGE)  3.51 us
    pallas_call x1, Pallas kernels, far_rows(): pl.pallas_call(functools.partial(far_body, slots, capacity, holders), out...  2.44 us
    pallas_call x2, Pallas kernels, shrink_partial(): pl.pallas_call(functools.partial(shrink_body, kept), out_shape=jax.ShapeD...  1.58 us
  transfers between devices with their start and end apart: 13, of which 8 were waited for; matrix products, arithmetic and copies ran while one was open for 1% of the time, Pallas kernels for 17%

profile of v15, /device:TPU:0, one launch (start us, length us, event | category | flops | bytes accessed | tf_op | source)
XLA Modules:
  0.0 54.9 jit_solution(3726301047298808708)
XLA Ops:
  0.0 2.4 %far_rows.1 = (s32[8,512]{1,0:T(8,128)S(1)}, bf16[2064,128]{1,0:T(8,128)(2,1)S(1)}, bf16[2064,128]{1,0:T(8,128)(2,1)S(1)}, bf16[512,2048]{1,0:T(8,128)(2,1)S(1)}, bf16[2048,512]{1,0:T(8,128)(2,1)S(1)}) custom-call(s32[1]{0:T(128)} %bitcast.1.me_ref, s32[1]{0:T(128)} %bitcast.z_ref, s32[1,512]{1,0:T(1,128)} %bitcast.5, s32[32,128]{1,0:T(8,128)} %bitcast.4, ...), custom_call_target="tpu_custom_call" | custom-call | flops 1073741824 | bytes 4194304 | tf_op jit(solution)/shard_map/far_rows/pallas_call | solution.py:125
  2.4 3.0 %collective-permute-start = (bf16[2064,128]{1,0:T(8,128)(2,1)S(1)}, bf16[2064,128]{1,0:T(8,128)(2,1)S(1)}, u32[]{:S(2)}, u32[]{:S(2)}) collective-permute-start(bf16[2064,128]{1,0:T(8,128)(2,1)S(1)} %get-tuple-element.36), channel_id=1, source_target_pairs={{0,2},{1,3},{2,0},{3,1},{4,6},{5,7},{6,4},{7,5},{8,10},{9,11},{10,... | collective-permute-start | bytes 1585160 | tf_op jit(solution)/shard_map/ppermute | solution.py:352
  5.5 1.2 %first_block.1 = bf16[512,512]{1,0:T(8,128)(2,1)S(1)} custom-call(bf16[512,2048]{1,0:T(8,128)(2,1)S(1)} %get-tuple-element.30.x_ref, bf16[2048,512]{1,0:T(8,128)(2,1)S(1)} %get-tuple-element.31.w_ref), custom_call_target="tpu_custom_call" | custom-call | flops 1073741824 | bytes 4194304 | tf_op jit(solution)/shard_map/first_block/pallas_call | solution.py:164
  6.7 3.5 %collective-permute-start.2 = (bf16[512,512]{1,0:T(8,128)(2,1)S(1)}, bf16[512,512]{1,0:T(8,128)(2,1)S(1)}, u32[]{:S(2)}, u32[]{:S(2)}) collective-permute-start(bf16[512,512]{1,0:T(8,128)(2,1)S(1)} %first_block.1), channel_id=1, source_target_pairs={{0,4},{12,8},{1,5},{13,9},{2,6},{14,10},{3,7},{15,11},{16,20},{28,... | collective-permute-start | bytes 1572872 | tf_op jit(solution)/shard_map/ppermute | solution.py:381
  10.3 5.5 %rest.1 = (bf16[2064,128]{1,0:T(8,128)(2,1)S(1)}, bf16[2064,128]{1,0:T(8,128)(2,1)S(1)}, bf16[512,512]{1,0:T(8,128)(2,1)S(1)}, bf16[512,512]{1,0:T(8,128)(2,1)S(...) custom-call(s32[1]{0:T(128)} %bitcast.z_ref, s32[8,512]{1,0:T(8,128)S(1)} %get-tuple-element.32.spots_ref, ...), custom_call_target="tpu_custom_call" | custom-call | flops 3221225472 | bytes 10485760 | tf_op jit(solution)/shard_map/rest/pallas_call | solution.py:202
  15.9 2.4 %collective-permute-done.refs_1_ = bf16[2064,128]{1,0:T(8,128)(2,1)S(1)} collective-permute-done((bf16[2064,128]{1,0:T(8,128)(2,1)S(1)}, bf16[2064,128]{1,0:T(8,128)(2,1)S(1)}, u32[]{:S(2)}, u32[]{:S(2)}) %collective-permute-start) | collective-permute-done | bytes 528416 | tf_op jit(solution)/shard_map/ppermute | solution.py:352
  18.3 0.8 %shrink_partial.2.refs_0_ = bf16[128,128]{1,0:T(8,128)(2,1)S(1)} custom-call(bf16[2048,512]{1,0:T(8,128)(2,1)S(1)} %copy-done, bf16[2064,128]{1,0:T(8,128)(2,1)S(1)} %get-tuple-element.35.refs_0_, bf16[2064,128]{1,0:T(8,128)(2,1)S(1)} %collective-permute-done.refs_1_), custom_call_target="tpu_custom_call" | custom-call | flops 536870912 | bytes 3145728 | tf_op jit(solution)/shard_map/shrink_partial/pallas_call | solution.py:250
  19.2 4.1 %collective-permute-start.4 = (bf16[512,512]{1,0:T(8,128)(2,1)S(1)}, bf16[512,512]{1,0:T(8,128)(2,1)S(1)}, u32[]{:S(2)}, u32[]{:S(2)}) collective-permute-start(bf16[512,512]{1,0:T(8,128)(2,1)S(1)} %get-tuple-element.44), channel_id=1, source_target_pairs={{0,4},{12,8},{1,5},{13,9},{2,6},{14,10},{3,7},{15,11},{16,20},{28,... | collective-permute-start | bytes 1572872 | tf_op jit(solution)/shard_map/ppermute | solution.py:383
  23.4 0.7 %collective-permute-start.10 = (bf16[512,512]{1,0:T(8,128)(2,1)S(1)}, bf16[512,512]{1,0:T(8,128)(2,1)S(1)}, u32[]{:S(2)}, u32[]{:S(2)}) collective-permute-start(bf16[512,512]{1,0:T(8,128)(2,1)S(1)} %add_convert_fusion.2), channel_id=1, source_target_pairs={{4,8},{8,4},{5,9},{9,5},{6,10},{10,6},{7,11},{11,7},{20,24},{24,20... | collective-permute-start | bytes 1572872 | tf_op jit(solution)/shard_map/ppermute | solution.py:387
  24.1 3.9 %collective-permute-done.3.refs_2_.refs_3_ = bf16[2064,128]{1,0:T(8,128)(2,1)S(1)} collective-permute-done((bf16[2064,128]{1,0:T(8,128)(2,1)S(1)}, bf16[2064,128]{1,0:T(8,128)(2,1)S(1)}, u32[]{:S(2)}, u32[]{:S(2)}) %collective-permute-start.3) | collective-permute-done | bytes 528416 | tf_op jit(solution)/shard_map/ppermute | solution.py:352
  28.0 0.8 %shrink_partial.3 = bf16[256,128]{1,0:T(8,128)(2,1)S(1)} custom-call(bf16[2048,512]{1,0:T(8,128)(2,1)S(1)} %copy-done, bf16[128,128]{1,0:T(8,128)(2,1)S(1)} %shrink_partial.2.refs_0_, bf16[2064,128]{1,0:T(8,128)(2,1)S(1)} %collective-permute-done.1.refs_1_.refs_2_, bf16[2064,128]{1,0:T(8,128)(2,1)S(1)} %collective-permute-done.3.refs_2_.refs_3_), custom_call_target="tpu_custom_call" | custom-call | flops 536870912 | bytes 3145728 | tf_op jit(solution)/shard_map/shrink_partial/pallas_call | solution.py:250
  28.9 1.7 %collective-permute-start.5 = (bf16[256,128]{1,0:T(8,128)(2,1)S(1)}, bf16[256,128]{1,0:T(8,128)(2,1)S(1)}, u32[]{:S(2)}, u32[]{:S(2)}) collective-permute-start(bf16[256,128]{1,0:T(8,128)(2,1)S(1)} %shrink_partial.3), channel_id=1, source_target_pairs={{0,4},{4,0},{8,12},{12,8},{1,5},{5,1},{9,13},{13,9},{2,6},{6,2},{1... | collective-permute-start | bytes 196616 | tf_op jit(solution)/shard_map/ppermute | solution.py:352
  30.5 4.9 %collective-permute-done.4 = bf16[512,512]{1,0:T(8,128)(2,1)S(1)} collective-permute-done((bf16[512,512]{1,0:T(8,128)(2,1)S(1)}, bf16[512,512]{1,0:T(8,128)(2,1)S(1)}, u32[]{:S(2)}, u32[]{:S(2)}) %collective-permute-start.4) | collective-permute-done | bytes 524320 | tf_op jit(solution)/shard_map/ppermute | solution.py:383
  35.6 0.9 %collective-permute-done.5 = bf16[256,128]{1,0:T(8,128)(2,1)S(1)} collective-permute-done((bf16[256,128]{1,0:T(8,128)(2,1)S(1)}, bf16[256,128]{1,0:T(8,128)(2,1)S(1)}, u32[]{:S(2)}, u32[]{:S(2)}) %collective-permute-start.5) | collective-permute-done | bytes 65568 | tf_op jit(solution)/shard_map/ppermute | solution.py:352
  36.5 3.5 %collective-permute-start.6 = (bf16[256,128]{1,0:T(8,128)(2,1)S(1)}, bf16[256,128]{1,0:T(8,128)(2,1)S(1)}, u32[]{:S(2)}, u32[]{:S(2)}) collective-permute-start(bf16[256,128]{1,0:T(8,128)(2,1)S(1)} %add_convert_fusion.3.one_ref), channel_id=1, source_target_pairs={{0,8},{4,12},{8,0},{12,4},{1,9},{5,13},{9,1},{13,5},{2,10},{6,14},... | collective-permute-start | bytes 196616 | tf_op jit(solution)/shard_map/ppermute | solution.py:352
  40.2 0.7 %collective-permute-start.11 = (bf16[512,512]{1,0:T(8,128)(2,1)S(1)}, bf16[512,512]{1,0:T(8,128)(2,1)S(1)}, u32[]{:S(2)}, u32[]{:S(2)}) collective-permute-start(bf16[512,512]{1,0:T(8,128)(2,1)S(1)} %add_convert_fusion.1), channel_id=1, source_target_pairs={{4,8},{8,4},{5,9},{9,5},{6,10},{10,6},{7,11},{11,7},{20,24},{24,20... | collective-permute-start | bytes 1572872 | tf_op jit(solution)/shard_map/ppermute | solution.py:394
  41.0 2.1 %collective-permute-done.6.two_ref = bf16[256,128]{1,0:T(8,128)(2,1)S(1)} collective-permute-done((bf16[256,128]{1,0:T(8,128)(2,1)S(1)}, bf16[256,128]{1,0:T(8,128)(2,1)S(1)}, u32[]{:S(2)}, u32[]{:S(2)}) %collective-permute-start.6) | collective-permute-done | bytes 65568 | tf_op jit(solution)/shard_map/ppermute | solution.py:352
  43.1 0.5 expand.1
  43.7 1.6 %collective-permute-start.8 = (bf16[128,512]{1,0:T(8,128)(2,1)S(1)}, bf16[128,512]{1,0:T(8,128)(2,1)S(1)}, u32[]{:S(2)}, u32[]{:S(2)}) collective-permute-start(bf16[128,512]{1,0:T(8,128)(2,1)S(1)} %get-tuple-element.48), channel_id=1, source_target_pairs={{0,2},{1,3},{2,0},{3,1},{4,6},{5,7},{6,4},{7,5},{8,10},{9,11},{10,... | collective-permute-start | bytes 393224 | tf_op jit(solution)/shard_map/ppermute | solution.py:352
  45.5 4.5 %collective-permute-done.8.refs_2_ = bf16[128,512]{1,0:T(8,128)(2,1)S(1)} collective-permute-done((bf16[128,512]{1,0:T(8,128)(2,1)S(1)}, bf16[128,512]{1,0:T(8,128)(2,1)S(1)}, u32[]{:S(2)}, u32[]{:S(2)}) %collective-permute-start.8) | collective-permute-done | bytes 131104 | tf_op jit(solution)/shard_map/ppermute | solution.py:352
  50.0 1.9 %collective-permute-done.9.refs_3_ = bf16[128,512]{1,0:T(8,128)(2,1)S(1)} collective-permute-done((bf16[128,512]{1,0:T(8,128)(2,1)S(1)}, bf16[128,512]{1,0:T(8,128)(2,1)S(1)}, u32[]{:S(2)}, u32[]{:S(2)}) %collective-permute-start.9) | collective-permute-done | bytes 131104 | tf_op jit(solution)/shard_map/ppermute | solution.py:352
  51.9 0.4 with_deltas.1.start_ref
  52.4 1.6 %collective-permute-done.12.refs_1_ = bf16[512,512]{1,0:T(8,128)(2,1)S(1)} collective-permute-done((bf16[512,512]{1,0:T(8,128)(2,1)S(1)}, bf16[512,512]{1,0:T(8,128)(2,1)S(1)}, u32[]{:S(2)}, u32[]{:S(2)}) %collective-permute-start.12) | collective-permute-done | bytes 524320 | tf_op jit(solution)/shard_map/ppermute | solution.py:352
  54.0 0.9 %finish.1 = bf16[512,512]{1,0:T(8,128)(2,1)} custom-call(f32[512,512]{1,0:T(8,128)S(1)} %with_deltas.1.start_ref, bf16[512,512]{1,0:T(8,128)(2,1)S(1)} %collective-permute-done.11.refs_0_, bf16[512,512]{1,0:T(8,128)(2,1)S(1)} %collective-permute-done.12.refs_1_), custom_call_target="tpu_custom_call" | custom-call | flops 262144 | bytes 2097152 | tf_op jit(solution)/shard_map/finish/pallas_call | solution.py:331
  (18 shorter events, 1.1 us)
Async XLA Ops:
  2.4 15.8 %collective-permute-start = (bf16[2064,128]{1,0:T(8,128)(2,1)S(1)}, bf16[2064,128]{1,0:T(8,128)(2,1)S(1)}, u32[]{:S(2)}, u32[]{:S(2)}) collective-permute-start(bf16[2064,128]{1,0:T(8,128)(2,1)S(1)} %get-tuple-element.36), channel_id=1, source_target_pairs={{0,2},{1,3},{2,0},{3,1},{4,6},{5,7},{6,4},{7,5},{8,10},{9,11},{10,... | collective-permute-start | bytes 1585160 | tf_op jit(solution)/shard_map/ppermute | solution.py:352
  6.7 16.6 %collective-permute-start.2 = (bf16[512,512]{1,0:T(8,128)(2,1)S(1)}, bf16[512,512]{1,0:T(8,128)(2,1)S(1)}, u32[]{:S(2)}, u32[]{:S(2)}) collective-permute-start(bf16[512,512]{1,0:T(8,128)(2,1)S(1)} %first_block.1), channel_id=1, source_target_pairs={{0,4},{12,8},{1,5},{13,9},{2,6},{14,10},{3,7},{15,11},{16,20},{28,... | collective-permute-start | bytes 1572872 | tf_op jit(solution)/shard_map/ppermute | solution.py:381
  10.2 17.8 %collective-permute-start.3 = (bf16[2064,128]{1,0:T(8,128)(2,1)S(1)}, bf16[2064,128]{1,0:T(8,128)(2,1)S(1)}, u32[]{:S(2)}, u32[]{:S(2)}) collective-permute-start(bf16[2064,128]{1,0:T(8,128)(2,1)S(1)} %get-tuple-element.41), channel_id=1, source_target_pairs={{0,3},{1,2},{2,1},{3,0},{4,7},{5,6},{6,5},{7,4},{8,11},{9,10},{10,... | collective-permute-start | bytes 1585160 | tf_op jit(solution)/shard_map/ppermute | solution.py:352
  10.3 8.0 %copy-start = (bf16[2048,512]{1,0:T(8,128)(2,1)S(1)}, bf16[2048,512]{1,0:T(8,128)(2,1)}, u32[]{:S(2)}) copy-start(bf16[2048,512]{1,0:T(8,128)(2,1)} %down_ref.3) | copy-start | bytes 6291460
  19.1 9.0 %collective-permute-start.1 = (bf16[2064,128]{1,0:T(8,128)(2,1)S(1)}, bf16[2064,128]{1,0:T(8,128)(2,1)S(1)}, u32[]{:S(2)}, u32[]{:S(2)}) collective-permute-start(bf16[2064,128]{1,0:T(8,128)(2,1)S(1)} %get-tuple-element.38), channel_id=1, source_target_pairs={{0,1},{1,0},{2,3},{3,2},{4,5},{5,4},{6,7},{7,6},{8,9},{9,8},{10,11... | collective-permute-start | bytes 1585160 | tf_op jit(solution)/shard_map/ppermute | solution.py:352
  19.2 16.3 %collective-permute-start.4 = (bf16[512,512]{1,0:T(8,128)(2,1)S(1)}, bf16[512,512]{1,0:T(8,128)(2,1)S(1)}, u32[]{:S(2)}, u32[]{:S(2)}) collective-permute-start(bf16[512,512]{1,0:T(8,128)(2,1)S(1)} %get-tuple-element.44), channel_id=1, source_target_pairs={{0,4},{12,8},{1,5},{13,9},{2,6},{14,10},{3,7},{15,11},{16,20},{28,... | collective-permute-start | bytes 1572872 | tf_op jit(solution)/shard_map/ppermute | solution.py:383
  23.4 16.6 %collective-permute-start.10 = (bf16[512,512]{1,0:T(8,128)(2,1)S(1)}, bf16[512,512]{1,0:T(8,128)(2,1)S(1)}, u32[]{:S(2)}, u32[]{:S(2)}) collective-permute-start(bf16[512,512]{1,0:T(8,128)(2,1)S(1)} %add_convert_fusion.2), channel_id=1, source_target_pairs={{4,8},{8,4},{5,9},{9,5},{6,10},{10,6},{7,11},{11,7},{20,24},{24,20... | collective-permute-start | bytes 1572872 | tf_op jit(solution)/shard_map/ppermute | solution.py:387
  28.8 14.2 %copy-start.1 = (bf16[512,512]{1,0:T(8,128)(2,1)S(1)}, bf16[512,512]{1,0:T(8,128)(2,1)}, u32[]{:S(2)}) copy-start(bf16[512,512]{1,0:T(8,128)(2,1)} %up_ref.1) | copy-start | bytes 1572868
  28.9 7.6 %collective-permute-start.5 = (bf16[256,128]{1,0:T(8,128)(2,1)S(1)}, bf16[256,128]{1,0:T(8,128)(2,1)S(1)}, u32[]{:S(2)}, u32[]{:S(2)}) collective-permute-start(bf16[256,128]{1,0:T(8,128)(2,1)S(1)} %shrink_partial.3), channel_id=1, source_target_pairs={{0,4},{4,0},{8,12},{12,8},{1,5},{5,1},{9,13},{13,9},{2,6},{6,2},{1... | collective-permute-start | bytes 196616 | tf_op jit(solution)/shard_map/ppermute | solution.py:352
  36.5 6.6 %collective-permute-start.6 = (bf16[256,128]{1,0:T(8,128)(2,1)S(1)}, bf16[256,128]{1,0:T(8,128)(2,1)S(1)}, u32[]{:S(2)}, u32[]{:S(2)}) collective-permute-start(bf16[256,128]{1,0:T(8,128)(2,1)S(1)} %add_convert_fusion.3.one_ref), channel_id=1, source_target_pairs={{0,8},{4,12},{8,0},{12,4},{1,9},{5,13},{9,1},{13,5},{2,10},{6,14},... | collective-permute-start | bytes 196616 | tf_op jit(solution)/shard_map/ppermute | solution.py:352
  40.2 13.8 %collective-permute-start.12 = (bf16[512,512]{1,0:T(8,128)(2,1)S(1)}, bf16[512,512]{1,0:T(8,128)(2,1)S(1)}, u32[]{:S(2)}, u32[]{:S(2)}) collective-permute-start(bf16[512,512]{1,0:T(8,128)(2,1)S(1)} %add_convert_fusion), channel_id=1, source_target_pairs={{0,4},{4,0},{8,12},{12,8},{1,5},{5,1},{9,13},{13,9},{2,6},{6,2},{1... | collective-permute-start | bytes 1572872 | tf_op jit(solution)/shard_map/ppermute | solution.py:352
  40.2 12.1 %collective-permute-start.11 = (bf16[512,512]{1,0:T(8,128)(2,1)S(1)}, bf16[512,512]{1,0:T(8,128)(2,1)S(1)}, u32[]{:S(2)}, u32[]{:S(2)}) collective-permute-start(bf16[512,512]{1,0:T(8,128)(2,1)S(1)} %add_convert_fusion.1), channel_id=1, source_target_pairs={{4,8},{8,4},{5,9},{9,5},{6,10},{10,6},{7,11},{11,7},{20,24},{24,20... | collective-permute-start | bytes 1572872 | tf_op jit(solution)/shard_map/ppermute | solution.py:394
  43.6 1.9 %collective-permute-start.7 = (bf16[128,512]{1,0:T(8,128)(2,1)S(1)}, bf16[128,512]{1,0:T(8,128)(2,1)S(1)}, u32[]{:S(2)}, u32[]{:S(2)}) collective-permute-start(bf16[128,512]{1,0:T(8,128)(2,1)S(1)} %get-tuple-element.47), channel_id=1, source_target_pairs={{0,1},{1,0},{2,3},{3,2},{4,5},{5,4},{6,7},{7,6},{8,9},{9,8},{10,11... | collective-permute-start | bytes 393224 | tf_op jit(solution)/shard_map/ppermute | solution.py:352
  43.7 6.4 %collective-permute-start.8 = (bf16[128,512]{1,0:T(8,128)(2,1)S(1)}, bf16[128,512]{1,0:T(8,128)(2,1)S(1)}, u32[]{:S(2)}, u32[]{:S(2)}) collective-permute-start(bf16[128,512]{1,0:T(8,128)(2,1)S(1)} %get-tuple-element.48), channel_id=1, source_target_pairs={{0,2},{1,3},{2,0},{3,1},{4,6},{5,7},{6,4},{7,5},{8,10},{9,11},{10,... | collective-permute-start | bytes 393224 | tf_op jit(solution)/shard_map/ppermute | solution.py:352
  45.2 6.7 %collective-permute-start.9 = (bf16[128,512]{1,0:T(8,128)(2,1)S(1)}, bf16[128,512]{1,0:T(8,128)(2,1)S(1)}, u32[]{:S(2)}, u32[]{:S(2)}) collective-permute-start(bf16[128,512]{1,0:T(8,128)(2,1)S(1)} %get-tuple-element.49), channel_id=1, source_target_pairs={{0,3},{1,2},{2,1},{3,0},{4,7},{5,6},{6,5},{7,4},{8,11},{9,10},{10,... | collective-permute-start | bytes 393224 | tf_op jit(solution)/shard_map/ppermute | solution.py:352

commit v16 on v13

--- a/solution.py
+++ b/solution.py
@@ -170,20 +170,31 @@
     )(x, w)
 
 
-def rest_body(z_ref, spots_ref, x_ref, w_hbm, *refs):
-    near, (second, third, own, unsort, w_buf, sem) = refs[:NEAR], refs[NEAR:]
+def second_body(z_ref, spots_ref, x_ref, w_hbm, *refs):
+    near, (second, unsort, w_buf, sem) = refs[:NEAR], refs[NEAR:]
+    copies = weight_copies((jnp.where(z_ref[0] < 2, 2, 1),), w_hbm, w_buf, sem)
+    near_body(spots_ref, x_ref, *near)
+    unsort_matrix(spots_ref, unsort)
+    copies[0].wait()
+    second[...] = dot(x_ref[...], w_buf[0]).astype(bf16)
+
+
+def late_body(z_ref, x_ref, w_hbm, third, own, w_buf, sem):
     z = z_ref[0]
-    width = own.shape[1]
+    copies = weight_copies((z ^ 1, z), w_hbm, w_buf, sem)
+    for k, out in enumerate((third, own)):
+        copies[k].wait()
+        out[...] = dot(x_ref[...], w_buf[k]).astype(bf16)
+
+
+def weight_copies(blocks, w_hbm, w_buf, sem):
+    width = w_buf.shape[2]
     copies = []
-    for k, block in enumerate((jnp.where(z < 2, 2, 1), z ^ 1, z)):
+    for k, block in enumerate(blocks):
         column = pl.multiple_of(block * width, width)
         copies.append(pltpu.make_async_copy(w_hbm.at[:, pl.ds(column, width)], w_buf.at[k], sem.at[k]))
         copies[k].start()
-    near_body(spots_ref, x_ref, *near)
-    unsort_matrix(spots_ref, unsort)
-    for k, out in enumerate((second, third, own)):
-        copies[k].wait()
-        out[...] = dot(x_ref[...], w_buf[k]).astype(bf16)
+    return copies
 
 
 def unsort_matrix(place_ref, unsort):
@@ -194,21 +205,36 @@
         unsort[:, k * LANES:(k + 1) * LANES] = (place == lane + float(k * LANES)).astype(f32).astype(bf16)
 
 
-def rest(z, spots, x, weight, width, total, capacity):
+def second_block(z, spots, x, weight, width, total):
     rows, features = x.shape
     smem, vmem, hbm = (pl.BlockSpec(memory_space=m) for m in (pltpu.SMEM, pltpu.VMEM, pltpu.HBM))
     shapes = [part_shape(features)] * NEAR
-    shapes += [jax.ShapeDtypeStruct((rows, width), bf16)] * 3 + [jax.ShapeDtypeStruct((rows, total), bf16)]
-    return pl.pallas_call(
-        rest_body,
+    shapes += [jax.ShapeDtypeStruct((rows, width), bf16), jax.ShapeDtypeStruct((rows, total), bf16)]
+    return pl.pallas_call(
+        second_body,
         out_shape=shapes,
         in_specs=[smem, vmem, vmem, hbm],
         out_specs=[vmem] * len(shapes),
-        scratch_shapes=[pltpu.VMEM((3, features, width), bf16), pltpu.SemaphoreType.DMA((3,))],
+        scratch_shapes=[pltpu.VMEM((1, features, width), bf16), pltpu.SemaphoreType.DMA((1,))],
         compiler_params=params(),
         cost_estimate=cost(6 * rows * features * width, 2 * features * (rows + 4 * width)),
-        name="rest",
+        name="second_block",
     )(z.reshape(1), spots, x, in_hbm(weight))
+
+
+def late_blocks(z, x, weight, width):
+    rows, features = x.shape
+    smem, vmem, hbm = (pl.BlockSpec(memory_space=m) for m in (pltpu.SMEM, pltpu.VMEM, pltpu.HBM))
+    return pl.pallas_call(
+        late_body,
+        out_shape=[jax.ShapeDtypeStruct((rows, width), bf16)] * 2,
+        in_specs=[smem, vmem, hbm],
+        out_specs=[vmem] * 2,
+        scratch_shapes=[pltpu.VMEM((2, features, width), bf16), pltpu.SemaphoreType.DMA((2,))],
+        compiler_params=params(),
+        cost_estimate=cost(0, 0),
+        name="late_blocks",
+    )(z.reshape(1), x, in_hbm(weight))
 
 
 def unsort_only(place, total):
@@ -379,7 +405,7 @@
     if lax.axis_size("tp") == 4 and holders == 4:
         first = first_block(x, w)
         edge0 = lax.ppermute(first, "tp", EDGE)
-        *near, second, third, own, unsort = rest(z, after(spots, first), x, weight, width, total, capacity)
+        *near, second, unsort = second_block(z, after(spots, first), x, weight, width, total)
         near = [near[0], swap(near[1], "ad", 1)]
         edge1 = lax.ppermute(second, "tp", EDGE)
         early = shrink_partial(down, [near[0], far[0]])
@@ -388,7 +414,8 @@
         early = shrink_partial(down, [after(near[1], inner0)], [early])
         mine = shrink_partial(down, [after(far[1], early)], [early])
         parts, order = [near[0], far[0], near[1], far[1]], (0, 2, 1, 3)
-        inner1 = both(after(second, mine), edge1)
+        third, own = late_blocks(z, after(x, mine), weight, width)
+        inner1 = both(after(second, mine, third), edge1)
         steps, other = tp_sums(mine, inner1)
         inner2 = both(after(third, steps[-1]), middle0)
         last = swap(inner2, "tp", 1)

time: 52.2 us -> 53.2 us (1.019)
  waiting for transfers between devices: 23.1 us -> 20.8 us
  starting transfers between devices: 15.3 us -> 17.1 us
  Pallas kernels: 12.9 us -> 14.5 us
    ppermute x1, waiting for transfers between devices: 2.71 us -> 0.01 us  [shards(): edge1 = lax.ppermute(second, 'tp', EDGE)]
    ppermute x9, starting transfers between devices: 9.11 us -> 10.9 us  [swap(): lax.ppermute(value, axis, [(i, i ^ bit) for i in range(lax.axis_size(axis...]
    pallas_call x1 -> x2, Pallas kernels: 5.55 us -> 7.13 us  [the longest x1 4.12 us: late_blocks(): pl.pallas_call(late_body, out_shape=[jax.ShapeDtypeStruct((rows, width),...]
    ppermute x9, waiting for transfers between devices: 16.5 us -> 17.3 us  [swap(): lax.ppermute(value, axis, [(i, i ^ bit) for i in range(lax.axis_size(axis...]
  transfers between devices with their start and end apart: 13 -> 13, of which waited for: 8 -> 7; matrix products, arithmetic and copies ran while one was open for 1% -> 1% of each run, Pallas kernels for 18% -> 21%
where the time goes in v16:
time: 53.2 us; the launch traced here: 53 us
  waiting for transfers between devices  20.8 us (39%)
  starting transfers between devices  17.1 us (32%)
  Pallas kernels  14.5 us (27%)
    ppermute x9, waiting for transfers between devices, swap(): lax.ppermute(value, axis, [(i, i ^ bit) for i in range(lax.axis_size(axis...  17.3 us
    ppermute x9, starting transfers between devices, swap(): lax.ppermute(value, axis, [(i, i ^ bit) for i in range(lax.axis_size(axis...  10.9 us
    pallas_call x1, Pallas kernels, late_blocks(): pl.pallas_call(late_body, out_shape=[jax.ShapeDtypeStruct((rows, width),...  4.12 us
    ppermute x1, starting transfers between devices, shards(): edge0 = lax.ppermute(first, 'tp', EDGE)  3.51 us
    ppermute x1, waiting for transfers between devices, shards(): edge0 = lax.ppermute(first, 'tp', EDGE)  3.46 us
    pallas_call x1, Pallas kernels, second_block(): pl.pallas_call(second_body, out_shape=shapes, in_specs=[smem, vmem, vmem,...  3.01 us
    pallas_call x1, Pallas kernels, far_rows(): pl.pallas_call(functools.partial(far_body, slots, capacity, holders), out...  2.44 us
    pallas_call x3, Pallas kernels, shrink_partial(): pl.pallas_call(functools.partial(shrink_body, kept), out_shape=jax.ShapeD...  1.83 us
  transfers between devices with their start and end apart: 13, of which 7 were waited for; matrix products, arithmetic and copies ran while one was open for 1% of the time, Pallas kernels for 21%

profile of v16, /device:TPU:0, one launch (start us, length us, event | category | flops | bytes accessed | tf_op | source)
XLA Modules:
  0.0 53.0 jit_solution(8799207804462955804)
XLA Ops:
  0.0 2.4 %far_rows.1 = (s32[8,512]{1,0:T(8,128)S(1)}, bf16[2064,128]{1,0:T(8,128)(2,1)S(1)}, bf16[2064,128]{1,0:T(8,128)(2,1)S(1)}, bf16[512,2048]{1,0:T(8,128)(2,1)S(1)}, bf16[2048,512]{1,0:T(8,128)(2,1)S(1)}) custom-call(s32[1]{0:T(128)} %bitcast.1.me_ref, s32[1]{0:T(128)} %bitcast.z_ref, s32[1,512]{1,0:T(1,128)} %bitcast.5, s32[32,128]{1,0:T(8,128)} %bitcast.4, ...), custom_call_target="tpu_custom_call" | custom-call | flops 1073741824 | bytes 4194304 | tf_op jit(solution)/shard_map/far_rows/pallas_call | solution.py:125
  2.4 3.0 %collective-permute-start = (bf16[2064,128]{1,0:T(8,128)(2,1)S(1)}, bf16[2064,128]{1,0:T(8,128)(2,1)S(1)}, u32[]{:S(2)}, u32[]{:S(2)}) collective-permute-start(bf16[2064,128]{1,0:T(8,128)(2,1)S(1)} %get-tuple-element.35), channel_id=1, source_target_pairs={{0,2},{1,3},{2,0},{3,1},{4,6},{5,7},{6,4},{7,5},{8,10},{9,11},{10,... | collective-permute-start | bytes 1585160 | tf_op jit(solution)/shard_map/ppermute | solution.py:378
  5.5 1.2 %first_block.1 = bf16[512,512]{1,0:T(8,128)(2,1)S(1)} custom-call(bf16[512,2048]{1,0:T(8,128)(2,1)S(1)} %get-tuple-element.41.x_ref, bf16[2048,512]{1,0:T(8,128)(2,1)S(1)} %get-tuple-element.31.w_ref), custom_call_target="tpu_custom_call" | custom-call | flops 1073741824 | bytes 4194304 | tf_op jit(solution)/shard_map/first_block/pallas_call | solution.py:164
  6.7 3.5 %collective-permute-start.2 = (bf16[512,512]{1,0:T(8,128)(2,1)S(1)}, bf16[512,512]{1,0:T(8,128)(2,1)S(1)}, u32[]{:S(2)}, u32[]{:S(2)}) collective-permute-start(bf16[512,512]{1,0:T(8,128)(2,1)S(1)} %first_block.1), channel_id=1, source_target_pairs={{0,4},{12,8},{1,5},{13,9},{2,6},{14,10},{3,7},{15,11},{16,20},{28,... | collective-permute-start | bytes 1572872 | tf_op jit(solution)/shard_map/ppermute | solution.py:407
  10.2 3.0 %second_block.1 = (bf16[2064,128]{1,0:T(8,128)(2,1)S(1)}, bf16[2064,128]{1,0:T(8,128)(2,1)S(1)}, bf16[512,512]{1,0:T(8,128)(2,1)S(1)}, bf16[512,512]{1,0:T(8,128)(2,1)S(1)}) custom-call(s32[1]{0:T(128)} %bitcast.z_ref, s32[8,512]{1,0:T(8,128)S(1)} %get-tuple-element.32.spots_ref, bf16[512,2048]{1,0:T(8,128)(2,1)S(1)} %get-tuple-element.41.x_ref, ...), custom_call_target="tpu_custom_call" | custom-call | flops 3221225472 | bytes 10485760 | tf_op jit(solution)/shard_map/second_block/pallas_call | solution.py:213
  13.3 0.7 %collective-permute-start.3 = (bf16[2064,128]{1,0:T(8,128)(2,1)S(1)}, bf16[2064,128]{1,0:T(8,128)(2,1)S(1)}, u32[]{:S(2)}, u32[]{:S(2)}) collective-permute-start(bf16[2064,128]{1,0:T(8,128)(2,1)S(1)} %get-tuple-element.39), channel_id=1, source_target_pairs={{0,3},{1,2},{2,1},{3,0},{4,7},{5,6},{6,5},{7,4},{8,11},{9,10},{10,... | collective-permute-start | bytes 1585160 | tf_op jit(solution)/shard_map/ppermute | solution.py:378
  14.0 1.3 %collective-permute-start.4 = (bf16[512,512]{1,0:T(8,128)(2,1)S(1)}, bf16[512,512]{1,0:T(8,128)(2,1)S(1)}, u32[]{:S(2)}, u32[]{:S(2)}) collective-permute-start(bf16[512,512]{1,0:T(8,128)(2,1)S(1)} %get-tuple-element.45), channel_id=1, source_target_pairs={{0,4},{12,8},{1,5},{13,9},{2,6},{14,10},{3,7},{15,11},{16,20},{28,... | collective-permute-start | bytes 1572872 | tf_op jit(solution)/shard_map/ppermute | solution.py:410
  15.3 3.0 %collective-permute-done.refs_1_ = bf16[2064,128]{1,0:T(8,128)(2,1)S(1)} collective-permute-done((bf16[2064,128]{1,0:T(8,128)(2,1)S(1)}, bf16[2064,128]{1,0:T(8,128)(2,1)S(1)}, u32[]{:S(2)}, u32[]{:S(2)}) %collective-permute-start) | collective-permute-done | bytes 528416 | tf_op jit(solution)/shard_map/ppermute | solution.py:378
  18.3 0.8 %shrink_partial.3.refs_0_ = bf16[128,128]{1,0:T(8,128)(2,1)S(1)} custom-call(bf16[2048,512]{1,0:T(8,128)(2,1)S(1)} %copy-done, bf16[2064,128]{1,0:T(8,128)(2,1)S(1)} %get-tuple-element.34.refs_0_, bf16[2064,128]{1,0:T(8,128)(2,1)S(1)} %collective-permute-done.refs_1_), custom_call_target="tpu_custom_call" | custom-call | flops 536870912 | bytes 3145728 | tf_op jit(solution)/shard_map/shrink_partial/pallas_call | solution.py:276
  19.1 3.5 %collective-permute-done.2 = bf16[512,512]{1,0:T(8,128)(2,1)S(1)} collective-permute-done((bf16[512,512]{1,0:T(8,128)(2,1)S(1)}, bf16[512,512]{1,0:T(8,128)(2,1)S(1)}, u32[]{:S(2)}, u32[]{:S(2)}) %collective-permute-start.2) | collective-permute-done | bytes 524320 | tf_op jit(solution)/shard_map/ppermute | solution.py:407
  22.7 0.7 %collective-permute-start.10 = (bf16[512,512]{1,0:T(8,128)(2,1)S(1)}, bf16[512,512]{1,0:T(8,128)(2,1)S(1)}, u32[]{:S(2)}, u32[]{:S(2)}) collective-permute-start(bf16[512,512]{1,0:T(8,128)(2,1)S(1)} %add_convert_fusion.2), channel_id=1, source_target_pairs={{4,8},{8,4},{5,9},{9,5},{6,10},{10,6},{7,11},{11,7},{20,24},{24,20... | collective-permute-start | bytes 1572872 | tf_op jit(solution)/shard_map/ppermute | solution.py:413
  23.4 0.5 shrink_partial.4.refs_0_
  23.9 4.1 %collective-permute-done.3.refs_1_.refs_3_ = bf16[2064,128]{1,0:T(8,128)(2,1)S(1)} collective-permute-done((bf16[2064,128]{1,0:T(8,128)(2,1)S(1)}, bf16[2064,128]{1,0:T(8,128)(2,1)S(1)}, u32[]{:S(2)}, u32[]{:S(2)}) %collective-permute-start.3) | collective-permute-done | bytes 528416 | tf_op jit(solution)/shard_map/ppermute | solution.py:378
  28.6 1.6 %collective-permute-start.5 = (bf16[256,128]{1,0:T(8,128)(2,1)S(1)}, bf16[256,128]{1,0:T(8,128)(2,1)S(1)}, u32[]{:S(2)}, u32[]{:S(2)}) collective-permute-start(bf16[256,128]{1,0:T(8,128)(2,1)S(1)} %shrink_partial.5), channel_id=1, source_target_pairs={{0,4},{4,0},{8,12},{12,8},{1,5},{5,1},{9,13},{13,9},{2,6},{6,2},{1... | collective-permute-start | bytes 196616 | tf_op jit(solution)/shard_map/ppermute | solution.py:378
  30.2 4.1 %late_blocks.1 = (bf16[512,512]{1,0:T(8,128)(2,1)S(1)}, bf16[512,512]{1,0:T(8,128)(2,1)S(1)}) custom-call(s32[1]{0:T(128)} %bitcast.z_ref, bf16[512,2048]{1,0:T(8,128)(2,1)S(1)} %get-tuple-element.41.x_ref, bf16[2048,2048]{1,0:T(8,128)(2,1)} %w_hbm.5), custom_call_target="tpu_custom_call" | custom-call | tf_op jit(solution)/shard_map/late_blocks/pallas_call | solution.py:228
  34.5 2.8 %collective-permute-start.6 = (bf16[256,128]{1,0:T(8,128)(2,1)S(1)}, bf16[256,128]{1,0:T(8,128)(2,1)S(1)}, u32[]{:S(2)}, u32[]{:S(2)}) collective-permute-start(bf16[256,128]{1,0:T(8,128)(2,1)S(1)} %add_convert_fusion.3.one_ref), channel_id=1, source_target_pairs={{0,8},{4,12},{8,0},{12,4},{1,9},{5,13},{9,1},{13,5},{2,10},{6,14},... | collective-permute-start | bytes 196616 | tf_op jit(solution)/shard_map/ppermute | solution.py:378
  37.4 0.8 %collective-permute-start.12 = (bf16[512,512]{1,0:T(8,128)(2,1)S(1)}, bf16[512,512]{1,0:T(8,128)(2,1)S(1)}, u32[]{:S(2)}, u32[]{:S(2)}) collective-permute-start(bf16[512,512]{1,0:T(8,128)(2,1)S(1)} %add_convert_fusion), channel_id=1, source_target_pairs={{0,4},{4,0},{8,12},{12,8},{1,5},{5,1},{9,13},{13,9},{2,6},{6,2},{1... | collective-permute-start | bytes 1572872 | tf_op jit(solution)/shard_map/ppermute | solution.py:378
  38.3 0.7 %collective-permute-start.11 = (bf16[512,512]{1,0:T(8,128)(2,1)S(1)}, bf16[512,512]{1,0:T(8,128)(2,1)S(1)}, u32[]{:S(2)}, u32[]{:S(2)}) collective-permute-start(bf16[512,512]{1,0:T(8,128)(2,1)S(1)} %add_convert_fusion.1), channel_id=1, source_target_pairs={{4,8},{8,4},{5,9},{9,5},{6,10},{10,6},{7,11},{11,7},{20,24},{24,20... | collective-permute-start | bytes 1572872 | tf_op jit(solution)/shard_map/ppermute | solution.py:422
  39.0 2.6 %collective-permute-done.6.two_ref = bf16[256,128]{1,0:T(8,128)(2,1)S(1)} collective-permute-done((bf16[256,128]{1,0:T(8,128)(2,1)S(1)}, bf16[256,128]{1,0:T(8,128)(2,1)S(1)}, u32[]{:S(2)}, u32[]{:S(2)}) %collective-permute-start.6) | collective-permute-done | bytes 65568 | tf_op jit(solution)/shard_map/ppermute | solution.py:378
  42.3 1.6 %collective-permute-start.8 = (bf16[128,512]{1,0:T(8,128)(2,1)S(1)}, bf16[128,512]{1,0:T(8,128)(2,1)S(1)}, u32[]{:S(2)}, u32[]{:S(2)}) collective-permute-start(bf16[128,512]{1,0:T(8,128)(2,1)S(1)} %get-tuple-element.49), channel_id=1, source_target_pairs={{0,2},{1,3},{2,0},{3,1},{4,6},{5,7},{6,4},{7,5},{8,10},{9,11},{10,... | collective-permute-start | bytes 393224 | tf_op jit(solution)/shard_map/ppermute | solution.py:378
  44.0 4.5 %collective-permute-done.8.refs_2_ = bf16[128,512]{1,0:T(8,128)(2,1)S(1)} collective-permute-done((bf16[128,512]{1,0:T(8,128)(2,1)S(1)}, bf16[128,512]{1,0:T(8,128)(2,1)S(1)}, u32[]{:S(2)}, u32[]{:S(2)}) %collective-permute-start.8) | collective-permute-done | bytes 131104 | tf_op jit(solution)/shard_map/ppermute | solution.py:378
  48.6 1.9 %collective-permute-done.9.refs_3_ = bf16[128,512]{1,0:T(8,128)(2,1)S(1)} collective-permute-done((bf16[128,512]{1,0:T(8,128)(2,1)S(1)}, bf16[128,512]{1,0:T(8,128)(2,1)S(1)}, u32[]{:S(2)}, u32[]{:S(2)}) %collective-permute-start.9) | collective-permute-done | bytes 131104 | tf_op jit(solution)/shard_map/ppermute | solution.py:378
  50.9 1.2 %collective-permute-done.12.refs_1_ = bf16[512,512]{1,0:T(8,128)(2,1)S(1)} collective-permute-done((bf16[512,512]{1,0:T(8,128)(2,1)S(1)}, bf16[512,512]{1,0:T(8,128)(2,1)S(1)}, u32[]{:S(2)}, u32[]{:S(2)}) %collective-permute-start.12) | collective-permute-done | bytes 524320 | tf_op jit(solution)/shard_map/ppermute | solution.py:378
  52.1 0.9 %finish.1 = bf16[512,512]{1,0:T(8,128)(2,1)} custom-call(f32[512,512]{1,0:T(8,128)S(1)} %with_deltas.1.start_ref, bf16[512,512]{1,0:T(8,128)(2,1)S(1)} %collective-permute-done.11.refs_0_, bf16[512,512]{1,0:T(8,128)(2,1)S(1)} %collective-permute-done.12.refs_1_), custom_call_target="tpu_custom_call" | custom-call | flops 262144 | bytes 2097152 | tf_op jit(solution)/shard_map/finish/pallas_call | solution.py:357
  (20 shorter events, 2.4 us)
Async XLA Ops:
  2.4 15.8 %collective-permute-start = (bf16[2064,128]{1,0:T(8,128)(2,1)S(1)}, bf16[2064,128]{1,0:T(8,128)(2,1)S(1)}, u32[]{:S(2)}, u32[]{:S(2)}) collective-permute-start(bf16[2064,128]{1,0:T(8,128)(2,1)S(1)} %get-tuple-element.35), channel_id=1, source_target_pairs={{0,2},{1,3},{2,0},{3,1},{4,6},{5,7},{6,4},{7,5},{8,10},{9,11},{10,... | collective-permute-start | bytes 1585160 | tf_op jit(solution)/shard_map/ppermute | solution.py:378
  6.7 15.8 %collective-permute-start.2 = (bf16[512,512]{1,0:T(8,128)(2,1)S(1)}, bf16[512,512]{1,0:T(8,128)(2,1)S(1)}, u32[]{:S(2)}, u32[]{:S(2)}) collective-permute-start(bf16[512,512]{1,0:T(8,128)(2,1)S(1)} %first_block.1), channel_id=1, source_target_pairs={{0,4},{12,8},{1,5},{13,9},{2,6},{14,10},{3,7},{15,11},{16,20},{28,... | collective-permute-start | bytes 1572872 | tf_op jit(solution)/shard_map/ppermute | solution.py:407
  10.2 8.1 %copy-start = (bf16[2048,512]{1,0:T(8,128)(2,1)S(1)}, bf16[2048,512]{1,0:T(8,128)(2,1)}, u32[]{:S(2)}) copy-start(bf16[2048,512]{1,0:T(8,128)(2,1)} %down_ref.5) | copy-start | bytes 6291460
  13.3 10.1 %collective-permute-start.1 = (bf16[2064,128]{1,0:T(8,128)(2,1)S(1)}, bf16[2064,128]{1,0:T(8,128)(2,1)S(1)}, u32[]{:S(2)}, u32[]{:S(2)}) collective-permute-start(bf16[2064,128]{1,0:T(8,128)(2,1)S(1)} %get-tuple-element.36), channel_id=1, source_target_pairs={{0,1},{1,0},{2,3},{3,2},{4,5},{5,4},{6,7},{7,6},{8,9},{9,8},{10,11... | collective-permute-start | bytes 1585160 | tf_op jit(solution)/shard_map/ppermute | solution.py:378
  13.3 14.7 %collective-permute-start.3 = (bf16[2064,128]{1,0:T(8,128)(2,1)S(1)}, bf16[2064,128]{1,0:T(8,128)(2,1)S(1)}, u32[]{:S(2)}, u32[]{:S(2)}) collective-permute-start(bf16[2064,128]{1,0:T(8,128)(2,1)S(1)} %get-tuple-element.39), channel_id=1, source_target_pairs={{0,3},{1,2},{2,1},{3,0},{4,7},{5,6},{6,5},{7,4},{8,11},{9,10},{10,... | collective-permute-start | bytes 1585160 | tf_op jit(solution)/shard_map/ppermute | solution.py:378
  14.0 20.4 %collective-permute-start.4 = (bf16[512,512]{1,0:T(8,128)(2,1)S(1)}, bf16[512,512]{1,0:T(8,128)(2,1)S(1)}, u32[]{:S(2)}, u32[]{:S(2)}) collective-permute-start(bf16[512,512]{1,0:T(8,128)(2,1)S(1)} %get-tuple-element.45), channel_id=1, source_target_pairs={{0,4},{12,8},{1,5},{13,9},{2,6},{14,10},{3,7},{15,11},{16,20},{28,... | collective-permute-start | bytes 1572872 | tf_op jit(solution)/shard_map/ppermute | solution.py:410
  22.7 14.6 %collective-permute-start.10 = (bf16[512,512]{1,0:T(8,128)(2,1)S(1)}, bf16[512,512]{1,0:T(8,128)(2,1)S(1)}, u32[]{:S(2)}, u32[]{:S(2)}) collective-permute-start(bf16[512,512]{1,0:T(8,128)(2,1)S(1)} %add_convert_fusion.2), channel_id=1, source_target_pairs={{4,8},{8,4},{5,9},{9,5},{6,10},{10,6},{7,11},{11,7},{20,24},{24,20... | collective-permute-start | bytes 1572872 | tf_op jit(solution)/shard_map/ppermute | solution.py:413
  28.6 5.9 %collective-permute-start.5 = (bf16[256,128]{1,0:T(8,128)(2,1)S(1)}, bf16[256,128]{1,0:T(8,128)(2,1)S(1)}, u32[]{:S(2)}, u32[]{:S(2)}) collective-permute-start(bf16[256,128]{1,0:T(8,128)(2,1)S(1)} %shrink_partial.5), channel_id=1, source_target_pairs={{0,4},{4,0},{8,12},{12,8},{1,5},{5,1},{9,13},{13,9},{2,6},{6,2},{1... | collective-permute-start | bytes 196616 | tf_op jit(solution)/shard_map/ppermute | solution.py:378
  34.3 7.2 %copy-start.1 = (bf16[512,512]{1,0:T(8,128)(2,1)S(1)}, bf16[512,512]{1,0:T(8,128)(2,1)}, u32[]{:S(2)}) copy-start(bf16[512,512]{1,0:T(8,128)(2,1)} %up_ref.1) | copy-start | bytes 1572868
  34.5 7.0 %collective-permute-start.6 = (bf16[256,128]{1,0:T(8,128)(2,1)S(1)}, bf16[256,128]{1,0:T(8,128)(2,1)S(1)}, u32[]{:S(2)}, u32[]{:S(2)}) collective-permute-start(bf16[256,128]{1,0:T(8,128)(2,1)S(1)} %add_convert_fusion.3.one_ref), channel_id=1, source_target_pairs={{0,8},{4,12},{8,0},{12,4},{1,9},{5,13},{9,1},{13,5},{2,10},{6,14},... | collective-permute-start | bytes 196616 | tf_op jit(solution)/shard_map/ppermute | solution.py:378
  37.4 14.7 %collective-permute-start.12 = (bf16[512,512]{1,0:T(8,128)(2,1)S(1)}, bf16[512,512]{1,0:T(8,128)(2,1)S(1)}, u32[]{:S(2)}, u32[]{:S(2)}) collective-permute-start(bf16[512,512]{1,0:T(8,128)(2,1)S(1)} %add_convert_fusion), channel_id=1, source_target_pairs={{0,4},{4,0},{8,12},{12,8},{1,5},{5,1},{9,13},{13,9},{2,6},{6,2},{1... | collective-permute-start | bytes 1572872 | tf_op jit(solution)/shard_map/ppermute | solution.py:378
  38.3 12.6 %collective-permute-start.11 = (bf16[512,512]{1,0:T(8,128)(2,1)S(1)}, bf16[512,512]{1,0:T(8,128)(2,1)S(1)}, u32[]{:S(2)}, u32[]{:S(2)}) collective-permute-start(bf16[512,512]{1,0:T(8,128)(2,1)S(1)} %add_convert_fusion.1), channel_id=1, source_target_pairs={{4,8},{8,4},{5,9},{9,5},{6,10},{10,6},{7,11},{11,7},{20,24},{24,20... | collective-permute-start | bytes 1572872 | tf_op jit(solution)/shard_map/ppermute | solution.py:422
  42.1 1.9 %collective-permute-start.7 = (bf16[128,512]{1,0:T(8,128)(2,1)S(1)}, bf16[128,512]{1,0:T(8,128)(2,1)S(1)}, u32[]{:S(2)}, u32[]{:S(2)}) collective-permute-start(bf16[128,512]{1,0:T(8,128)(2,1)S(1)} %get-tuple-element.48), channel_id=1, source_target_pairs={{0,1},{1,0},{2,3},{3,2},{4,5},{5,4},{6,7},{7,6},{8,9},{9,8},{10,11... | collective-permute-start | bytes 393224 | tf_op jit(solution)/shard_map/ppermute | solution.py:378
  42.3 6.3 %collective-permute-start.8 = (bf16[128,512]{1,0:T(8,128)(2,1)S(1)}, bf16[128,512]{1,0:T(8,128)(2,1)S(1)}, u32[]{:S(2)}, u32[]{:S(2)}) collective-permute-start(bf16[128,512]{1,0:T(8,128)(2,1)S(1)} %get-tuple-element.49), channel_id=1, source_target_pairs={{0,2},{1,3},{2,0},{3,1},{4,6},{5,7},{6,4},{7,5},{8,10},{9,11},{10,... | collective-permute-start | bytes 393224 | tf_op jit(solution)/shard_map/ppermute | solution.py:378
  43.8 6.6 %collective-permute-start.9 = (bf16[128,512]{1,0:T(8,128)(2,1)S(1)}, bf16[128,512]{1,0:T(8,128)(2,1)S(1)}, u32[]{:S(2)}, u32[]{:S(2)}) collective-permute-start(bf16[128,512]{1,0:T(8,128)(2,1)S(1)} %get-tuple-element.50), channel_id=1, source_target_pairs={{0,3},{1,2},{2,1},{3,0},{4,7},{5,6},{6,5},{7,4},{8,11},{9,10},{10,... | collective-permute-start | bytes 393224 | tf_op jit(solution)/shard_map/ppermute | solution.py:378

commit v17 on v13

--- a/solution.py
+++ b/solution.py
@@ -382,12 +382,12 @@
         *near, second, third, own, unsort = rest(z, after(spots, first), x, weight, width, total, capacity)
         near = [near[0], swap(near[1], "ad", 1)]
         edge1 = lax.ppermute(second, "tp", EDGE)
-        early = shrink_partial(down, [near[0], far[0]])
+        early = shrink_partial(down, [near[0], far[1]])
         inner0 = both(after(first, early), edge0)
         middle0 = lax.ppermute(inner0, "tp", MIDDLE)
         early = shrink_partial(down, [after(near[1], inner0)], [early])
-        mine = shrink_partial(down, [after(far[1], early)], [early])
-        parts, order = [near[0], far[0], near[1], far[1]], (0, 2, 1, 3)
+        mine = shrink_partial(down, [after(far[0], early)], [early])
+        parts, order = [near[0], far[1], near[1], far[0]], (0, 3, 1, 2)
         inner1 = both(after(second, mine), edge1)
         steps, other = tp_sums(mine, inner1)
         inner2 = both(after(third, steps[-1]), middle0)

time: 52.2 us -> 53.4 us (1.023)
  starting transfers between devices: 15.3 us -> 19.9 us
  waiting for transfers between devices: 23.1 us -> 19.7 us
    ppermute x9, starting transfers between devices: 9.11 us -> 13.5 us  [swap(): lax.ppermute(value, axis, [(i, i ^ bit) for i in range(lax.axis_size(axis...]
    ppermute x9, waiting for transfers between devices: 16.5 us -> 15 us  [swap(): lax.ppermute(value, axis, [(i, i ^ bit) for i in range(lax.axis_size(axis...]
    ppermute x1, waiting for transfers between devices: 2.71 us -> 1.39 us  [shards(): edge1 = lax.ppermute(second, 'tp', EDGE)]
    ppermute x1, waiting for transfers between devices: 3.89 us -> 3.31 us  [shards(): edge0 = lax.ppermute(first, 'tp', EDGE)]
where the time goes in v17:
time: 53.4 us; the launch traced here: 53.2 us
  starting transfers between devices  19.9 us (37%)
  waiting for transfers between devices  19.7 us (37%)
  Pallas kernels  12.9 us (24%)
    ppermute x9, waiting for transfers between devices, swap(): lax.ppermute(value, axis, [(i, i ^ bit) for i in range(lax.axis_size(axis...  15 us
    ppermute x9, starting transfers between devices, swap(): lax.ppermute(value, axis, [(i, i ^ bit) for i in range(lax.axis_size(axis...  13.5 us
    pallas_call x1, Pallas kernels, rest(): pl.pallas_call(rest_body, out_shape=shapes, in_specs=[smem, vmem, vmem, h...  5.54 us
    ppermute x1, starting transfers between devices, shards(): edge0 = lax.ppermute(first, 'tp', EDGE)  3.51 us
    ppermute x1, waiting for transfers between devices, shards(): edge0 = lax.ppermute(first, 'tp', EDGE)  3.31 us
    pallas_call x1, Pallas kernels, far_rows(): pl.pallas_call(functools.partial(far_body, slots, capacity, holders), out...  2.44 us
    pallas_call x3, Pallas kernels, shrink_partial(): pl.pallas_call(functools.partial(shrink_body, kept), out_shape=jax.ShapeD...  1.84 us
    ppermute x1, starting transfers between devices, shards(): edge1 = lax.ppermute(second, 'tp', EDGE)  1.56 us
  transfers between devices with their start and end apart: 13, of which 8 were waited for; matrix products, arithmetic and copies ran while one was open for 1% of the time, Pallas kernels for 18%

profile of v17, /device:TPU:0, one launch (start us, length us, event | category | flops | bytes accessed | tf_op | source)
XLA Modules:
  0.0 53.2 jit_solution(7484420343847059577)
XLA Ops:
  0.0 2.4 %far_rows.1 = (s32[8,512]{1,0:T(8,128)S(1)}, bf16[2064,128]{1,0:T(8,128)(2,1)S(1)}, bf16[2064,128]{1,0:T(8,128)(2,1)S(1)}, bf16[512,2048]{1,0:T(8,128)(2,1)S(1)}, bf16[2048,512]{1,0:T(8,128)(2,1)S(1)}) custom-call(s32[1]{0:T(128)} %bitcast.1.me_ref, s32[1]{0:T(128)} %bitcast.z_ref, s32[1,512]{1,0:T(1,128)} %bitcast.5, s32[32,128]{1,0:T(8,128)} %bitcast.4, ...), custom_call_target="tpu_custom_call" | custom-call | flops 1073741824 | bytes 4194304 | tf_op jit(solution)/shard_map/far_rows/pallas_call | solution.py:125
  2.4 2.4 %collective-permute-start = (bf16[2064,128]{1,0:T(8,128)(2,1)S(1)}, bf16[2064,128]{1,0:T(8,128)(2,1)S(1)}, u32[]{:S(2)}, u32[]{:S(2)}) collective-permute-start(bf16[2064,128]{1,0:T(8,128)(2,1)S(1)} %get-tuple-element.35), channel_id=1, source_target_pairs={{0,3},{1,2},{2,1},{3,0},{4,7},{5,6},{6,5},{7,4},{8,11},{9,10},{10,... | collective-permute-start | bytes 1585160 | tf_op jit(solution)/shard_map/ppermute | solution.py:352
  4.9 1.2 %first_block.1 = bf16[512,512]{1,0:T(8,128)(2,1)S(1)} custom-call(bf16[512,2048]{1,0:T(8,128)(2,1)S(1)} %get-tuple-element.29.x_ref, bf16[2048,512]{1,0:T(8,128)(2,1)S(1)} %get-tuple-element.30.w_ref), custom_call_target="tpu_custom_call" | custom-call | flops 1073741824 | bytes 4194304 | tf_op jit(solution)/shard_map/first_block/pallas_call | solution.py:164
  6.1 3.5 %collective-permute-start.2 = (bf16[512,512]{1,0:T(8,128)(2,1)S(1)}, bf16[512,512]{1,0:T(8,128)(2,1)S(1)}, u32[]{:S(2)}, u32[]{:S(2)}) collective-permute-start(bf16[512,512]{1,0:T(8,128)(2,1)S(1)} %first_block.1), channel_id=1, source_target_pairs={{0,4},{12,8},{1,5},{13,9},{2,6},{14,10},{3,7},{15,11},{16,20},{28,... | collective-permute-start | bytes 1572872 | tf_op jit(solution)/shard_map/ppermute | solution.py:381
  9.7 5.5 %rest.1 = (bf16[2064,128]{1,0:T(8,128)(2,1)S(1)}, bf16[2064,128]{1,0:T(8,128)(2,1)S(1)}, bf16[512,512]{1,0:T(8,128)(2,1)S(1)}, bf16[512,512]{1,0:T(8,128)(2,1)S(...) custom-call(s32[1]{0:T(128)} %bitcast.z_ref, s32[8,512]{1,0:T(8,128)S(1)} %get-tuple-element.31.spots_ref, ...), custom_call_target="tpu_custom_call" | custom-call | flops 3221225472 | bytes 10485760 | tf_op jit(solution)/shard_map/rest/pallas_call | solution.py:202
  15.7 0.5 %collective-permute-start.3 = (bf16[2064,128]{1,0:T(8,128)(2,1)S(1)}, bf16[2064,128]{1,0:T(8,128)(2,1)S(1)}, u32[]{:S(2)}, u32[]{:S(2)}) collective-permute-start(bf16[2064,128]{1,0:T(8,128)(2,1)S(1)} %get-tuple-element.39), channel_id=1, source_target_pairs={{0,2},{1,3},{2,0},{3,1},{4,6},{5,7},{6,4},{7,5},{8,10},{9,11},{10,... | collective-permute-start | bytes 1585160 | tf_op jit(solution)/shard_map/ppermute | solution.py:352
  16.2 1.6 %collective-permute-start.4 = (bf16[512,512]{1,0:T(8,128)(2,1)S(1)}, bf16[512,512]{1,0:T(8,128)(2,1)S(1)}, u32[]{:S(2)}, u32[]{:S(2)}) collective-permute-start(bf16[512,512]{1,0:T(8,128)(2,1)S(1)} %get-tuple-element.42), channel_id=1, source_target_pairs={{0,4},{12,8},{1,5},{13,9},{2,6},{14,10},{3,7},{15,11},{16,20},{28,... | collective-permute-start | bytes 1572872 | tf_op jit(solution)/shard_map/ppermute | solution.py:384
  17.8 0.8 %shrink_partial.3.refs_0_ = bf16[128,128]{1,0:T(8,128)(2,1)S(1)} custom-call(bf16[2048,512]{1,0:T(8,128)(2,1)S(1)} %copy-done, bf16[2064,128]{1,0:T(8,128)(2,1)S(1)} %get-tuple-element.34.refs_0_, bf16[2064,128]{1,0:T(8,128)(2,1)S(1)} %collective-permute-done.refs_1_), custom_call_target="tpu_custom_call" | custom-call | flops 536870912 | bytes 3145728 | tf_op jit(solution)/shard_map/shrink_partial/pallas_call | solution.py:250
  18.6 3.3 %collective-permute-done.2 = bf16[512,512]{1,0:T(8,128)(2,1)S(1)} collective-permute-done((bf16[512,512]{1,0:T(8,128)(2,1)S(1)}, bf16[512,512]{1,0:T(8,128)(2,1)S(1)}, u32[]{:S(2)}, u32[]{:S(2)}) %collective-permute-start.2) | collective-permute-done | bytes 524320 | tf_op jit(solution)/shard_map/ppermute | solution.py:381
  22.1 0.7 %collective-permute-start.10 = (bf16[512,512]{1,0:T(8,128)(2,1)S(1)}, bf16[512,512]{1,0:T(8,128)(2,1)S(1)}, u32[]{:S(2)}, u32[]{:S(2)}) collective-permute-start(bf16[512,512]{1,0:T(8,128)(2,1)S(1)} %add_convert_fusion.2), channel_id=1, source_target_pairs={{4,8},{8,4},{5,9},{9,5},{6,10},{10,6},{7,11},{11,7},{20,24},{24,20... | collective-permute-start | bytes 1572872 | tf_op jit(solution)/shard_map/ppermute | solution.py:387
  22.8 0.5 shrink_partial.4.refs_0_
  23.3 6.4 %collective-permute-done.3.refs_1_.refs_3_ = bf16[2064,128]{1,0:T(8,128)(2,1)S(1)} collective-permute-done((bf16[2064,128]{1,0:T(8,128)(2,1)S(1)}, bf16[2064,128]{1,0:T(8,128)(2,1)S(1)}, u32[]{:S(2)}, u32[]{:S(2)}) %collective-permute-start.3) | collective-permute-done | bytes 528416 | tf_op jit(solution)/shard_map/ppermute | solution.py:352
  30.3 1.5 %collective-permute-start.5 = (bf16[256,128]{1,0:T(8,128)(2,1)S(1)}, bf16[256,128]{1,0:T(8,128)(2,1)S(1)}, u32[]{:S(2)}, u32[]{:S(2)}) collective-permute-start(bf16[256,128]{1,0:T(8,128)(2,1)S(1)} %shrink_partial.5), channel_id=1, source_target_pairs={{0,4},{4,0},{8,12},{12,8},{1,5},{5,1},{9,13},{13,9},{2,6},{6,2},{1... | collective-permute-start | bytes 196616 | tf_op jit(solution)/shard_map/ppermute | solution.py:352
  31.8 1.4 %collective-permute-done.4 = bf16[512,512]{1,0:T(8,128)(2,1)S(1)} collective-permute-done((bf16[512,512]{1,0:T(8,128)(2,1)S(1)}, bf16[512,512]{1,0:T(8,128)(2,1)S(1)}, u32[]{:S(2)}, u32[]{:S(2)}) %collective-permute-start.4) | collective-permute-done | bytes 524320 | tf_op jit(solution)/shard_map/ppermute | solution.py:384
  33.3 1.3 %collective-permute-done.5 = bf16[256,128]{1,0:T(8,128)(2,1)S(1)} collective-permute-done((bf16[256,128]{1,0:T(8,128)(2,1)S(1)}, bf16[256,128]{1,0:T(8,128)(2,1)S(1)}, u32[]{:S(2)}, u32[]{:S(2)}) %collective-permute-start.5) | collective-permute-done | bytes 65568 | tf_op jit(solution)/shard_map/ppermute | solution.py:352
  34.6 3.2 %collective-permute-start.6 = (bf16[256,128]{1,0:T(8,128)(2,1)S(1)}, bf16[256,128]{1,0:T(8,128)(2,1)S(1)}, u32[]{:S(2)}, u32[]{:S(2)}) collective-permute-start(bf16[256,128]{1,0:T(8,128)(2,1)S(1)} %add_convert_fusion.3.one_ref), channel_id=1, source_target_pairs={{0,8},{4,12},{8,0},{12,4},{1,9},{5,13},{9,1},{13,5},{2,10},{6,14},... | collective-permute-start | bytes 196616 | tf_op jit(solution)/shard_map/ppermute | solution.py:352
  38.0 3.4 %collective-permute-start.12 = (bf16[512,512]{1,0:T(8,128)(2,1)S(1)}, bf16[512,512]{1,0:T(8,128)(2,1)S(1)}, u32[]{:S(2)}, u32[]{:S(2)}) collective-permute-start(bf16[512,512]{1,0:T(8,128)(2,1)S(1)} %add_convert_fusion), channel_id=1, source_target_pairs={{0,4},{4,0},{8,12},{12,8},{1,5},{5,1},{9,13},{13,9},{2,6},{6,2},{1... | collective-permute-start | bytes 1572872 | tf_op jit(solution)/shard_map/ppermute | solution.py:352
  41.4 0.7 %collective-permute-start.11 = (bf16[512,512]{1,0:T(8,128)(2,1)S(1)}, bf16[512,512]{1,0:T(8,128)(2,1)S(1)}, u32[]{:S(2)}, u32[]{:S(2)}) collective-permute-start(bf16[512,512]{1,0:T(8,128)(2,1)S(1)} %add_convert_fusion.1), channel_id=1, source_target_pairs={{4,8},{8,4},{5,9},{9,5},{6,10},{10,6},{7,11},{11,7},{20,24},{24,20... | collective-permute-start | bytes 1572872 | tf_op jit(solution)/shard_map/ppermute | solution.py:395
  42.8 0.6 %collective-permute-start.8 = (bf16[128,512]{1,0:T(8,128)(2,1)S(1)}, bf16[128,512]{1,0:T(8,128)(2,1)S(1)}, u32[]{:S(2)}, u32[]{:S(2)}) collective-permute-start(bf16[128,512]{1,0:T(8,128)(2,1)S(1)} %get-tuple-element.46), channel_id=1, source_target_pairs={{0,2},{1,3},{2,0},{3,1},{4,6},{5,7},{6,4},{7,5},{8,10},{9,11},{10,... | collective-permute-start | bytes 393224 | tf_op jit(solution)/shard_map/ppermute | solution.py:352
  43.3 1.3 %collective-permute-start.9 = (bf16[128,512]{1,0:T(8,128)(2,1)S(1)}, bf16[128,512]{1,0:T(8,128)(2,1)S(1)}, u32[]{:S(2)}, u32[]{:S(2)}) collective-permute-start(bf16[128,512]{1,0:T(8,128)(2,1)S(1)} %get-tuple-element.47), channel_id=1, source_target_pairs={{0,3},{1,2},{2,1},{3,0},{4,7},{5,6},{6,5},{7,4},{8,11},{9,10},{10,... | collective-permute-start | bytes 393224 | tf_op jit(solution)/shard_map/ppermute | solution.py:352
  44.6 4.5 %collective-permute-done.8.refs_2_ = bf16[128,512]{1,0:T(8,128)(2,1)S(1)} collective-permute-done((bf16[128,512]{1,0:T(8,128)(2,1)S(1)}, bf16[128,512]{1,0:T(8,128)(2,1)S(1)}, u32[]{:S(2)}, u32[]{:S(2)}) %collective-permute-start.8) | collective-permute-done | bytes 131104 | tf_op jit(solution)/shard_map/ppermute | solution.py:352
  49.1 1.9 %collective-permute-done.9.refs_3_ = bf16[128,512]{1,0:T(8,128)(2,1)S(1)} collective-permute-done((bf16[128,512]{1,0:T(8,128)(2,1)S(1)}, bf16[128,512]{1,0:T(8,128)(2,1)S(1)}, u32[]{:S(2)}, u32[]{:S(2)}) %collective-permute-start.9) | collective-permute-done | bytes 131104 | tf_op jit(solution)/shard_map/ppermute | solution.py:352
  51.5 0.8 %collective-permute-done.12.refs_1_ = bf16[512,512]{1,0:T(8,128)(2,1)S(1)} collective-permute-done((bf16[512,512]{1,0:T(8,128)(2,1)S(1)}, bf16[512,512]{1,0:T(8,128)(2,1)S(1)}, u32[]{:S(2)}, u32[]{:S(2)}) %collective-permute-start.12) | collective-permute-done | bytes 524320 | tf_op jit(solution)/shard_map/ppermute | solution.py:352
  52.3 0.9 %finish.1 = bf16[512,512]{1,0:T(8,128)(2,1)} custom-call(f32[512,512]{1,0:T(8,128)S(1)} %with_deltas.1.start_ref, bf16[512,512]{1,0:T(8,128)(2,1)S(1)} %collective-permute-done.11.refs_0_, bf16[512,512]{1,0:T(8,128)(2,1)S(1)} %collective-permute-done.12.refs_1_), custom_call_target="tpu_custom_call" | custom-call | flops 262144 | bytes 2097152 | tf_op jit(solution)/shard_map/finish/pallas_call | solution.py:331
  (19 shorter events, 2.6 us)
Async XLA Ops:
  2.4 15.4 %collective-permute-start = (bf16[2064,128]{1,0:T(8,128)(2,1)S(1)}, bf16[2064,128]{1,0:T(8,128)(2,1)S(1)}, u32[]{:S(2)}, u32[]{:S(2)}) collective-permute-start(bf16[2064,128]{1,0:T(8,128)(2,1)S(1)} %get-tuple-element.35), channel_id=1, source_target_pairs={{0,3},{1,2},{2,1},{3,0},{4,7},{5,6},{6,5},{7,4},{8,11},{9,10},{10,... | collective-permute-start | bytes 1585160 | tf_op jit(solution)/shard_map/ppermute | solution.py:352
  6.1 15.8 %collective-permute-start.2 = (bf16[512,512]{1,0:T(8,128)(2,1)S(1)}, bf16[512,512]{1,0:T(8,128)(2,1)S(1)}, u32[]{:S(2)}, u32[]{:S(2)}) collective-permute-start(bf16[512,512]{1,0:T(8,128)(2,1)S(1)} %first_block.1), channel_id=1, source_target_pairs={{0,4},{12,8},{1,5},{13,9},{2,6},{14,10},{3,7},{15,11},{16,20},{28,... | collective-permute-start | bytes 1572872 | tf_op jit(solution)/shard_map/ppermute | solution.py:381
  9.7 8.1 %copy-start = (bf16[2048,512]{1,0:T(8,128)(2,1)S(1)}, bf16[2048,512]{1,0:T(8,128)(2,1)}, u32[]{:S(2)}) copy-start(bf16[2048,512]{1,0:T(8,128)(2,1)} %down_ref.5) | copy-start | bytes 6291460
  15.2 7.5 %collective-permute-start.1 = (bf16[2064,128]{1,0:T(8,128)(2,1)S(1)}, bf16[2064,128]{1,0:T(8,128)(2,1)S(1)}, u32[]{:S(2)}, u32[]{:S(2)}) collective-permute-start(bf16[2064,128]{1,0:T(8,128)(2,1)S(1)} %get-tuple-element.36), channel_id=1, source_target_pairs={{0,1},{1,0},{2,3},{3,2},{4,5},{5,4},{6,7},{7,6},{8,9},{9,8},{10,11... | collective-permute-start | bytes 1585160 | tf_op jit(solution)/shard_map/ppermute | solution.py:352
  15.7 14.0 %collective-permute-start.3 = (bf16[2064,128]{1,0:T(8,128)(2,1)S(1)}, bf16[2064,128]{1,0:T(8,128)(2,1)S(1)}, u32[]{:S(2)}, u32[]{:S(2)}) collective-permute-start(bf16[2064,128]{1,0:T(8,128)(2,1)S(1)} %get-tuple-element.39), channel_id=1, source_target_pairs={{0,2},{1,3},{2,0},{3,1},{4,6},{5,7},{6,4},{7,5},{8,10},{9,11},{10,... | collective-permute-start | bytes 1585160 | tf_op jit(solution)/shard_map/ppermute | solution.py:352
  16.2 16.9 %collective-permute-start.4 = (bf16[512,512]{1,0:T(8,128)(2,1)S(1)}, bf16[512,512]{1,0:T(8,128)(2,1)S(1)}, u32[]{:S(2)}, u32[]{:S(2)}) collective-permute-start(bf16[512,512]{1,0:T(8,128)(2,1)S(1)} %get-tuple-element.42), channel_id=1, source_target_pairs={{0,4},{12,8},{1,5},{13,9},{2,6},{14,10},{3,7},{15,11},{16,20},{28,... | collective-permute-start | bytes 1572872 | tf_op jit(solution)/shard_map/ppermute | solution.py:384
  22.1 15.8 %collective-permute-start.10 = (bf16[512,512]{1,0:T(8,128)(2,1)S(1)}, bf16[512,512]{1,0:T(8,128)(2,1)S(1)}, u32[]{:S(2)}, u32[]{:S(2)}) collective-permute-start(bf16[512,512]{1,0:T(8,128)(2,1)S(1)} %add_convert_fusion.2), channel_id=1, source_target_pairs={{4,8},{8,4},{5,9},{9,5},{6,10},{10,6},{7,11},{11,7},{20,24},{24,20... | collective-permute-start | bytes 1572872 | tf_op jit(solution)/shard_map/ppermute | solution.py:387
  30.3 11.9 %copy-start.1 = (bf16[512,512]{1,0:T(8,128)(2,1)S(1)}, bf16[512,512]{1,0:T(8,128)(2,1)}, u32[]{:S(2)}) copy-start(bf16[512,512]{1,0:T(8,128)(2,1)} %up_ref.1) | copy-start | bytes 1572868
  30.3 4.3 %collective-permute-start.5 = (bf16[256,128]{1,0:T(8,128)(2,1)S(1)}, bf16[256,128]{1,0:T(8,128)(2,1)S(1)}, u32[]{:S(2)}, u32[]{:S(2)}) collective-permute-start(bf16[256,128]{1,0:T(8,128)(2,1)S(1)} %shrink_partial.5), channel_id=1, source_target_pairs={{0,4},{4,0},{8,12},{12,8},{1,5},{5,1},{9,13},{13,9},{2,6},{6,2},{1... | collective-permute-start | bytes 196616 | tf_op jit(solution)/shard_map/ppermute | solution.py:352
  34.6 7.5 %collective-permute-start.6 = (bf16[256,128]{1,0:T(8,128)(2,1)S(1)}, bf16[256,128]{1,0:T(8,128)(2,1)S(1)}, u32[]{:S(2)}, u32[]{:S(2)}) collective-permute-start(bf16[256,128]{1,0:T(8,128)(2,1)S(1)} %add_convert_fusion.3.one_ref), channel_id=1, source_target_pairs={{0,8},{4,12},{8,0},{12,4},{1,9},{5,13},{9,1},{13,5},{2,10},{6,14},... | collective-permute-start | bytes 196616 | tf_op jit(solution)/shard_map/ppermute | solution.py:352
  38.0 14.3 %collective-permute-start.12 = (bf16[512,512]{1,0:T(8,128)(2,1)S(1)}, bf16[512,512]{1,0:T(8,128)(2,1)S(1)}, u32[]{:S(2)}, u32[]{:S(2)}) collective-permute-start(bf16[512,512]{1,0:T(8,128)(2,1)S(1)} %add_convert_fusion), channel_id=1, source_target_pairs={{0,4},{4,0},{8,12},{12,8},{1,5},{5,1},{9,13},{13,9},{2,6},{6,2},{1... | collective-permute-start | bytes 1572872 | tf_op jit(solution)/shard_map/ppermute | solution.py:352
  41.4 10.1 %collective-permute-start.11 = (bf16[512,512]{1,0:T(8,128)(2,1)S(1)}, bf16[512,512]{1,0:T(8,128)(2,1)S(1)}, u32[]{:S(2)}, u32[]{:S(2)}) collective-permute-start(bf16[512,512]{1,0:T(8,128)(2,1)S(1)} %add_convert_fusion.1), channel_id=1, source_target_pairs={{4,8},{8,4},{5,9},{9,5},{6,10},{10,6},{7,11},{11,7},{20,24},{24,20... | collective-permute-start | bytes 1572872 | tf_op jit(solution)/shard_map/ppermute | solution.py:395
  42.7 1.9 %collective-permute-start.7 = (bf16[128,512]{1,0:T(8,128)(2,1)S(1)}, bf16[128,512]{1,0:T(8,128)(2,1)S(1)}, u32[]{:S(2)}, u32[]{:S(2)}) collective-permute-start(bf16[128,512]{1,0:T(8,128)(2,1)S(1)} %get-tuple-element.45), channel_id=1, source_target_pairs={{0,1},{1,0},{2,3},{3,2},{4,5},{5,4},{6,7},{7,6},{8,9},{9,8},{10,11... | collective-permute-start | bytes 393224 | tf_op jit(solution)/shard_map/ppermute | solution.py:352
  42.8 6.4 %collective-permute-start.8 = (bf16[128,512]{1,0:T(8,128)(2,1)S(1)}, bf16[128,512]{1,0:T(8,128)(2,1)S(1)}, u32[]{:S(2)}, u32[]{:S(2)}) collective-permute-start(bf16[128,512]{1,0:T(8,128)(2,1)S(1)} %get-tuple-element.46), channel_id=1, source_target_pairs={{0,2},{1,3},{2,0},{3,1},{4,6},{5,7},{6,4},{7,5},{8,10},{9,11},{10,... | collective-permute-start | bytes 393224 | tf_op jit(solution)/shard_map/ppermute | solution.py:352
  43.3 7.7 %collective-permute-start.9 = (bf16[128,512]{1,0:T(8,128)(2,1)S(1)}, bf16[128,512]{1,0:T(8,128)(2,1)S(1)}, u32[]{:S(2)}, u32[]{:S(2)}) collective-permute-start(bf16[128,512]{1,0:T(8,128)(2,1)S(1)} %get-tuple-element.47), channel_id=1, source_target_pairs={{0,3},{1,2},{2,1},{3,0},{4,7},{5,6},{6,5},{7,4},{8,11},{9,10},{10,... | collective-permute-start | bytes 393224 | tf_op jit(solution)/shard_map/ppermute | solution.py:352

commit v18 on v16

--- a/solution.py
+++ b/solution.py
@@ -232,7 +232,7 @@
         out_specs=[vmem] * 2,
         scratch_shapes=[pltpu.VMEM((2, features, width), bf16), pltpu.SemaphoreType.DMA((2,))],
         compiler_params=params(),
-        cost_estimate=cost(0, 0),
+        cost_estimate=cost(4 * rows * features * width, 2 * features * (rows + 2 * width)),
         name="late_blocks",
     )(z.reshape(1), x, in_hbm(weight))
 
@@ -414,7 +414,7 @@
         early = shrink_partial(down, [after(near[1], inner0)], [early])
         mine = shrink_partial(down, [after(far[1], early)], [early])
         parts, order = [near[0], far[0], near[1], far[1]], (0, 2, 1, 3)
-        third, own = late_blocks(z, after(x, mine), weight, width)
+        third, own = late_blocks(z, after(x, early), weight, width)
         inner1 = both(after(second, mine, third), edge1)
         steps, other = tp_sums(mine, inner1)
         inner2 = both(after(third, steps[-1]), middle0)

time: 53.2 us -> 52.7 us (level); the launches traced: 53 us -> 51.9 us
  waiting for transfers between devices: 20.8 us -> 17.5 us
  starting transfers between devices: 17.1 us -> 19.4 us
    ppermute x9, waiting for transfers between devices: 17.3 us -> 14 us  [swap(): lax.ppermute(value, axis, [(i, i ^ bit) for i in range(lax.axis_size(axis...]
    ppermute x9, starting transfers between devices: 10.9 us -> 13.2 us  [swap(): lax.ppermute(value, axis, [(i, i ^ bit) for i in range(lax.axis_size(axis...]
where the time goes in v18:
time: 52.7 us; the launch traced here: 51.9 us
  starting transfers between devices  19.4 us (37%)
  waiting for transfers between devices  17.5 us (33%)
  Pallas kernels  14.5 us (28%)
    ppermute x9, waiting for transfers between devices, swap(): lax.ppermute(value, axis, [(i, i ^ bit) for i in range(lax.axis_size(axis...  14 us
    ppermute x9, starting transfers between devices, swap(): lax.ppermute(value, axis, [(i, i ^ bit) for i in range(lax.axis_size(axis...  13.2 us
    pallas_call x1, Pallas kernels, late_blocks(): pl.pallas_call(late_body, out_shape=[jax.ShapeDtypeStruct((rows, width),...  4.13 us
    ppermute x1, starting transfers between devices, shards(): edge0 = lax.ppermute(first, 'tp', EDGE)  3.51 us
    ppermute x1, waiting for transfers between devices, shards(): edge0 = lax.ppermute(first, 'tp', EDGE)  3.46 us
    pallas_call x1, Pallas kernels, second_block(): pl.pallas_call(second_body, out_shape=shapes, in_specs=[smem, vmem, vmem,...  3.01 us
    pallas_call x1, Pallas kernels, far_rows(): pl.pallas_call(functools.partial(far_body, slots, capacity, holders), out...  2.44 us
    pallas_call x3, Pallas kernels, shrink_partial(): pl.pallas_call(functools.partial(shrink_body, kept), out_shape=jax.ShapeD...  1.83 us
  transfers between devices with their start and end apart: 13, of which 7 were waited for; matrix products, arithmetic and copies ran while one was open for 1% of the time, Pallas kernels for 21%

profile of v18, /device:TPU:0, one launch (start us, length us, event | category | flops | bytes accessed | tf_op | source)
XLA Modules:
  0.0 51.9 jit_solution(12233242574423673336)
XLA Ops:
  0.0 2.4 %far_rows.1 = (s32[8,512]{1,0:T(8,128)S(1)}, bf16[2064,128]{1,0:T(8,128)(2,1)S(1)}, bf16[2064,128]{1,0:T(8,128)(2,1)S(1)}, bf16[512,2048]{1,0:T(8,128)(2,1)S(1)}, bf16[2048,512]{1,0:T(8,128)(2,1)S(1)}) custom-call(s32[1]{0:T(128)} %bitcast.1.me_ref, s32[1]{0:T(128)} %bitcast.z_ref, s32[1,512]{1,0:T(1,128)} %bitcast.5, s32[32,128]{1,0:T(8,128)} %bitcast.4, ...), custom_call_target="tpu_custom_call" | custom-call | flops 1073741824 | bytes 4194304 | tf_op jit(solution)/shard_map/far_rows/pallas_call | solution.py:125
  2.4 3.0 %collective-permute-start = (bf16[2064,128]{1,0:T(8,128)(2,1)S(1)}, bf16[2064,128]{1,0:T(8,128)(2,1)S(1)}, u32[]{:S(2)}, u32[]{:S(2)}) collective-permute-start(bf16[2064,128]{1,0:T(8,128)(2,1)S(1)} %get-tuple-element.35), channel_id=1, source_target_pairs={{0,2},{1,3},{2,0},{3,1},{4,6},{5,7},{6,4},{7,5},{8,10},{9,11},{10,... | collective-permute-start | bytes 1585160 | tf_op jit(solution)/shard_map/ppermute | solution.py:378
  5.5 1.2 %first_block.1 = bf16[512,512]{1,0:T(8,128)(2,1)S(1)} custom-call(bf16[512,2048]{1,0:T(8,128)(2,1)S(1)} %get-tuple-element.39.x_ref, bf16[2048,512]{1,0:T(8,128)(2,1)S(1)} %get-tuple-element.31.w_ref), custom_call_target="tpu_custom_call" | custom-call | flops 1073741824 | bytes 4194304 | tf_op jit(solution)/shard_map/first_block/pallas_call | solution.py:164
  6.7 3.5 %collective-permute-start.2 = (bf16[512,512]{1,0:T(8,128)(2,1)S(1)}, bf16[512,512]{1,0:T(8,128)(2,1)S(1)}, u32[]{:S(2)}, u32[]{:S(2)}) collective-permute-start(bf16[512,512]{1,0:T(8,128)(2,1)S(1)} %first_block.1), channel_id=1, source_target_pairs={{0,4},{12,8},{1,5},{13,9},{2,6},{14,10},{3,7},{15,11},{16,20},{28,... | collective-permute-start | bytes 1572872 | tf_op jit(solution)/shard_map/ppermute | solution.py:407
  10.2 3.0 %second_block.1 = (bf16[2064,128]{1,0:T(8,128)(2,1)S(1)}, bf16[2064,128]{1,0:T(8,128)(2,1)S(1)}, bf16[512,512]{1,0:T(8,128)(2,1)S(1)}, bf16[512,512]{1,0:T(8,128)(2,1)S(1)}) custom-call(s32[1]{0:T(128)} %bitcast.z_ref, s32[8,512]{1,0:T(8,128)S(1)} %get-tuple-element.32.spots_ref, bf16[512,2048]{1,0:T(8,128)(2,1)S(1)} %get-tuple-element.39.x_ref, ...), custom_call_target="tpu_custom_call" | custom-call | flops 3221225472 | bytes 10485760 | tf_op jit(solution)/shard_map/second_block/pallas_call | solution.py:213
  13.3 0.7 %collective-permute-start.3 = (bf16[2064,128]{1,0:T(8,128)(2,1)S(1)}, bf16[2064,128]{1,0:T(8,128)(2,1)S(1)}, u32[]{:S(2)}, u32[]{:S(2)}) collective-permute-start(bf16[2064,128]{1,0:T(8,128)(2,1)S(1)} %get-tuple-element.41), channel_id=1, source_target_pairs={{0,3},{1,2},{2,1},{3,0},{4,7},{5,6},{6,5},{7,4},{8,11},{9,10},{10,... | collective-permute-start | bytes 1585160 | tf_op jit(solution)/shard_map/ppermute | solution.py:378
  14.0 1.3 %collective-permute-start.4 = (bf16[512,512]{1,0:T(8,128)(2,1)S(1)}, bf16[512,512]{1,0:T(8,128)(2,1)S(1)}, u32[]{:S(2)}, u32[]{:S(2)}) collective-permute-start(bf16[512,512]{1,0:T(8,128)(2,1)S(1)} %get-tuple-element.45), channel_id=1, source_target_pairs={{0,4},{12,8},{1,5},{13,9},{2,6},{14,10},{3,7},{15,11},{16,20},{28,... | collective-permute-start | bytes 1572872 | tf_op jit(solution)/shard_map/ppermute | solution.py:410
  15.3 3.0 %collective-permute-done.refs_1_ = bf16[2064,128]{1,0:T(8,128)(2,1)S(1)} collective-permute-done((bf16[2064,128]{1,0:T(8,128)(2,1)S(1)}, bf16[2064,128]{1,0:T(8,128)(2,1)S(1)}, u32[]{:S(2)}, u32[]{:S(2)}) %collective-permute-start) | collective-permute-done | bytes 528416 | tf_op jit(solution)/shard_map/ppermute | solution.py:378
  18.3 0.8 %shrink_partial.3.refs_0_ = bf16[128,128]{1,0:T(8,128)(2,1)S(1)} custom-call(bf16[2048,512]{1,0:T(8,128)(2,1)S(1)} %copy-done, bf16[2064,128]{1,0:T(8,128)(2,1)S(1)} %get-tuple-element.34.refs_0_, bf16[2064,128]{1,0:T(8,128)(2,1)S(1)} %collective-permute-done.refs_1_), custom_call_target="tpu_custom_call" | custom-call | flops 536870912 | bytes 3145728 | tf_op jit(solution)/shard_map/shrink_partial/pallas_call | solution.py:276
  19.1 3.5 %collective-permute-done.2 = bf16[512,512]{1,0:T(8,128)(2,1)S(1)} collective-permute-done((bf16[512,512]{1,0:T(8,128)(2,1)S(1)}, bf16[512,512]{1,0:T(8,128)(2,1)S(1)}, u32[]{:S(2)}, u32[]{:S(2)}) %collective-permute-start.2) | collective-permute-done | bytes 524320 | tf_op jit(solution)/shard_map/ppermute | solution.py:407
  22.7 0.7 %collective-permute-start.10 = (bf16[512,512]{1,0:T(8,128)(2,1)S(1)}, bf16[512,512]{1,0:T(8,128)(2,1)S(1)}, u32[]{:S(2)}, u32[]{:S(2)}) collective-permute-start(bf16[512,512]{1,0:T(8,128)(2,1)S(1)} %add_convert_fusion.2), channel_id=1, source_target_pairs={{4,8},{8,4},{5,9},{9,5},{6,10},{10,6},{7,11},{11,7},{20,24},{24,20... | collective-permute-start | bytes 1572872 | tf_op jit(solution)/shard_map/ppermute | solution.py:413
  23.4 0.5 shrink_partial.4.refs_0_
  23.9 4.1 %late_blocks.1 = (bf16[512,512]{1,0:T(8,128)(2,1)S(1)}, bf16[512,512]{1,0:T(8,128)(2,1)S(1)}) custom-call(s32[1]{0:T(128)} %bitcast.z_ref, bf16[512,2048]{1,0:T(8,128)(2,1)S(1)} %get-tuple-element.39.x_ref, bf16[2048,2048]{1,0:T(8,128)(2,1)} %w_hbm.5), custom_call_target="tpu_custom_call" | custom-call | flops 2147483648 | bytes 6291456 | tf_op jit(solution)/shard_map/late_blocks/pallas_call | solution.py:228
  28.1 0.5 shrink_partial.5
  28.6 5.4 %collective-permute-start.5 = (bf16[256,128]{1,0:T(8,128)(2,1)S(1)}, bf16[256,128]{1,0:T(8,128)(2,1)S(1)}, u32[]{:S(2)}, u32[]{:S(2)}) collective-permute-start(bf16[256,128]{1,0:T(8,128)(2,1)S(1)} %shrink_partial.5), channel_id=1, source_target_pairs={{0,4},{4,0},{8,12},{12,8},{1,5},{5,1},{9,13},{13,9},{2,6},{6,2},{1... | collective-permute-start | bytes 196616 | tf_op jit(solution)/shard_map/ppermute | solution.py:378
  34.1 2.1 %collective-permute-done.5 = bf16[256,128]{1,0:T(8,128)(2,1)S(1)} collective-permute-done((bf16[256,128]{1,0:T(8,128)(2,1)S(1)}, bf16[256,128]{1,0:T(8,128)(2,1)S(1)}, u32[]{:S(2)}, u32[]{:S(2)}) %collective-permute-start.5) | collective-permute-done | bytes 65568 | tf_op jit(solution)/shard_map/ppermute | solution.py:378
  36.2 2.0 %collective-permute-start.6 = (bf16[256,128]{1,0:T(8,128)(2,1)S(1)}, bf16[256,128]{1,0:T(8,128)(2,1)S(1)}, u32[]{:S(2)}, u32[]{:S(2)}) collective-permute-start(bf16[256,128]{1,0:T(8,128)(2,1)S(1)} %add_convert_fusion.3.one_ref), channel_id=1, source_target_pairs={{0,8},{4,12},{8,0},{12,4},{1,9},{5,13},{9,1},{13,5},{2,10},{6,14},... | collective-permute-start | bytes 196616 | tf_op jit(solution)/shard_map/ppermute | solution.py:378
  38.5 0.7 %collective-permute-start.11 = (bf16[512,512]{1,0:T(8,128)(2,1)S(1)}, bf16[512,512]{1,0:T(8,128)(2,1)S(1)}, u32[]{:S(2)}, u32[]{:S(2)}) collective-permute-start(bf16[512,512]{1,0:T(8,128)(2,1)S(1)} %add_convert_fusion.1), channel_id=1, source_target_pairs={{4,8},{8,4},{5,9},{9,5},{6,10},{10,6},{7,11},{11,7},{20,24},{24,20... | collective-permute-start | bytes 1572872 | tf_op jit(solution)/shard_map/ppermute | solution.py:422
  39.2 2.3 %collective-permute-done.6.two_ref = bf16[256,128]{1,0:T(8,128)(2,1)S(1)} collective-permute-done((bf16[256,128]{1,0:T(8,128)(2,1)S(1)}, bf16[256,128]{1,0:T(8,128)(2,1)S(1)}, u32[]{:S(2)}, u32[]{:S(2)}) %collective-permute-start.6) | collective-permute-done | bytes 65568 | tf_op jit(solution)/shard_map/ppermute | solution.py:378
  42.2 0.6 %collective-permute-start.8 = (bf16[128,512]{1,0:T(8,128)(2,1)S(1)}, bf16[128,512]{1,0:T(8,128)(2,1)S(1)}, u32[]{:S(2)}, u32[]{:S(2)}) collective-permute-start(bf16[128,512]{1,0:T(8,128)(2,1)S(1)} %get-tuple-element.49), channel_id=1, source_target_pairs={{0,2},{1,3},{2,0},{3,1},{4,6},{5,7},{6,4},{7,5},{8,10},{9,11},{10,... | collective-permute-start | bytes 393224 | tf_op jit(solution)/shard_map/ppermute | solution.py:378
  42.8 1.3 %collective-permute-start.9 = (bf16[128,512]{1,0:T(8,128)(2,1)S(1)}, bf16[128,512]{1,0:T(8,128)(2,1)S(1)}, u32[]{:S(2)}, u32[]{:S(2)}) collective-permute-start(bf16[128,512]{1,0:T(8,128)(2,1)S(1)} %get-tuple-element.50), channel_id=1, source_target_pairs={{0,3},{1,2},{2,1},{3,0},{4,7},{5,6},{6,5},{7,4},{8,11},{9,10},{10,... | collective-permute-start | bytes 393224 | tf_op jit(solution)/shard_map/ppermute | solution.py:378
  44.0 4.5 %collective-permute-done.8.refs_2_ = bf16[128,512]{1,0:T(8,128)(2,1)S(1)} collective-permute-done((bf16[128,512]{1,0:T(8,128)(2,1)S(1)}, bf16[128,512]{1,0:T(8,128)(2,1)S(1)}, u32[]{:S(2)}, u32[]{:S(2)}) %collective-permute-start.8) | collective-permute-done | bytes 131104 | tf_op jit(solution)/shard_map/ppermute | solution.py:378
  48.5 1.9 %collective-permute-done.9.refs_3_ = bf16[128,512]{1,0:T(8,128)(2,1)S(1)} collective-permute-done((bf16[128,512]{1,0:T(8,128)(2,1)S(1)}, bf16[128,512]{1,0:T(8,128)(2,1)S(1)}, u32[]{:S(2)}, u32[]{:S(2)}) %collective-permute-start.9) | collective-permute-done | bytes 131104 | tf_op jit(solution)/shard_map/ppermute | solution.py:378
  51.1 0.9 %finish.1 = bf16[512,512]{1,0:T(8,128)(2,1)} custom-call(f32[512,512]{1,0:T(8,128)S(1)} %with_deltas.1.start_ref, bf16[512,512]{1,0:T(8,128)(2,1)S(1)} %collective-permute-done.11.refs_0_, bf16[512,512]{1,0:T(8,128)(2,1)S(1)} %collective-permute-done.12.refs_1_), custom_call_target="tpu_custom_call" | custom-call | flops 262144 | bytes 2097152 | tf_op jit(solution)/shard_map/finish/pallas_call | solution.py:357
  (20 shorter events, 1.9 us)
Async XLA Ops:
  2.4 15.8 %collective-permute-start = (bf16[2064,128]{1,0:T(8,128)(2,1)S(1)}, bf16[2064,128]{1,0:T(8,128)(2,1)S(1)}, u32[]{:S(2)}, u32[]{:S(2)}) collective-permute-start(bf16[2064,128]{1,0:T(8,128)(2,1)S(1)} %get-tuple-element.35), channel_id=1, source_target_pairs={{0,2},{1,3},{2,0},{3,1},{4,6},{5,7},{6,4},{7,5},{8,10},{9,11},{10,... | collective-permute-start | bytes 1585160 | tf_op jit(solution)/shard_map/ppermute | solution.py:378
  6.7 15.8 %collective-permute-start.2 = (bf16[512,512]{1,0:T(8,128)(2,1)S(1)}, bf16[512,512]{1,0:T(8,128)(2,1)S(1)}, u32[]{:S(2)}, u32[]{:S(2)}) collective-permute-start(bf16[512,512]{1,0:T(8,128)(2,1)S(1)} %first_block.1), channel_id=1, source_target_pairs={{0,4},{12,8},{1,5},{13,9},{2,6},{14,10},{3,7},{15,11},{16,20},{28,... | collective-permute-start | bytes 1572872 | tf_op jit(solution)/shard_map/ppermute | solution.py:407
  10.2 8.1 %copy-start = (bf16[2048,512]{1,0:T(8,128)(2,1)S(1)}, bf16[2048,512]{1,0:T(8,128)(2,1)}, u32[]{:S(2)}) copy-start(bf16[2048,512]{1,0:T(8,128)(2,1)} %down_ref.5) | copy-start | bytes 6291460
  13.3 10.1 %collective-permute-start.1 = (bf16[2064,128]{1,0:T(8,128)(2,1)S(1)}, bf16[2064,128]{1,0:T(8,128)(2,1)S(1)}, u32[]{:S(2)}, u32[]{:S(2)}) collective-permute-start(bf16[2064,128]{1,0:T(8,128)(2,1)S(1)} %get-tuple-element.36), channel_id=1, source_target_pairs={{0,1},{1,0},{2,3},{3,2},{4,5},{5,4},{6,7},{7,6},{8,9},{9,8},{10,11... | collective-permute-start | bytes 1585160 | tf_op jit(solution)/shard_map/ppermute | solution.py:378
  13.3 14.7 %collective-permute-start.3 = (bf16[2064,128]{1,0:T(8,128)(2,1)S(1)}, bf16[2064,128]{1,0:T(8,128)(2,1)S(1)}, u32[]{:S(2)}, u32[]{:S(2)}) collective-permute-start(bf16[2064,128]{1,0:T(8,128)(2,1)S(1)} %get-tuple-element.41), channel_id=1, source_target_pairs={{0,3},{1,2},{2,1},{3,0},{4,7},{5,6},{6,5},{7,4},{8,11},{9,10},{10,... | collective-permute-start | bytes 1585160 | tf_op jit(solution)/shard_map/ppermute | solution.py:378
  14.0 20.0 %collective-permute-start.4 = (bf16[512,512]{1,0:T(8,128)(2,1)S(1)}, bf16[512,512]{1,0:T(8,128)(2,1)S(1)}, u32[]{:S(2)}, u32[]{:S(2)}) collective-permute-start(bf16[512,512]{1,0:T(8,128)(2,1)S(1)} %get-tuple-element.45), channel_id=1, source_target_pairs={{0,4},{12,8},{1,5},{13,9},{2,6},{14,10},{3,7},{15,11},{16,20},{28,... | collective-permute-start | bytes 1572872 | tf_op jit(solution)/shard_map/ppermute | solution.py:410
  22.7 15.5 %collective-permute-start.10 = (bf16[512,512]{1,0:T(8,128)(2,1)S(1)}, bf16[512,512]{1,0:T(8,128)(2,1)S(1)}, u32[]{:S(2)}, u32[]{:S(2)}) collective-permute-start(bf16[512,512]{1,0:T(8,128)(2,1)S(1)} %add_convert_fusion.2), channel_id=1, source_target_pairs={{4,8},{8,4},{5,9},{9,5},{6,10},{10,6},{7,11},{11,7},{20,24},{24,20... | collective-permute-start | bytes 1572872 | tf_op jit(solution)/shard_map/ppermute | solution.py:413
  28.6 13.0 %copy-start.1 = (bf16[512,512]{1,0:T(8,128)(2,1)S(1)}, bf16[512,512]{1,0:T(8,128)(2,1)}, u32[]{:S(2)}) copy-start(bf16[512,512]{1,0:T(8,128)(2,1)} %up_ref.1) | copy-start | bytes 1572868
  28.6 7.6 %collective-permute-start.5 = (bf16[256,128]{1,0:T(8,128)(2,1)S(1)}, bf16[256,128]{1,0:T(8,128)(2,1)S(1)}, u32[]{:S(2)}, u32[]{:S(2)}) collective-permute-start(bf16[256,128]{1,0:T(8,128)(2,1)S(1)} %shrink_partial.5), channel_id=1, source_target_pairs={{0,4},{4,0},{8,12},{12,8},{1,5},{5,1},{9,13},{13,9},{2,6},{6,2},{1... | collective-permute-start | bytes 196616 | tf_op jit(solution)/shard_map/ppermute | solution.py:378
  36.2 5.3 %collective-permute-start.6 = (bf16[256,128]{1,0:T(8,128)(2,1)S(1)}, bf16[256,128]{1,0:T(8,128)(2,1)S(1)}, u32[]{:S(2)}, u32[]{:S(2)}) collective-permute-start(bf16[256,128]{1,0:T(8,128)(2,1)S(1)} %add_convert_fusion.3.one_ref), channel_id=1, source_target_pairs={{0,8},{4,12},{8,0},{12,4},{1,9},{5,13},{9,1},{13,5},{2,10},{6,14},... | collective-permute-start | bytes 196616 | tf_op jit(solution)/shard_map/ppermute | solution.py:378
  38.3 12.7 %collective-permute-start.12 = (bf16[512,512]{1,0:T(8,128)(2,1)S(1)}, bf16[512,512]{1,0:T(8,128)(2,1)S(1)}, u32[]{:S(2)}, u32[]{:S(2)}) collective-permute-start(bf16[512,512]{1,0:T(8,128)(2,1)S(1)} %add_convert_fusion), channel_id=1, source_target_pairs={{0,4},{4,0},{8,12},{12,8},{1,5},{5,1},{9,13},{13,9},{2,6},{6,2},{1... | collective-permute-start | bytes 1572872 | tf_op jit(solution)/shard_map/ppermute | solution.py:378
  38.5 12.3 %collective-permute-start.11 = (bf16[512,512]{1,0:T(8,128)(2,1)S(1)}, bf16[512,512]{1,0:T(8,128)(2,1)S(1)}, u32[]{:S(2)}, u32[]{:S(2)}) collective-permute-start(bf16[512,512]{1,0:T(8,128)(2,1)S(1)} %add_convert_fusion.1), channel_id=1, source_target_pairs={{4,8},{8,4},{5,9},{9,5},{6,10},{10,6},{7,11},{11,7},{20,24},{24,20... | collective-permute-start | bytes 1572872 | tf_op jit(solution)/shard_map/ppermute | solution.py:422
  42.1 1.9 %collective-permute-start.7 = (bf16[128,512]{1,0:T(8,128)(2,1)S(1)}, bf16[128,512]{1,0:T(8,128)(2,1)S(1)}, u32[]{:S(2)}, u32[]{:S(2)}) collective-permute-start(bf16[128,512]{1,0:T(8,128)(2,1)S(1)} %get-tuple-element.48), channel_id=1, source_target_pairs={{0,1},{1,0},{2,3},{3,2},{4,5},{5,4},{6,7},{7,6},{8,9},{9,8},{10,11... | collective-permute-start | bytes 393224 | tf_op jit(solution)/shard_map/ppermute | solution.py:378
  42.2 6.4 %collective-permute-start.8 = (bf16[128,512]{1,0:T(8,128)(2,1)S(1)}, bf16[128,512]{1,0:T(8,128)(2,1)S(1)}, u32[]{:S(2)}, u32[]{:S(2)}) collective-permute-start(bf16[128,512]{1,0:T(8,128)(2,1)S(1)} %get-tuple-element.49), channel_id=1, source_target_pairs={{0,2},{1,3},{2,0},{3,1},{4,6},{5,7},{6,4},{7,5},{8,10},{9,11},{10,... | collective-permute-start | bytes 393224 | tf_op jit(solution)/shard_map/ppermute | solution.py:378
  42.8 7.7 %collective-permute-start.9 = (bf16[128,512]{1,0:T(8,128)(2,1)S(1)}, bf16[128,512]{1,0:T(8,128)(2,1)S(1)}, u32[]{:S(2)}, u32[]{:S(2)}) collective-permute-start(bf16[128,512]{1,0:T(8,128)(2,1)S(1)} %get-tuple-element.50), channel_id=1, source_target_pairs={{0,3},{1,2},{2,1},{3,0},{4,7},{5,6},{6,5},{7,4},{8,11},{9,10},{10,... | collective-permute-start | bytes 393224 | tf_op jit(solution)/shard_map/ppermute | solution.py:378

commit v19 on v18

--- a/solution.py
+++ b/solution.py
@@ -409,13 +409,13 @@
         near = [near[0], swap(near[1], "ad", 1)]
         edge1 = lax.ppermute(second, "tp", EDGE)
         early = shrink_partial(down, [near[0], far[0]])
-        inner0 = both(after(first, early), edge0)
+        third, own = late_blocks(z, after(x, early), weight, width)
+        inner0 = both(after(first, early, third), edge0)
         middle0 = lax.ppermute(inner0, "tp", MIDDLE)
         early = shrink_partial(down, [after(near[1], inner0)], [early])
         mine = shrink_partial(down, [after(far[1], early)], [early])
         parts, order = [near[0], far[0], near[1], far[1]], (0, 2, 1, 3)
-        third, own = late_blocks(z, after(x, early), weight, width)
-        inner1 = both(after(second, mine, third), edge1)
+        inner1 = both(after(second, mine), edge1)
         steps, other = tp_sums(mine, inner1)
         inner2 = both(after(third, steps[-1]), middle0)
         last = swap(inner2, "tp", 1)

time: 52.7 us -> 52.5 us (level)
  starting transfers between devices: 19.4 us -> 20.7 us
  waiting for transfers between devices: 17.5 us -> 16.3 us
    ppermute x1, waiting for transfers between devices: 3.46 us -> 0.01 us  [shards(): edge0 = lax.ppermute(first, 'tp', EDGE)]
    ppermute x1, waiting for transfers between devices: 0.01 us -> 2.8 us  [shards(): edge1 = lax.ppermute(second, 'tp', EDGE)]
    ppermute x9, starting transfers between devices: 13.2 us -> 14.5 us  [swap(): lax.ppermute(value, axis, [(i, i ^ bit) for i in range(lax.axis_size(axis...]
  transfers between devices with their start and end apart: 13 -> 13, of which waited for: 7 -> 6; matrix products, arithmetic and copies ran while one was open for 1% -> 1% of each run, Pallas kernels for 21% -> 21%
where the time goes in v19:
time: 52.5 us; the launch traced here: 52.2 us
  starting transfers between devices  20.7 us (39%)
  waiting for transfers between devices  16.3 us (31%)
  Pallas kernels  14.5 us (28%)
    ppermute x9, starting transfers between devices, swap(): lax.ppermute(value, axis, [(i, i ^ bit) for i in range(lax.axis_size(axis...  14.5 us
    ppermute x9, waiting for transfers between devices, swap(): lax.ppermute(value, axis, [(i, i ^ bit) for i in range(lax.axis_size(axis...  13.5 us
    pallas_call x1, Pallas kernels, late_blocks(): pl.pallas_call(late_body, out_shape=[jax.ShapeDtypeStruct((rows, width),...  4.13 us
    ppermute x1, starting transfers between devices, shards(): edge0 = lax.ppermute(first, 'tp', EDGE)  3.51 us
    pallas_call x1, Pallas kernels, second_block(): pl.pallas_call(second_body, out_shape=shapes, in_specs=[smem, vmem, vmem,...  3.01 us
    ppermute x1, waiting for transfers between devices, shards(): edge1 = lax.ppermute(second, 'tp', EDGE)  2.8 us
    pallas_call x1, Pallas kernels, far_rows(): pl.pallas_call(functools.partial(far_body, slots, capacity, holders), out...  2.44 us
    pallas_call x3, Pallas kernels, shrink_partial(): pl.pallas_call(functools.partial(shrink_body, kept), out_shape=jax.ShapeD...  1.84 us
  transfers between devices with their start and end apart: 13, of which 6 were waited for; matrix products, arithmetic and copies ran while one was open for 1% of the time, Pallas kernels for 21%

profile of v19, /device:TPU:0, one launch (start us, length us, event | category | flops | bytes accessed | tf_op | source)
XLA Modules:
  0.0 52.2 jit_solution(3839146264164191653)
XLA Ops:
  0.0 2.4 %far_rows.1 = (s32[8,512]{1,0:T(8,128)S(1)}, bf16[2064,128]{1,0:T(8,128)(2,1)S(1)}, bf16[2064,128]{1,0:T(8,128)(2,1)S(1)}, bf16[512,2048]{1,0:T(8,128)(2,1)S(1)}, bf16[2048,512]{1,0:T(8,128)(2,1)S(1)}) custom-call(s32[1]{0:T(128)} %bitcast.1.me_ref, s32[1]{0:T(128)} %bitcast.z_ref, s32[1,512]{1,0:T(1,128)} %bitcast.5, s32[32,128]{1,0:T(8,128)} %bitcast.4, ...), custom_call_target="tpu_custom_call" | custom-call | flops 1073741824 | bytes 4194304 | tf_op jit(solution)/shard_map/far_rows/pallas_call | solution.py:125
  2.4 3.0 %collective-permute-start = (bf16[2064,128]{1,0:T(8,128)(2,1)S(1)}, bf16[2064,128]{1,0:T(8,128)(2,1)S(1)}, u32[]{:S(2)}, u32[]{:S(2)}) collective-permute-start(bf16[2064,128]{1,0:T(8,128)(2,1)S(1)} %get-tuple-element.35), channel_id=1, source_target_pairs={{0,2},{1,3},{2,0},{3,1},{4,6},{5,7},{6,4},{7,5},{8,10},{9,11},{10,... | collective-permute-start | bytes 1585160 | tf_op jit(solution)/shard_map/ppermute | solution.py:378
  5.5 1.2 %first_block.1 = bf16[512,512]{1,0:T(8,128)(2,1)S(1)} custom-call(bf16[512,2048]{1,0:T(8,128)(2,1)S(1)} %get-tuple-element.36.x_ref, bf16[2048,512]{1,0:T(8,128)(2,1)S(1)} %get-tuple-element.31.w_ref), custom_call_target="tpu_custom_call" | custom-call | flops 1073741824 | bytes 4194304 | tf_op jit(solution)/shard_map/first_block/pallas_call | solution.py:164
  6.7 3.5 %collective-permute-start.2 = (bf16[512,512]{1,0:T(8,128)(2,1)S(1)}, bf16[512,512]{1,0:T(8,128)(2,1)S(1)}, u32[]{:S(2)}, u32[]{:S(2)}) collective-permute-start(bf16[512,512]{1,0:T(8,128)(2,1)S(1)} %first_block.1), channel_id=1, source_target_pairs={{0,4},{12,8},{1,5},{13,9},{2,6},{14,10},{3,7},{15,11},{16,20},{28,... | collective-permute-start | bytes 1572872 | tf_op jit(solution)/shard_map/ppermute | solution.py:407
  10.2 3.0 %second_block.1 = (bf16[2064,128]{1,0:T(8,128)(2,1)S(1)}, bf16[2064,128]{1,0:T(8,128)(2,1)S(1)}, bf16[512,512]{1,0:T(8,128)(2,1)S(1)}, bf16[512,512]{1,0:T(8,128)(2,1)S(1)}) custom-call(s32[1]{0:T(128)} %bitcast.z_ref, s32[8,512]{1,0:T(8,128)S(1)} %get-tuple-element.32.spots_ref, bf16[512,2048]{1,0:T(8,128)(2,1)S(1)} %get-tuple-element.36.x_ref, ...), custom_call_target="tpu_custom_call" | custom-call | flops 3221225472 | bytes 10485760 | tf_op jit(solution)/shard_map/second_block/pallas_call | solution.py:213
  13.3 0.7 %collective-permute-start.3 = (bf16[2064,128]{1,0:T(8,128)(2,1)S(1)}, bf16[2064,128]{1,0:T(8,128)(2,1)S(1)}, u32[]{:S(2)}, u32[]{:S(2)}) collective-permute-start(bf16[2064,128]{1,0:T(8,128)(2,1)S(1)} %get-tuple-element.42), channel_id=1, source_target_pairs={{0,3},{1,2},{2,1},{3,0},{4,7},{5,6},{6,5},{7,4},{8,11},{9,10},{10,... | collective-permute-start | bytes 1585160 | tf_op jit(solution)/shard_map/ppermute | solution.py:378
  14.0 1.3 %collective-permute-start.4 = (bf16[512,512]{1,0:T(8,128)(2,1)S(1)}, bf16[512,512]{1,0:T(8,128)(2,1)S(1)}, u32[]{:S(2)}, u32[]{:S(2)}) collective-permute-start(bf16[512,512]{1,0:T(8,128)(2,1)S(1)} %get-tuple-element.45), channel_id=1, source_target_pairs={{0,4},{12,8},{1,5},{13,9},{2,6},{14,10},{3,7},{15,11},{16,20},{28,... | collective-permute-start | bytes 1572872 | tf_op jit(solution)/shard_map/ppermute | solution.py:410
  15.3 3.0 %collective-permute-done.refs_1_ = bf16[2064,128]{1,0:T(8,128)(2,1)S(1)} collective-permute-done((bf16[2064,128]{1,0:T(8,128)(2,1)S(1)}, bf16[2064,128]{1,0:T(8,128)(2,1)S(1)}, u32[]{:S(2)}, u32[]{:S(2)}) %collective-permute-start) | collective-permute-done | bytes 528416 | tf_op jit(solution)/shard_map/ppermute | solution.py:378
  18.3 0.8 %shrink_partial.3.refs_0_ = bf16[128,128]{1,0:T(8,128)(2,1)S(1)} custom-call(bf16[2048,512]{1,0:T(8,128)(2,1)S(1)} %copy-done, bf16[2064,128]{1,0:T(8,128)(2,1)S(1)} %get-tuple-element.34.refs_0_, bf16[2064,128]{1,0:T(8,128)(2,1)S(1)} %collective-permute-done.refs_1_), custom_call_target="tpu_custom_call" | custom-call | flops 536870912 | bytes 3145728 | tf_op jit(solution)/shard_map/shrink_partial/pallas_call | solution.py:276
  19.1 4.1 %late_blocks.1 = (bf16[512,512]{1,0:T(8,128)(2,1)S(1)}, bf16[512,512]{1,0:T(8,128)(2,1)S(1)}) custom-call(s32[1]{0:T(128)} %bitcast.z_ref, bf16[512,2048]{1,0:T(8,128)(2,1)S(1)} %get-tuple-element.36.x_ref, bf16[2048,2048]{1,0:T(8,128)(2,1)} %w_hbm.5), custom_call_target="tpu_custom_call" | custom-call | flops 2147483648 | bytes 6291456 | tf_op jit(solution)/shard_map/late_blocks/pallas_call | solution.py:228
  23.4 0.7 %collective-permute-start.10 = (bf16[512,512]{1,0:T(8,128)(2,1)S(1)}, bf16[512,512]{1,0:T(8,128)(2,1)S(1)}, u32[]{:S(2)}, u32[]{:S(2)}) collective-permute-start(bf16[512,512]{1,0:T(8,128)(2,1)S(1)} %add_convert_fusion.2), channel_id=1, source_target_pairs={{4,8},{8,4},{5,9},{9,5},{6,10},{10,6},{7,11},{11,7},{20,24},{24,20... | collective-permute-start | bytes 1572872 | tf_op jit(solution)/shard_map/ppermute | solution.py:414
  24.1 0.5 %shrink_partial.4.refs_0_ = bf16[192,128]{1,0:T(8,128)(2,1)S(1)} custom-call(bf16[2048,512]{1,0:T(8,128)(2,1)S(1)} %copy-done, bf16[128,128]{1,0:T(8,128)(2,1)S(1)} %shrink_partial.3.refs_0_, bf16[2064,128]{1,0:T(8,128)(2,1)S(1)} %collective-permute-done.1.refs_1_.refs_2_), custom_call_target="tpu_custom_call" | custom-call | flops 268435456 | bytes 2621440 | tf_op jit(solution)/shard_map/shrink_partial/pallas_call | solution.py:276
  24.6 3.4 %collective-permute-done.3.refs_1_.refs_3_ = bf16[2064,128]{1,0:T(8,128)(2,1)S(1)} collective-permute-done((bf16[2064,128]{1,0:T(8,128)(2,1)S(1)}, bf16[2064,128]{1,0:T(8,128)(2,1)S(1)}, u32[]{:S(2)}, u32[]{:S(2)}) %collective-permute-start.3) | collective-permute-done | bytes 528416 | tf_op jit(solution)/shard_map/ppermute | solution.py:378
  28.0 0.5 shrink_partial.5
  28.6 1.6 %collective-permute-start.5 = (bf16[256,128]{1,0:T(8,128)(2,1)S(1)}, bf16[256,128]{1,0:T(8,128)(2,1)S(1)}, u32[]{:S(2)}, u32[]{:S(2)}) collective-permute-start(bf16[256,128]{1,0:T(8,128)(2,1)S(1)} %shrink_partial.5), channel_id=1, source_target_pairs={{0,4},{4,0},{8,12},{12,8},{1,5},{5,1},{9,13},{13,9},{2,6},{6,2},{1... | collective-permute-start | bytes 196616 | tf_op jit(solution)/shard_map/ppermute | solution.py:378
  30.2 2.8 %collective-permute-done.4 = bf16[512,512]{1,0:T(8,128)(2,1)S(1)} collective-permute-done((bf16[512,512]{1,0:T(8,128)(2,1)S(1)}, bf16[512,512]{1,0:T(8,128)(2,1)S(1)}, u32[]{:S(2)}, u32[]{:S(2)}) %collective-permute-start.4) | collective-permute-done | bytes 524320 | tf_op jit(solution)/shard_map/ppermute | solution.py:410
  33.2 0.6 %collective-permute-done.5 = bf16[256,128]{1,0:T(8,128)(2,1)S(1)} collective-permute-done((bf16[256,128]{1,0:T(8,128)(2,1)S(1)}, bf16[256,128]{1,0:T(8,128)(2,1)S(1)}, u32[]{:S(2)}, u32[]{:S(2)}) %collective-permute-start.5) | collective-permute-done | bytes 65568 | tf_op jit(solution)/shard_map/ppermute | solution.py:378
  33.7 3.6 %collective-permute-start.6 = (bf16[256,128]{1,0:T(8,128)(2,1)S(1)}, bf16[256,128]{1,0:T(8,128)(2,1)S(1)}, u32[]{:S(2)}, u32[]{:S(2)}) collective-permute-start(bf16[256,128]{1,0:T(8,128)(2,1)S(1)} %add_convert_fusion.3.one_ref), channel_id=1, source_target_pairs={{0,8},{4,12},{8,0},{12,4},{1,9},{5,13},{9,1},{13,5},{2,10},{6,14},... | collective-permute-start | bytes 196616 | tf_op jit(solution)/shard_map/ppermute | solution.py:378
  37.4 3.2 %collective-permute-start.12 = (bf16[512,512]{1,0:T(8,128)(2,1)S(1)}, bf16[512,512]{1,0:T(8,128)(2,1)S(1)}, u32[]{:S(2)}, u32[]{:S(2)}) collective-permute-start(bf16[512,512]{1,0:T(8,128)(2,1)S(1)} %add_convert_fusion), channel_id=1, source_target_pairs={{0,4},{4,0},{8,12},{12,8},{1,5},{5,1},{9,13},{13,9},{2,6},{6,2},{1... | collective-permute-start | bytes 1572872 | tf_op jit(solution)/shard_map/ppermute | solution.py:378
  40.7 0.7 %collective-permute-start.11 = (bf16[512,512]{1,0:T(8,128)(2,1)S(1)}, bf16[512,512]{1,0:T(8,128)(2,1)S(1)}, u32[]{:S(2)}, u32[]{:S(2)}) collective-permute-start(bf16[512,512]{1,0:T(8,128)(2,1)S(1)} %add_convert_fusion.1), channel_id=1, source_target_pairs={{4,8},{8,4},{5,9},{9,5},{6,10},{10,6},{7,11},{11,7},{20,24},{24,20... | collective-permute-start | bytes 1572872 | tf_op jit(solution)/shard_map/ppermute | solution.py:422
  42.0 2.2 %collective-permute-start.8 = (bf16[128,512]{1,0:T(8,128)(2,1)S(1)}, bf16[128,512]{1,0:T(8,128)(2,1)S(1)}, u32[]{:S(2)}, u32[]{:S(2)}) collective-permute-start(bf16[128,512]{1,0:T(8,128)(2,1)S(1)} %get-tuple-element.49), channel_id=1, source_target_pairs={{0,2},{1,3},{2,0},{3,1},{4,6},{5,7},{6,4},{7,5},{8,10},{9,11},{10,... | collective-permute-start | bytes 393224 | tf_op jit(solution)/shard_map/ppermute | solution.py:378
  44.3 4.3 %collective-permute-done.8.refs_2_ = bf16[128,512]{1,0:T(8,128)(2,1)S(1)} collective-permute-done((bf16[128,512]{1,0:T(8,128)(2,1)S(1)}, bf16[128,512]{1,0:T(8,128)(2,1)S(1)}, u32[]{:S(2)}, u32[]{:S(2)}) %collective-permute-start.8) | collective-permute-done | bytes 131104 | tf_op jit(solution)/shard_map/ppermute | solution.py:378
  48.6 2.3 %collective-permute-done.9.refs_3_ = bf16[128,512]{1,0:T(8,128)(2,1)S(1)} collective-permute-done((bf16[128,512]{1,0:T(8,128)(2,1)S(1)}, bf16[128,512]{1,0:T(8,128)(2,1)S(1)}, u32[]{:S(2)}, u32[]{:S(2)}) %collective-permute-start.9) | collective-permute-done | bytes 131104 | tf_op jit(solution)/shard_map/ppermute | solution.py:378
  51.3 0.9 %finish.1 = bf16[512,512]{1,0:T(8,128)(2,1)} custom-call(f32[512,512]{1,0:T(8,128)S(1)} %with_deltas.1.start_ref, bf16[512,512]{1,0:T(8,128)(2,1)S(1)} %collective-permute-done.11.refs_0_, bf16[512,512]{1,0:T(8,128)(2,1)S(1)} %collective-permute-done.12.refs_1_), custom_call_target="tpu_custom_call" | custom-call | flops 262144 | bytes 2097152 | tf_op jit(solution)/shard_map/finish/pallas_call | solution.py:357
  (20 shorter events, 1.6 us)
Async XLA Ops:
  2.4 15.8 %collective-permute-start = (bf16[2064,128]{1,0:T(8,128)(2,1)S(1)}, bf16[2064,128]{1,0:T(8,128)(2,1)S(1)}, u32[]{:S(2)}, u32[]{:S(2)}) collective-permute-start(bf16[2064,128]{1,0:T(8,128)(2,1)S(1)} %get-tuple-element.35), channel_id=1, source_target_pairs={{0,2},{1,3},{2,0},{3,1},{4,6},{5,7},{6,4},{7,5},{8,10},{9,11},{10,... | collective-permute-start | bytes 1585160 | tf_op jit(solution)/shard_map/ppermute | solution.py:378
  6.7 16.5 %collective-permute-start.2 = (bf16[512,512]{1,0:T(8,128)(2,1)S(1)}, bf16[512,512]{1,0:T(8,128)(2,1)S(1)}, u32[]{:S(2)}, u32[]{:S(2)}) collective-permute-start(bf16[512,512]{1,0:T(8,128)(2,1)S(1)} %first_block.1), channel_id=1, source_target_pairs={{0,4},{12,8},{1,5},{13,9},{2,6},{14,10},{3,7},{15,11},{16,20},{28,... | collective-permute-start | bytes 1572872 | tf_op jit(solution)/shard_map/ppermute | solution.py:407
  10.2 8.1 %copy-start = (bf16[2048,512]{1,0:T(8,128)(2,1)S(1)}, bf16[2048,512]{1,0:T(8,128)(2,1)}, u32[]{:S(2)}) copy-start(bf16[2048,512]{1,0:T(8,128)(2,1)} %down_ref.5) | copy-start | bytes 6291460
  13.3 10.8 %collective-permute-start.1 = (bf16[2064,128]{1,0:T(8,128)(2,1)S(1)}, bf16[2064,128]{1,0:T(8,128)(2,1)S(1)}, u32[]{:S(2)}, u32[]{:S(2)}) collective-permute-start(bf16[2064,128]{1,0:T(8,128)(2,1)S(1)} %get-tuple-element.38), channel_id=1, source_target_pairs={{0,1},{1,0},{2,3},{3,2},{4,5},{5,4},{6,7},{7,6},{8,9},{9,8},{10,11... | collective-permute-start | bytes 1585160 | tf_op jit(solution)/shard_map/ppermute | solution.py:378
  13.3 14.7 %collective-permute-start.3 = (bf16[2064,128]{1,0:T(8,128)(2,1)S(1)}, bf16[2064,128]{1,0:T(8,128)(2,1)S(1)}, u32[]{:S(2)}, u32[]{:S(2)}) collective-permute-start(bf16[2064,128]{1,0:T(8,128)(2,1)S(1)} %get-tuple-element.42), channel_id=1, source_target_pairs={{0,3},{1,2},{2,1},{3,0},{4,7},{5,6},{6,5},{7,4},{8,11},{9,10},{10,... | collective-permute-start | bytes 1585160 | tf_op jit(solution)/shard_map/ppermute | solution.py:378
  14.0 19.0 %collective-permute-start.4 = (bf16[512,512]{1,0:T(8,128)(2,1)S(1)}, bf16[512,512]{1,0:T(8,128)(2,1)S(1)}, u32[]{:S(2)}, u32[]{:S(2)}) collective-permute-start(bf16[512,512]{1,0:T(8,128)(2,1)S(1)} %get-tuple-element.45), channel_id=1, source_target_pairs={{0,4},{12,8},{1,5},{13,9},{2,6},{14,10},{3,7},{15,11},{16,20},{28,... | collective-permute-start | bytes 1572872 | tf_op jit(solution)/shard_map/ppermute | solution.py:410
  23.4 13.9 %collective-permute-start.10 = (bf16[512,512]{1,0:T(8,128)(2,1)S(1)}, bf16[512,512]{1,0:T(8,128)(2,1)S(1)}, u32[]{:S(2)}, u32[]{:S(2)}) collective-permute-start(bf16[512,512]{1,0:T(8,128)(2,1)S(1)} %add_convert_fusion.2), channel_id=1, source_target_pairs={{4,8},{8,4},{5,9},{9,5},{6,10},{10,6},{7,11},{11,7},{20,24},{24,20... | collective-permute-start | bytes 1572872 | tf_op jit(solution)/shard_map/ppermute | solution.py:414
  28.6 12.8 %copy-start.1 = (bf16[512,512]{1,0:T(8,128)(2,1)S(1)}, bf16[512,512]{1,0:T(8,128)(2,1)}, u32[]{:S(2)}) copy-start(bf16[512,512]{1,0:T(8,128)(2,1)} %up_ref.1) | copy-start | bytes 1572868
  28.6 5.1 %collective-permute-start.5 = (bf16[256,128]{1,0:T(8,128)(2,1)S(1)}, bf16[256,128]{1,0:T(8,128)(2,1)S(1)}, u32[]{:S(2)}, u32[]{:S(2)}) collective-permute-start(bf16[256,128]{1,0:T(8,128)(2,1)S(1)} %shrink_partial.5), channel_id=1, source_target_pairs={{0,4},{4,0},{8,12},{12,8},{1,5},{5,1},{9,13},{13,9},{2,6},{6,2},{1... | collective-permute-start | bytes 196616 | tf_op jit(solution)/shard_map/ppermute | solution.py:378
  33.7 7.6 %collective-permute-start.6 = (bf16[256,128]{1,0:T(8,128)(2,1)S(1)}, bf16[256,128]{1,0:T(8,128)(2,1)S(1)}, u32[]{:S(2)}, u32[]{:S(2)}) collective-permute-start(bf16[256,128]{1,0:T(8,128)(2,1)S(1)} %add_convert_fusion.3.one_ref), channel_id=1, source_target_pairs={{0,8},{4,12},{8,0},{12,4},{1,9},{5,13},{9,1},{13,5},{2,10},{6,14},... | collective-permute-start | bytes 196616 | tf_op jit(solution)/shard_map/ppermute | solution.py:378
  37.4 13.9 %collective-permute-start.12 = (bf16[512,512]{1,0:T(8,128)(2,1)S(1)}, bf16[512,512]{1,0:T(8,128)(2,1)S(1)}, u32[]{:S(2)}, u32[]{:S(2)}) collective-permute-start(bf16[512,512]{1,0:T(8,128)(2,1)S(1)} %add_convert_fusion), channel_id=1, source_target_pairs={{0,4},{4,0},{8,12},{12,8},{1,5},{5,1},{9,13},{13,9},{2,6},{6,2},{1... | collective-permute-start | bytes 1572872 | tf_op jit(solution)/shard_map/ppermute | solution.py:378
  40.7 10.6 %collective-permute-start.11 = (bf16[512,512]{1,0:T(8,128)(2,1)S(1)}, bf16[512,512]{1,0:T(8,128)(2,1)S(1)}, u32[]{:S(2)}, u32[]{:S(2)}) collective-permute-start(bf16[512,512]{1,0:T(8,128)(2,1)S(1)} %add_convert_fusion.1), channel_id=1, source_target_pairs={{4,8},{8,4},{5,9},{9,5},{6,10},{10,6},{7,11},{11,7},{20,24},{24,20... | collective-permute-start | bytes 1572872 | tf_op jit(solution)/shard_map/ppermute | solution.py:422
  41.9 2.4 %collective-permute-start.7 = (bf16[128,512]{1,0:T(8,128)(2,1)S(1)}, bf16[128,512]{1,0:T(8,128)(2,1)S(1)}, u32[]{:S(2)}, u32[]{:S(2)}) collective-permute-start(bf16[128,512]{1,0:T(8,128)(2,1)S(1)} %get-tuple-element.48), channel_id=1, source_target_pairs={{0,1},{1,0},{2,3},{3,2},{4,5},{5,4},{6,7},{7,6},{8,9},{9,8},{10,11... | collective-permute-start | bytes 393224 | tf_op jit(solution)/shard_map/ppermute | solution.py:378
  42.0 6.6 %collective-permute-start.8 = (bf16[128,512]{1,0:T(8,128)(2,1)S(1)}, bf16[128,512]{1,0:T(8,128)(2,1)S(1)}, u32[]{:S(2)}, u32[]{:S(2)}) collective-permute-start(bf16[128,512]{1,0:T(8,128)(2,1)S(1)} %get-tuple-element.49), channel_id=1, source_target_pairs={{0,2},{1,3},{2,0},{3,1},{4,6},{5,7},{6,4},{7,5},{8,10},{9,11},{10,... | collective-permute-start | bytes 393224 | tf_op jit(solution)/shard_map/ppermute | solution.py:378
  44.2 6.6 %collective-permute-start.9 = (bf16[128,512]{1,0:T(8,128)(2,1)S(1)}, bf16[128,512]{1,0:T(8,128)(2,1)S(1)}, u32[]{:S(2)}, u32[]{:S(2)}) collective-permute-start(bf16[128,512]{1,0:T(8,128)(2,1)S(1)} %get-tuple-element.50), channel_id=1, source_target_pairs={{0,3},{1,2},{2,1},{3,0},{4,7},{5,6},{6,5},{7,4},{8,11},{9,10},{10,... | collective-permute-start | bytes 393224 | tf_op jit(solution)/shard_map/ppermute | solution.py:378

commit v20 on v13

--- a/solution.py
+++ b/solution.py
@@ -391,8 +391,8 @@
         inner1 = both(after(second, mine), edge1)
         steps, other = tp_sums(mine, inner1)
         inner2 = both(after(third, steps[-1]), middle0)
+        middle1 = lax.ppermute(after(inner1, steps[-1]), "tp", MIDDLE)
         last = swap(inner2, "tp", 1)
-        middle1 = lax.ppermute(after(inner1, inner2), "tp", MIDDLE)
         sums = [middle1, last]
     else:
         near = near_rows(spots, x, capacity)

time: 52.2 us -> 52.7 us (level)
  starting transfers between devices: 15.3 us -> 16.8 us
  waiting for transfers between devices: 23.1 us -> 22.2 us
    ppermute x9, starting transfers between devices: 9.11 us -> 10.6 us  [swap(): lax.ppermute(value, axis, [(i, i ^ bit) for i in range(lax.axis_size(axis...]
    ppermute x9, waiting for transfers between devices: 16.5 us -> 15.6 us  [swap(): lax.ppermute(value, axis, [(i, i ^ bit) for i in range(lax.axis_size(axis...]
  transfers between devices with their start and end apart: 13 -> 13, of which waited for: 8 -> 7; matrix products, arithmetic and copies ran while one was open for 1% -> 1% of each run, Pallas kernels for 18% -> 18%
where the time goes in v20:
time: 52.7 us; the launch traced here: 52.5 us
  waiting for transfers between devices  22.2 us (42%)
  starting transfers between devices  16.8 us (32%)
  Pallas kernels  12.9 us (24%)
    ppermute x9, waiting for transfers between devices, swap(): lax.ppermute(value, axis, [(i, i ^ bit) for i in range(lax.axis_size(axis...  15.6 us
    ppermute x9, starting transfers between devices, swap(): lax.ppermute(value, axis, [(i, i ^ bit) for i in range(lax.axis_size(axis...  10.6 us
    pallas_call x1, Pallas kernels, rest(): pl.pallas_call(rest_body, out_shape=shapes, in_specs=[smem, vmem, vmem, h...  5.55 us
    ppermute x1, waiting for transfers between devices, shards(): edge0 = lax.ppermute(first, 'tp', EDGE)  3.89 us
    ppermute x1, starting transfers between devices, shards(): edge0 = lax.ppermute(first, 'tp', EDGE)  3.51 us
    ppermute x1, waiting for transfers between devices, shards(): edge1 = lax.ppermute(second, 'tp', EDGE)  2.71 us
    pallas_call x1, Pallas kernels, far_rows(): pl.pallas_call(functools.partial(far_body, slots, capacity, holders), out...  2.44 us
    pallas_call x3, Pallas kernels, shrink_partial(): pl.pallas_call(functools.partial(shrink_body, kept), out_shape=jax.ShapeD...  1.84 us
  transfers between devices with their start and end apart: 13, of which 7 were waited for; matrix products, arithmetic and copies ran while one was open for 1% of the time, Pallas kernels for 18%

profile of v20, /device:TPU:0, one launch (start us, length us, event | category | flops | bytes accessed | tf_op | source)
XLA Modules:
  0.0 52.5 jit_solution(14753785988883334028)
XLA Ops:
  0.0 2.4 %far_rows.1 = (s32[8,512]{1,0:T(8,128)S(1)}, bf16[2064,128]{1,0:T(8,128)(2,1)S(1)}, bf16[2064,128]{1,0:T(8,128)(2,1)S(1)}, bf16[512,2048]{1,0:T(8,128)(2,1)S(1)}, bf16[2048,512]{1,0:T(8,128)(2,1)S(1)}) custom-call(s32[1]{0:T(128)} %bitcast.1.me_ref, s32[1]{0:T(128)} %bitcast.z_ref, s32[1,512]{1,0:T(1,128)} %bitcast.5, s32[32,128]{1,0:T(8,128)} %bitcast.4, ...), custom_call_target="tpu_custom_call" | custom-call | flops 1073741824 | bytes 4194304 | tf_op jit(solution)/shard_map/far_rows/pallas_call | solution.py:125
  2.4 3.0 %collective-permute-start = (bf16[2064,128]{1,0:T(8,128)(2,1)S(1)}, bf16[2064,128]{1,0:T(8,128)(2,1)S(1)}, u32[]{:S(2)}, u32[]{:S(2)}) collective-permute-start(bf16[2064,128]{1,0:T(8,128)(2,1)S(1)} %get-tuple-element.35), channel_id=1, source_target_pairs={{0,2},{1,3},{2,0},{3,1},{4,6},{5,7},{6,4},{7,5},{8,10},{9,11},{10,... | collective-permute-start | bytes 1585160 | tf_op jit(solution)/shard_map/ppermute | solution.py:352
  5.5 1.2 %first_block.1 = bf16[512,512]{1,0:T(8,128)(2,1)S(1)} custom-call(bf16[512,2048]{1,0:T(8,128)(2,1)S(1)} %get-tuple-element.29.x_ref, bf16[2048,512]{1,0:T(8,128)(2,1)S(1)} %get-tuple-element.30.w_ref), custom_call_target="tpu_custom_call" | custom-call | flops 1073741824 | bytes 4194304 | tf_op jit(solution)/shard_map/first_block/pallas_call | solution.py:164
  6.7 3.5 %collective-permute-start.2 = (bf16[512,512]{1,0:T(8,128)(2,1)S(1)}, bf16[512,512]{1,0:T(8,128)(2,1)S(1)}, u32[]{:S(2)}, u32[]{:S(2)}) collective-permute-start(bf16[512,512]{1,0:T(8,128)(2,1)S(1)} %first_block.1), channel_id=1, source_target_pairs={{0,4},{12,8},{1,5},{13,9},{2,6},{14,10},{3,7},{15,11},{16,20},{28,... | collective-permute-start | bytes 1572872 | tf_op jit(solution)/shard_map/ppermute | solution.py:381
  10.2 5.5 %rest.1 = (bf16[2064,128]{1,0:T(8,128)(2,1)S(1)}, bf16[2064,128]{1,0:T(8,128)(2,1)S(1)}, bf16[512,512]{1,0:T(8,128)(2,1)S(1)}, bf16[512,512]{1,0:T(8,128)(2,1)S(...) custom-call(s32[1]{0:T(128)} %bitcast.z_ref, s32[8,512]{1,0:T(8,128)S(1)} %get-tuple-element.31.spots_ref, ...), custom_call_target="tpu_custom_call" | custom-call | flops 3221225472 | bytes 10485760 | tf_op jit(solution)/shard_map/rest/pallas_call | solution.py:202
  15.9 0.6 %collective-permute-start.3 = (bf16[2064,128]{1,0:T(8,128)(2,1)S(1)}, bf16[2064,128]{1,0:T(8,128)(2,1)S(1)}, u32[]{:S(2)}, u32[]{:S(2)}) collective-permute-start(bf16[2064,128]{1,0:T(8,128)(2,1)S(1)} %get-tuple-element.39), channel_id=1, source_target_pairs={{0,3},{1,2},{2,1},{3,0},{4,7},{5,6},{6,5},{7,4},{8,11},{9,10},{10,... | collective-permute-start | bytes 1585160 | tf_op jit(solution)/shard_map/ppermute | solution.py:352
  16.5 1.3 %collective-permute-start.4 = (bf16[512,512]{1,0:T(8,128)(2,1)S(1)}, bf16[512,512]{1,0:T(8,128)(2,1)S(1)}, u32[]{:S(2)}, u32[]{:S(2)}) collective-permute-start(bf16[512,512]{1,0:T(8,128)(2,1)S(1)} %get-tuple-element.42), channel_id=1, source_target_pairs={{0,4},{12,8},{1,5},{13,9},{2,6},{14,10},{3,7},{15,11},{16,20},{28,... | collective-permute-start | bytes 1572872 | tf_op jit(solution)/shard_map/ppermute | solution.py:384
  17.9 0.8 %shrink_partial.3.refs_0_ = bf16[128,128]{1,0:T(8,128)(2,1)S(1)} custom-call(bf16[2048,512]{1,0:T(8,128)(2,1)S(1)} %copy-done, bf16[2064,128]{1,0:T(8,128)(2,1)S(1)} %get-tuple-element.34.refs_0_, bf16[2064,128]{1,0:T(8,128)(2,1)S(1)} %collective-permute-done.refs_1_), custom_call_target="tpu_custom_call" | custom-call | flops 536870912 | bytes 3145728 | tf_op jit(solution)/shard_map/shrink_partial/pallas_call | solution.py:250
  18.7 3.9 %collective-permute-done.2 = bf16[512,512]{1,0:T(8,128)(2,1)S(1)} collective-permute-done((bf16[512,512]{1,0:T(8,128)(2,1)S(1)}, bf16[512,512]{1,0:T(8,128)(2,1)S(1)}, u32[]{:S(2)}, u32[]{:S(2)}) %collective-permute-start.2) | collective-permute-done | bytes 524320 | tf_op jit(solution)/shard_map/ppermute | solution.py:381
  22.7 0.7 %collective-permute-start.11 = (bf16[512,512]{1,0:T(8,128)(2,1)S(1)}, bf16[512,512]{1,0:T(8,128)(2,1)S(1)}, u32[]{:S(2)}, u32[]{:S(2)}) collective-permute-start(bf16[512,512]{1,0:T(8,128)(2,1)S(1)} %add_convert_fusion.2), channel_id=1, source_target_pairs={{4,8},{8,4},{5,9},{9,5},{6,10},{10,6},{7,11},{11,7},{20,24},{24,20... | collective-permute-start | bytes 1572872 | tf_op jit(solution)/shard_map/ppermute | solution.py:387
  23.4 0.5 %shrink_partial.4.refs_0_ = bf16[192,128]{1,0:T(8,128)(2,1)S(1)} custom-call(bf16[2048,512]{1,0:T(8,128)(2,1)S(1)} %copy-done, bf16[128,128]{1,0:T(8,128)(2,1)S(1)} %shrink_partial.3.refs_0_, bf16[2064,128]{1,0:T(8,128)(2,1)S(1)} %collective-permute-done.1.refs_1_.refs_2_), custom_call_target="tpu_custom_call" | custom-call | flops 268435456 | bytes 2621440 | tf_op jit(solution)/shard_map/shrink_partial/pallas_call | solution.py:250
  23.9 5.7 %collective-permute-done.3.refs_1_.refs_3_ = bf16[2064,128]{1,0:T(8,128)(2,1)S(1)} collective-permute-done((bf16[2064,128]{1,0:T(8,128)(2,1)S(1)}, bf16[2064,128]{1,0:T(8,128)(2,1)S(1)}, u32[]{:S(2)}, u32[]{:S(2)}) %collective-permute-start.3) | collective-permute-done | bytes 528416 | tf_op jit(solution)/shard_map/ppermute | solution.py:352
  29.7 0.5 shrink_partial.5
  30.3 2.7 %collective-permute-done.4 = bf16[512,512]{1,0:T(8,128)(2,1)S(1)} collective-permute-done((bf16[512,512]{1,0:T(8,128)(2,1)S(1)}, bf16[512,512]{1,0:T(8,128)(2,1)S(1)}, u32[]{:S(2)}, u32[]{:S(2)}) %collective-permute-start.4) | collective-permute-done | bytes 524320 | tf_op jit(solution)/shard_map/ppermute | solution.py:384
  33.2 1.6 %collective-permute-done.5 = bf16[256,128]{1,0:T(8,128)(2,1)S(1)} collective-permute-done((bf16[256,128]{1,0:T(8,128)(2,1)S(1)}, bf16[256,128]{1,0:T(8,128)(2,1)S(1)}, u32[]{:S(2)}, u32[]{:S(2)}) %collective-permute-start.5) | collective-permute-done | bytes 65568 | tf_op jit(solution)/shard_map/ppermute | solution.py:352
  34.7 2.6 %collective-permute-start.6 = (bf16[256,128]{1,0:T(8,128)(2,1)S(1)}, bf16[256,128]{1,0:T(8,128)(2,1)S(1)}, u32[]{:S(2)}, u32[]{:S(2)}) collective-permute-start(bf16[256,128]{1,0:T(8,128)(2,1)S(1)} %add_convert_fusion.3.one_ref), channel_id=1, source_target_pairs={{0,8},{4,12},{8,0},{12,4},{1,9},{5,13},{9,1},{13,5},{2,10},{6,14},... | collective-permute-start | bytes 196616 | tf_op jit(solution)/shard_map/ppermute | solution.py:352
  37.3 0.7 %collective-permute-start.10 = (bf16[512,512]{1,0:T(8,128)(2,1)S(1)}, bf16[512,512]{1,0:T(8,128)(2,1)S(1)}, u32[]{:S(2)}, u32[]{:S(2)}) collective-permute-start(bf16[512,512]{1,0:T(8,128)(2,1)S(1)} %add_convert_fusion.1), channel_id=1, source_target_pairs={{4,8},{8,4},{5,9},{9,5},{6,10},{10,6},{7,11},{11,7},{20,24},{24,20... | collective-permute-start | bytes 1572872 | tf_op jit(solution)/shard_map/ppermute | solution.py:394
  38.1 2.3 %collective-permute-start.12 = (bf16[512,512]{1,0:T(8,128)(2,1)S(1)}, bf16[512,512]{1,0:T(8,128)(2,1)S(1)}, u32[]{:S(2)}, u32[]{:S(2)}) collective-permute-start(bf16[512,512]{1,0:T(8,128)(2,1)S(1)} %add_convert_fusion), channel_id=1, source_target_pairs={{0,4},{4,0},{8,12},{12,8},{1,5},{5,1},{9,13},{13,9},{2,6},{6,2},{1... | collective-permute-start | bytes 1572872 | tf_op jit(solution)/shard_map/ppermute | solution.py:352
  40.4 0.5 expand.1
  41.0 1.5 %collective-permute-start.8 = (bf16[128,512]{1,0:T(8,128)(2,1)S(1)}, bf16[128,512]{1,0:T(8,128)(2,1)S(1)}, u32[]{:S(2)}, u32[]{:S(2)}) collective-permute-start(bf16[128,512]{1,0:T(8,128)(2,1)S(1)} %get-tuple-element.46), channel_id=1, source_target_pairs={{0,2},{1,3},{2,0},{3,1},{4,6},{5,7},{6,4},{7,5},{8,10},{9,11},{10,... | collective-permute-start | bytes 393224 | tf_op jit(solution)/shard_map/ppermute | solution.py:352
  42.9 4.5 %collective-permute-done.8.refs_2_ = bf16[128,512]{1,0:T(8,128)(2,1)S(1)} collective-permute-done((bf16[128,512]{1,0:T(8,128)(2,1)S(1)}, bf16[128,512]{1,0:T(8,128)(2,1)S(1)}, u32[]{:S(2)}, u32[]{:S(2)}) %collective-permute-start.8) | collective-permute-done | bytes 131104 | tf_op jit(solution)/shard_map/ppermute | solution.py:352
  47.4 1.9 %collective-permute-done.9.refs_3_ = bf16[128,512]{1,0:T(8,128)(2,1)S(1)} collective-permute-done((bf16[128,512]{1,0:T(8,128)(2,1)S(1)}, bf16[128,512]{1,0:T(8,128)(2,1)S(1)}, u32[]{:S(2)}, u32[]{:S(2)}) %collective-permute-start.9) | collective-permute-done | bytes 131104 | tf_op jit(solution)/shard_map/ppermute | solution.py:352
  49.7 1.8 %collective-permute-done.12.refs_1_ = bf16[512,512]{1,0:T(8,128)(2,1)S(1)} collective-permute-done((bf16[512,512]{1,0:T(8,128)(2,1)S(1)}, bf16[512,512]{1,0:T(8,128)(2,1)S(1)}, u32[]{:S(2)}, u32[]{:S(2)}) %collective-permute-start.12) | collective-permute-done | bytes 524320 | tf_op jit(solution)/shard_map/ppermute | solution.py:352
  51.6 0.9 %finish.1 = bf16[512,512]{1,0:T(8,128)(2,1)} custom-call(f32[512,512]{1,0:T(8,128)S(1)} %with_deltas.1.start_ref, bf16[512,512]{1,0:T(8,128)(2,1)S(1)} %collective-permute-done.10.refs_0_, bf16[512,512]{1,0:T(8,128)(2,1)S(1)} %collective-permute-done.12.refs_1_), custom_call_target="tpu_custom_call" | custom-call | flops 262144 | bytes 2097152 | tf_op jit(solution)/shard_map/finish/pallas_call | solution.py:331
  (19 shorter events, 1.4 us)
Async XLA Ops:
  2.4 15.4 %collective-permute-start = (bf16[2064,128]{1,0:T(8,128)(2,1)S(1)}, bf16[2064,128]{1,0:T(8,128)(2,1)S(1)}, u32[]{:S(2)}, u32[]{:S(2)}) collective-permute-start(bf16[2064,128]{1,0:T(8,128)(2,1)S(1)} %get-tuple-element.35), channel_id=1, source_target_pairs={{0,2},{1,3},{2,0},{3,1},{4,6},{5,7},{6,4},{7,5},{8,10},{9,11},{10,... | collective-permute-start | bytes 1585160 | tf_op jit(solution)/shard_map/ppermute | solution.py:352
  6.7 15.8 %collective-permute-start.2 = (bf16[512,512]{1,0:T(8,128)(2,1)S(1)}, bf16[512,512]{1,0:T(8,128)(2,1)S(1)}, u32[]{:S(2)}, u32[]{:S(2)}) collective-permute-start(bf16[512,512]{1,0:T(8,128)(2,1)S(1)} %first_block.1), channel_id=1, source_target_pairs={{0,4},{12,8},{1,5},{13,9},{2,6},{14,10},{3,7},{15,11},{16,20},{28,... | collective-permute-start | bytes 1572872 | tf_op jit(solution)/shard_map/ppermute | solution.py:381
  10.2 7.6 %copy-start = (bf16[2048,512]{1,0:T(8,128)(2,1)S(1)}, bf16[2048,512]{1,0:T(8,128)(2,1)}, u32[]{:S(2)}) copy-start(bf16[2048,512]{1,0:T(8,128)(2,1)} %down_ref.5) | copy-start | bytes 6291460
  15.8 7.6 %collective-permute-start.1 = (bf16[2064,128]{1,0:T(8,128)(2,1)S(1)}, bf16[2064,128]{1,0:T(8,128)(2,1)S(1)}, u32[]{:S(2)}, u32[]{:S(2)}) collective-permute-start(bf16[2064,128]{1,0:T(8,128)(2,1)S(1)} %get-tuple-element.36), channel_id=1, source_target_pairs={{0,1},{1,0},{2,3},{3,2},{4,5},{5,4},{6,7},{7,6},{8,9},{9,8},{10,11... | collective-permute-start | bytes 1585160 | tf_op jit(solution)/shard_map/ppermute | solution.py:352
  15.9 13.8 %collective-permute-start.3 = (bf16[2064,128]{1,0:T(8,128)(2,1)S(1)}, bf16[2064,128]{1,0:T(8,128)(2,1)S(1)}, u32[]{:S(2)}, u32[]{:S(2)}) collective-permute-start(bf16[2064,128]{1,0:T(8,128)(2,1)S(1)} %get-tuple-element.39), channel_id=1, source_target_pairs={{0,3},{1,2},{2,1},{3,0},{4,7},{5,6},{6,5},{7,4},{8,11},{9,10},{10,... | collective-permute-start | bytes 1585160 | tf_op jit(solution)/shard_map/ppermute | solution.py:352
  16.5 16.5 %collective-permute-start.4 = (bf16[512,512]{1,0:T(8,128)(2,1)S(1)}, bf16[512,512]{1,0:T(8,128)(2,1)S(1)}, u32[]{:S(2)}, u32[]{:S(2)}) collective-permute-start(bf16[512,512]{1,0:T(8,128)(2,1)S(1)} %get-tuple-element.42), channel_id=1, source_target_pairs={{0,4},{12,8},{1,5},{13,9},{2,6},{14,10},{3,7},{15,11},{16,20},{28,... | collective-permute-start | bytes 1572872 | tf_op jit(solution)/shard_map/ppermute | solution.py:384
  22.7 15.3 %collective-permute-start.11 = (bf16[512,512]{1,0:T(8,128)(2,1)S(1)}, bf16[512,512]{1,0:T(8,128)(2,1)S(1)}, u32[]{:S(2)}, u32[]{:S(2)}) collective-permute-start(bf16[512,512]{1,0:T(8,128)(2,1)S(1)} %add_convert_fusion.2), channel_id=1, source_target_pairs={{4,8},{8,4},{5,9},{9,5},{6,10},{10,6},{7,11},{11,7},{20,24},{24,20... | collective-permute-start | bytes 1572872 | tf_op jit(solution)/shard_map/ppermute | solution.py:387
  30.2 10.2 %copy-start.1 = (bf16[512,512]{1,0:T(8,128)(2,1)S(1)}, bf16[512,512]{1,0:T(8,128)(2,1)}, u32[]{:S(2)}) copy-start(bf16[512,512]{1,0:T(8,128)(2,1)} %up_ref.1) | copy-start | bytes 1572868
  30.2 4.5 %collective-permute-start.5 = (bf16[256,128]{1,0:T(8,128)(2,1)S(1)}, bf16[256,128]{1,0:T(8,128)(2,1)S(1)}, u32[]{:S(2)}, u32[]{:S(2)}) collective-permute-start(bf16[256,128]{1,0:T(8,128)(2,1)S(1)} %shrink_partial.5), channel_id=1, source_target_pairs={{0,4},{4,0},{8,12},{12,8},{1,5},{5,1},{9,13},{13,9},{2,6},{6,2},{1... | collective-permute-start | bytes 196616 | tf_op jit(solution)/shard_map/ppermute | solution.py:352
  34.7 5.7 %collective-permute-start.6 = (bf16[256,128]{1,0:T(8,128)(2,1)S(1)}, bf16[256,128]{1,0:T(8,128)(2,1)S(1)}, u32[]{:S(2)}, u32[]{:S(2)}) collective-permute-start(bf16[256,128]{1,0:T(8,128)(2,1)S(1)} %add_convert_fusion.3.one_ref), channel_id=1, source_target_pairs={{0,8},{4,12},{8,0},{12,4},{1,9},{5,13},{9,1},{13,5},{2,10},{6,14},... | collective-permute-start | bytes 196616 | tf_op jit(solution)/shard_map/ppermute | solution.py:352
  37.3 12.4 %collective-permute-start.10 = (bf16[512,512]{1,0:T(8,128)(2,1)S(1)}, bf16[512,512]{1,0:T(8,128)(2,1)S(1)}, u32[]{:S(2)}, u32[]{:S(2)}) collective-permute-start(bf16[512,512]{1,0:T(8,128)(2,1)S(1)} %add_convert_fusion.1), channel_id=1, source_target_pairs={{4,8},{8,4},{5,9},{9,5},{6,10},{10,6},{7,11},{11,7},{20,24},{24,20... | collective-permute-start | bytes 1572872 | tf_op jit(solution)/shard_map/ppermute | solution.py:394
  38.1 13.4 %collective-permute-start.12 = (bf16[512,512]{1,0:T(8,128)(2,1)S(1)}, bf16[512,512]{1,0:T(8,128)(2,1)S(1)}, u32[]{:S(2)}, u32[]{:S(2)}) collective-permute-start(bf16[512,512]{1,0:T(8,128)(2,1)S(1)} %add_convert_fusion), channel_id=1, source_target_pairs={{0,4},{4,0},{8,12},{12,8},{1,5},{5,1},{9,13},{13,9},{2,6},{6,2},{1... | collective-permute-start | bytes 1572872 | tf_op jit(solution)/shard_map/ppermute | solution.py:352
  40.9 1.9 %collective-permute-start.7 = (bf16[128,512]{1,0:T(8,128)(2,1)S(1)}, bf16[128,512]{1,0:T(8,128)(2,1)S(1)}, u32[]{:S(2)}, u32[]{:S(2)}) collective-permute-start(bf16[128,512]{1,0:T(8,128)(2,1)S(1)} %get-tuple-element.45), channel_id=1, source_target_pairs={{0,1},{1,0},{2,3},{3,2},{4,5},{5,4},{6,7},{7,6},{8,9},{9,8},{10,11... | collective-permute-start | bytes 393224 | tf_op jit(solution)/shard_map/ppermute | solution.py:352
  41.0 6.4 %collective-permute-start.8 = (bf16[128,512]{1,0:T(8,128)(2,1)S(1)}, bf16[128,512]{1,0:T(8,128)(2,1)S(1)}, u32[]{:S(2)}, u32[]{:S(2)}) collective-permute-start(bf16[128,512]{1,0:T(8,128)(2,1)S(1)} %get-tuple-element.46), channel_id=1, source_target_pairs={{0,2},{1,3},{2,0},{3,1},{4,6},{5,7},{6,4},{7,5},{8,10},{9,11},{10,... | collective-permute-start | bytes 393224 | tf_op jit(solution)/shard_map/ppermute | solution.py:352
  42.5 6.7 %collective-permute-start.9 = (bf16[128,512]{1,0:T(8,128)(2,1)S(1)}, bf16[128,512]{1,0:T(8,128)(2,1)S(1)}, u32[]{:S(2)}, u32[]{:S(2)}) collective-permute-start(bf16[128,512]{1,0:T(8,128)(2,1)S(1)} %get-tuple-element.47), channel_id=1, source_target_pairs={{0,3},{1,2},{2,1},{3,0},{4,7},{5,6},{6,5},{7,4},{8,11},{9,10},{10,... | collective-permute-start | bytes 393224 | tf_op jit(solution)/shard_map/ppermute | solution.py:352
